TPU v7x, 32 devices: a whole 2x2x4 slice. The times are simulated.
32 devices in a mesh: rows: 32 (over z, y, x, core), rhs: 1.
Axes of the slice: x: 2, y: 2, z: 4, core: 2. Of those that a mesh axis runs over, the one named last changes fastest.
Arguments:
- rhs_block: bfloat16 [4, 32, 64, 256], P(None, 'rows', 'rhs'), may hold values from -6 to 6
- diag_inv: bfloat16 [4, 32, 256, 256], P(None, 'rows'), as said below
- off_tiles: bfloat16 [3, 32, 16, 256, 256], P(None, 'rows', 'rhs'), may hold values from -0.09375 to 0.09375
- pattern: int32 [3, 32, 16], P(None, 'rows'), may hold values from 0 to 31, all different within a row
Outputs:
- forward_sol: bfloat16 [4, 32, 64, 256], P(None, 'rows', 'rhs')
- backward_sol: bfloat16 [4, 32, 64, 256], P(None, 'rows', 'rhs')
Inputs may be any that keep to these rules, and one draw needn't show every extreme that they name: `pattern`: the 16 entries of one block row are distinct. `diag_inv`: every tile is lower triangular with a positive diagonal.
All inputs are finite; a program needn't handle non-finite values.
Results may differ from a plain program's by a relative error of at most 0.013.
Values may be sent and summed in bfloat16 or wider, within the bound.
No kernel may reach another device: no remote copies, remote signals or barrier semaphores. Data moves between devices by JAX's collectives and lax.ppermute only.
A program may use at most 64 MiB of HBM per device.

v0:
```python
import jax
import jax.numpy as jnp
from jax import lax
from jax.sharding import PartitionSpec as P


def to_level(residual, inverse):
    return jnp.einsum("rc,ac->ra", residual, inverse, preferred_element_type=jnp.float32).astype(
        jnp.bfloat16
    )


def from_level(residual, inverse):
    return jnp.dot(residual, inverse, preferred_element_type=jnp.float32).astype(jnp.bfloat16)


def couple_fold(previous, pattern_row, couplings):
    stacked = previous[None]
    pieces = lax.all_gather(stacked, "rows", axis=0, tiled=True)
    number = pieces.shape[0]
    targets = lax.broadcasted_iota(jnp.int32, (1, number), 1)
    chooser = (pattern_row[:, None] == targets).astype(jnp.bfloat16)
    chosen = jnp.einsum("kp,prc->krc", chooser, pieces, preferred_element_type=jnp.float32).astype(
        jnp.bfloat16
    )
    return jnp.einsum("krc,kac->ra", chosen, couplings, preferred_element_type=jnp.float32)


def push_down(solved, pattern_row, couplings, block_rows):
    products = jnp.einsum("ra,kac->krc", solved, couplings, preferred_element_type=jnp.float32)
    targets = lax.broadcasted_iota(jnp.int32, (1, block_rows), 1)
    chooser = (pattern_row[:, None] == targets).astype(jnp.float32)
    outgoing = jnp.einsum("kp,krc->prc", chooser, products, precision=lax.Precision.HIGHEST)
    incoming = lax.all_to_all(
        outgoing.astype(jnp.bfloat16), "rows", split_axis=0, concat_axis=0, tiled=True
    ).astype(outgoing.dtype)
    return jnp.sum(incoming, axis=0)


def body(rhs_block, diag_inv, off_tiles, pattern):
    levels = rhs_block.shape[0]
    block_rows = lax.axis_size("rows")
    splits = 1
    columns = rhs_block.shape[2] // splits
    inverses = diag_inv[:, 0]
    pattern_rows = pattern[:, 0]
    kept_tiles = []
    forward = [to_level(rhs_block[0, 0], inverses[0])]
    for level_now in range(1, levels):
        couplings = lax.all_gather(off_tiles[level_now - 1, 0], "rhs", axis=0, tiled=True)
        kept_tiles.append(couplings)
        portions = []
        portion = 0
        lower_edge = portion * columns
        previous = forward[-1]
        coupled = couple_fold(previous, pattern_rows[level_now - 1], couplings)
        given = rhs_block[level_now, 0, lower_edge : lower_edge + columns].astype(jnp.float32)
        residual = (given - coupled).astype(jnp.bfloat16)
        portions.append(to_level(residual, inverses[level_now]))
        forward.append(portions[0])
    backward = [None] * levels
    backward[levels - 1] = from_level(forward[-1], inverses[levels - 1])
    for level_now in range(levels - 2, -1, -1):
        couplings = kept_tiles[level_now]
        portions = []
        portion = 0
        lower_edge = portion * columns
        solved = backward[level_now + 1]
        pushed = push_down(solved, pattern_rows[level_now], couplings, block_rows)
        known = forward[level_now].astype(jnp.float32)
        residual = (known - pushed).astype(jnp.bfloat16)
        portions.append(from_level(residual, inverses[level_now]))
        backward[level_now] = portions[0]
    return (jnp.stack(forward)[:, None], jnp.stack(backward)[:, None])


def solution(mesh):
    return jax.shard_map(
        body,
        mesh=mesh,
        in_specs=(
            P(None, "rows", "rhs", None),
            P(None, "rows", None, None),
            P(None, "rows", "rhs", None, None),
            P(None, "rows", None),
        ),
        out_specs=(P(None, "rows", "rhs", None), P(None, "rows", "rhs", None)),
        check_vma=False,
    )
```

profile of v0, /device:TPU:0, one launch (start us, length us, event | category | flops | bytes accessed | tf_op | source)
XLA Modules:
  0.0 296.1 jit_solution(2700232413930597055)
XLA Ops:
  7.2 0.0 copy-start.4
  7.2 0.0 copy-start
  7.2 0.0 all-gather.7.cloned.1.call-start
  7.2 1.8 convolution_convert_fusion.7
  9.0 0.0 all-gather.7.cloned.1.call-update
  9.0 0.0 all-gather.9.cloned.1.call-start
  9.1 0.7 slice_bitcast_fusion
  9.8 58.1 %all-gather.7.cloned.1.call-done = bf16[2048,256]{1,0:T(8,128)(2,1)} async-done(((bf16[64,256]{1,0:T(8,128)(2,1)}), bf16[2048,256]{1,0:T(8,128)(2,1)}) %all-gather.7.cloned.1.call-update) | async-done | bytes 1048592 | tf_op jit(solution)/shard_map/all_gather | solution.py:19
  67.9 1.9 fusion.65
  69.7 3.1 %convolution_convert_fusion.6 = bf16[64,256]{1,0:T(8,128)(2,1)} fusion(bf16[3,1,16,256,256]{4,3,2,1,0:T(8,128)(2,1)} %param.6, bf16[16,64,256]{2,0,1:T(8,128)(2,1)S(1)} %fusion.65, bf16[4,1,256,256]{3,2,1,0:T(8,128)(2,1)} %param.5, bf16[4,1,64,256]{3,2,1,0:T(8,128)(2,1)} %param.4), kind=kOutput, calls=%fused_computation.39 | convolution fusion | flops 142671872 | bytes 2818048 | tf_op jit(solution)/shard_map/rc,ac->ra/dot_general | solution.py:8
  72.9 0.0 all-gather.9.cloned.1.call-update
  72.9 0.0 all-gather.11.cloned.1.call-start
  73.0 52.7 %all-gather.9.cloned.1.call-done = bf16[2048,256]{1,0:T(8,128)(2,1)} async-done(((bf16[64,256]{1,0:T(8,128)(2,1)}), bf16[2048,256]{1,0:T(8,128)(2,1)}) %all-gather.9.cloned.1.call-update) | async-done | bytes 1048592 | tf_op jit(solution)/shard_map/all_gather | solution.py:19
  125.7 1.9 fusion.63
  127.6 0.0 copy-done.4
  127.6 0.0 copy-done
  127.6 3.1 %convolution_convert_fusion.5 = bf16[64,256]{1,0:T(8,128)(2,1)} fusion(bf16[3,1,16,256,256]{4,3,2,1,0:T(8,128)(2,1)} %param.6, bf16[16,64,256]{2,0,1:T(8,128)(2,1)S(1)} %fusion.63, bf16[4,1,256,256]{3,2,1,0:T(8,128)(2,1)S(1)} %copy-done, bf16[4,1,64,256]{3,2,1,0:T(8,128)(2,1)S(1)} %copy-done.4), kind=kOutput, calls=%fused_computation.38 | convolution fusion | flops 142671872 | bytes 2818048 | tf_op jit(solution)/shard_map/rc,ac->ra/dot_general | solution.py:8
  130.7 0.0 all-gather.11.cloned.1.call-update
  130.7 52.8 %all-gather.11.cloned.1.call-done = bf16[2048,256]{1,0:T(8,128)(2,1)} async-done(((bf16[64,256]{1,0:T(8,128)(2,1)}), bf16[2048,256]{1,0:T(8,128)(2,1)}) %all-gather.11.cloned.1.call-update) | async-done | bytes 1048592 | tf_op jit(solution)/shard_map/all_gather | solution.py:19
  183.5 1.9 fusion.61
  185.4 0.0 copy-start.3
  185.4 0.0 slice-start
  185.4 2.6 convolution_convert_fusion.4
  188.1 0.1 convolution_convert_fusion.3
  188.2 2.1 fusion
  190.3 0.0 slice-start.1
  190.3 1.6 fusion.56
  191.9 0.6 copy.54
  192.5 29.6 %all_to_all.15 = bf16[32,64,256]{2,1,0:T(8,128)(2,1)S(1)} all-to-all(bf16[32,64,256]{2,1,0:T(8,128)(2,1)S(1)} %copy.54), channel_id=1, replica_groups=mesh['rows'=32,'rhs'=1] {'rows'}, dimensions={0} | all-to-all | bytes 2097152 | tf_op jit(solution)/shard_map/all_to_all | solution.py:34
  222.1 0.0 copy-start.2
  222.1 0.2 convert_reduce_fusion.2
  222.2 0.0 copy-done.3
  222.2 0.1 convolution_convert_fusion.2
  222.4 0.0 slice-done
  222.4 0.0 slice-done.1
  222.4 0.5 fusion.4
  222.9 1.6 fusion.54
  224.5 0.6 copy.53
  225.1 0.0 copy-start.1
  225.1 29.7 %all_to_all.16 = bf16[32,64,256]{2,1,0:T(8,128)(2,1)S(1)} all-to-all(bf16[32,64,256]{2,1,0:T(8,128)(2,1)S(1)} %copy.53), channel_id=1, replica_groups=mesh['rows'=32,'rhs'=1] {'rows'}, dimensions={0} | all-to-all | bytes 2097152 | tf_op jit(solution)/shard_map/all_to_all | solution.py:34
  254.8 0.2 convert_reduce_fusion.1
  254.9 0.0 copy-done.2
  254.9 0.1 convolution_convert_fusion.1
  255.1 0.5 fusion.8
  255.6 1.6 fusion.52
  257.1 1.6 copy.52
  258.7 3.6 %all-to-all-start.2 = ((bf16[32,64,256]{2,1,0:T(8,128)(2,1)}), bf16[32,64,256]{2,1,0:T(8,128)(2,1)S(1)}, u32[]{:S(2)}, u32[]{:S(2)}) async-start(bf16[32,64,256]{2,1,0:T(8,128)(2,1)} %copy.52), calls=%async_computation.2 | async-start | bytes 2097152 | tf_op jit(solution)/shard_map/all_to_all | solution.py:34
  262.3 0.0 copy-done.1
  262.3 0.7 maximum_bitcast_fusion
  263.0 25.6 %all-to-all-done.2 = bf16[32,64,256]{2,1,0:T(8,128)(2,1)S(1)} async-done(((bf16[32,64,256]{2,1,0:T(8,128)(2,1)}), bf16[32,64,256]{2,1,0:T(8,128)(2,1)S(1)}, u32[]{:S(2)}, u32[]{:S(2)}) %all-to-all-start.2) | async-done | bytes 1048608 | tf_op jit(solution)/shard_map/all_to_all | solution.py:34
  288.5 0.2 convert_reduce_fusion
  288.7 0.1 fusion.45
  288.8 0.7 maximum_bitcast_fusion.1
  (1 shorter events, 0.0 us)
Async XLA Ops:
  7.2 120.4 %copy-start.4 = (bf16[4,1,64,256]{3,2,1,0:T(8,128)(2,1)S(1)}, bf16[4,1,64,256]{3,2,1,0:T(8,128)(2,1)}, u32[]{:S(2)}) copy-start(bf16[4,1,64,256]{3,2,1,0:T(8,128)(2,1)} %param.4) | copy-start | bytes 393220
  7.2 120.4 %copy-start = (bf16[4,1,256,256]{3,2,1,0:T(8,128)(2,1)S(1)}, bf16[4,1,256,256]{3,2,1,0:T(8,128)(2,1)}, u32[]{:S(2)}) copy-start(bf16[4,1,256,256]{3,2,1,0:T(8,128)(2,1)} %param.5) | copy-start | bytes 1572868
  7.2 60.7 %all-gather.7.cloned.1.call-start = ((), (), s32[]{:S(2)}) async-start(), calls=%async_computation.3 | async-start | bytes 1081344 | tf_op jit(solution)/shard_map/all_gather | solution.py:19
  9.0 116.6 %all-gather.9.cloned.1.call-start = ((), (), s32[]{:S(2)}) async-start(), calls=%async_computation.4 | async-start | bytes 1081344 | tf_op jit(solution)/shard_map/all_gather | solution.py:19
  72.9 110.6 %all-gather.11.cloned.1.call-start = ((), (), s32[]{:S(2)}) async-start(), calls=%async_computation.5 | async-start | bytes 1081344 | tf_op jit(solution)/shard_map/all_gather | solution.py:19
  185.4 36.8 %copy-start.3 = (bf16[64,256]{1,0:T(8,128)(2,1)S(1)}, bf16[64,256]{1,0:T(8,128)(2,1)}, u32[]{:S(2)}) copy-start(bf16[64,256]{1,0:T(8,128)(2,1)} %convolution_convert_fusion.5) | copy-start | bytes 98308
  185.4 37.0 %slice-start = ((s8[6291456]{0:T(1024)(128)(4,1)}), s8[2097152]{0:T(1024)(128)(4,1)S(1)}, s32[]{:S(2)}) async-start(s8[6291456]{0:T(1024)(128)(4,1)} %bitcast.161), calls=%async_computation.6 | async-start | bytes 4194304
  190.3 32.1 %slice-start.1 = ((s8[6291456]{0:T(1024)(128)(4,1)}), s8[4194304]{0:T(1024)(128)(4,1)S(1)}, s32[]{:S(2)}) async-start(s8[6291456]{0:T(1024)(128)(4,1)} %bitcast.161), calls=%async_computation.7 | async-start | bytes 8388608
  222.1 32.8 %copy-start.2 = (bf16[64,256]{1,0:T(8,128)(2,1)S(1)}, bf16[64,256]{1,0:T(8,128)(2,1)}, u32[]{:S(2)}) copy-start(bf16[64,256]{1,0:T(8,128)(2,1)} %convolution_convert_fusion.6) | copy-start | bytes 98308
  225.1 37.2 %copy-start.1 = (bf16[64,256]{1,0:T(8,128)(2,1)S(1)}, bf16[64,256]{1,0:T(8,128)(2,1)}, u32[]{:S(2)}) copy-start(bf16[64,256]{1,0:T(8,128)(2,1)} %convolution_convert_fusion.7) | copy-start | bytes 98308
  258.7 29.9 %all-to-all-start.2 = ((bf16[32,64,256]{2,1,0:T(8,128)(2,1)}), bf16[32,64,256]{2,1,0:T(8,128)(2,1)S(1)}, u32[]{:S(2)}, u32[]{:S(2)}) async-start(bf16[32,64,256]{2,1,0:T(8,128)(2,1)} %copy.52), calls=%async_computation.2 | async-start | bytes 2097152 | tf_op jit(solution)/shard_map/all_to_all | solution.py:34
Sparse Core Ops, SparseCore 0:
  11.5 56.3 all-gather.6
  73.0 52.6 all-gather.8
  130.9 52.6 all-gather.10
where the time goes:
time: 297 us; the launch traced here: 296 us
  waiting for transfers between devices  189 us (64%)
  blocking collectives  59.3 us (20%)
  matrix products  24.7 us (8%)
  between operations  13.9 us (5%)
  starting transfers between devices  3.74 us (1%)
  local copies, waits for them, and re-layouts  3.47 us (1%)
    all_gather x3, waiting for transfers between devices, couple_fold(): pieces = lax.all_gather(stacked, 'rows', axis=0, tiled=True)  164 us
    all_to_all x2, blocking collectives, push_down(): lax.all_to_all(outgoing.astype(jnp.bfloat16), 'rows', split_axis=0, conca...  59.3 us
    all_to_all x1, waiting for transfers between devices, push_down(): lax.all_to_all(outgoing.astype(jnp.bfloat16), 'rows', split_axis=0, conca...  25.6 us
    dot_general x4, matrix products, to_level(): jnp.einsum('rc,ac->ra', residual, inverse, preferred_element_type=jnp.flo...  10.7 us
  transfers between devices with their start and end apart: 4, of which 4 were waited for; matrix products, arithmetic and copies ran while one was open for 0% of the time, Pallas kernels for 0%

commit v1 on v0

v1 whole, which is shorter than its diff:
```python
import functools

import jax
import jax.numpy as jnp
from jax import lax
from jax.experimental import pallas as pl
from jax.experimental.pallas import tpu as pltpu
from jax.sharding import PartitionSpec as P

VMEM_SPEC = pl.BlockSpec(memory_space=pltpu.VMEM)
SMEM_SPEC = pl.BlockSpec(memory_space=pltpu.SMEM)
VMEM_GRANT = 24 * 1024 * 1024


def swap(value, mask):
    size = lax.axis_size("rows")
    return lax.ppermute(value, "rows", [(i, i ^ mask) for i in range(size)])


def times_transposed(left, right):
    return lax.dot_general(left, right, (((1,), (1,)), ((), ())), preferred_element_type=jnp.float32)


def times(left, right):
    return jnp.dot(left, right, preferred_element_type=jnp.float32)


def call(kernel, out_shape, operands, smem=0, scratch=(), flops=0, moved=0):
    return pl.pallas_call(
        kernel,
        out_shape=out_shape,
        in_specs=[SMEM_SPEC] * smem + [VMEM_SPEC] * (len(operands) - smem),
        out_specs=jax.tree.map(lambda _: VMEM_SPEC, out_shape),
        scratch_shapes=list(scratch),
        compiler_params=pltpu.CompilerParams(vmem_limit_bytes=VMEM_GRANT),
        cost_estimate=pl.CostEstimate(flops=flops, bytes_accessed=moved, transcendentals=0),
    )(*operands)


def first_kernel(rhs_own, rhs_other, diag_own, diag_other, out):
    out[0] = times_transposed(rhs_own[...], diag_own[...]).astype(out.dtype)
    out[1] = times_transposed(rhs_other[...], diag_other[...]).astype(out.dtype)


def gather_columns(parts, held):
    count = parts[0].shape[0] * 2
    for j, part in enumerate(parts):
        for z in range(part.shape[0]):
            for s in range(2):
                held[j * count + z * 2 + s] = part[z, s]


def forward_step(slots, parts, tiles, rhs, diag, held):
    gather_columns(parts, held)
    solved = []
    for i in range(2):
        total = None
        for k in range(tiles[i].shape[0]):
            term = times_transposed(held[slots[i, k]], tiles[i][k])
            total = term if total is None else total + term
        residual = (rhs[i][...].astype(jnp.float32) - total).astype(jnp.bfloat16)
        solved.append(times_transposed(residual, diag[i][...]).astype(jnp.bfloat16))
    return solved


def push_step(slots, solved, tiles, total):
    total[...] = jnp.zeros_like(total)
    for i in range(2):
        for k in range(tiles[i].shape[0]):
            total[slots[i, k]] += times(solved[i], tiles[i][k])


def spread(total, keep, outs):
    count = keep.shape[0] * 2
    for z in range(keep.shape[0]):
        for s in range(2):
            keep[z, s] = total[z * 2 + s]
            for j, out in enumerate(outs):
                out[z, s] = total[(j + 1) * count + z * 2 + s].astype(out.dtype)


def forward_kernel(slots, *refs):
    parts, (t0, t1, r0, r1, d0, d1, out, held) = refs[:-8], refs[-8:]
    solved = forward_step(slots, parts, (t0, t1), (r0, r1), (d0, d1), held)
    out[0], out[1] = solved


def turn_kernel(slots, push_slots, *refs):
    parts = refs[:4]
    t0, t1, r0, r1, d0, d1, p0, p1, out, back, keep, o1, o2, o3, held, total = refs[4:]
    solved = forward_step(slots, parts, (t0, t1), (r0, r1), (d0, d1), held)
    out[0], out[1] = solved
    down = [times(solved[i], d[...]).astype(jnp.bfloat16) for i, d in enumerate((d0, d1))]
    back[0], back[1] = down
    push_step(push_slots, down, (p0, p1), total)
    spread(total, keep, (o1, o2, o3))


def reduce_kernel(keep, a, b, c, own, *outs):
    for z in range(keep.shape[0]):
        terms = [part[z].astype(jnp.float32) for part in (a, b, c)]
        value = keep[z] + ((terms[0] + terms[1]) + terms[2])
        if z == 0:
            own[...] = value
        else:
            outs[z - 1][...] = value.astype(jnp.bfloat16)


def backward_step(own, arrived, known, diag):
    pushed = own[...]
    for part in arrived:
        pushed = pushed + part[...].astype(jnp.float32)
    residual = (known[...].astype(jnp.float32) - pushed).astype(jnp.bfloat16)
    return [times(residual[i], d[...]).astype(jnp.bfloat16) for i, d in enumerate(diag)]


def backward_kernel(push_slots, own, known, d0, d1, p0, p1, *refs):
    arrived, (back, keep, o1, o2, o3, total) = refs[:-6], refs[-6:]
    down = backward_step(own, arrived, known, (d0, d1))
    back[0], back[1] = down
    push_step(push_slots, down, (p0, p1), total)
    spread(total, keep, (o1, o2, o3))


def last_kernel(own, known, d0, d1, *refs):
    arrived, back = refs[:-1], refs[-1]
    down = backward_step(own, arrived, known, (d0, d1))
    back[0], back[1] = down


def join_kernel(core, own, other, out):
    half = own.shape[1]
    here = pl.multiple_of(core[0] * half, half)
    there = pl.multiple_of((1 - core[0]) * half, half)
    out[:, 0, pl.ds(here, half)] = own[...]
    out[:, 0, pl.ds(there, half)] = other[...]


def body(rhs_block, diag_inv, off_tiles, pattern):
    levels, _, width, size = rhs_block.shape
    devices = lax.axis_size("rows")
    half = width // 2
    me = lax.axis_index("rows")
    core = lax.rem(me, 2)
    low = [2 * j for j in range(4)]
    high = [8 * j for j in range(devices // 8)]
    deep = len(high)
    if lax.axis_size("rhs") > 1:
        off_tiles = lax.all_gather(off_tiles, "rhs", axis=2, tiled=True)
    fan = off_tiles.shape[2]

    rhs = rhs_block[:, 0]
    rhs_own = lax.dynamic_slice_in_dim(rhs, core * half, half, 1)
    rhs_other = swap(lax.dynamic_slice_in_dim(rhs, (1 - core) * half, half, 1), 1)
    diag_own = [diag_inv[l, 0] for l in range(levels)]
    diag_other = [swap(d, 1) for d in diag_own]
    both = jnp.stack([pattern[:, 0], swap(pattern[:, 0], 1)], axis=1)
    place = jnp.bitwise_xor(both, me.astype(jnp.int32))
    slots = ((place >> 1) & 3) * (2 * deep) + (place >> 3) * 2 + (place & 1)
    tiles_own = [off_tiles[l, 0] for l in range(levels - 1)]
    tiles_other = [swap(t, 1) for t in tiles_own]

    pair = jax.ShapeDtypeStruct((2, half, size), jnp.bfloat16)
    pair_wide = jax.ShapeDtypeStruct((2, half, size), jnp.float32)
    column = jax.ShapeDtypeStruct((deep, 2, half, size), jnp.bfloat16)
    column_wide = jax.ShapeDtypeStruct((deep, 2, half, size), jnp.float32)
    held = pltpu.VMEM((devices, half, size), jnp.bfloat16)
    total = pltpu.VMEM((devices, half, size), jnp.float32)
    work = 2 * 2 * fan * half * size * size

    def gathered(block):
        stack = jnp.stack([block] + [swap(block, m) for m in high[1:]])
        return [stack] + [swap(stack, m) for m in low[1:]]

    def scattered(keep, outs):
        arrived = [swap(out, m) for out, m in zip(outs, low[1:])]
        summed = call(reduce_kernel, [pair_wide] + [pair] * (deep - 1), [keep] + arrived)
        return summed[0], [swap(part, m) for part, m in zip(summed[1:], high[1:])]

    forward = [call(first_kernel, pair, [rhs_own[0], rhs_other[0], diag_own[0], diag_other[0]])]
    for l in range(1, levels - 1):
        parts = gathered(forward[-1])
        forward.append(
            call(
                forward_kernel,
                pair,
                [slots[l - 1]] + parts
                + [tiles_own[l - 1], tiles_other[l - 1], rhs_own[l], rhs_other[l], diag_own[l], diag_other[l]],
                smem=1,
                scratch=[held],
                flops=work,
            )
        )
    l = levels - 1
    parts = gathered(forward[-1])
    top, down, keep, *outs = call(
        turn_kernel,
        [pair, pair, column_wide] + [column] * 3,
        [slots[l - 1], slots[l - 1]] + parts
        + [tiles_own[l - 1], tiles_other[l - 1], rhs_own[l], rhs_other[l], diag_own[l], diag_other[l]]
        + [tiles_own[l - 1], tiles_other[l - 1]],
        smem=2,
        scratch=[held, total],
        flops=2 * work,
    )
    forward.append(top)
    backward = [None] * levels
    backward[l] = down
    for l in range(levels - 2, 0, -1):
        own, arrived = scattered(keep, outs)
        down, keep, *outs = call(
            backward_kernel,
            [pair, column_wide] + [column] * 3,
            [slots[l - 1], own, forward[l], diag_own[l], diag_other[l], tiles_own[l - 1], tiles_other[l - 1]] + arrived,
            smem=1,
            scratch=[total],
            flops=work,
        )
        backward[l] = down
    own, arrived = scattered(keep, outs)
    backward[0] = call(last_kernel, pair, [own, forward[0], diag_own[0], diag_other[0]] + arrived)

    where = core.astype(jnp.int32)[None]
    whole = jax.ShapeDtypeStruct((levels, 1, width, size), jnp.bfloat16)

    def joined(blocks):
        mine = jnp.stack([b[0] for b in blocks])
        other = swap(jnp.stack([b[1] for b in blocks]), 1)
        return call(join_kernel, whole, [where, mine, other], smem=1)

    return joined(forward), joined(backward)


def solution(mesh):
    return jax.shard_map(
        body,
        mesh=mesh,
        in_specs=(
            P(None, "rows", "rhs", None),
            P(None, "rows", None, None),
            P(None, "rows", "rhs", None, None),
            P(None, "rows", None),
        ),
        out_specs=(P(None, "rows", "rhs", None), P(None, "rows", "rhs", None)),
        check_vma=False,
    )
```

time: 297 us -> 143 us (0.48)
  waiting for transfers between devices: 189 us -> 59.8 us
  blocking collectives: 59.3 us -> 0 us
  starting transfers between devices: 3.74 us -> 53.3 us
  matrix products: 24.7 us -> 0 us
  Pallas kernels: 0 us -> 23.4 us
  between operations: 13.9 us -> 0.85 us
    all_gather x3 -> x0, waiting for transfers between devices: 164 us -> none  [couple_fold(): pieces = lax.all_gather(stacked, 'rows', axis=0, tiled=True)]
    ppermute x0 -> x47, waiting for transfers between devices: none -> 59.8 us  [swap(): return lax.ppermute(value, 'rows', [(i, i ^ mask) for i in range(size)])]
    all_to_all x2 -> x0, blocking collectives: 59.3 us -> none  [push_down(): lax.all_to_all(outgoing.astype(jnp.bfloat16), 'rows', split_axis=0, conca...]
    ppermute x0 -> x47, starting transfers between devices: none -> 53.3 us  [swap(): return lax.ppermute(value, 'rows', [(i, i ^ mask) for i in range(size)])]
    all_to_all x1 -> x0, waiting for transfers between devices: 25.6 us -> none  [push_down(): lax.all_to_all(outgoing.astype(jnp.bfloat16), 'rows', split_axis=0, conca...]
    dot_general x17 -> x0, matrix products: 24.7 us -> none  [the longest x4 10.7 us: to_level(): jnp.einsum('rc,ac->ra', residual, inverse, preferred_element_type=jnp.flo...]
    pallas_call x0 -> x12, Pallas kernels: none -> 23.4 us  [call(): pl.pallas_call(kernel, out_shape=out_shape, in_specs=[SMEM_SPEC] * smem +...]
    squeeze x0 -> x4, local copies, waits for them, and re-layouts: none -> 5.57 us  [the longest x1 5.52 us: body(): tiles_own = [off_tiles[l, 0] for l in range(levels - 1)]]
  transfers between devices with their start and end apart: 4 -> 47, of which waited for: 4 -> 32; matrix products, arithmetic and copies ran while one was open for 0% -> 0% of each run, Pallas kernels for 0% -> 9%
where the time goes in v1:
time: 143 us
  waiting for transfers between devices  59.8 us (42%)
  starting transfers between devices  53.3 us (37%)
  Pallas kernels  23.4 us (16%)
  local copies, waits for them, and re-layouts  5.62 us (4%)
    ppermute x47, waiting for transfers between devices, swap(): return lax.ppermute(value, 'rows', [(i, i ^ mask) for i in range(size)])  59.8 us
    ppermute x47, starting transfers between devices, swap(): return lax.ppermute(value, 'rows', [(i, i ^ mask) for i in range(size)])  53.3 us
    pallas_call x12, Pallas kernels, call(): pl.pallas_call(kernel, out_shape=out_shape, in_specs=[SMEM_SPEC] * smem +...  23.4 us
    squeeze x1, local copies, waits for them, and re-layouts, body(): tiles_own = [off_tiles[l, 0] for l in range(levels - 1)]  5.52 us
  transfers between devices with their start and end apart: 47, of which 32 were waited for; matrix products, arithmetic and copies ran while one was open for 0% of the time, Pallas kernels for 9%

profile of v1, /device:TPU:0, one launch (start us, length us, event | category | flops | bytes accessed | tf_op | source)
XLA Modules:
  0.0 143.1 jit_solution(6756331213026732734)
XLA Ops:
  0.7 5.5 %slice_bitcast_fusion = (bf16[16,256,256]{2,1,0:T(8,128)(2,1)S(1)}, bf16[16,256,256]{2,1,0:T(8,128)(2,1)}, bf16[16,256,256]{2,1,0:T(8,128)(2,1)}) fusion(bf16[3,1,16,256,256]{4,3,2,1,0:T(8,128)(2,1)} %param.6), kind=kLoop, calls=%fused_computation | loop fusion | bytes 12582912 | tf_op jit(solution)/shard_map/squeeze | solution.py:160
  7.8 2.9 %collective-permute-done = bf16[4,32,256]{2,1,0:T(8,128)(2,1)S(1)} collective-permute-done((bf16[4,32,256]{2,1,0:T(8,128)(2,1)S(1)}, bf16[4,32,256]{2,1,0:T(8,128)(2,1)S(1)}, u32[]{:S(2)}, u32[]{:S(2)}) %collective-permute-start) | collective-permute-done | bytes 65568 | tf_op jit(solution)/shard_map/ppermute | solution.py:17
  10.7 0.6 collective-permute-done.1.diag_other.d1
  11.4 5.0 %collective-permute-start.5 = (bf16[2,32,256]{2,1,0:T(8,128)(2,1)S(1)}, bf16[2,32,256]{2,1,0:T(8,128)(2,1)S(1)}, u32[]{:S(2)}, u32[]{:S(2)}) collective-permute-start(bf16[2,32,256]{2,1,0:T(8,128)(2,1)S(1)} %shard_map.59.known), channel_id=1, source_target_pairs={{0,24},{1,25},{2,26},{3,27},{4,28},{5,29},{6,30},{7,31},{8,16},{9,... | collective-permute-start | bytes 98312 | tf_op jit(solution)/shard_map/ppermute | solution.py:17
  16.4 2.0 %collective-permute-done.5 = bf16[2,32,256]{2,1,0:T(8,128)(2,1)S(1)} collective-permute-done((bf16[2,32,256]{2,1,0:T(8,128)(2,1)S(1)}, bf16[2,32,256]{2,1,0:T(8,128)(2,1)S(1)}, u32[]{:S(2)}, u32[]{:S(2)}) %collective-permute-start.5) | collective-permute-done | bytes 32800 | tf_op jit(solution)/shard_map/ppermute | solution.py:17
  18.5 0.9 collective-permute-start.4
  19.3 1.0 collective-permute-done.3
  20.4 2.9 %collective-permute-done.4 = bf16[2,32,256]{2,1,0:T(8,128)(2,1)S(1)} collective-permute-done((bf16[2,32,256]{2,1,0:T(8,128)(2,1)S(1)}, bf16[2,32,256]{2,1,0:T(8,128)(2,1)S(1)}, u32[]{:S(2)}, u32[]{:S(2)}) %collective-permute-start.4) | collective-permute-done | bytes 32800 | tf_op jit(solution)/shard_map/ppermute | solution.py:17
  23.3 1.6 %collective-permute-start.6 = (bf16[4,2,32,256]{3,2,1,0:T(8,128)(2,1)S(1)}, bf16[4,2,32,256]{3,2,1,0:T(8,128)(2,1)S(1)}, u32[]{:S(2)}, u32[]{:S(2)}) collective-permute-start(bf16[4,2,32,256]{3,2,1,0:T(8,128)(2,1)S(1)} %pad_maximum_fusion.refs_0_), channel_id=1, source_target_pairs={{0,2},{1,3},{2,0},{3,1},{4,6},{5,7},{6,4},{7,5},{8,10},{9,11},{10,... | collective-permute-start | bytes 393224 | tf_op jit(solution)/shard_map/ppermute | solution.py:17
  25.0 1.6 %collective-permute-start.7 = (bf16[4,2,32,256]{3,2,1,0:T(8,128)(2,1)S(1)}, bf16[4,2,32,256]{3,2,1,0:T(8,128)(2,1)S(1)}, u32[]{:S(2)}, u32[]{:S(2)}) collective-permute-start(bf16[4,2,32,256]{3,2,1,0:T(8,128)(2,1)S(1)} %pad_maximum_fusion.refs_0_), channel_id=1, source_target_pairs={{0,4},{1,5},{2,6},{3,7},{4,0},{5,1},{6,2},{7,3},{8,12},{9,13},{10,... | collective-permute-start | bytes 393224 | tf_op jit(solution)/shard_map/ppermute | solution.py:17
  26.6 2.8 %collective-permute-done.6.refs_1_ = bf16[4,2,32,256]{3,2,1,0:T(8,128)(2,1)S(1)} collective-permute-done((bf16[4,2,32,256]{3,2,1,0:T(8,128)(2,1)S(1)}, bf16[4,2,32,256]{3,2,1,0:T(8,128)(2,1)S(1)}, u32[]{:S(2)}, u32[]{:S(2)}) %collective-permute-start.6) | collective-permute-done | bytes 131104 | tf_op jit(solution)/shard_map/ppermute | solution.py:17
  29.3 2.5 %collective-permute-start.8 = (bf16[4,2,32,256]{3,2,1,0:T(8,128)(2,1)S(1)}, bf16[4,2,32,256]{3,2,1,0:T(8,128)(2,1)S(1)}, u32[]{:S(2)}, u32[]{:S(2)}) collective-permute-start(bf16[4,2,32,256]{3,2,1,0:T(8,128)(2,1)S(1)} %pad_maximum_fusion.refs_0_), channel_id=1, source_target_pairs={{0,6},{1,7},{2,4},{3,5},{4,2},{5,3},{6,0},{7,1},{8,14},{9,15},{10,... | collective-permute-start | bytes 393224 | tf_op jit(solution)/shard_map/ppermute | solution.py:17
  31.8 3.5 %collective-permute-done.8.refs_3_ = bf16[4,2,32,256]{3,2,1,0:T(8,128)(2,1)S(1)} collective-permute-done((bf16[4,2,32,256]{3,2,1,0:T(8,128)(2,1)S(1)}, bf16[4,2,32,256]{3,2,1,0:T(8,128)(2,1)S(1)}, u32[]{:S(2)}, u32[]{:S(2)}) %collective-permute-start.8) | collective-permute-done | bytes 131104 | tf_op jit(solution)/shard_map/ppermute | solution.py:17
  35.3 4.7 %shard_map.60.known = bf16[2,32,256]{2,1,0:T(8,128)(2,1)S(1)} custom-call(s32[2,16]{1,0:T(2,128)S(1)} %bitcast.56, bf16[4,2,32,256]{3,2,1,0:T(8,128)(2,1)S(1)} %pad_maximum_fusion.refs_0_, bf16[4,2,32,256]{3,2,1,0:T(8,128)(2,1)S(1)} %collective-permute-done.6.refs_1_, bf16[4,2,32,256]{3,2,1,0:T(8,128)(2,1)S(1)} %collective-permute-done.7.refs_2_, ...), custom_call_target="tpu_custom_call" | custom-call | flops 134217728 | tf_op jit(solution)/shard_map/pallas_call | solution.py:29
  40.0 1.3 collective-permute-start.11
  41.4 2.9 %collective-permute-start.12 = (bf16[2,32,256]{2,1,0:T(8,128)(2,1)S(1)}, bf16[2,32,256]{2,1,0:T(8,128)(2,1)S(1)}, u32[]{:S(2)}, u32[]{:S(2)}) collective-permute-start(bf16[2,32,256]{2,1,0:T(8,128)(2,1)S(1)} %shard_map.60.known), channel_id=1, source_target_pairs={{0,16},{1,17},{2,18},{3,19},{4,20},{5,21},{6,22},{7,23},{8,24},{9,... | collective-permute-start | bytes 98312 | tf_op jit(solution)/shard_map/ppermute | solution.py:17
  44.5 2.1 %collective-permute-done.12 = bf16[2,32,256]{2,1,0:T(8,128)(2,1)S(1)} collective-permute-done((bf16[2,32,256]{2,1,0:T(8,128)(2,1)S(1)}, bf16[2,32,256]{2,1,0:T(8,128)(2,1)S(1)}, u32[]{:S(2)}, u32[]{:S(2)}) %collective-permute-start.12) | collective-permute-done | bytes 32800 | tf_op jit(solution)/shard_map/ppermute | solution.py:17
  46.6 3.5 %collective-permute-done.13 = bf16[2,32,256]{2,1,0:T(8,128)(2,1)S(1)} collective-permute-done((bf16[2,32,256]{2,1,0:T(8,128)(2,1)S(1)}, bf16[2,32,256]{2,1,0:T(8,128)(2,1)S(1)}, u32[]{:S(2)}, u32[]{:S(2)}) %collective-permute-start.13) | collective-permute-done | bytes 32800 | tf_op jit(solution)/shard_map/ppermute | solution.py:17
  50.1 1.6 %collective-permute-start.14 = (bf16[4,2,32,256]{3,2,1,0:T(8,128)(2,1)S(1)}, bf16[4,2,32,256]{3,2,1,0:T(8,128)(2,1)S(1)}, u32[]{:S(2)}, u32[]{:S(2)}) collective-permute-start(bf16[4,2,32,256]{3,2,1,0:T(8,128)(2,1)S(1)} %pad_maximum_fusion.1.refs_0_), channel_id=1, source_target_pairs={{0,2},{1,3},{2,0},{3,1},{4,6},{5,7},{6,4},{7,5},{8,10},{9,11},{10,... | collective-permute-start | bytes 393224 | tf_op jit(solution)/shard_map/ppermute | solution.py:17
  51.6 1.5 %collective-permute-start.15 = (bf16[4,2,32,256]{3,2,1,0:T(8,128)(2,1)S(1)}, bf16[4,2,32,256]{3,2,1,0:T(8,128)(2,1)S(1)}, u32[]{:S(2)}, u32[]{:S(2)}) collective-permute-start(bf16[4,2,32,256]{3,2,1,0:T(8,128)(2,1)S(1)} %pad_maximum_fusion.1.refs_0_), channel_id=1, source_target_pairs={{0,4},{1,5},{2,6},{3,7},{4,0},{5,1},{6,2},{7,3},{8,12},{9,13},{10,... | collective-permute-start | bytes 393224 | tf_op jit(solution)/shard_map/ppermute | solution.py:17
  53.6 1.5 %collective-permute-done.14.refs_1_ = bf16[4,2,32,256]{3,2,1,0:T(8,128)(2,1)S(1)} collective-permute-done((bf16[4,2,32,256]{3,2,1,0:T(8,128)(2,1)S(1)}, bf16[4,2,32,256]{3,2,1,0:T(8,128)(2,1)S(1)}, u32[]{:S(2)}, u32[]{:S(2)}) %collective-permute-start.14) | collective-permute-done | bytes 131104 | tf_op jit(solution)/shard_map/ppermute | solution.py:17
  55.1 1.5 %collective-permute-done.15.refs_2_ = bf16[4,2,32,256]{3,2,1,0:T(8,128)(2,1)S(1)} collective-permute-done((bf16[4,2,32,256]{3,2,1,0:T(8,128)(2,1)S(1)}, bf16[4,2,32,256]{3,2,1,0:T(8,128)(2,1)S(1)}, u32[]{:S(2)}, u32[]{:S(2)}) %collective-permute-start.15) | collective-permute-done | bytes 131104 | tf_op jit(solution)/shard_map/ppermute | solution.py:17
  56.6 2.4 %collective-permute-done.16.refs_3_ = bf16[4,2,32,256]{3,2,1,0:T(8,128)(2,1)S(1)} collective-permute-done((bf16[4,2,32,256]{3,2,1,0:T(8,128)(2,1)S(1)}, bf16[4,2,32,256]{3,2,1,0:T(8,128)(2,1)S(1)}, u32[]{:S(2)}, u32[]{:S(2)}) %collective-permute-start.16) | collective-permute-done | bytes 131104 | tf_op jit(solution)/shard_map/ppermute | solution.py:17
  59.0 4.7 %shard_map.61.known = bf16[2,32,256]{2,1,0:T(8,128)(2,1)S(1)} custom-call(s32[2,16]{1,0:T(2,128)S(1)} %bitcast.58, bf16[4,2,32,256]{3,2,1,0:T(8,128)(2,1)S(1)} %pad_maximum_fusion.1.refs_0_, bf16[4,2,32,256]{3,2,1,0:T(8,128)(2,1)S(1)} %collective-permute-done.14.refs_1_, bf16[4,2,32,256]{3,2,1,0:T(8,128)(2,1)S(1)} %collective-permute-done.15.refs_2_, ...), custom_call_target="tpu_custom_call" | custom-call | flops 134217728 | tf_op jit(solution)/shard_map/pallas_call | solution.py:29
  63.8 0.9 collective-permute-start.20
  64.7 3.5 %collective-permute-start.21 = (bf16[2,32,256]{2,1,0:T(8,128)(2,1)S(1)}, bf16[2,32,256]{2,1,0:T(8,128)(2,1)S(1)}, u32[]{:S(2)}, u32[]{:S(2)}) collective-permute-start(bf16[2,32,256]{2,1,0:T(8,128)(2,1)S(1)} %shard_map.61.known), channel_id=1, source_target_pairs={{0,24},{1,25},{2,26},{3,27},{4,28},{5,29},{6,30},{7,31},{8,16},{9,... | collective-permute-start | bytes 98312 | tf_op jit(solution)/shard_map/ppermute | solution.py:17
  68.6 1.7 %collective-permute-done.21 = bf16[2,32,256]{2,1,0:T(8,128)(2,1)S(1)} collective-permute-done((bf16[2,32,256]{2,1,0:T(8,128)(2,1)S(1)}, bf16[2,32,256]{2,1,0:T(8,128)(2,1)S(1)}, u32[]{:S(2)}, u32[]{:S(2)}) %collective-permute-start.21) | collective-permute-done | bytes 32800 | tf_op jit(solution)/shard_map/ppermute | solution.py:17
  70.4 0.6 collective-permute-start.22
  71.0 0.8 collective-permute-start.23
  71.8 2.2 %collective-permute-start.24 = (bf16[4,2,32,256]{3,2,1,0:T(8,128)(2,1)S(1)}, bf16[4,2,32,256]{3,2,1,0:T(8,128)(2,1)S(1)}, u32[]{:S(2)}, u32[]{:S(2)}) collective-permute-start(bf16[4,2,32,256]{3,2,1,0:T(8,128)(2,1)S(1)} %pad_maximum_fusion.2.refs_0_), channel_id=1, source_target_pairs={{0,6},{1,7},{2,4},{3,5},{4,2},{5,3},{6,0},{7,1},{8,14},{9,15},{10,... | collective-permute-start | bytes 393224 | tf_op jit(solution)/shard_map/ppermute | solution.py:17
  74.0 1.5 %collective-permute-done.22.refs_1_ = bf16[4,2,32,256]{3,2,1,0:T(8,128)(2,1)S(1)} collective-permute-done((bf16[4,2,32,256]{3,2,1,0:T(8,128)(2,1)S(1)}, bf16[4,2,32,256]{3,2,1,0:T(8,128)(2,1)S(1)}, u32[]{:S(2)}, u32[]{:S(2)}) %collective-permute-start.22) | collective-permute-done | bytes 131104 | tf_op jit(solution)/shard_map/ppermute | solution.py:17
  75.4 0.5 collective-permute-done.23.refs_2_
  76.0 1.7 %collective-permute-done.24.refs_3_ = bf16[4,2,32,256]{3,2,1,0:T(8,128)(2,1)S(1)} collective-permute-done((bf16[4,2,32,256]{3,2,1,0:T(8,128)(2,1)S(1)}, bf16[4,2,32,256]{3,2,1,0:T(8,128)(2,1)S(1)}, u32[]{:S(2)}, u32[]{:S(2)}) %collective-permute-start.24) | collective-permute-done | bytes 131104 | tf_op jit(solution)/shard_map/ppermute | solution.py:17
  77.7 5.6 %shard_map.62 = (bf16[2,32,256]{2,1,0:T(8,128)(2,1)S(1)}, bf16[2,32,256]{2,1,0:T(8,128)(2,1)S(1)}, f32[4,2,32,256]{3,2,1,0:T(8,128)S(1)}, bf16[4,2,32,256]{3,2,1...) custom-call(s32[2,16]{1,0:T(2,128)S(1)} %bitcast.54, ...), custom_call_target="tpu_custom_call" | custom-call | flops 268435456 | tf_op jit(solution)/shard_map/pallas_call | solution.py:29
  83.3 1.6 %collective-permute-start.28 = (bf16[4,2,32,256]{3,2,1,0:T(8,128)(2,1)S(1)}, bf16[4,2,32,256]{3,2,1,0:T(8,128)(2,1)S(1)}, u32[]{:S(2)}, u32[]{:S(2)}) collective-permute-start(bf16[4,2,32,256]{3,2,1,0:T(8,128)(2,1)S(1)} %get-tuple-element.32), channel_id=1, source_target_pairs={{0,2},{1,3},{2,0},{3,1},{4,6},{5,7},{6,4},{7,5},{8,10},{9,11},{10,... | collective-permute-start | bytes 393224 | tf_op jit(solution)/shard_map/ppermute | solution.py:17
  84.9 1.2 collective-permute-start.29
  86.1 0.8 collective-permute-start.30
  86.8 1.5 %collective-permute-done.28.a = bf16[4,2,32,256]{3,2,1,0:T(8,128)(2,1)S(1)} collective-permute-done((bf16[4,2,32,256]{3,2,1,0:T(8,128)(2,1)S(1)}, bf16[4,2,32,256]{3,2,1,0:T(8,128)(2,1)S(1)}, u32[]{:S(2)}, u32[]{:S(2)}) %collective-permute-start.28) | collective-permute-done | bytes 131104 | tf_op jit(solution)/shard_map/ppermute | solution.py:17
  88.3 1.6 %collective-permute-done.29.b = bf16[4,2,32,256]{3,2,1,0:T(8,128)(2,1)S(1)} collective-permute-done((bf16[4,2,32,256]{3,2,1,0:T(8,128)(2,1)S(1)}, bf16[4,2,32,256]{3,2,1,0:T(8,128)(2,1)S(1)}, u32[]{:S(2)}, u32[]{:S(2)}) %collective-permute-start.29) | collective-permute-done | bytes 131104 | tf_op jit(solution)/shard_map/ppermute | solution.py:17
  89.9 2.1 %collective-permute-done.30.c = bf16[4,2,32,256]{3,2,1,0:T(8,128)(2,1)S(1)} collective-permute-done((bf16[4,2,32,256]{3,2,1,0:T(8,128)(2,1)S(1)}, bf16[4,2,32,256]{3,2,1,0:T(8,128)(2,1)S(1)}, u32[]{:S(2)}, u32[]{:S(2)}) %collective-permute-start.30) | collective-permute-done | bytes 131104 | tf_op jit(solution)/shard_map/ppermute | solution.py:17
  92.3 3.8 %collective-permute-start.32 = (bf16[2,32,256]{2,1,0:T(8,128)(2,1)S(1)}, bf16[2,32,256]{2,1,0:T(8,128)(2,1)S(1)}, u32[]{:S(2)}, u32[]{:S(2)}) collective-permute-start(bf16[2,32,256]{2,1,0:T(8,128)(2,1)S(1)} %get-tuple-element.37), channel_id=1, source_target_pairs={{0,16},{1,17},{2,18},{3,19},{4,20},{5,21},{6,22},{7,23},{8,24},{9,... | collective-permute-start | bytes 98312 | tf_op jit(solution)/shard_map/ppermute | solution.py:17
  96.6 1.4 %collective-permute-done.32.refs_1_ = bf16[2,32,256]{2,1,0:T(8,128)(2,1)S(1)} collective-permute-done((bf16[2,32,256]{2,1,0:T(8,128)(2,1)S(1)}, bf16[2,32,256]{2,1,0:T(8,128)(2,1)S(1)}, u32[]{:S(2)}, u32[]{:S(2)}) %collective-permute-start.32) | collective-permute-done | bytes 32800 | tf_op jit(solution)/shard_map/ppermute | solution.py:17
  98.0 3.8 %collective-permute-done.33.refs_2_ = bf16[2,32,256]{2,1,0:T(8,128)(2,1)S(1)} collective-permute-done((bf16[2,32,256]{2,1,0:T(8,128)(2,1)S(1)}, bf16[2,32,256]{2,1,0:T(8,128)(2,1)S(1)}, u32[]{:S(2)}, u32[]{:S(2)}) %collective-permute-start.33) | collective-permute-done | bytes 32800 | tf_op jit(solution)/shard_map/ppermute | solution.py:17
  101.8 3.2 %shard_map.65 = (bf16[2,32,256]{2,1,0:T(8,128)(2,1)S(1)}, f32[4,2,32,256]{3,2,1,0:T(8,128)S(1)}, bf16[4,2,32,256]{3,2,1,0:T(8,128)(2,1)S(1)}, bf16[4,2,32,256]{3...) custom-call(s32[2,16]{1,0:T(2,128)S(1)} %bitcast.59, f32[2,32,256]{2,1,0:T(8,128)S(1)} %get-tuple-element.35.own, ...), custom_call_target="tpu_custom_call" | custom-call | flops 134217728 | tf_op jit(solution)/shard_map/pallas_call | solution.py:29
  105.1 0.6 collective-permute-start.34
  106.2 2.4 %collective-permute-start.36 = (bf16[4,2,32,256]{3,2,1,0:T(8,128)(2,1)S(1)}, bf16[4,2,32,256]{3,2,1,0:T(8,128)(2,1)S(1)}, u32[]{:S(2)}, u32[]{:S(2)}) collective-permute-start(bf16[4,2,32,256]{3,2,1,0:T(8,128)(2,1)S(1)} %get-tuple-element.42), channel_id=1, source_target_pairs={{0,6},{1,7},{2,4},{3,5},{4,2},{5,3},{6,0},{7,1},{8,14},{9,15},{10,... | collective-permute-start | bytes 393224 | tf_op jit(solution)/shard_map/ppermute | solution.py:17
  108.6 1.5 %collective-permute-done.34.a = bf16[4,2,32,256]{3,2,1,0:T(8,128)(2,1)S(1)} collective-permute-done((bf16[4,2,32,256]{3,2,1,0:T(8,128)(2,1)S(1)}, bf16[4,2,32,256]{3,2,1,0:T(8,128)(2,1)S(1)}, u32[]{:S(2)}, u32[]{:S(2)}) %collective-permute-start.34) | collective-permute-done | bytes 131104 | tf_op jit(solution)/shard_map/ppermute | solution.py:17
  110.7 1.4 collective-permute-done.36.c
  112.2 1.2 collective-permute-start.38
  113.4 3.2 %collective-permute-start.39 = (bf16[2,32,256]{2,1,0:T(8,128)(2,1)S(1)}, bf16[2,32,256]{2,1,0:T(8,128)(2,1)S(1)}, u32[]{:S(2)}, u32[]{:S(2)}) collective-permute-start(bf16[2,32,256]{2,1,0:T(8,128)(2,1)S(1)} %get-tuple-element.46), channel_id=1, source_target_pairs={{0,24},{1,25},{2,26},{3,27},{4,28},{5,29},{6,30},{7,31},{8,16},{9,... | collective-permute-start | bytes 98312 | tf_op jit(solution)/shard_map/ppermute | solution.py:17
  116.6 0.7 shard_map.63
  117.3 1.8 %collective-permute-done.39.refs_2_ = bf16[2,32,256]{2,1,0:T(8,128)(2,1)S(1)} collective-permute-done((bf16[2,32,256]{2,1,0:T(8,128)(2,1)S(1)}, bf16[2,32,256]{2,1,0:T(8,128)(2,1)S(1)}, u32[]{:S(2)}, u32[]{:S(2)}) %collective-permute-start.39) | collective-permute-done | bytes 32800 | tf_op jit(solution)/shard_map/ppermute | solution.py:17
  119.1 3.2 %shard_map.67 = (bf16[2,32,256]{2,1,0:T(8,128)(2,1)S(1)}, f32[4,2,32,256]{3,2,1,0:T(8,128)S(1)}, bf16[4,2,32,256]{3,2,1,0:T(8,128)(2,1)S(1)}, bf16[4,2,32,256]{3...) custom-call(s32[2,16]{1,0:T(2,128)S(1)} %bitcast.57, f32[2,32,256]{2,1,0:T(8,128)S(1)} %get-tuple-element.43.own, ...), custom_call_target="tpu_custom_call" | custom-call | flops 134217728 | tf_op jit(solution)/shard_map/pallas_call | solution.py:29
  122.4 1.6 %collective-permute-start.40 = (bf16[4,2,32,256]{3,2,1,0:T(8,128)(2,1)S(1)}, bf16[4,2,32,256]{3,2,1,0:T(8,128)(2,1)S(1)}, u32[]{:S(2)}, u32[]{:S(2)}) collective-permute-start(bf16[4,2,32,256]{3,2,1,0:T(8,128)(2,1)S(1)} %get-tuple-element.48), channel_id=1, source_target_pairs={{0,2},{1,3},{2,0},{3,1},{4,6},{5,7},{6,4},{7,5},{8,10},{9,11},{10,... | collective-permute-start | bytes 393224 | tf_op jit(solution)/shard_map/ppermute | solution.py:17
  124.0 1.3 collective-permute-start.41
  125.2 0.7 collective-permute-start.42
  125.9 1.5 %collective-permute-done.40.a = bf16[4,2,32,256]{3,2,1,0:T(8,128)(2,1)S(1)} collective-permute-done((bf16[4,2,32,256]{3,2,1,0:T(8,128)(2,1)S(1)}, bf16[4,2,32,256]{3,2,1,0:T(8,128)(2,1)S(1)}, u32[]{:S(2)}, u32[]{:S(2)}) %collective-permute-start.40) | collective-permute-done | bytes 131104 | tf_op jit(solution)/shard_map/ppermute | solution.py:17
  127.4 1.6 %collective-permute-done.41.b = bf16[4,2,32,256]{3,2,1,0:T(8,128)(2,1)S(1)} collective-permute-done((bf16[4,2,32,256]{3,2,1,0:T(8,128)(2,1)S(1)}, bf16[4,2,32,256]{3,2,1,0:T(8,128)(2,1)S(1)}, u32[]{:S(2)}, u32[]{:S(2)}) %collective-permute-start.41) | collective-permute-done | bytes 131104 | tf_op jit(solution)/shard_map/ppermute | solution.py:17
  128.9 2.2 %collective-permute-done.42.c = bf16[4,2,32,256]{3,2,1,0:T(8,128)(2,1)S(1)} collective-permute-done((bf16[4,2,32,256]{3,2,1,0:T(8,128)(2,1)S(1)}, bf16[4,2,32,256]{3,2,1,0:T(8,128)(2,1)S(1)}, u32[]{:S(2)}, u32[]{:S(2)}) %collective-permute-start.42) | collective-permute-done | bytes 131104 | tf_op jit(solution)/shard_map/ppermute | solution.py:17
  131.4 3.8 %collective-permute-start.44 = (bf16[2,32,256]{2,1,0:T(8,128)(2,1)S(1)}, bf16[2,32,256]{2,1,0:T(8,128)(2,1)S(1)}, u32[]{:S(2)}, u32[]{:S(2)}) collective-permute-start(bf16[2,32,256]{2,1,0:T(8,128)(2,1)S(1)} %get-tuple-element.53), channel_id=1, source_target_pairs={{0,16},{1,17},{2,18},{3,19},{4,20},{5,21},{6,22},{7,23},{8,24},{9,... | collective-permute-start | bytes 98312 | tf_op jit(solution)/shard_map/ppermute | solution.py:17
  135.6 1.4 %collective-permute-done.44.refs_1_ = bf16[2,32,256]{2,1,0:T(8,128)(2,1)S(1)} collective-permute-done((bf16[2,32,256]{2,1,0:T(8,128)(2,1)S(1)}, bf16[2,32,256]{2,1,0:T(8,128)(2,1)S(1)}, u32[]{:S(2)}, u32[]{:S(2)}) %collective-permute-start.44) | collective-permute-done | bytes 32800 | tf_op jit(solution)/shard_map/ppermute | solution.py:17
  137.1 3.8 %collective-permute-done.45.refs_2_ = bf16[2,32,256]{2,1,0:T(8,128)(2,1)S(1)} collective-permute-done((bf16[2,32,256]{2,1,0:T(8,128)(2,1)S(1)}, bf16[2,32,256]{2,1,0:T(8,128)(2,1)S(1)}, u32[]{:S(2)}, u32[]{:S(2)}) %collective-permute-start.45) | collective-permute-done | bytes 32800 | tf_op jit(solution)/shard_map/ppermute | solution.py:17
  141.2 1.2 collective-permute-done.46.other
  142.4 0.7 shard_map.70
  (71 shorter events, 6.1 us)
Async XLA Ops:
  0.6 6.1 %copy-start.1 = (bf16[4,1,64,256]{3,2,1,0:T(8,128)(2,1)S(1)}, bf16[4,1,64,256]{3,2,1,0:T(8,128)(2,1)}, u32[]{:S(2)}) copy-start(bf16[4,1,64,256]{3,2,1,0:T(8,128)(2,1)} %param.4) | copy-start | bytes 393220
  0.6 6.7 %copy-start = (bf16[4,1,256,256]{3,2,1,0:T(8,128)(2,1)S(1)}, bf16[4,1,256,256]{3,2,1,0:T(8,128)(2,1)}, u32[]{:S(2)}) copy-start(bf16[4,1,256,256]{3,2,1,0:T(8,128)(2,1)} %param.5) | copy-start | bytes 1572868
  0.7 18.7 %copy-start.2 = (s32[3,1,16]{2,1,0:T(1,128)S(1)}, s32[3,1,16]{2,1,0:T(1,128)}, u32[]{:S(2)}) copy-start(s32[3,1,16]{2,1,0:T(1,128)} %param.7) | copy-start | bytes 580
  6.2 29.1 %collective-permute-start.9 = (bf16[16,256,256]{2,1,0:T(8,128)(2,1)}, bf16[16,256,256]{2,1,0:T(8,128)(2,1)}, u32[]{:S(2)}, u32[]{:S(2)}) collective-permute-start(bf16[16,256,256]{2,1,0:T(8,128)(2,1)} %get-tuple-element.59.refs_4_.p0), channel_id=1, source_target_pairs={{0,1},{1,0},{2,3},{3,2},{4,5},{5,4},{6,7},{7,6},{8,9},{9,8},{10,11... | collective-permute-start | bytes 6291464 | tf_op jit(solution)/shard_map/ppermute | solution.py:17
  6.6 47.0 %collective-permute-start.17 = (bf16[16,256,256]{2,1,0:T(8,128)(2,1)}, bf16[16,256,256]{2,1,0:T(8,128)(2,1)}, u32[]{:S(2)}, u32[]{:S(2)}) collective-permute-start(bf16[16,256,256]{2,1,0:T(8,128)(2,1)} %get-tuple-element.60.refs_4_.p0), channel_id=1, source_target_pairs={{0,1},{1,0},{2,3},{3,2},{4,5},{5,4},{6,7},{7,6},{8,9},{9,8},{10,11... | collective-permute-start | bytes 6291464 | tf_op jit(solution)/shard_map/ppermute | solution.py:17
  6.7 4.0 %collective-permute-start = (bf16[4,32,256]{2,1,0:T(8,128)(2,1)S(1)}, bf16[4,32,256]{2,1,0:T(8,128)(2,1)S(1)}, u32[]{:S(2)}, u32[]{:S(2)}) collective-permute-start(bf16[4,32,256]{2,1,0:T(8,128)(2,1)S(1)} %dynamic-slice_bitcast_fusion), channel_id=1, source_target_pairs={{0,1},{1,0},{2,3},{3,2},{4,5},{5,4},{6,7},{7,6},{8,9},{9,8},{10,11... | collective-permute-start | bytes 196616 | tf_op jit(solution)/shard_map/ppermute | solution.py:17
  7.2 66.7 %collective-permute-start.25 = (bf16[16,256,256]{2,1,0:T(8,128)(2,1)S(1)}, bf16[16,256,256]{2,1,0:T(8,128)(2,1)}, u32[]{:S(2)}, u32[]{:S(2)}) collective-permute-start(bf16[16,256,256]{2,1,0:T(8,128)(2,1)S(1)} %get-tuple-element.58.refs_4_.refs_10_), channel_id=1, source_target_pairs={{0,1},{1,0},{2,3},{3,2},{4,5},{5,4},{6,7},{7,6},{8,9},{9,8},{10,11... | collective-permute-start | bytes 6291464 | tf_op jit(solution)/shard_map/ppermute | solution.py:17
  7.3 3.9 %collective-permute-start.1 = (bf16[256,256]{1,0:T(8,128)(2,1)S(1)}, bf16[256,256]{1,0:T(8,128)(2,1)S(1)}, u32[]{:S(2)}, u32[]{:S(2)}) collective-permute-start(bf16[256,256]{1,0:T(8,128)(2,1)S(1)} %get-tuple-element.63.diag_own.d0), channel_id=1, source_target_pairs={{0,1},{1,0},{2,3},{3,2},{4,5},{5,4},{6,7},{7,6},{8,9},{9,8},{10,11... | collective-permute-start | bytes 393224 | tf_op jit(solution)/shard_map/ppermute | solution.py:17
  11.4 7.0 %collective-permute-start.5 = (bf16[2,32,256]{2,1,0:T(8,128)(2,1)S(1)}, bf16[2,32,256]{2,1,0:T(8,128)(2,1)S(1)}, u32[]{:S(2)}, u32[]{:S(2)}) collective-permute-start(bf16[2,32,256]{2,1,0:T(8,128)(2,1)S(1)} %shard_map.59.known), channel_id=1, source_target_pairs={{0,24},{1,25},{2,26},{3,27},{4,28},{5,29},{6,30},{7,31},{8,16},{9,... | collective-permute-start | bytes 98312 | tf_op jit(solution)/shard_map/ppermute | solution.py:17
  16.4 3.9 %collective-permute-start.3 = (bf16[2,32,256]{2,1,0:T(8,128)(2,1)S(1)}, bf16[2,32,256]{2,1,0:T(8,128)(2,1)S(1)}, u32[]{:S(2)}, u32[]{:S(2)}) collective-permute-start(bf16[2,32,256]{2,1,0:T(8,128)(2,1)S(1)} %shard_map.59.known), channel_id=1, source_target_pairs={{0,8},{1,9},{2,10},{3,11},{4,12},{5,13},{6,14},{7,15},{8,0},{9,1},... | collective-permute-start | bytes 98312 | tf_op jit(solution)/shard_map/ppermute | solution.py:17
  18.5 4.8 %collective-permute-start.4 = (bf16[2,32,256]{2,1,0:T(8,128)(2,1)S(1)}, bf16[2,32,256]{2,1,0:T(8,128)(2,1)S(1)}, u32[]{:S(2)}, u32[]{:S(2)}) collective-permute-start(bf16[2,32,256]{2,1,0:T(8,128)(2,1)S(1)} %shard_map.59.known), channel_id=1, source_target_pairs={{0,16},{1,17},{2,18},{3,19},{4,20},{5,21},{6,22},{7,23},{8,24},{9,... | collective-permute-start | bytes 98312 | tf_op jit(solution)/shard_map/ppermute | solution.py:17
  20.3 3.0 %collective-permute-start.2 = (s32[3,16]{1,0:T(4,128)S(1)}, s32[3,16]{1,0:T(4,128)S(1)}, u32[]{:S(2)}, u32[]{:S(2)}) collective-permute-start(s32[3,16]{1,0:T(4,128)S(1)} %bitcast.69), channel_id=1, source_target_pairs={{0,1},{1,0},{2,3},{3,2},{4,5},{5,4},{6,7},{7,6},{8,9},{9,8},{10,11... | collective-permute-start | bytes 584 | tf_op jit(solution)/shard_map/ppermute | solution.py:17
  23.3 1.7 %collective-permute-start.10 = (bf16[256,256]{1,0:T(8,128)(2,1)S(1)}, bf16[256,256]{1,0:T(8,128)(2,1)S(1)}, u32[]{:S(2)}, u32[]{:S(2)}) collective-permute-start(bf16[256,256]{1,0:T(8,128)(2,1)S(1)} %get-tuple-element.62.refs_8_.d0), channel_id=1, source_target_pairs={{0,1},{1,0},{2,3},{3,2},{4,5},{5,4},{6,7},{7,6},{8,9},{9,8},{10,11... | collective-permute-start | bytes 393224 | tf_op jit(solution)/shard_map/ppermute | solution.py:17
  23.3 6.0 %collective-permute-start.6 = (bf16[4,2,32,256]{3,2,1,0:T(8,128)(2,1)S(1)}, bf16[4,2,32,256]{3,2,1,0:T(8,128)(2,1)S(1)}, u32[]{:S(2)}, u32[]{:S(2)}) collective-permute-start(bf16[4,2,32,256]{3,2,1,0:T(8,128)(2,1)S(1)} %pad_maximum_fusion.refs_0_), channel_id=1, source_target_pairs={{0,2},{1,3},{2,0},{3,1},{4,6},{5,7},{6,4},{7,5},{8,10},{9,11},{10,... | collective-permute-start | bytes 393224 | tf_op jit(solution)/shard_map/ppermute | solution.py:17
  25.0 6.9 %collective-permute-start.7 = (bf16[4,2,32,256]{3,2,1,0:T(8,128)(2,1)S(1)}, bf16[4,2,32,256]{3,2,1,0:T(8,128)(2,1)S(1)}, u32[]{:S(2)}, u32[]{:S(2)}) collective-permute-start(bf16[4,2,32,256]{3,2,1,0:T(8,128)(2,1)S(1)} %pad_maximum_fusion.refs_0_), channel_id=1, source_target_pairs={{0,4},{1,5},{2,6},{3,7},{4,0},{5,1},{6,2},{7,3},{8,12},{9,13},{10,... | collective-permute-start | bytes 393224 | tf_op jit(solution)/shard_map/ppermute | solution.py:17
  29.3 6.0 %collective-permute-start.8 = (bf16[4,2,32,256]{3,2,1,0:T(8,128)(2,1)S(1)}, bf16[4,2,32,256]{3,2,1,0:T(8,128)(2,1)S(1)}, u32[]{:S(2)}, u32[]{:S(2)}) collective-permute-start(bf16[4,2,32,256]{3,2,1,0:T(8,128)(2,1)S(1)} %pad_maximum_fusion.refs_0_), channel_id=1, source_target_pairs={{0,6},{1,7},{2,4},{3,5},{4,2},{5,3},{6,0},{7,1},{8,14},{9,15},{10,... | collective-permute-start | bytes 393224 | tf_op jit(solution)/shard_map/ppermute | solution.py:17
  40.0 4.4 %collective-permute-start.11 = (bf16[2,32,256]{2,1,0:T(8,128)(2,1)S(1)}, bf16[2,32,256]{2,1,0:T(8,128)(2,1)S(1)}, u32[]{:S(2)}, u32[]{:S(2)}) collective-permute-start(bf16[2,32,256]{2,1,0:T(8,128)(2,1)S(1)} %shard_map.60.known), channel_id=1, source_target_pairs={{0,8},{1,9},{2,10},{3,11},{4,12},{5,13},{6,14},{7,15},{8,0},{9,1},... | collective-permute-start | bytes 98312 | tf_op jit(solution)/shard_map/ppermute | solution.py:17
  41.4 5.2 %collective-permute-start.12 = (bf16[2,32,256]{2,1,0:T(8,128)(2,1)S(1)}, bf16[2,32,256]{2,1,0:T(8,128)(2,1)S(1)}, u32[]{:S(2)}, u32[]{:S(2)}) collective-permute-start(bf16[2,32,256]{2,1,0:T(8,128)(2,1)S(1)} %shard_map.60.known), channel_id=1, source_target_pairs={{0,16},{1,17},{2,18},{3,19},{4,20},{5,21},{6,22},{7,23},{8,24},{9,... | collective-permute-start | bytes 98312 | tf_op jit(solution)/shard_map/ppermute | solution.py:17
  44.3 5.7 %collective-permute-start.13 = (bf16[2,32,256]{2,1,0:T(8,128)(2,1)S(1)}, bf16[2,32,256]{2,1,0:T(8,128)(2,1)S(1)}, u32[]{:S(2)}, u32[]{:S(2)}) collective-permute-start(bf16[2,32,256]{2,1,0:T(8,128)(2,1)S(1)} %shard_map.60.known), channel_id=1, source_target_pairs={{0,24},{1,25},{2,26},{3,27},{4,28},{5,29},{6,30},{7,31},{8,16},{9,... | collective-permute-start | bytes 98312 | tf_op jit(solution)/shard_map/ppermute | solution.py:17
  44.5 8.7 %collective-permute-start.18 = (bf16[256,256]{1,0:T(8,128)(2,1)S(1)}, bf16[256,256]{1,0:T(8,128)(2,1)S(1)}, u32[]{:S(2)}, u32[]{:S(2)}) collective-permute-start(bf16[256,256]{1,0:T(8,128)(2,1)S(1)} %get-tuple-element.64.refs_8_.d0), channel_id=1, source_target_pairs={{0,1},{1,0},{2,3},{3,2},{4,5},{5,4},{6,7},{7,6},{8,9},{9,8},{10,11... | collective-permute-start | bytes 393224 | tf_op jit(solution)/shard_map/ppermute | solution.py:17
  50.1 5.0 %collective-permute-start.14 = (bf16[4,2,32,256]{3,2,1,0:T(8,128)(2,1)S(1)}, bf16[4,2,32,256]{3,2,1,0:T(8,128)(2,1)S(1)}, u32[]{:S(2)}, u32[]{:S(2)}) collective-permute-start(bf16[4,2,32,256]{3,2,1,0:T(8,128)(2,1)S(1)} %pad_maximum_fusion.1.refs_0_), channel_id=1, source_target_pairs={{0,2},{1,3},{2,0},{3,1},{4,6},{5,7},{6,4},{7,5},{8,10},{9,11},{10,... | collective-permute-start | bytes 393224 | tf_op jit(solution)/shard_map/ppermute | solution.py:17
  51.6 5.0 %collective-permute-start.15 = (bf16[4,2,32,256]{3,2,1,0:T(8,128)(2,1)S(1)}, bf16[4,2,32,256]{3,2,1,0:T(8,128)(2,1)S(1)}, u32[]{:S(2)}, u32[]{:S(2)}) collective-permute-start(bf16[4,2,32,256]{3,2,1,0:T(8,128)(2,1)S(1)} %pad_maximum_fusion.1.refs_0_), channel_id=1, source_target_pairs={{0,4},{1,5},{2,6},{3,7},{4,0},{5,1},{6,2},{7,3},{8,12},{9,13},{10,... | collective-permute-start | bytes 393224 | tf_op jit(solution)/shard_map/ppermute | solution.py:17
  53.1 5.9 %collective-permute-start.16 = (bf16[4,2,32,256]{3,2,1,0:T(8,128)(2,1)S(1)}, bf16[4,2,32,256]{3,2,1,0:T(8,128)(2,1)S(1)}, u32[]{:S(2)}, u32[]{:S(2)}) collective-permute-start(bf16[4,2,32,256]{3,2,1,0:T(8,128)(2,1)S(1)} %pad_maximum_fusion.1.refs_0_), channel_id=1, source_target_pairs={{0,6},{1,7},{2,4},{3,5},{4,2},{5,3},{6,0},{7,1},{8,14},{9,15},{10,... | collective-permute-start | bytes 393224 | tf_op jit(solution)/shard_map/ppermute | solution.py:17
  53.6 20.3 %collective-permute-start.26 = (bf16[256,256]{1,0:T(8,128)(2,1)S(1)}, bf16[256,256]{1,0:T(8,128)(2,1)S(1)}, u32[]{:S(2)}, u32[]{:S(2)}) collective-permute-start(bf16[256,256]{1,0:T(8,128)(2,1)S(1)} %get-tuple-element.61.refs_8_), channel_id=1, source_target_pairs={{0,1},{1,0},{2,3},{3,2},{4,5},{5,4},{6,7},{7,6},{8,9},{9,8},{10,11... | collective-permute-start | bytes 393224 | tf_op jit(solution)/shard_map/ppermute | solution.py:17
  63.7 4.4 %collective-permute-start.19 = (bf16[2,32,256]{2,1,0:T(8,128)(2,1)S(1)}, bf16[2,32,256]{2,1,0:T(8,128)(2,1)S(1)}, u32[]{:S(2)}, u32[]{:S(2)}) collective-permute-start(bf16[2,32,256]{2,1,0:T(8,128)(2,1)S(1)} %shard_map.61.known), channel_id=1, source_target_pairs={{0,8},{1,9},{2,10},{3,11},{4,12},{5,13},{6,14},{7,15},{8,0},{9,1},... | collective-permute-start | bytes 98312 | tf_op jit(solution)/shard_map/ppermute | solution.py:17
  63.8 4.9 %collective-permute-start.20 = (bf16[2,32,256]{2,1,0:T(8,128)(2,1)S(1)}, bf16[2,32,256]{2,1,0:T(8,128)(2,1)S(1)}, u32[]{:S(2)}, u32[]{:S(2)}) collective-permute-start(bf16[2,32,256]{2,1,0:T(8,128)(2,1)S(1)} %shard_map.61.known), channel_id=1, source_target_pairs={{0,16},{1,17},{2,18},{3,19},{4,20},{5,21},{6,22},{7,23},{8,24},{9,... | collective-permute-start | bytes 98312 | tf_op jit(solution)/shard_map/ppermute | solution.py:17
  64.7 5.7 %collective-permute-start.21 = (bf16[2,32,256]{2,1,0:T(8,128)(2,1)S(1)}, bf16[2,32,256]{2,1,0:T(8,128)(2,1)S(1)}, u32[]{:S(2)}, u32[]{:S(2)}) collective-permute-start(bf16[2,32,256]{2,1,0:T(8,128)(2,1)S(1)} %shard_map.61.known), channel_id=1, source_target_pairs={{0,24},{1,25},{2,26},{3,27},{4,28},{5,29},{6,30},{7,31},{8,16},{9,... | collective-permute-start | bytes 98312 | tf_op jit(solution)/shard_map/ppermute | solution.py:17
  70.4 5.0 %collective-permute-start.22 = (bf16[4,2,32,256]{3,2,1,0:T(8,128)(2,1)S(1)}, bf16[4,2,32,256]{3,2,1,0:T(8,128)(2,1)S(1)}, u32[]{:S(2)}, u32[]{:S(2)}) collective-permute-start(bf16[4,2,32,256]{3,2,1,0:T(8,128)(2,1)S(1)} %pad_maximum_fusion.2.refs_0_), channel_id=1, source_target_pairs={{0,2},{1,3},{2,0},{3,1},{4,6},{5,7},{6,4},{7,5},{8,10},{9,11},{10,... | collective-permute-start | bytes 393224 | tf_op jit(solution)/shard_map/ppermute | solution.py:17
  71.0 5.0 %collective-permute-start.23 = (bf16[4,2,32,256]{3,2,1,0:T(8,128)(2,1)S(1)}, bf16[4,2,32,256]{3,2,1,0:T(8,128)(2,1)S(1)}, u32[]{:S(2)}, u32[]{:S(2)}) collective-permute-start(bf16[4,2,32,256]{3,2,1,0:T(8,128)(2,1)S(1)} %pad_maximum_fusion.2.refs_0_), channel_id=1, source_target_pairs={{0,4},{1,5},{2,6},{3,7},{4,0},{5,1},{6,2},{7,3},{8,12},{9,13},{10,... | collective-permute-start | bytes 393224 | tf_op jit(solution)/shard_map/ppermute | solution.py:17
  71.8 5.9 %collective-permute-start.24 = (bf16[4,2,32,256]{3,2,1,0:T(8,128)(2,1)S(1)}, bf16[4,2,32,256]{3,2,1,0:T(8,128)(2,1)S(1)}, u32[]{:S(2)}, u32[]{:S(2)}) collective-permute-start(bf16[4,2,32,256]{3,2,1,0:T(8,128)(2,1)S(1)} %pad_maximum_fusion.2.refs_0_), channel_id=1, source_target_pairs={{0,6},{1,7},{2,4},{3,5},{4,2},{5,3},{6,0},{7,1},{8,14},{9,15},{10,... | collective-permute-start | bytes 393224 | tf_op jit(solution)/shard_map/ppermute | solution.py:17
  83.3 5.0 %collective-permute-start.28 = (bf16[4,2,32,256]{3,2,1,0:T(8,128)(2,1)S(1)}, bf16[4,2,32,256]{3,2,1,0:T(8,128)(2,1)S(1)}, u32[]{:S(2)}, u32[]{:S(2)}) collective-permute-start(bf16[4,2,32,256]{3,2,1,0:T(8,128)(2,1)S(1)} %get-tuple-element.32), channel_id=1, source_target_pairs={{0,2},{1,3},{2,0},{3,1},{4,6},{5,7},{6,4},{7,5},{8,10},{9,11},{10,... | collective-permute-start | bytes 393224 | tf_op jit(solution)/shard_map/ppermute | solution.py:17
  84.9 5.0 %collective-permute-start.29 = (bf16[4,2,32,256]{3,2,1,0:T(8,128)(2,1)S(1)}, bf16[4,2,32,256]{3,2,1,0:T(8,128)(2,1)S(1)}, u32[]{:S(2)}, u32[]{:S(2)}) collective-permute-start(bf16[4,2,32,256]{3,2,1,0:T(8,128)(2,1)S(1)} %get-tuple-element.33), channel_id=1, source_target_pairs={{0,4},{1,5},{2,6},{3,7},{4,0},{5,1},{6,2},{7,3},{8,12},{9,13},{10,... | collective-permute-start | bytes 393224 | tf_op jit(solution)/shard_map/ppermute | solution.py:17
  86.1 5.9 %collective-permute-start.30 = (bf16[4,2,32,256]{3,2,1,0:T(8,128)(2,1)S(1)}, bf16[4,2,32,256]{3,2,1,0:T(8,128)(2,1)S(1)}, u32[]{:S(2)}, u32[]{:S(2)}) collective-permute-start(bf16[4,2,32,256]{3,2,1,0:T(8,128)(2,1)S(1)} %get-tuple-element.34), channel_id=1, source_target_pairs={{0,6},{1,7},{2,4},{3,5},{4,2},{5,3},{6,0},{7,1},{8,14},{9,15},{10,... | collective-permute-start | bytes 393224 | tf_op jit(solution)/shard_map/ppermute | solution.py:17
  92.0 4.5 %collective-permute-start.31 = (bf16[2,32,256]{2,1,0:T(8,128)(2,1)S(1)}, bf16[2,32,256]{2,1,0:T(8,128)(2,1)S(1)}, u32[]{:S(2)}, u32[]{:S(2)}) collective-permute-start(bf16[2,32,256]{2,1,0:T(8,128)(2,1)S(1)} %get-tuple-element.36), channel_id=1, source_target_pairs={{0,8},{1,9},{2,10},{3,11},{4,12},{5,13},{6,14},{7,15},{8,0},{9,1},... | collective-permute-start | bytes 98312 | tf_op jit(solution)/shard_map/ppermute | solution.py:17
  92.3 5.7 %collective-permute-start.32 = (bf16[2,32,256]{2,1,0:T(8,128)(2,1)S(1)}, bf16[2,32,256]{2,1,0:T(8,128)(2,1)S(1)}, u32[]{:S(2)}, u32[]{:S(2)}) collective-permute-start(bf16[2,32,256]{2,1,0:T(8,128)(2,1)S(1)} %get-tuple-element.37), channel_id=1, source_target_pairs={{0,16},{1,17},{2,18},{3,19},{4,20},{5,21},{6,22},{7,23},{8,24},{9,... | collective-permute-start | bytes 98312 | tf_op jit(solution)/shard_map/ppermute | solution.py:17
  96.1 5.7 %collective-permute-start.33 = (bf16[2,32,256]{2,1,0:T(8,128)(2,1)S(1)}, bf16[2,32,256]{2,1,0:T(8,128)(2,1)S(1)}, u32[]{:S(2)}, u32[]{:S(2)}) collective-permute-start(bf16[2,32,256]{2,1,0:T(8,128)(2,1)S(1)} %get-tuple-element.38), channel_id=1, source_target_pairs={{0,24},{1,25},{2,26},{3,27},{4,28},{5,29},{6,30},{7,31},{8,16},{9,... | collective-permute-start | bytes 98312 | tf_op jit(solution)/shard_map/ppermute | solution.py:17
  96.5 20.1 %collective-permute-start.27 = (bf16[4,32,256]{2,1,0:T(8,128)(2,1)S(1)}, bf16[4,32,256]{2,1,0:T(8,128)(2,1)S(1)}, u32[]{:S(2)}, u32[]{:S(2)}) collective-permute-start(bf16[4,32,256]{2,1,0:T(8,128)(2,1)S(1)} %pad_maximum_fusion.4), channel_id=1, source_target_pairs={{0,1},{1,0},{2,3},{3,2},{4,5},{5,4},{6,7},{7,6},{8,9},{9,8},{10,11... | collective-permute-start | bytes 196616 | tf_op jit(solution)/shard_map/ppermute | solution.py:17
  105.1 5.0 %collective-permute-start.34 = (bf16[4,2,32,256]{3,2,1,0:T(8,128)(2,1)S(1)}, bf16[4,2,32,256]{3,2,1,0:T(8,128)(2,1)S(1)}, u32[]{:S(2)}, u32[]{:S(2)}) collective-permute-start(bf16[4,2,32,256]{3,2,1,0:T(8,128)(2,1)S(1)} %get-tuple-element.40), channel_id=1, source_target_pairs={{0,2},{1,3},{2,0},{3,1},{4,6},{5,7},{6,4},{7,5},{8,10},{9,11},{10,... | collective-permute-start | bytes 393224 | tf_op jit(solution)/shard_map/ppermute | solution.py:17
  105.7 5.0 %collective-permute-start.35 = (bf16[4,2,32,256]{3,2,1,0:T(8,128)(2,1)S(1)}, bf16[4,2,32,256]{3,2,1,0:T(8,128)(2,1)S(1)}, u32[]{:S(2)}, u32[]{:S(2)}) collective-permute-start(bf16[4,2,32,256]{3,2,1,0:T(8,128)(2,1)S(1)} %get-tuple-element.41), channel_id=1, source_target_pairs={{0,4},{1,5},{2,6},{3,7},{4,0},{5,1},{6,2},{7,3},{8,12},{9,13},{10,... | collective-permute-start | bytes 393224 | tf_op jit(solution)/shard_map/ppermute | solution.py:17
  106.2 5.9 %collective-permute-start.36 = (bf16[4,2,32,256]{3,2,1,0:T(8,128)(2,1)S(1)}, bf16[4,2,32,256]{3,2,1,0:T(8,128)(2,1)S(1)}, u32[]{:S(2)}, u32[]{:S(2)}) collective-permute-start(bf16[4,2,32,256]{3,2,1,0:T(8,128)(2,1)S(1)} %get-tuple-element.42), channel_id=1, source_target_pairs={{0,6},{1,7},{2,4},{3,5},{4,2},{5,3},{6,0},{7,1},{8,14},{9,15},{10,... | collective-permute-start | bytes 393224 | tf_op jit(solution)/shard_map/ppermute | solution.py:17
  112.1 5.2 %collective-permute-start.37 = (bf16[2,32,256]{2,1,0:T(8,128)(2,1)S(1)}, bf16[2,32,256]{2,1,0:T(8,128)(2,1)S(1)}, u32[]{:S(2)}, u32[]{:S(2)}) collective-permute-start(bf16[2,32,256]{2,1,0:T(8,128)(2,1)S(1)} %get-tuple-element.44), channel_id=1, source_target_pairs={{0,8},{1,9},{2,10},{3,11},{4,12},{5,13},{6,14},{7,15},{8,0},{9,1},... | collective-permute-start | bytes 98312 | tf_op jit(solution)/shard_map/ppermute | solution.py:17
  112.2 5.1 %collective-permute-start.38 = (bf16[2,32,256]{2,1,0:T(8,128)(2,1)S(1)}, bf16[2,32,256]{2,1,0:T(8,128)(2,1)S(1)}, u32[]{:S(2)}, u32[]{:S(2)}) collective-permute-start(bf16[2,32,256]{2,1,0:T(8,128)(2,1)S(1)} %get-tuple-element.45), channel_id=1, source_target_pairs={{0,16},{1,17},{2,18},{3,19},{4,20},{5,21},{6,22},{7,23},{8,24},{9,... | collective-permute-start | bytes 98312 | tf_op jit(solution)/shard_map/ppermute | solution.py:17
  113.4 5.7 %collective-permute-start.39 = (bf16[2,32,256]{2,1,0:T(8,128)(2,1)S(1)}, bf16[2,32,256]{2,1,0:T(8,128)(2,1)S(1)}, u32[]{:S(2)}, u32[]{:S(2)}) collective-permute-start(bf16[2,32,256]{2,1,0:T(8,128)(2,1)S(1)} %get-tuple-element.46), channel_id=1, source_target_pairs={{0,24},{1,25},{2,26},{3,27},{4,28},{5,29},{6,30},{7,31},{8,16},{9,... | collective-permute-start | bytes 98312 | tf_op jit(solution)/shard_map/ppermute | solution.py:17
  122.4 5.0 %collective-permute-start.40 = (bf16[4,2,32,256]{3,2,1,0:T(8,128)(2,1)S(1)}, bf16[4,2,32,256]{3,2,1,0:T(8,128)(2,1)S(1)}, u32[]{:S(2)}, u32[]{:S(2)}) collective-permute-start(bf16[4,2,32,256]{3,2,1,0:T(8,128)(2,1)S(1)} %get-tuple-element.48), channel_id=1, source_target_pairs={{0,2},{1,3},{2,0},{3,1},{4,6},{5,7},{6,4},{7,5},{8,10},{9,11},{10,... | collective-permute-start | bytes 393224 | tf_op jit(solution)/shard_map/ppermute | solution.py:17
  124.0 5.0 %collective-permute-start.41 = (bf16[4,2,32,256]{3,2,1,0:T(8,128)(2,1)S(1)}, bf16[4,2,32,256]{3,2,1,0:T(8,128)(2,1)S(1)}, u32[]{:S(2)}, u32[]{:S(2)}) collective-permute-start(bf16[4,2,32,256]{3,2,1,0:T(8,128)(2,1)S(1)} %get-tuple-element.49), channel_id=1, source_target_pairs={{0,4},{1,5},{2,6},{3,7},{4,0},{5,1},{6,2},{7,3},{8,12},{9,13},{10,... | collective-permute-start | bytes 393224 | tf_op jit(solution)/shard_map/ppermute | solution.py:17
  125.2 5.9 %collective-permute-start.42 = (bf16[4,2,32,256]{3,2,1,0:T(8,128)(2,1)S(1)}, bf16[4,2,32,256]{3,2,1,0:T(8,128)(2,1)S(1)}, u32[]{:S(2)}, u32[]{:S(2)}) collective-permute-start(bf16[4,2,32,256]{3,2,1,0:T(8,128)(2,1)S(1)} %get-tuple-element.50), channel_id=1, source_target_pairs={{0,6},{1,7},{2,4},{3,5},{4,2},{5,3},{6,0},{7,1},{8,14},{9,15},{10,... | collective-permute-start | bytes 393224 | tf_op jit(solution)/shard_map/ppermute | solution.py:17
  131.2 4.5 %collective-permute-start.43 = (bf16[2,32,256]{2,1,0:T(8,128)(2,1)S(1)}, bf16[2,32,256]{2,1,0:T(8,128)(2,1)S(1)}, u32[]{:S(2)}, u32[]{:S(2)}) collective-permute-start(bf16[2,32,256]{2,1,0:T(8,128)(2,1)S(1)} %get-tuple-element.52), channel_id=1, source_target_pairs={{0,8},{1,9},{2,10},{3,11},{4,12},{5,13},{6,14},{7,15},{8,0},{9,1},... | collective-permute-start | bytes 98312 | tf_op jit(solution)/shard_map/ppermute | solution.py:17
  131.4 5.7 %collective-permute-start.44 = (bf16[2,32,256]{2,1,0:T(8,128)(2,1)S(1)}, bf16[2,32,256]{2,1,0:T(8,128)(2,1)S(1)}, u32[]{:S(2)}, u32[]{:S(2)}) collective-permute-start(bf16[2,32,256]{2,1,0:T(8,128)(2,1)S(1)} %get-tuple-element.53), channel_id=1, source_target_pairs={{0,16},{1,17},{2,18},{3,19},{4,20},{5,21},{6,22},{7,23},{8,24},{9,... | collective-permute-start | bytes 98312 | tf_op jit(solution)/shard_map/ppermute | solution.py:17
  135.2 5.7 %collective-permute-start.45 = (bf16[2,32,256]{2,1,0:T(8,128)(2,1)S(1)}, bf16[2,32,256]{2,1,0:T(8,128)(2,1)S(1)}, u32[]{:S(2)}, u32[]{:S(2)}) collective-permute-start(bf16[2,32,256]{2,1,0:T(8,128)(2,1)S(1)} %get-tuple-element.54), channel_id=1, source_target_pairs={{0,24},{1,25},{2,26},{3,27},{4,28},{5,29},{6,30},{7,31},{8,16},{9,... | collective-permute-start | bytes 98312 | tf_op jit(solution)/shard_map/ppermute | solution.py:17
  141.1 1.3 collective-permute-start.46

commit v2 on v0

v2 whole, which is shorter than its diff:
```python
import functools

import jax
import jax.numpy as jnp
from jax import lax
from jax.experimental import pallas as pl
from jax.experimental.pallas import tpu as pltpu
from jax.sharding import PartitionSpec as P

VMEM_SPEC = pl.BlockSpec(memory_space=pltpu.VMEM)
SMEM_SPEC = pl.BlockSpec(memory_space=pltpu.SMEM)
ANY_SPEC = pl.BlockSpec(memory_space=pl.ANY)
HBM_SPEC = pl.BlockSpec(memory_space=pltpu.HBM)
VMEM_GRANT = 8 * 1024 * 1024
PLANE = (6, 2, 4)


def swap(value, mask):
    size = lax.axis_size("rows")
    return lax.ppermute(value, "rows", [(i, i ^ mask) for i in range(size)])


def times_transposed(left, right):
    return lax.dot_general(left, right, (((1,), (1,)), ((), ())), preferred_element_type=jnp.float32)


def times(left, right):
    return jnp.dot(left, right, preferred_element_type=jnp.float32)


def call(kernel, out_shape, operands, in_specs=None, scratch=(), flops=0):
    return pl.pallas_call(
        kernel,
        out_shape=out_shape,
        in_specs=[VMEM_SPEC] * len(operands) if in_specs is None else in_specs,
        out_specs=jax.tree.map(lambda _: VMEM_SPEC, out_shape),
        scratch_shapes=list(scratch),
        compiler_params=pltpu.CompilerParams(vmem_limit_bytes=VMEM_GRANT),
        cost_estimate=pl.CostEstimate(flops=flops, bytes_accessed=0, transcendentals=0),
    )(*operands)


def side(index):
    return jnp.bitwise_and(index, 1)


def halves(width):
    mine = side(lax.axis_index("rows"))
    half = width // 2
    return (
        pl.ds(pl.multiple_of(mine * half, half), half),
        pl.ds(pl.multiple_of((1 - mine) * half, half), half),
    )


def first_kernel(rhs, diag, rhs_mine, rhs_sent, mine, sent, rhs_held, diag_held, arrived):
    here, there = halves(rhs.shape[2])
    loads = [
        pltpu.make_async_copy(rhs, rhs_held, arrived.at[0]),
        pltpu.make_async_copy(diag.at[0, 0], diag_held, arrived.at[1]),
    ]
    for load in loads:
        load.start()
    for load in loads:
        load.wait()
    sent[...] = times_transposed(rhs_held[0, 0, there], diag_held[...]).astype(sent.dtype)
    mine[...] = times_transposed(rhs_held[0, 0, here], diag_held[...]).astype(mine.dtype)
    for l in range(rhs.shape[0]):
        rhs_mine[l] = rhs_held[l, 0, here]
        rhs_sent[l] = rhs_held[l, 0, there]


def place_kernel(
    level, solve_levels, own_pattern, other_pattern, after, tiles0, tiles1, diag0, diag1, spread, diag, held, arrived
):
    me = lax.axis_index("rows")
    deep = spread.shape[1] // 8
    loads = []
    for i, (tiles, inverse) in enumerate(((tiles0, diag0), (tiles1, diag1))):
        loads.append(pltpu.make_async_copy(tiles.at[level - 1, 0], held.at[i], arrived.at[i]))
        for n, l in enumerate(solve_levels):
            loads.append(pltpu.make_async_copy(inverse.at[l, 0], diag.at[n, i], arrived.at[2 + 2 * n + i]))
    for load in loads:
        load.start()

    def clear(e, nothing):
        for i in range(2):
            spread[i, e] = jnp.zeros(spread.shape[2:], spread.dtype)
        return nothing

    lax.fori_loop(0, spread.shape[1], clear, 0)
    for load in loads:
        load.wait()
    for i, pattern in enumerate((own_pattern, other_pattern)):
        for k in range(held.shape[1]):
            away = jnp.bitwise_xor(pattern[level - 1, 0, k], me)
            flat = jnp.bitwise_and(away, 6)
            part = jnp.where(flat == PLANE[0], 1, jnp.where(flat == PLANE[1], 2, jnp.where(flat == PLANE[2], 3, 0)))
            spread[i, part * (2 * deep) + (away >> 3) * 2 + side(away)] = held[i, k]


def own_kernel(spread, stack, out):
    for i in range(2):
        out[i] = meet(stack, spread, i, 0, None)


def meet(part, spread, i, j, total):
    deep = part.shape[0]
    for z in range(deep):
        for s in range(2):
            term = times_transposed(part[z, s], spread[i, j * 2 * deep + 2 * z + s])
            total = term if total is None else total + term
    return total


def more_kernel(j, spread, part, partial, out):
    for i in range(2):
        out[i] = meet(part, spread, i, j, partial[i])


def finish(spread, c, partial, rhs, diag):
    solved = []
    for i in range(2):
        coupled = meet(c, spread, i, 3, partial[i])
        residual = (rhs[i].astype(jnp.float32) - coupled).astype(jnp.bfloat16)
        solved.append(times_transposed(residual, diag[i]).astype(jnp.bfloat16))
    return solved


def push(solved, spread, j, out):
    deep = out.shape[0]
    for z in range(deep):
        for s in range(2):
            e = j * 2 * deep + 2 * z + s
            total = times(solved[0], spread[0, e]) + times(solved[1], spread[1, e])
            out[z, s] = total.astype(out.dtype)


def forward_kernel(level, spread, c, partial, r0, r1, diag, out):
    out[0], out[1] = finish(spread, c, partial, (r0[level], r1[level]), diag)


def turn_kernel(level, spread, c, partial, r0, r1, diag, out, back, o1, o2, o3):
    solved = finish(spread, c, partial, (r0[level], r1[level]), diag)
    out[0], out[1] = solved
    down = [times(solved[i], diag[i]).astype(jnp.bfloat16) for i in range(2)]
    back[0], back[1] = down
    for j, part in enumerate((o1, o2, o3)):
        push(down, spread, j + 1, part)


def keep_kernel(spread, back, keep):
    push((back[0], back[1]), spread, 0, keep)


def reduce_kernel(keep, a, b, c, own, *outs):
    for z in range(keep.shape[0]):
        terms = [part[z].astype(jnp.float32) for part in (a, b, c)]
        value = keep[z] + ((terms[0] + terms[1]) + terms[2])
        if z == 0:
            own[...] = value
        else:
            outs[z - 1][...] = value.astype(jnp.bfloat16)


def backward_step(own, arrived, known, diag):
    pushed = own[...]
    for part in arrived:
        pushed = pushed + part[...].astype(jnp.float32)
    residual = (known[...].astype(jnp.float32) - pushed).astype(jnp.bfloat16)
    return [times(residual[i], diag[i]).astype(jnp.bfloat16) for i in range(2)]


def backward_kernel(spread, own, known, diag, *refs):
    arrived, (back, o1, o2, o3) = refs[:-4], refs[-4:]
    down = backward_step(own, arrived, known, diag)
    back[0], back[1] = down
    for j, part in enumerate((o1, o2, o3)):
        push(down, spread, j + 1, part)


def last_kernel(own, known, diag, *refs):
    arrived, (mine, sent) = refs[:-2], refs[-2:]
    mine[...], sent[...] = backward_step(own, arrived, known, diag)


def split_kernel(*refs):
    blocks, (mine, sent) = refs[:-2], refs[-2:]
    for l, block in enumerate(blocks):
        mine[l] = block[0]
        sent[l] = block[1]


def join_kernel(*refs):
    pairs, out = refs[:-1], refs[-1]
    here, there = halves(out.shape[2])
    l = 0
    for mine, other in zip(pairs[0::2], pairs[1::2]):
        for m in range(mine.shape[0]):
            out[l, 0, here] = mine[m]
            out[l, 0, there] = other[m]
            l += 1


def body(rhs_block, diag_inv, off_tiles, pattern):
    levels, _, width, size = rhs_block.shape
    devices = lax.axis_size("rows")
    half = width // 2
    line = [8 * j for j in range(1, devices // 8)]
    deep = len(line) + 1
    if lax.axis_size("rhs") > 1:
        off_tiles = lax.all_gather(off_tiles, "rhs", axis=2, tiled=True)

    def shape(*dims, dtype=jnp.bfloat16):
        return jax.ShapeDtypeStruct(dims + (half, size), dtype)

    def in_hbm(value):
        return pltpu.with_memory_space_constraint(value, pltpu.HBM)

    rhs_own, rhs_sent, mine, sent = call(
        first_kernel,
        [shape(levels)] * 2 + [shape()] * 2,
        [in_hbm(rhs_block), in_hbm(diag_inv)],
        [HBM_SPEC] * 2,
        scratch=[
            pltpu.VMEM(rhs_block.shape, jnp.bfloat16),
            pltpu.VMEM((size, size), jnp.bfloat16),
            pltpu.SemaphoreType.DMA((2,)),
        ],
    )
    other_pattern = swap(pattern, 1)
    other = swap(sent, 1)
    forward = [jnp.stack([mine, other])]
    rhs_sent, diag_own, own_tiles, other, other_pattern = lax.optimization_barrier(
        (rhs_sent, diag_inv, off_tiles, other, other_pattern)
    )
    other_tiles = swap(own_tiles, 1)
    rhs_other, diag_other = swap(rhs_sent, 1), swap(diag_own, 1)
    own_tiles, diag_own = in_hbm(off_tiles), in_hbm(diag_inv)
    work = 2 * 2 * devices // 4 * half * size * size
    diag = [None] * levels

    def met(level, block):
        arrived = [block] + [swap(block, m) for m in line]
        solve_levels = (1, 0) if level == 1 else (level,)
        spread, inverses = call(
            functools.partial(place_kernel, level, solve_levels),
            [
                pltpu.VMEM((2, devices, size, size), jnp.bfloat16),
                pltpu.VMEM((len(solve_levels), 2, size, size), jnp.bfloat16),
            ],
            [pattern, other_pattern, block, own_tiles, other_tiles, diag_own, diag_other],
            [SMEM_SPEC] * 2 + [VMEM_SPEC] + [HBM_SPEC, ANY_SPEC] * 2,
            scratch=[
                pltpu.VMEM((2,) + off_tiles.shape[2:], jnp.bfloat16),
                pltpu.SemaphoreType.DMA((2 + 2 * len(solve_levels),)),
            ],
            flops=2 * work,
        )
        for n, l in enumerate(solve_levels):
            diag[l] = inverses[n]
        if level > 1:
            *arrived, spread = lax.optimization_barrier((*arrived, spread))
        stack = jnp.stack(arrived)
        parts = [swap(stack, m) for m in PLANE]
        partial = call(own_kernel, shape(2, dtype=jnp.float32), [spread, stack], flops=work)
        for j in (1, 2):
            kernel = functools.partial(more_kernel, j)
            partial = call(kernel, shape(2, dtype=jnp.float32), [spread, parts[j - 1], partial], flops=work)
        return spread, [spread, parts[2], partial, rhs_own, rhs_other, diag[level]]

    def scattered(spread, back, outs):
        keep = call(keep_kernel, shape(deep, 2, dtype=jnp.float32), [spread, back], flops=work)
        arrived = [swap(out, m) for out, m in zip(outs, PLANE)]
        summed = call(reduce_kernel, [shape(2, dtype=jnp.float32)] + [shape(2)] * (deep - 1), [keep] + arrived)
        return summed[0], [swap(part, m) for part, m in zip(summed[1:], line)]

    spreads = []
    for l in range(1, levels - 1):
        spread, operands = met(l, forward[-1])
        spreads.append(spread)
        forward.append(call(functools.partial(forward_kernel, l), shape(2), operands, flops=work))
    l = levels - 1
    spread, operands = met(l, forward[-1])
    spreads.append(spread)
    top, back, *outs = call(
        functools.partial(turn_kernel, l), [shape(2)] * 2 + [shape(deep, 2)] * 3, operands, flops=4 * work
    )
    forward.append(top)
    backward = [back]
    for l in range(levels - 2, 0, -1):
        own, arrived = scattered(spreads[l], back, outs)
        back, *outs = call(
            backward_kernel,
            [shape(2)] + [shape(deep, 2)] * 3,
            [spreads[l - 1], own, forward[l], diag[l]] + arrived,
            flops=3 * work,
        )
        backward.insert(0, back)
    own, arrived = scattered(spreads[0], back, outs)
    last, last_sent = call(last_kernel, [shape()] * 2, [own, forward[0], diag[0]] + arrived)

    whole = jax.ShapeDtypeStruct((levels, 1, width, size), jnp.bfloat16)
    mine, sent = call(split_kernel, [shape(levels)] * 2, forward)
    forward_sol = call(join_kernel, whole, [mine, swap(sent, 1)])
    mine, sent = call(split_kernel, [shape(levels - 1)] * 2, backward)
    backward_sol = call(join_kernel, whole, [last[None], swap(last_sent, 1)[None], mine, swap(sent, 1)])
    return forward_sol, backward_sol


def solution(mesh):
    return jax.shard_map(
        body,
        mesh=mesh,
        in_specs=(
            P(None, "rows", "rhs", None),
            P(None, "rows", None, None),
            P(None, "rows", "rhs", None, None),
            P(None, "rows", None),
        ),
        out_specs=(P(None, "rows", "rhs", None), P(None, "rows", "rhs", None)),
        check_vma=False,
    )
```

time: 297 us -> 114 us (0.38)
  waiting for transfers between devices: 189 us -> 36.2 us
  blocking collectives: 59.3 us -> 0 us
  starting transfers between devices: 3.74 us -> 50 us
  Pallas kernels: 0 us -> 26.2 us
  matrix products: 24.7 us -> 0 us
  between operations: 13.9 us -> 0.91 us
    all_gather x3 -> x0, waiting for transfers between devices: 164 us -> none  [couple_fold(): pieces = lax.all_gather(stacked, 'rows', axis=0, tiled=True)]
    all_to_all x2 -> x0, blocking collectives: 59.3 us -> none  [push_down(): lax.all_to_all(outgoing.astype(jnp.bfloat16), 'rows', split_axis=0, conca...]
    ppermute x0 -> x44, starting transfers between devices: none -> 50 us  [swap(): return lax.ppermute(value, 'rows', [(i, i ^ mask) for i in range(size)])]
    ppermute x0 -> x44, waiting for transfers between devices: none -> 36.2 us  [swap(): return lax.ppermute(value, 'rows', [(i, i ^ mask) for i in range(size)])]
    pallas_call x0 -> x29, Pallas kernels: none -> 26.2 us  [call(): pl.pallas_call(kernel, out_shape=out_shape, in_specs=[VMEM_SPEC] * len(op...]
    all_to_all x1 -> x0, waiting for transfers between devices: 25.6 us -> none  [push_down(): lax.all_to_all(outgoing.astype(jnp.bfloat16), 'rows', split_axis=0, conca...]
    dot_general x17 -> x0, matrix products: 24.7 us -> none  [the longest x4 10.7 us: to_level(): jnp.einsum('rc,ac->ra', residual, inverse, preferred_element_type=jnp.flo...]
    all_to_all x1 -> x0, starting transfers between devices: 3.62 us -> none  [push_down(): lax.all_to_all(outgoing.astype(jnp.bfloat16), 'rows', split_axis=0, conca...]
  transfers between devices with their start and end apart: 4 -> 44, of which waited for: 4 -> 24; matrix products, arithmetic and copies ran while one was open for 0% -> 0% of each run, Pallas kernels for 0% -> 14%
where the time goes in v2:
time: 114 us
  starting transfers between devices  50 us (44%)
  waiting for transfers between devices  36.2 us (32%)
  Pallas kernels  26.2 us (23%)
    ppermute x44, starting transfers between devices, swap(): return lax.ppermute(value, 'rows', [(i, i ^ mask) for i in range(size)])  50 us
    ppermute x44, waiting for transfers between devices, swap(): return lax.ppermute(value, 'rows', [(i, i ^ mask) for i in range(size)])  36.2 us
    pallas_call x29, Pallas kernels, call(): pl.pallas_call(kernel, out_shape=out_shape, in_specs=[VMEM_SPEC] * len(op...  26.2 us
  transfers between devices with their start and end apart: 44, of which 24 were waited for; matrix products, arithmetic and copies ran while one was open for 0% of the time, Pallas kernels for 14%

profile of v2, /device:TPU:0, one launch (start us, length us, event | category | flops | bytes accessed | tf_op | source)
XLA Modules:
  0.0 114.1 jit_solution(12237202350691631214)
XLA Ops:
  0.6 1.2 %shard_map.59 = (bf16[4,32,256]{2,1,0:T(8,128)(2,1)S(1)}, bf16[4,32,256]{2,1,0:T(8,128)(2,1)S(1)}, bf16[32,256]{1,0:T(8,128)(2,1)S(1)}, bf16[32,256]{1,0:T(8,128)(2,1)S(1)}) custom-call(bf16[4,1,64,256]{3,2,1,0:T(8,128)(2,1)} %rhs.1, bf16[4,1,256,256]{3,2,1,0:T(8,128)(2,1)} %diag0.5), custom_call_target="tpu_custom_call" | custom-call | tf_op jit(solution)/shard_map/pallas_call | solution.py:32
  2.4 1.3 %collective-permute-done.1.other_pattern = s32[3,1,16]{2,1,0:T(1,128)S(1)} collective-permute-done((s32[3,1,16]{2,1,0:T(1,128)}, s32[3,1,16]{2,1,0:T(1,128)S(1)}, u32[]{:S(2)}, u32[]{:S(2)}) %collective-permute-start.1) | collective-permute-done | bytes 224 | tf_op jit(solution)/shard_map/ppermute | solution.py:20
  4.2 2.8 %collective-permute-start.4 = (bf16[2,32,256]{2,1,0:T(8,128)(2,1)S(1)}, bf16[2,32,256]{2,1,0:T(8,128)(2,1)S(1)}, u32[]{:S(2)}, u32[]{:S(2)}) collective-permute-start(bf16[2,32,256]{2,1,0:T(8,128)(2,1)S(1)} %get-tuple-element.115.after.refs_0_.known), channel_id=1, source_target_pairs={{0,8},{1,9},{2,10},{3,11},{4,12},{5,13},{6,14},{7,15},{8,0},{9,1},... | collective-permute-start | bytes 98312 | tf_op jit(solution)/shard_map/ppermute | solution.py:20
  7.0 2.6 %collective-permute-start.5 = (bf16[2,32,256]{2,1,0:T(8,128)(2,1)S(1)}, bf16[2,32,256]{2,1,0:T(8,128)(2,1)S(1)}, u32[]{:S(2)}, u32[]{:S(2)}) collective-permute-start(bf16[2,32,256]{2,1,0:T(8,128)(2,1)S(1)} %get-tuple-element.115.after.refs_0_.known), channel_id=1, source_target_pairs={{0,16},{1,17},{2,18},{3,19},{4,20},{5,21},{6,22},{7,23},{8,24},{9,... | collective-permute-start | bytes 98312 | tf_op jit(solution)/shard_map/ppermute | solution.py:20
  9.6 2.8 %collective-permute-done.5 = bf16[2,32,256]{2,1,0:T(8,128)(2,1)S(1)} collective-permute-done((bf16[2,32,256]{2,1,0:T(8,128)(2,1)S(1)}, bf16[2,32,256]{2,1,0:T(8,128)(2,1)S(1)}, u32[]{:S(2)}, u32[]{:S(2)}) %collective-permute-start.5) | collective-permute-done | bytes 32800 | tf_op jit(solution)/shard_map/ppermute | solution.py:20
  12.4 2.9 %collective-permute-done.6 = bf16[2,32,256]{2,1,0:T(8,128)(2,1)S(1)} collective-permute-done((bf16[2,32,256]{2,1,0:T(8,128)(2,1)S(1)}, bf16[2,32,256]{2,1,0:T(8,128)(2,1)S(1)}, u32[]{:S(2)}, u32[]{:S(2)}) %collective-permute-start.6) | collective-permute-done | bytes 32800 | tf_op jit(solution)/shard_map/ppermute | solution.py:20
  15.3 2.5 %collective-permute-start.9 = (bf16[4,2,32,256]{3,2,1,0:T(8,128)(2,1)S(1)}, bf16[4,2,32,256]{3,2,1,0:T(8,128)(2,1)S(1)}, u32[]{:S(2)}, u32[]{:S(2)}) collective-permute-start(bf16[4,2,32,256]{3,2,1,0:T(8,128)(2,1)S(1)} %pad_maximum_fusion.stack), channel_id=1, source_target_pairs={{0,6},{1,7},{2,4},{3,5},{4,2},{5,3},{6,0},{7,1},{8,14},{9,15},{10,... | collective-permute-start | bytes 393224 | tf_op jit(solution)/shard_map/ppermute | solution.py:20
  18.9 0.7 copy-done
  19.5 2.5 %shard_map.60 = (bf16[2,32,256,256]{3,2,1,0:T(8,128)(2,1)S(1)}, bf16[2,2,256,256]{3,2,1,0:T(8,128)(2,1)S(1)}) custom-call(s32[3,1,16]{2,1,0:T(1,128)S(1)} %copy-done, s32[3,1,16]{2,1,0:T(1,128)S(1)} %collective-permute-done.1.other_pattern, bf16[2,32,256]{2,1,0:T(8,128)(2,1)S(1)} %get-tuple-element.115.after.refs_0_.known, ...), custom_call_target="tpu_custom_call" | custom-call | flops 134217728 | tf_op jit(solution)/shard_map/pallas_call | solution.py:32
  22.1 0.7 shard_map.61.partial
  22.8 0.7 shard_map.62.partial
  23.6 0.7 shard_map.63.partial
  24.3 1.4 %shard_map.64.after.refs_1_.known = bf16[2,32,256]{2,1,0:T(8,128)(2,1)S(1)} custom-call(bf16[2,32,256,256]{3,2,1,0:T(8,128)(2,1)S(1)} %get-tuple-element.63.spread, bf16[4,2,32,256]{3,2,1,0:T(8,128)(2,1)S(1)} %collective-permute-done.7.c, f32[2,32,256]{2,1,0:T(8,128)S(1)} %shard_map.63.partial, bf16[4,32,256]{2,1,0:T(8,128)(2,1)S(1)} %get-tuple-element.64.r0, ...), custom_call_target="tpu_custom_call" | custom-call | flops 67108864 | tf_op jit(solution)/shard_map/pallas_call | solution.py:32
  26.1 2.6 %collective-permute-start.12 = (bf16[2,32,256]{2,1,0:T(8,128)(2,1)S(1)}, bf16[2,32,256]{2,1,0:T(8,128)(2,1)S(1)}, u32[]{:S(2)}, u32[]{:S(2)}) collective-permute-start(bf16[2,32,256]{2,1,0:T(8,128)(2,1)S(1)} %shard_map.64.after.refs_1_.known), channel_id=1, source_target_pairs={{0,16},{1,17},{2,18},{3,19},{4,20},{5,21},{6,22},{7,23},{8,24},{9,... | collective-permute-start | bytes 98312 | tf_op jit(solution)/shard_map/ppermute | solution.py:20
  28.6 1.5 %collective-permute-start.13 = (bf16[2,32,256]{2,1,0:T(8,128)(2,1)S(1)}, bf16[2,32,256]{2,1,0:T(8,128)(2,1)S(1)}, u32[]{:S(2)}, u32[]{:S(2)}) collective-permute-start(bf16[2,32,256]{2,1,0:T(8,128)(2,1)S(1)} %shard_map.64.after.refs_1_.known), channel_id=1, source_target_pairs={{0,24},{1,25},{2,26},{3,27},{4,28},{5,29},{6,30},{7,31},{8,16},{9,... | collective-permute-start | bytes 98312 | tf_op jit(solution)/shard_map/ppermute | solution.py:20
  30.1 2.5 %shard_map.65 = (bf16[2,32,256,256]{3,2,1,0:T(8,128)(2,1)S(1)}, bf16[1,2,256,256]{3,2,1,0:T(8,128)(2,1)S(1)}) custom-call(s32[3,1,16]{2,1,0:T(1,128)S(1)} %copy-done.1, s32[3,1,16]{2,1,0:T(1,128)S(1)} %collective-permute-done.1.other_pattern, bf16[2,32,256]{2,1,0:T(8,128)(2,1)S(1)} %shard_map.64.after.refs_1_.known, bf16[3,1,16,256,256]{4,3,2,1,0:T(8,128)(2,1)} %tiles0.5, ...), custom_call_target="tpu_custom_call" | custom-call | flops 134217728 | tf_op jit(solution)/shard_map/pallas_call | solution.py:32
  32.6 1.7 %collective-permute-done.13 = bf16[2,32,256]{2,1,0:T(8,128)(2,1)S(1)} collective-permute-done((bf16[2,32,256]{2,1,0:T(8,128)(2,1)S(1)}, bf16[2,32,256]{2,1,0:T(8,128)(2,1)S(1)}, u32[]{:S(2)}, u32[]{:S(2)}) %collective-permute-start.13) | collective-permute-done | bytes 32800 | tf_op jit(solution)/shard_map/ppermute | solution.py:20
  34.4 1.5 %collective-permute-start.16 = (bf16[4,2,32,256]{3,2,1,0:T(8,128)(2,1)S(1)}, bf16[4,2,32,256]{3,2,1,0:T(8,128)(2,1)S(1)}, u32[]{:S(2)}, u32[]{:S(2)}) collective-permute-start(bf16[4,2,32,256]{3,2,1,0:T(8,128)(2,1)S(1)} %pad_maximum_fusion.1.stack), channel_id=1, source_target_pairs={{0,6},{1,7},{2,4},{3,5},{4,2},{5,3},{6,0},{7,1},{8,14},{9,15},{10,... | collective-permute-start | bytes 393224 | tf_op jit(solution)/shard_map/ppermute | solution.py:20
  36.4 1.5 %collective-permute-start.14 = (bf16[4,2,32,256]{3,2,1,0:T(8,128)(2,1)S(1)}, bf16[4,2,32,256]{3,2,1,0:T(8,128)(2,1)S(1)}, u32[]{:S(2)}, u32[]{:S(2)}) collective-permute-start(bf16[4,2,32,256]{3,2,1,0:T(8,128)(2,1)S(1)} %pad_maximum_fusion.1.stack), channel_id=1, source_target_pairs={{0,4},{1,5},{2,6},{3,7},{4,0},{5,1},{6,2},{7,3},{8,12},{9,13},{10,... | collective-permute-start | bytes 393224 | tf_op jit(solution)/shard_map/ppermute | solution.py:20
  37.9 0.7 shard_map.66.partial
  38.6 1.9 %collective-permute-done.16.part = bf16[4,2,32,256]{3,2,1,0:T(8,128)(2,1)S(1)} collective-permute-done((bf16[4,2,32,256]{3,2,1,0:T(8,128)(2,1)S(1)}, bf16[4,2,32,256]{3,2,1,0:T(8,128)(2,1)S(1)}, u32[]{:S(2)}, u32[]{:S(2)}) %collective-permute-start.16) | collective-permute-done | bytes 131104 | tf_op jit(solution)/shard_map/ppermute | solution.py:20
  40.6 0.7 shard_map.67.partial
  41.3 0.7 shard_map.68.partial
  42.0 1.4 %shard_map.69.after.refs_2_.known = bf16[2,32,256]{2,1,0:T(8,128)(2,1)S(1)} custom-call(bf16[2,32,256,256]{3,2,1,0:T(8,128)(2,1)S(1)} %get-tuple-element.68.spread, bf16[4,2,32,256]{3,2,1,0:T(8,128)(2,1)S(1)} %collective-permute-done.14.c, f32[2,32,256]{2,1,0:T(8,128)S(1)} %shard_map.68.partial, bf16[4,32,256]{2,1,0:T(8,128)(2,1)S(1)} %get-tuple-element.64.r0, ...), custom_call_target="tpu_custom_call" | custom-call | flops 67108864 | tf_op jit(solution)/shard_map/pallas_call | solution.py:32
  43.4 2.6 %collective-permute-start.18 = (bf16[2,32,256]{2,1,0:T(8,128)(2,1)S(1)}, bf16[2,32,256]{2,1,0:T(8,128)(2,1)S(1)}, u32[]{:S(2)}, u32[]{:S(2)}) collective-permute-start(bf16[2,32,256]{2,1,0:T(8,128)(2,1)S(1)} %shard_map.69.after.refs_2_.known), channel_id=1, source_target_pairs={{0,16},{1,17},{2,18},{3,19},{4,20},{5,21},{6,22},{7,23},{8,24},{9,... | collective-permute-start | bytes 98312 | tf_op jit(solution)/shard_map/ppermute | solution.py:20
  46.1 1.8 %collective-permute-start.19 = (bf16[2,32,256]{2,1,0:T(8,128)(2,1)S(1)}, bf16[2,32,256]{2,1,0:T(8,128)(2,1)S(1)}, u32[]{:S(2)}, u32[]{:S(2)}) collective-permute-start(bf16[2,32,256]{2,1,0:T(8,128)(2,1)S(1)} %shard_map.69.after.refs_2_.known), channel_id=1, source_target_pairs={{0,24},{1,25},{2,26},{3,27},{4,28},{5,29},{6,30},{7,31},{8,16},{9,... | collective-permute-start | bytes 98312 | tf_op jit(solution)/shard_map/ppermute | solution.py:20
  47.8 2.5 %shard_map.70 = (bf16[2,32,256,256]{3,2,1,0:T(8,128)(2,1)S(1)}, bf16[1,2,256,256]{3,2,1,0:T(8,128)(2,1)S(1)}) custom-call(s32[3,1,16]{2,1,0:T(1,128)S(1)} %copy-done.1, s32[3,1,16]{2,1,0:T(1,128)S(1)} %collective-permute-done.1.other_pattern, bf16[2,32,256]{2,1,0:T(8,128)(2,1)S(1)} %shard_map.69.after.refs_2_.known, bf16[3,1,16,256,256]{4,3,2,1,0:T(8,128)(2,1)} %tiles0.5, ...), custom_call_target="tpu_custom_call" | custom-call | flops 134217728 | tf_op jit(solution)/shard_map/pallas_call | solution.py:32
  50.4 1.4 %collective-permute-done.19 = bf16[2,32,256]{2,1,0:T(8,128)(2,1)S(1)} collective-permute-done((bf16[2,32,256]{2,1,0:T(8,128)(2,1)S(1)}, bf16[2,32,256]{2,1,0:T(8,128)(2,1)S(1)}, u32[]{:S(2)}, u32[]{:S(2)}) %collective-permute-start.19) | collective-permute-done | bytes 32800 | tf_op jit(solution)/shard_map/ppermute | solution.py:20
  51.8 1.7 %collective-permute-start.22 = (bf16[4,2,32,256]{3,2,1,0:T(8,128)(2,1)S(1)}, bf16[4,2,32,256]{3,2,1,0:T(8,128)(2,1)S(1)}, u32[]{:S(2)}, u32[]{:S(2)}) collective-permute-start(bf16[4,2,32,256]{3,2,1,0:T(8,128)(2,1)S(1)} %pad_maximum_fusion.2.stack), channel_id=1, source_target_pairs={{0,6},{1,7},{2,4},{3,5},{4,2},{5,3},{6,0},{7,1},{8,14},{9,15},{10,... | collective-permute-start | bytes 393224 | tf_op jit(solution)/shard_map/ppermute | solution.py:20
  54.1 1.3 %collective-permute-start.20 = (bf16[4,2,32,256]{3,2,1,0:T(8,128)(2,1)S(1)}, bf16[4,2,32,256]{3,2,1,0:T(8,128)(2,1)S(1)}, u32[]{:S(2)}, u32[]{:S(2)}) collective-permute-start(bf16[4,2,32,256]{3,2,1,0:T(8,128)(2,1)S(1)} %pad_maximum_fusion.2.stack), channel_id=1, source_target_pairs={{0,4},{1,5},{2,6},{3,7},{4,0},{5,1},{6,2},{7,3},{8,12},{9,13},{10,... | collective-permute-start | bytes 393224 | tf_op jit(solution)/shard_map/ppermute | solution.py:20
  55.4 0.7 shard_map.71.partial
  56.1 1.7 %collective-permute-done.22.part = bf16[4,2,32,256]{3,2,1,0:T(8,128)(2,1)S(1)} collective-permute-done((bf16[4,2,32,256]{3,2,1,0:T(8,128)(2,1)S(1)}, bf16[4,2,32,256]{3,2,1,0:T(8,128)(2,1)S(1)}, u32[]{:S(2)}, u32[]{:S(2)}) %collective-permute-start.22) | collective-permute-done | bytes 131104 | tf_op jit(solution)/shard_map/ppermute | solution.py:20
  57.7 0.7 shard_map.72.partial
  58.5 0.7 shard_map.73.partial
  59.2 2.7 %shard_map.74 = (bf16[2,32,256]{2,1,0:T(8,128)(2,1)S(1)}, bf16[2,32,256]{2,1,0:T(8,128)(2,1)S(1)}, bf16[4,2,32,256]{3,2,1,0:T(8,128)(2,1)S(1)}, bf16[4,2,32,256]...) custom-call(bf16[2,32,256,256]{3,2,1,0:T(8,128)(2,1)S(1)} %get-tuple-element.75.spread, ...), custom_call_target="tpu_custom_call" | custom-call | flops 268435456 | tf_op jit(solution)/shard_map/pallas_call | solution.py:32
  61.9 2.1 %collective-permute-start.24 = (bf16[4,2,32,256]{3,2,1,0:T(8,128)(2,1)S(1)}, bf16[4,2,32,256]{3,2,1,0:T(8,128)(2,1)S(1)}, u32[]{:S(2)}, u32[]{:S(2)}) collective-permute-start(bf16[4,2,32,256]{3,2,1,0:T(8,128)(2,1)S(1)} %get-tuple-element.85), channel_id=1, source_target_pairs={{0,6},{1,7},{2,4},{3,5},{4,2},{5,3},{6,0},{7,1},{8,14},{9,15},{10,... | collective-permute-start | bytes 393224 | tf_op jit(solution)/shard_map/ppermute | solution.py:20
  64.0 0.6 collective-permute-start.25
  64.6 0.8 collective-permute-start.26
  65.9 1.9 %collective-permute-done.24.a = bf16[4,2,32,256]{3,2,1,0:T(8,128)(2,1)S(1)} collective-permute-done((bf16[4,2,32,256]{3,2,1,0:T(8,128)(2,1)S(1)}, bf16[4,2,32,256]{3,2,1,0:T(8,128)(2,1)S(1)}, u32[]{:S(2)}, u32[]{:S(2)}) %collective-permute-start.24) | collective-permute-done | bytes 131104 | tf_op jit(solution)/shard_map/ppermute | solution.py:20
  67.8 1.2 %collective-permute-done.25.b = bf16[4,2,32,256]{3,2,1,0:T(8,128)(2,1)S(1)} collective-permute-done((bf16[4,2,32,256]{3,2,1,0:T(8,128)(2,1)S(1)}, bf16[4,2,32,256]{3,2,1,0:T(8,128)(2,1)S(1)}, u32[]{:S(2)}, u32[]{:S(2)}) %collective-permute-start.25) | collective-permute-done | bytes 131104 | tf_op jit(solution)/shard_map/ppermute | solution.py:20
  69.7 2.4 %collective-permute-start.28 = (bf16[2,32,256]{2,1,0:T(8,128)(2,1)S(1)}, bf16[2,32,256]{2,1,0:T(8,128)(2,1)S(1)}, u32[]{:S(2)}, u32[]{:S(2)}) collective-permute-start(bf16[2,32,256]{2,1,0:T(8,128)(2,1)S(1)} %get-tuple-element.90), channel_id=1, source_target_pairs={{0,16},{1,17},{2,18},{3,19},{4,20},{5,21},{6,22},{7,23},{8,24},{9,... | collective-permute-start | bytes 98312 | tf_op jit(solution)/shard_map/ppermute | solution.py:20
  72.2 2.0 %collective-permute-start.29 = (bf16[2,32,256]{2,1,0:T(8,128)(2,1)S(1)}, bf16[2,32,256]{2,1,0:T(8,128)(2,1)S(1)}, u32[]{:S(2)}, u32[]{:S(2)}) collective-permute-start(bf16[2,32,256]{2,1,0:T(8,128)(2,1)S(1)} %get-tuple-element.91), channel_id=1, source_target_pairs={{0,24},{1,25},{2,26},{3,27},{4,28},{5,29},{6,30},{7,31},{8,16},{9,... | collective-permute-start | bytes 98312 | tf_op jit(solution)/shard_map/ppermute | solution.py:20
  74.6 3.2 %collective-permute-done.29.refs_2_ = bf16[2,32,256]{2,1,0:T(8,128)(2,1)S(1)} collective-permute-done((bf16[2,32,256]{2,1,0:T(8,128)(2,1)S(1)}, bf16[2,32,256]{2,1,0:T(8,128)(2,1)S(1)}, u32[]{:S(2)}, u32[]{:S(2)}) %collective-permute-start.29) | collective-permute-done | bytes 32800 | tf_op jit(solution)/shard_map/ppermute | solution.py:20
  77.9 1.3 %shard_map.79 = (bf16[2,32,256]{2,1,0:T(8,128)(2,1)S(1)}, bf16[4,2,32,256]{3,2,1,0:T(8,128)(2,1)S(1)}, bf16[4,2,32,256]{3,2,1,0:T(8,128)(2,1)S(1)}, bf16[4,2,32,256]{3,2,1,0:T(8,128)(2,1)S(1)}) custom-call(bf16[2,32,256,256]{3,2,1,0:T(8,128)(2,1)S(1)} %get-tuple-element.68.spread, f32[2,32,256]{2,1,0:T(8,128)S(1)} %get-tuple-element.88.own, ...), custom_call_target="tpu_custom_call" | custom-call | flops 201326592 | tf_op jit(solution)/shard_map/pallas_call | solution.py:32
  79.2 2.1 %collective-permute-start.30 = (bf16[4,2,32,256]{3,2,1,0:T(8,128)(2,1)S(1)}, bf16[4,2,32,256]{3,2,1,0:T(8,128)(2,1)S(1)}, u32[]{:S(2)}, u32[]{:S(2)}) collective-permute-start(bf16[4,2,32,256]{3,2,1,0:T(8,128)(2,1)S(1)} %get-tuple-element.93), channel_id=1, source_target_pairs={{0,6},{1,7},{2,4},{3,5},{4,2},{5,3},{6,0},{7,1},{8,14},{9,15},{10,... | collective-permute-start | bytes 393224 | tf_op jit(solution)/shard_map/ppermute | solution.py:20
  81.2 0.6 collective-permute-start.31
  81.9 0.8 collective-permute-start.32
  83.2 1.9 %collective-permute-done.30.a = bf16[4,2,32,256]{3,2,1,0:T(8,128)(2,1)S(1)} collective-permute-done((bf16[4,2,32,256]{3,2,1,0:T(8,128)(2,1)S(1)}, bf16[4,2,32,256]{3,2,1,0:T(8,128)(2,1)S(1)}, u32[]{:S(2)}, u32[]{:S(2)}) %collective-permute-start.30) | collective-permute-done | bytes 131104 | tf_op jit(solution)/shard_map/ppermute | solution.py:20
  85.1 1.1 collective-permute-done.31.b
  87.0 2.2 %collective-permute-start.34 = (bf16[2,32,256]{2,1,0:T(8,128)(2,1)S(1)}, bf16[2,32,256]{2,1,0:T(8,128)(2,1)S(1)}, u32[]{:S(2)}, u32[]{:S(2)}) collective-permute-start(bf16[2,32,256]{2,1,0:T(8,128)(2,1)S(1)} %get-tuple-element.98), channel_id=1, source_target_pairs={{0,16},{1,17},{2,18},{3,19},{4,20},{5,21},{6,22},{7,23},{8,24},{9,... | collective-permute-start | bytes 98312 | tf_op jit(solution)/shard_map/ppermute | solution.py:20
  89.1 2.2 %collective-permute-start.35 = (bf16[2,32,256]{2,1,0:T(8,128)(2,1)S(1)}, bf16[2,32,256]{2,1,0:T(8,128)(2,1)S(1)}, u32[]{:S(2)}, u32[]{:S(2)}) collective-permute-start(bf16[2,32,256]{2,1,0:T(8,128)(2,1)S(1)} %get-tuple-element.99), channel_id=1, source_target_pairs={{0,24},{1,25},{2,26},{3,27},{4,28},{5,29},{6,30},{7,31},{8,16},{9,... | collective-permute-start | bytes 98312 | tf_op jit(solution)/shard_map/ppermute | solution.py:20
  91.9 3.0 %collective-permute-done.35.refs_2_ = bf16[2,32,256]{2,1,0:T(8,128)(2,1)S(1)} collective-permute-done((bf16[2,32,256]{2,1,0:T(8,128)(2,1)S(1)}, bf16[2,32,256]{2,1,0:T(8,128)(2,1)S(1)}, u32[]{:S(2)}, u32[]{:S(2)}) %collective-permute-start.35) | collective-permute-done | bytes 32800 | tf_op jit(solution)/shard_map/ppermute | solution.py:20
  94.9 1.3 %shard_map.82 = (bf16[2,32,256]{2,1,0:T(8,128)(2,1)S(1)}, bf16[4,2,32,256]{3,2,1,0:T(8,128)(2,1)S(1)}, bf16[4,2,32,256]{3,2,1,0:T(8,128)(2,1)S(1)}, bf16[4,2,32,256]{3,2,1,0:T(8,128)(2,1)S(1)}) custom-call(bf16[2,32,256,256]{3,2,1,0:T(8,128)(2,1)S(1)} %get-tuple-element.63.spread, f32[2,32,256]{2,1,0:T(8,128)S(1)} %get-tuple-element.96.own, ...), custom_call_target="tpu_custom_call" | custom-call | flops 201326592 | tf_op jit(solution)/shard_map/pallas_call | solution.py:32
  96.2 2.1 %collective-permute-start.36 = (bf16[4,2,32,256]{3,2,1,0:T(8,128)(2,1)S(1)}, bf16[4,2,32,256]{3,2,1,0:T(8,128)(2,1)S(1)}, u32[]{:S(2)}, u32[]{:S(2)}) collective-permute-start(bf16[4,2,32,256]{3,2,1,0:T(8,128)(2,1)S(1)} %get-tuple-element.101), channel_id=1, source_target_pairs={{0,6},{1,7},{2,4},{3,5},{4,2},{5,3},{6,0},{7,1},{8,14},{9,15},{10,... | collective-permute-start | bytes 393224 | tf_op jit(solution)/shard_map/ppermute | solution.py:20
  98.2 0.6 collective-permute-start.37
  98.8 0.8 collective-permute-start.38
  100.2 1.8 %collective-permute-done.36.a = bf16[4,2,32,256]{3,2,1,0:T(8,128)(2,1)S(1)} collective-permute-done((bf16[4,2,32,256]{3,2,1,0:T(8,128)(2,1)S(1)}, bf16[4,2,32,256]{3,2,1,0:T(8,128)(2,1)S(1)}, u32[]{:S(2)}, u32[]{:S(2)}) %collective-permute-start.36) | collective-permute-done | bytes 131104 | tf_op jit(solution)/shard_map/ppermute | solution.py:20
  102.1 1.1 collective-permute-done.37.b
  103.2 0.6 collective-permute-done.38.c
  104.0 2.4 %collective-permute-start.40 = (bf16[2,32,256]{2,1,0:T(8,128)(2,1)S(1)}, bf16[2,32,256]{2,1,0:T(8,128)(2,1)S(1)}, u32[]{:S(2)}, u32[]{:S(2)}) collective-permute-start(bf16[2,32,256]{2,1,0:T(8,128)(2,1)S(1)} %get-tuple-element.106), channel_id=1, source_target_pairs={{0,16},{1,17},{2,18},{3,19},{4,20},{5,21},{6,22},{7,23},{8,24},{9,... | collective-permute-start | bytes 98312 | tf_op jit(solution)/shard_map/ppermute | solution.py:20
  106.4 2.0 %collective-permute-start.41 = (bf16[2,32,256]{2,1,0:T(8,128)(2,1)S(1)}, bf16[2,32,256]{2,1,0:T(8,128)(2,1)S(1)}, u32[]{:S(2)}, u32[]{:S(2)}) collective-permute-start(bf16[2,32,256]{2,1,0:T(8,128)(2,1)S(1)} %get-tuple-element.107), channel_id=1, source_target_pairs={{0,24},{1,25},{2,26},{3,27},{4,28},{5,29},{6,30},{7,31},{8,16},{9,... | collective-permute-start | bytes 98312 | tf_op jit(solution)/shard_map/ppermute | solution.py:20
  108.8 3.2 %collective-permute-done.41.refs_2_ = bf16[2,32,256]{2,1,0:T(8,128)(2,1)S(1)} collective-permute-done((bf16[2,32,256]{2,1,0:T(8,128)(2,1)S(1)}, bf16[2,32,256]{2,1,0:T(8,128)(2,1)S(1)}, u32[]{:S(2)}, u32[]{:S(2)}) %collective-permute-start.41) | collective-permute-done | bytes 32800 | tf_op jit(solution)/shard_map/ppermute | solution.py:20
  112.3 0.7 shard_map.76
  113.5 0.7 shard_map.87
  (62 shorter events, 9.1 us)
Async XLA Ops:
  1.8 1.9 %collective-permute-start = (bf16[32,256]{1,0:T(8,128)(2,1)S(1)}, bf16[32,256]{1,0:T(8,128)(2,1)S(1)}, u32[]{:S(2)}, u32[]{:S(2)}) collective-permute-start(bf16[32,256]{1,0:T(8,128)(2,1)S(1)} %get-tuple-element.58), channel_id=1, source_target_pairs={{0,1},{1,0},{2,3},{3,2},{4,5},{5,4},{6,7},{7,6},{8,9},{9,8},{10,11... | collective-permute-start | bytes 49160 | tf_op jit(solution)/shard_map/ppermute | solution.py:20
  2.3 1.4 %collective-permute-start.1 = (s32[3,1,16]{2,1,0:T(1,128)}, s32[3,1,16]{2,1,0:T(1,128)S(1)}, u32[]{:S(2)}, u32[]{:S(2)}) collective-permute-start(s32[3,1,16]{2,1,0:T(1,128)} %own_pattern.5), channel_id=1, source_target_pairs={{0,1},{1,0},{2,3},{3,2},{4,5},{5,4},{6,7},{7,6},{8,9},{9,8},{10,11... | collective-permute-start | bytes 584 | tf_op jit(solution)/shard_map/ppermute | solution.py:20
  3.7 15.2 %collective-permute-start.2 = (bf16[3,1,16,256,256]{4,3,2,1,0:T(8,128)(2,1)}, bf16[3,1,16,256,256]{4,3,2,1,0:T(8,128)(2,1)S(1)}, u32[]{:S(2)}, u32[]{:S(2)}) collective-permute-start(bf16[3,1,16,256,256]{4,3,2,1,0:T(8,128)(2,1)} %tiles0.5), channel_id=1, source_target_pairs={{0,1},{1,0},{2,3},{3,2},{4,5},{5,4},{6,7},{7,6},{8,9},{9,8},{10,11... | collective-permute-start | bytes 18874376 | tf_op jit(solution)/shard_map/ppermute | solution.py:20
  3.9 14.5 %collective-permute-start.3 = (bf16[4,1,256,256]{3,2,1,0:T(8,128)(2,1)}, bf16[4,1,256,256]{3,2,1,0:T(8,128)(2,1)S(1)}, u32[]{:S(2)}, u32[]{:S(2)}) collective-permute-start(bf16[4,1,256,256]{3,2,1,0:T(8,128)(2,1)} %diag0.5), channel_id=1, source_target_pairs={{0,1},{1,0},{2,3},{3,2},{4,5},{5,4},{6,7},{7,6},{8,9},{9,8},{10,11... | collective-permute-start | bytes 1572872 | tf_op jit(solution)/shard_map/ppermute | solution.py:20
  4.2 5.3 %collective-permute-start.4 = (bf16[2,32,256]{2,1,0:T(8,128)(2,1)S(1)}, bf16[2,32,256]{2,1,0:T(8,128)(2,1)S(1)}, u32[]{:S(2)}, u32[]{:S(2)}) collective-permute-start(bf16[2,32,256]{2,1,0:T(8,128)(2,1)S(1)} %get-tuple-element.115.after.refs_0_.known), channel_id=1, source_target_pairs={{0,8},{1,9},{2,10},{3,11},{4,12},{5,13},{6,14},{7,15},{8,0},{9,1},... | collective-permute-start | bytes 98312 | tf_op jit(solution)/shard_map/ppermute | solution.py:20
  7.0 5.4 %collective-permute-start.5 = (bf16[2,32,256]{2,1,0:T(8,128)(2,1)S(1)}, bf16[2,32,256]{2,1,0:T(8,128)(2,1)S(1)}, u32[]{:S(2)}, u32[]{:S(2)}) collective-permute-start(bf16[2,32,256]{2,1,0:T(8,128)(2,1)S(1)} %get-tuple-element.115.after.refs_0_.known), channel_id=1, source_target_pairs={{0,16},{1,17},{2,18},{3,19},{4,20},{5,21},{6,22},{7,23},{8,24},{9,... | collective-permute-start | bytes 98312 | tf_op jit(solution)/shard_map/ppermute | solution.py:20
  9.6 5.7 %collective-permute-start.6 = (bf16[2,32,256]{2,1,0:T(8,128)(2,1)S(1)}, bf16[2,32,256]{2,1,0:T(8,128)(2,1)S(1)}, u32[]{:S(2)}, u32[]{:S(2)}) collective-permute-start(bf16[2,32,256]{2,1,0:T(8,128)(2,1)S(1)} %get-tuple-element.115.after.refs_0_.known), channel_id=1, source_target_pairs={{0,24},{1,25},{2,26},{3,27},{4,28},{5,29},{6,30},{7,31},{8,16},{9,... | collective-permute-start | bytes 98312 | tf_op jit(solution)/shard_map/ppermute | solution.py:20
  9.6 14.7 %collective-permute-start.10 = (bf16[4,32,256]{2,1,0:T(8,128)(2,1)S(1)}, bf16[4,32,256]{2,1,0:T(8,128)(2,1)S(1)}, u32[]{:S(2)}, u32[]{:S(2)}) collective-permute-start(bf16[4,32,256]{2,1,0:T(8,128)(2,1)S(1)} %get-tuple-element.65), channel_id=1, source_target_pairs={{0,1},{1,0},{2,3},{3,2},{4,5},{5,4},{6,7},{7,6},{8,9},{9,8},{10,11... | collective-permute-start | bytes 196616 | tf_op jit(solution)/shard_map/ppermute | solution.py:20
  15.3 7.5 %collective-permute-start.9 = (bf16[4,2,32,256]{3,2,1,0:T(8,128)(2,1)S(1)}, bf16[4,2,32,256]{3,2,1,0:T(8,128)(2,1)S(1)}, u32[]{:S(2)}, u32[]{:S(2)}) collective-permute-start(bf16[4,2,32,256]{3,2,1,0:T(8,128)(2,1)S(1)} %pad_maximum_fusion.stack), channel_id=1, source_target_pairs={{0,6},{1,7},{2,4},{3,5},{4,2},{5,3},{6,0},{7,1},{8,14},{9,15},{10,... | collective-permute-start | bytes 393224 | tf_op jit(solution)/shard_map/ppermute | solution.py:20
  17.8 5.7 %collective-permute-start.8 = (bf16[4,2,32,256]{3,2,1,0:T(8,128)(2,1)S(1)}, bf16[4,2,32,256]{3,2,1,0:T(8,128)(2,1)S(1)}, u32[]{:S(2)}, u32[]{:S(2)}) collective-permute-start(bf16[4,2,32,256]{3,2,1,0:T(8,128)(2,1)S(1)} %pad_maximum_fusion.stack), channel_id=1, source_target_pairs={{0,2},{1,3},{2,0},{3,1},{4,6},{5,7},{6,4},{7,5},{8,10},{9,11},{10,... | collective-permute-start | bytes 393224 | tf_op jit(solution)/shard_map/ppermute | solution.py:20
  18.3 5.9 %collective-permute-start.7 = (bf16[4,2,32,256]{3,2,1,0:T(8,128)(2,1)S(1)}, bf16[4,2,32,256]{3,2,1,0:T(8,128)(2,1)S(1)}, u32[]{:S(2)}, u32[]{:S(2)}) collective-permute-start(bf16[4,2,32,256]{3,2,1,0:T(8,128)(2,1)S(1)} %pad_maximum_fusion.stack), channel_id=1, source_target_pairs={{0,4},{1,5},{2,6},{3,7},{4,0},{5,1},{6,2},{7,3},{8,12},{9,13},{10,... | collective-permute-start | bytes 393224 | tf_op jit(solution)/shard_map/ppermute | solution.py:20
  18.9 0.7 copy-start
  23.5 6.6 %copy-start.1 = (s32[3,1,16]{2,1,0:T(1,128)S(1)}, s32[3,1,16]{2,1,0:T(1,128)}, u32[]{:S(2)}) copy-start(s32[3,1,16]{2,1,0:T(1,128)} %own_pattern.5) | copy-start | bytes 580
  25.7 6.9 %collective-permute-start.11 = (bf16[2,32,256]{2,1,0:T(8,128)(2,1)S(1)}, bf16[2,32,256]{2,1,0:T(8,128)(2,1)S(1)}, u32[]{:S(2)}, u32[]{:S(2)}) collective-permute-start(bf16[2,32,256]{2,1,0:T(8,128)(2,1)S(1)} %shard_map.64.after.refs_1_.known), channel_id=1, source_target_pairs={{0,8},{1,9},{2,10},{3,11},{4,12},{5,13},{6,14},{7,15},{8,0},{9,1},... | collective-permute-start | bytes 98312 | tf_op jit(solution)/shard_map/ppermute | solution.py:20
  26.1 6.6 %collective-permute-start.12 = (bf16[2,32,256]{2,1,0:T(8,128)(2,1)S(1)}, bf16[2,32,256]{2,1,0:T(8,128)(2,1)S(1)}, u32[]{:S(2)}, u32[]{:S(2)}) collective-permute-start(bf16[2,32,256]{2,1,0:T(8,128)(2,1)S(1)} %shard_map.64.after.refs_1_.known), channel_id=1, source_target_pairs={{0,16},{1,17},{2,18},{3,19},{4,20},{5,21},{6,22},{7,23},{8,24},{9,... | collective-permute-start | bytes 98312 | tf_op jit(solution)/shard_map/ppermute | solution.py:20
  28.6 5.7 %collective-permute-start.13 = (bf16[2,32,256]{2,1,0:T(8,128)(2,1)S(1)}, bf16[2,32,256]{2,1,0:T(8,128)(2,1)S(1)}, u32[]{:S(2)}, u32[]{:S(2)}) collective-permute-start(bf16[2,32,256]{2,1,0:T(8,128)(2,1)S(1)} %shard_map.64.after.refs_1_.known), channel_id=1, source_target_pairs={{0,24},{1,25},{2,26},{3,27},{4,28},{5,29},{6,30},{7,31},{8,16},{9,... | collective-permute-start | bytes 98312 | tf_op jit(solution)/shard_map/ppermute | solution.py:20
  34.4 6.2 %collective-permute-start.16 = (bf16[4,2,32,256]{3,2,1,0:T(8,128)(2,1)S(1)}, bf16[4,2,32,256]{3,2,1,0:T(8,128)(2,1)S(1)}, u32[]{:S(2)}, u32[]{:S(2)}) collective-permute-start(bf16[4,2,32,256]{3,2,1,0:T(8,128)(2,1)S(1)} %pad_maximum_fusion.1.stack), channel_id=1, source_target_pairs={{0,6},{1,7},{2,4},{3,5},{4,2},{5,3},{6,0},{7,1},{8,14},{9,15},{10,... | collective-permute-start | bytes 393224 | tf_op jit(solution)/shard_map/ppermute | solution.py:20
  35.9 5.4 %collective-permute-start.15 = (bf16[4,2,32,256]{3,2,1,0:T(8,128)(2,1)S(1)}, bf16[4,2,32,256]{3,2,1,0:T(8,128)(2,1)S(1)}, u32[]{:S(2)}, u32[]{:S(2)}) collective-permute-start(bf16[4,2,32,256]{3,2,1,0:T(8,128)(2,1)S(1)} %pad_maximum_fusion.1.stack), channel_id=1, source_target_pairs={{0,2},{1,3},{2,0},{3,1},{4,6},{5,7},{6,4},{7,5},{8,10},{9,11},{10,... | collective-permute-start | bytes 393224 | tf_op jit(solution)/shard_map/ppermute | solution.py:20
  36.4 5.6 %collective-permute-start.14 = (bf16[4,2,32,256]{3,2,1,0:T(8,128)(2,1)S(1)}, bf16[4,2,32,256]{3,2,1,0:T(8,128)(2,1)S(1)}, u32[]{:S(2)}, u32[]{:S(2)}) collective-permute-start(bf16[4,2,32,256]{3,2,1,0:T(8,128)(2,1)S(1)} %pad_maximum_fusion.1.stack), channel_id=1, source_target_pairs={{0,4},{1,5},{2,6},{3,7},{4,0},{5,1},{6,2},{7,3},{8,12},{9,13},{10,... | collective-permute-start | bytes 393224 | tf_op jit(solution)/shard_map/ppermute | solution.py:20
  43.4 6.9 %collective-permute-start.17 = (bf16[2,32,256]{2,1,0:T(8,128)(2,1)S(1)}, bf16[2,32,256]{2,1,0:T(8,128)(2,1)S(1)}, u32[]{:S(2)}, u32[]{:S(2)}) collective-permute-start(bf16[2,32,256]{2,1,0:T(8,128)(2,1)S(1)} %shard_map.69.after.refs_2_.known), channel_id=1, source_target_pairs={{0,8},{1,9},{2,10},{3,11},{4,12},{5,13},{6,14},{7,15},{8,0},{9,1},... | collective-permute-start | bytes 98312 | tf_op jit(solution)/shard_map/ppermute | solution.py:20
  43.4 6.9 %collective-permute-start.18 = (bf16[2,32,256]{2,1,0:T(8,128)(2,1)S(1)}, bf16[2,32,256]{2,1,0:T(8,128)(2,1)S(1)}, u32[]{:S(2)}, u32[]{:S(2)}) collective-permute-start(bf16[2,32,256]{2,1,0:T(8,128)(2,1)S(1)} %shard_map.69.after.refs_2_.known), channel_id=1, source_target_pairs={{0,16},{1,17},{2,18},{3,19},{4,20},{5,21},{6,22},{7,23},{8,24},{9,... | collective-permute-start | bytes 98312 | tf_op jit(solution)/shard_map/ppermute | solution.py:20
  46.1 5.7 %collective-permute-start.19 = (bf16[2,32,256]{2,1,0:T(8,128)(2,1)S(1)}, bf16[2,32,256]{2,1,0:T(8,128)(2,1)S(1)}, u32[]{:S(2)}, u32[]{:S(2)}) collective-permute-start(bf16[2,32,256]{2,1,0:T(8,128)(2,1)S(1)} %shard_map.69.after.refs_2_.known), channel_id=1, source_target_pairs={{0,24},{1,25},{2,26},{3,27},{4,28},{5,29},{6,30},{7,31},{8,16},{9,... | collective-permute-start | bytes 98312 | tf_op jit(solution)/shard_map/ppermute | solution.py:20
  51.8 5.9 %collective-permute-start.22 = (bf16[4,2,32,256]{3,2,1,0:T(8,128)(2,1)S(1)}, bf16[4,2,32,256]{3,2,1,0:T(8,128)(2,1)S(1)}, u32[]{:S(2)}, u32[]{:S(2)}) collective-permute-start(bf16[4,2,32,256]{3,2,1,0:T(8,128)(2,1)S(1)} %pad_maximum_fusion.2.stack), channel_id=1, source_target_pairs={{0,6},{1,7},{2,4},{3,5},{4,2},{5,3},{6,0},{7,1},{8,14},{9,15},{10,... | collective-permute-start | bytes 393224 | tf_op jit(solution)/shard_map/ppermute | solution.py:20
  53.5 5.0 %collective-permute-start.21 = (bf16[4,2,32,256]{3,2,1,0:T(8,128)(2,1)S(1)}, bf16[4,2,32,256]{3,2,1,0:T(8,128)(2,1)S(1)}, u32[]{:S(2)}, u32[]{:S(2)}) collective-permute-start(bf16[4,2,32,256]{3,2,1,0:T(8,128)(2,1)S(1)} %pad_maximum_fusion.2.stack), channel_id=1, source_target_pairs={{0,2},{1,3},{2,0},{3,1},{4,6},{5,7},{6,4},{7,5},{8,10},{9,11},{10,... | collective-permute-start | bytes 393224 | tf_op jit(solution)/shard_map/ppermute | solution.py:20
  54.1 5.1 %collective-permute-start.20 = (bf16[4,2,32,256]{3,2,1,0:T(8,128)(2,1)S(1)}, bf16[4,2,32,256]{3,2,1,0:T(8,128)(2,1)S(1)}, u32[]{:S(2)}, u32[]{:S(2)}) collective-permute-start(bf16[4,2,32,256]{3,2,1,0:T(8,128)(2,1)S(1)} %pad_maximum_fusion.2.stack), channel_id=1, source_target_pairs={{0,4},{1,5},{2,6},{3,7},{4,0},{5,1},{6,2},{7,3},{8,12},{9,13},{10,... | collective-permute-start | bytes 393224 | tf_op jit(solution)/shard_map/ppermute | solution.py:20
  61.9 5.9 %collective-permute-start.24 = (bf16[4,2,32,256]{3,2,1,0:T(8,128)(2,1)S(1)}, bf16[4,2,32,256]{3,2,1,0:T(8,128)(2,1)S(1)}, u32[]{:S(2)}, u32[]{:S(2)}) collective-permute-start(bf16[4,2,32,256]{3,2,1,0:T(8,128)(2,1)S(1)} %get-tuple-element.85), channel_id=1, source_target_pairs={{0,6},{1,7},{2,4},{3,5},{4,2},{5,3},{6,0},{7,1},{8,14},{9,15},{10,... | collective-permute-start | bytes 393224 | tf_op jit(solution)/shard_map/ppermute | solution.py:20
  64.0 5.0 %collective-permute-start.25 = (bf16[4,2,32,256]{3,2,1,0:T(8,128)(2,1)S(1)}, bf16[4,2,32,256]{3,2,1,0:T(8,128)(2,1)S(1)}, u32[]{:S(2)}, u32[]{:S(2)}) collective-permute-start(bf16[4,2,32,256]{3,2,1,0:T(8,128)(2,1)S(1)} %get-tuple-element.86), channel_id=1, source_target_pairs={{0,2},{1,3},{2,0},{3,1},{4,6},{5,7},{6,4},{7,5},{8,10},{9,11},{10,... | collective-permute-start | bytes 393224 | tf_op jit(solution)/shard_map/ppermute | solution.py:20
  64.6 5.0 %collective-permute-start.26 = (bf16[4,2,32,256]{3,2,1,0:T(8,128)(2,1)S(1)}, bf16[4,2,32,256]{3,2,1,0:T(8,128)(2,1)S(1)}, u32[]{:S(2)}, u32[]{:S(2)}) collective-permute-start(bf16[4,2,32,256]{3,2,1,0:T(8,128)(2,1)S(1)} %get-tuple-element.87), channel_id=1, source_target_pairs={{0,4},{1,5},{2,6},{3,7},{4,0},{5,1},{6,2},{7,3},{8,12},{9,13},{10,... | collective-permute-start | bytes 393224 | tf_op jit(solution)/shard_map/ppermute | solution.py:20
  69.7 4.5 %collective-permute-start.27 = (bf16[2,32,256]{2,1,0:T(8,128)(2,1)S(1)}, bf16[2,32,256]{2,1,0:T(8,128)(2,1)S(1)}, u32[]{:S(2)}, u32[]{:S(2)}) collective-permute-start(bf16[2,32,256]{2,1,0:T(8,128)(2,1)S(1)} %get-tuple-element.89), channel_id=1, source_target_pairs={{0,8},{1,9},{2,10},{3,11},{4,12},{5,13},{6,14},{7,15},{8,0},{9,1},... | collective-permute-start | bytes 98312 | tf_op jit(solution)/shard_map/ppermute | solution.py:20
  69.7 4.9 %collective-permute-start.28 = (bf16[2,32,256]{2,1,0:T(8,128)(2,1)S(1)}, bf16[2,32,256]{2,1,0:T(8,128)(2,1)S(1)}, u32[]{:S(2)}, u32[]{:S(2)}) collective-permute-start(bf16[2,32,256]{2,1,0:T(8,128)(2,1)S(1)} %get-tuple-element.90), channel_id=1, source_target_pairs={{0,16},{1,17},{2,18},{3,19},{4,20},{5,21},{6,22},{7,23},{8,24},{9,... | collective-permute-start | bytes 98312 | tf_op jit(solution)/shard_map/ppermute | solution.py:20
  72.2 5.7 %collective-permute-start.29 = (bf16[2,32,256]{2,1,0:T(8,128)(2,1)S(1)}, bf16[2,32,256]{2,1,0:T(8,128)(2,1)S(1)}, u32[]{:S(2)}, u32[]{:S(2)}) collective-permute-start(bf16[2,32,256]{2,1,0:T(8,128)(2,1)S(1)} %get-tuple-element.91), channel_id=1, source_target_pairs={{0,24},{1,25},{2,26},{3,27},{4,28},{5,29},{6,30},{7,31},{8,16},{9,... | collective-permute-start | bytes 98312 | tf_op jit(solution)/shard_map/ppermute | solution.py:20
  79.2 5.9 %collective-permute-start.30 = (bf16[4,2,32,256]{3,2,1,0:T(8,128)(2,1)S(1)}, bf16[4,2,32,256]{3,2,1,0:T(8,128)(2,1)S(1)}, u32[]{:S(2)}, u32[]{:S(2)}) collective-permute-start(bf16[4,2,32,256]{3,2,1,0:T(8,128)(2,1)S(1)} %get-tuple-element.93), channel_id=1, source_target_pairs={{0,6},{1,7},{2,4},{3,5},{4,2},{5,3},{6,0},{7,1},{8,14},{9,15},{10,... | collective-permute-start | bytes 393224 | tf_op jit(solution)/shard_map/ppermute | solution.py:20
  81.2 5.0 %collective-permute-start.31 = (bf16[4,2,32,256]{3,2,1,0:T(8,128)(2,1)S(1)}, bf16[4,2,32,256]{3,2,1,0:T(8,128)(2,1)S(1)}, u32[]{:S(2)}, u32[]{:S(2)}) collective-permute-start(bf16[4,2,32,256]{3,2,1,0:T(8,128)(2,1)S(1)} %get-tuple-element.94), channel_id=1, source_target_pairs={{0,2},{1,3},{2,0},{3,1},{4,6},{5,7},{6,4},{7,5},{8,10},{9,11},{10,... | collective-permute-start | bytes 393224 | tf_op jit(solution)/shard_map/ppermute | solution.py:20
  81.9 5.0 %collective-permute-start.32 = (bf16[4,2,32,256]{3,2,1,0:T(8,128)(2,1)S(1)}, bf16[4,2,32,256]{3,2,1,0:T(8,128)(2,1)S(1)}, u32[]{:S(2)}, u32[]{:S(2)}) collective-permute-start(bf16[4,2,32,256]{3,2,1,0:T(8,128)(2,1)S(1)} %get-tuple-element.95), channel_id=1, source_target_pairs={{0,4},{1,5},{2,6},{3,7},{4,0},{5,1},{6,2},{7,3},{8,12},{9,13},{10,... | collective-permute-start | bytes 393224 | tf_op jit(solution)/shard_map/ppermute | solution.py:20
  86.9 4.5 %collective-permute-start.33 = (bf16[2,32,256]{2,1,0:T(8,128)(2,1)S(1)}, bf16[2,32,256]{2,1,0:T(8,128)(2,1)S(1)}, u32[]{:S(2)}, u32[]{:S(2)}) collective-permute-start(bf16[2,32,256]{2,1,0:T(8,128)(2,1)S(1)} %get-tuple-element.97), channel_id=1, source_target_pairs={{0,8},{1,9},{2,10},{3,11},{4,12},{5,13},{6,14},{7,15},{8,0},{9,1},... | collective-permute-start | bytes 98312 | tf_op jit(solution)/shard_map/ppermute | solution.py:20
  87.0 4.9 %collective-permute-start.34 = (bf16[2,32,256]{2,1,0:T(8,128)(2,1)S(1)}, bf16[2,32,256]{2,1,0:T(8,128)(2,1)S(1)}, u32[]{:S(2)}, u32[]{:S(2)}) collective-permute-start(bf16[2,32,256]{2,1,0:T(8,128)(2,1)S(1)} %get-tuple-element.98), channel_id=1, source_target_pairs={{0,16},{1,17},{2,18},{3,19},{4,20},{5,21},{6,22},{7,23},{8,24},{9,... | collective-permute-start | bytes 98312 | tf_op jit(solution)/shard_map/ppermute | solution.py:20
  89.1 5.7 %collective-permute-start.35 = (bf16[2,32,256]{2,1,0:T(8,128)(2,1)S(1)}, bf16[2,32,256]{2,1,0:T(8,128)(2,1)S(1)}, u32[]{:S(2)}, u32[]{:S(2)}) collective-permute-start(bf16[2,32,256]{2,1,0:T(8,128)(2,1)S(1)} %get-tuple-element.99), channel_id=1, source_target_pairs={{0,24},{1,25},{2,26},{3,27},{4,28},{5,29},{6,30},{7,31},{8,16},{9,... | collective-permute-start | bytes 98312 | tf_op jit(solution)/shard_map/ppermute | solution.py:20
  96.2 5.9 %collective-permute-start.36 = (bf16[4,2,32,256]{3,2,1,0:T(8,128)(2,1)S(1)}, bf16[4,2,32,256]{3,2,1,0:T(8,128)(2,1)S(1)}, u32[]{:S(2)}, u32[]{:S(2)}) collective-permute-start(bf16[4,2,32,256]{3,2,1,0:T(8,128)(2,1)S(1)} %get-tuple-element.101), channel_id=1, source_target_pairs={{0,6},{1,7},{2,4},{3,5},{4,2},{5,3},{6,0},{7,1},{8,14},{9,15},{10,... | collective-permute-start | bytes 393224 | tf_op jit(solution)/shard_map/ppermute | solution.py:20
  98.2 5.0 %collective-permute-start.37 = (bf16[4,2,32,256]{3,2,1,0:T(8,128)(2,1)S(1)}, bf16[4,2,32,256]{3,2,1,0:T(8,128)(2,1)S(1)}, u32[]{:S(2)}, u32[]{:S(2)}) collective-permute-start(bf16[4,2,32,256]{3,2,1,0:T(8,128)(2,1)S(1)} %get-tuple-element.102), channel_id=1, source_target_pairs={{0,2},{1,3},{2,0},{3,1},{4,6},{5,7},{6,4},{7,5},{8,10},{9,11},{10,... | collective-permute-start | bytes 393224 | tf_op jit(solution)/shard_map/ppermute | solution.py:20
  98.8 5.0 %collective-permute-start.38 = (bf16[4,2,32,256]{3,2,1,0:T(8,128)(2,1)S(1)}, bf16[4,2,32,256]{3,2,1,0:T(8,128)(2,1)S(1)}, u32[]{:S(2)}, u32[]{:S(2)}) collective-permute-start(bf16[4,2,32,256]{3,2,1,0:T(8,128)(2,1)S(1)} %get-tuple-element.103), channel_id=1, source_target_pairs={{0,4},{1,5},{2,6},{3,7},{4,0},{5,1},{6,2},{7,3},{8,12},{9,13},{10,... | collective-permute-start | bytes 393224 | tf_op jit(solution)/shard_map/ppermute | solution.py:20
  99.7 12.6 %collective-permute-start.23 = (bf16[4,32,256]{2,1,0:T(8,128)(2,1)S(1)}, bf16[4,32,256]{2,1,0:T(8,128)(2,1)S(1)}, u32[]{:S(2)}, u32[]{:S(2)}) collective-permute-start(bf16[4,32,256]{2,1,0:T(8,128)(2,1)S(1)} %get-tuple-element.83), channel_id=1, source_target_pairs={{0,1},{1,0},{2,3},{3,2},{4,5},{5,4},{6,7},{7,6},{8,9},{9,8},{10,11... | collective-permute-start | bytes 196616 | tf_op jit(solution)/shard_map/ppermute | solution.py:20
  103.9 4.5 %collective-permute-start.39 = (bf16[2,32,256]{2,1,0:T(8,128)(2,1)S(1)}, bf16[2,32,256]{2,1,0:T(8,128)(2,1)S(1)}, u32[]{:S(2)}, u32[]{:S(2)}) collective-permute-start(bf16[2,32,256]{2,1,0:T(8,128)(2,1)S(1)} %get-tuple-element.105), channel_id=1, source_target_pairs={{0,8},{1,9},{2,10},{3,11},{4,12},{5,13},{6,14},{7,15},{8,0},{9,1},... | collective-permute-start | bytes 98312 | tf_op jit(solution)/shard_map/ppermute | solution.py:20
  104.0 4.9 %collective-permute-start.40 = (bf16[2,32,256]{2,1,0:T(8,128)(2,1)S(1)}, bf16[2,32,256]{2,1,0:T(8,128)(2,1)S(1)}, u32[]{:S(2)}, u32[]{:S(2)}) collective-permute-start(bf16[2,32,256]{2,1,0:T(8,128)(2,1)S(1)} %get-tuple-element.106), channel_id=1, source_target_pairs={{0,16},{1,17},{2,18},{3,19},{4,20},{5,21},{6,22},{7,23},{8,24},{9,... | collective-permute-start | bytes 98312 | tf_op jit(solution)/shard_map/ppermute | solution.py:20
  106.4 5.7 %collective-permute-start.41 = (bf16[2,32,256]{2,1,0:T(8,128)(2,1)S(1)}, bf16[2,32,256]{2,1,0:T(8,128)(2,1)S(1)}, u32[]{:S(2)}, u32[]{:S(2)}) collective-permute-start(bf16[2,32,256]{2,1,0:T(8,128)(2,1)S(1)} %get-tuple-element.107), channel_id=1, source_target_pairs={{0,24},{1,25},{2,26},{3,27},{4,28},{5,29},{6,30},{7,31},{8,16},{9,... | collective-permute-start | bytes 98312 | tf_op jit(solution)/shard_map/ppermute | solution.py:20
  108.3 4.6 %collective-permute-start.43 = (bf16[3,32,256]{2,1,0:T(8,128)(2,1)S(1)}, bf16[3,32,256]{2,1,0:T(8,128)(2,1)S(1)}, u32[]{:S(2)}, u32[]{:S(2)}) collective-permute-start(bf16[3,32,256]{2,1,0:T(8,128)(2,1)S(1)} %get-tuple-element.111), channel_id=1, source_target_pairs={{0,1},{1,0},{2,3},{3,2},{4,5},{5,4},{6,7},{7,6},{8,9},{9,8},{10,11... | collective-permute-start | bytes 147464 | tf_op jit(solution)/shard_map/ppermute | solution.py:20
  112.2 1.2 %collective-permute-start.42 = (bf16[32,256]{1,0:T(8,128)(2,1)S(1)}, bf16[32,256]{1,0:T(8,128)(2,1)S(1)}, u32[]{:S(2)}, u32[]{:S(2)}) collective-permute-start(bf16[32,256]{1,0:T(8,128)(2,1)S(1)} %get-tuple-element.109), channel_id=1, source_target_pairs={{0,1},{1,0},{2,3},{3,2},{4,5},{5,4},{6,7},{7,6},{8,9},{9,8},{10,11... | collective-permute-start | bytes 49160 | tf_op jit(solution)/shard_map/ppermute | solution.py:20

commit v3 on v2

--- a/solution.py
+++ b/solution.py
@@ -13,6 +13,9 @@
 HBM_SPEC = pl.BlockSpec(memory_space=pltpu.HBM)
 VMEM_GRANT = 8 * 1024 * 1024
 PLANE = (6, 2, 4)
+
+
+FIRST = 3
 
 
 def swap(value, mask):
@@ -53,21 +56,25 @@
     )
 
 
-def first_kernel(rhs, diag, rhs_mine, rhs_sent, mine, sent, rhs_held, diag_held, arrived):
+def first_kernel(rhs, diag, mine, sent, rhs_held, diag_held, arrived):
     here, there = halves(rhs.shape[2])
     loads = [
-        pltpu.make_async_copy(rhs, rhs_held, arrived.at[0]),
+        pltpu.make_async_copy(rhs.at[0, 0], rhs_held, arrived.at[0]),
         pltpu.make_async_copy(diag.at[0, 0], diag_held, arrived.at[1]),
     ]
     for load in loads:
         load.start()
     for load in loads:
         load.wait()
-    sent[...] = times_transposed(rhs_held[0, 0, there], diag_held[...]).astype(sent.dtype)
-    mine[...] = times_transposed(rhs_held[0, 0, here], diag_held[...]).astype(mine.dtype)
+    sent[...] = times_transposed(rhs_held[there], diag_held[...]).astype(sent.dtype)
+    mine[...] = times_transposed(rhs_held[here], diag_held[...]).astype(mine.dtype)
+
+
+def halve_kernel(after, rhs, rhs_mine, rhs_sent):
+    here, there = halves(rhs.shape[2])
     for l in range(rhs.shape[0]):
-        rhs_mine[l] = rhs_held[l, 0, here]
-        rhs_sent[l] = rhs_held[l, 0, there]
+        rhs_mine[l] = rhs[l, 0, here]
+        rhs_sent[l] = rhs[l, 0, there]
 
 
 def place_kernel(
@@ -99,13 +106,9 @@
             spread[i, part * (2 * deep) + (away >> 3) * 2 + side(away)] = held[i, k]
 
 
-def own_kernel(spread, stack, out):
-    for i in range(2):
-        out[i] = meet(stack, spread, i, 0, None)
-
-
-def meet(part, spread, i, j, total):
+def meet(part, spread, i, j):
     deep = part.shape[0]
+    total = None
     for z in range(deep):
         for s in range(2):
             term = times_transposed(part[z, s], spread[i, j * 2 * deep + 2 * z + s])
@@ -113,18 +116,23 @@
     return total
 
 
-def more_kernel(j, spread, part, partial, out):
+def more_kernel(j, spread, part, *refs):
+    terms = [meet(part, spread, i, j) for i in range(2)]
     for i in range(2):
-        out[i] = meet(part, spread, i, j, partial[i])
-
-
-def finish(spread, c, partial, rhs, diag):
-    solved = []
+        refs[-1][i] = refs[0][i] + terms[i] if len(refs) > 1 else terms[i]
+
+
+def finish(spread, late, partial, rhs, diag):
+    terms = [None, None]
+    for j, part in late:
+        for i in range(2):
+            term = meet(part, spread, i, j)
+            terms[i] = term if terms[i] is None else terms[i] + term
+    residuals = []
     for i in range(2):
-        coupled = meet(c, spread, i, 3, partial[i])
-        residual = (rhs[i].astype(jnp.float32) - coupled).astype(jnp.bfloat16)
-        solved.append(times_transposed(residual, diag[i]).astype(jnp.bfloat16))
-    return solved
+        coupled = terms[i] if partial is None else partial[i] + terms[i]
+        residuals.append((rhs[i].astype(jnp.float32) - coupled).astype(jnp.bfloat16))
+    return [times_transposed(residuals[i], diag[i]).astype(jnp.bfloat16) for i in range(2)]
 
 
 def push(solved, spread, j, out):
@@ -136,12 +144,14 @@
             out[z, s] = total.astype(out.dtype)
 
 
-def forward_kernel(level, spread, c, partial, r0, r1, diag, out):
-    out[0], out[1] = finish(spread, c, partial, (r0[level], r1[level]), diag)
-
-
-def turn_kernel(level, spread, c, partial, r0, r1, diag, out, back, o1, o2, o3):
-    solved = finish(spread, c, partial, (r0[level], r1[level]), diag)
+def forward_kernel(level, first, spread, r0, r1, diag, *refs):
+    late, partial, out = list(enumerate(refs[: 4 - first], first)), refs[4 - first] if first else None, refs[-1]
+    out[0], out[1] = finish(spread, late, partial, (r0[level], r1[level]), diag)
+
+
+def turn_kernel(level, first, spread, r0, r1, diag, *refs):
+    late, partial, (out, back, o1, o2, o3) = list(enumerate(refs[: 4 - first], first)), refs[4 - first], refs[-5:]
+    solved = finish(spread, late, partial, (r0[level], r1[level]), diag)
     out[0], out[1] = solved
     down = [times(solved[i], diag[i]).astype(jnp.bfloat16) for i in range(2)]
     back[0], back[1] = down
@@ -217,31 +227,33 @@
     def in_hbm(value):
         return pltpu.with_memory_space_constraint(value, pltpu.HBM)
 
-    rhs_own, rhs_sent, mine, sent = call(
+    own_tiles, diag_own = in_hbm(off_tiles), in_hbm(diag_inv)
+    mine, sent = call(
         first_kernel,
-        [shape(levels)] * 2 + [shape()] * 2,
-        [in_hbm(rhs_block), in_hbm(diag_inv)],
+        [shape()] * 2,
+        [in_hbm(rhs_block), diag_own],
         [HBM_SPEC] * 2,
         scratch=[
-            pltpu.VMEM(rhs_block.shape, jnp.bfloat16),
+            pltpu.VMEM((width, size), jnp.bfloat16),
             pltpu.VMEM((size, size), jnp.bfloat16),
             pltpu.SemaphoreType.DMA((2,)),
         ],
     )
     other_pattern = swap(pattern, 1)
     other = swap(sent, 1)
+    rhs_own, rhs_sent = call(halve_kernel, [shape(levels)] * 2, [sent, rhs_block])
+    rhs_sent, diag_sent, tiles_sent, other, other_pattern = lax.optimization_barrier(
+        (rhs_sent, diag_inv, off_tiles, other, other_pattern)
+    )
     forward = [jnp.stack([mine, other])]
-    rhs_sent, diag_own, own_tiles, other, other_pattern = lax.optimization_barrier(
-        (rhs_sent, diag_inv, off_tiles, other, other_pattern)
-    )
-    other_tiles = swap(own_tiles, 1)
-    rhs_other, diag_other = swap(rhs_sent, 1), swap(diag_own, 1)
-    own_tiles, diag_own = in_hbm(off_tiles), in_hbm(diag_inv)
+    rhs_other, diag_other, other_tiles = swap(rhs_sent, 1), swap(diag_sent, 1), swap(tiles_sent, 1)
     work = 2 * 2 * devices // 4 * half * size * size
     diag = [None] * levels
 
-    def met(level, block):
-        arrived = [block] + [swap(block, m) for m in line]
+    def along(block):
+        return [block] + [swap(block, m) for m in line]
+
+    def placed(level, block):
         solve_levels = (1, 0) if level == 1 else (level,)
         spread, inverses = call(
             functools.partial(place_kernel, level, solve_levels),
@@ -249,7 +261,7 @@
                 pltpu.VMEM((2, devices, size, size), jnp.bfloat16),
                 pltpu.VMEM((len(solve_levels), 2, size, size), jnp.bfloat16),
             ],
-            [pattern, other_pattern, block, own_tiles, other_tiles, diag_own, diag_other],
+            [in_hbm(pattern), other_pattern, block, own_tiles, other_tiles, diag_own, diag_other],
             [SMEM_SPEC] * 2 + [VMEM_SPEC] + [HBM_SPEC, ANY_SPEC] * 2,
             scratch=[
                 pltpu.VMEM((2,) + off_tiles.shape[2:], jnp.bfloat16),
@@ -259,15 +271,16 @@
         )
         for n, l in enumerate(solve_levels):
             diag[l] = inverses[n]
-        if level > 1:
-            *arrived, spread = lax.optimization_barrier((*arrived, spread))
-        stack = jnp.stack(arrived)
-        parts = [swap(stack, m) for m in PLANE]
-        partial = call(own_kernel, shape(2, dtype=jnp.float32), [spread, stack], flops=work)
-        for j in (1, 2):
+        return spread
+
+    def met(level, arrived, spread, first):
+        parts = [jnp.stack(arrived)]
+        parts += [swap(parts[0], m) for m in PLANE]
+        partial = []
+        for j in range(first):
             kernel = functools.partial(more_kernel, j)
-            partial = call(kernel, shape(2, dtype=jnp.float32), [spread, parts[j - 1], partial], flops=work)
-        return spread, [spread, parts[2], partial, rhs_own, rhs_other, diag[level]]
+            partial = [call(kernel, shape(2, dtype=jnp.float32), [spread, parts[j]] + partial, flops=work)]
+        return [spread, rhs_own, rhs_other, diag[level]] + parts[first:] + partial
 
     def scattered(spread, back, outs):
         keep = call(keep_kernel, shape(deep, 2, dtype=jnp.float32), [spread, back], flops=work)
@@ -275,16 +288,20 @@
         summed = call(reduce_kernel, [shape(2, dtype=jnp.float32)] + [shape(2)] * (deep - 1), [keep] + arrived)
         return summed[0], [swap(part, m) for part, m in zip(summed[1:], line)]
 
-    spreads = []
+    arrived = along(forward[0])
+    spreads = [placed(1, forward[0])]
     for l in range(1, levels - 1):
-        spread, operands = met(l, forward[-1])
+        first = FIRST
+        operands = met(l, arrived, spreads[-1], first)
+        forward.append(call(functools.partial(forward_kernel, l, first), shape(2), operands, flops=work))
+        arrived = along(forward[l])
+        spread = placed(l + 1, forward[l])
+        *arrived, spread = lax.optimization_barrier((*arrived, spread))
         spreads.append(spread)
-        forward.append(call(functools.partial(forward_kernel, l), shape(2), operands, flops=work))
     l = levels - 1
-    spread, operands = met(l, forward[-1])
-    spreads.append(spread)
+    operands = met(l, arrived, spreads[-1], FIRST)
     top, back, *outs = call(
-        functools.partial(turn_kernel, l), [shape(2)] * 2 + [shape(deep, 2)] * 3, operands, flops=4 * work
+        functools.partial(turn_kernel, l, FIRST), [shape(2)] * 2 + [shape(deep, 2)] * 3, operands, flops=4 * work
     )
     forward.append(top)
     backward = [back]

time: 114 us -> 112 us (0.982)
  Pallas kernels: 26.2 us -> 24.7 us
  waiting for transfers between devices: 36.2 us -> 34.7 us
    ppermute x44, waiting for transfers between devices: 36.2 us -> 34.7 us  [swap(): return lax.ppermute(value, 'rows', [(i, i ^ mask) for i in range(size)])]
    pallas_call x29 -> x30, Pallas kernels: 26.2 us -> 24.7 us  [call(): pl.pallas_call(kernel, out_shape=out_shape, in_specs=[VMEM_SPEC] * len(op...]
  transfers between devices with their start and end apart: 44 -> 44, of which waited for: 24 -> 25; matrix products, arithmetic and copies ran while one was open for 0% -> 0% of each run, Pallas kernels for 14% -> 15%
where the time goes in v3:
time: 112 us
  starting transfers between devices  50.4 us (45%)
  waiting for transfers between devices  34.7 us (31%)
  Pallas kernels  24.7 us (22%)
    ppermute x44, starting transfers between devices, swap(): return lax.ppermute(value, 'rows', [(i, i ^ mask) for i in range(size)])  50.4 us
    ppermute x44, waiting for transfers between devices, swap(): return lax.ppermute(value, 'rows', [(i, i ^ mask) for i in range(size)])  34.7 us
    pallas_call x30, Pallas kernels, call(): pl.pallas_call(kernel, out_shape=out_shape, in_specs=[VMEM_SPEC] * len(op...  24.7 us
  transfers between devices with their start and end apart: 44, of which 25 were waited for; matrix products, arithmetic and copies ran while one was open for 0% of the time, Pallas kernels for 15%

profile of v3, /device:TPU:0, one launch (start us, length us, event | category | flops | bytes accessed | tf_op | source)
XLA Modules:
  0.0 111.7 jit_solution(6963941279526245985)
XLA Ops:
  0.6 1.1 %shard_map.59 = (bf16[32,256]{1,0:T(8,128)(2,1)S(1)}, bf16[32,256]{1,0:T(8,128)(2,1)S(1)}) custom-call(bf16[4,1,64,256]{3,2,1,0:T(8,128)(2,1)} %rhs.3, bf16[4,1,256,256]{3,2,1,0:T(8,128)(2,1)} %diag0.5), custom_call_target="tpu_custom_call" | custom-call | tf_op jit(solution)/shard_map/pallas_call | solution.py:35
  2.4 0.9 copy-done
  4.2 2.8 %collective-permute-start.5 = (bf16[2,32,256]{2,1,0:T(8,128)(2,1)S(1)}, bf16[2,32,256]{2,1,0:T(8,128)(2,1)S(1)}, u32[]{:S(2)}, u32[]{:S(2)}) collective-permute-start(bf16[2,32,256]{2,1,0:T(8,128)(2,1)S(1)} %get-tuple-element.117.after.refs_0_.known), channel_id=1, source_target_pairs={{0,8},{1,9},{2,10},{3,11},{4,12},{5,13},{6,14},{7,15},{8,0},{9,1},... | collective-permute-start | bytes 98312 | tf_op jit(solution)/shard_map/ppermute | solution.py:23
  6.9 2.6 %collective-permute-start.6 = (bf16[2,32,256]{2,1,0:T(8,128)(2,1)S(1)}, bf16[2,32,256]{2,1,0:T(8,128)(2,1)S(1)}, u32[]{:S(2)}, u32[]{:S(2)}) collective-permute-start(bf16[2,32,256]{2,1,0:T(8,128)(2,1)S(1)} %get-tuple-element.117.after.refs_0_.known), channel_id=1, source_target_pairs={{0,16},{1,17},{2,18},{3,19},{4,20},{5,21},{6,22},{7,23},{8,24},{9,... | collective-permute-start | bytes 98312 | tf_op jit(solution)/shard_map/ppermute | solution.py:23
  9.5 2.8 %collective-permute-done.6 = bf16[2,32,256]{2,1,0:T(8,128)(2,1)S(1)} collective-permute-done((bf16[2,32,256]{2,1,0:T(8,128)(2,1)S(1)}, bf16[2,32,256]{2,1,0:T(8,128)(2,1)S(1)}, u32[]{:S(2)}, u32[]{:S(2)}) %collective-permute-start.6) | collective-permute-done | bytes 32800 | tf_op jit(solution)/shard_map/ppermute | solution.py:23
  12.3 2.9 %collective-permute-done.7 = bf16[2,32,256]{2,1,0:T(8,128)(2,1)S(1)} collective-permute-done((bf16[2,32,256]{2,1,0:T(8,128)(2,1)S(1)}, bf16[2,32,256]{2,1,0:T(8,128)(2,1)S(1)}, u32[]{:S(2)}, u32[]{:S(2)}) %collective-permute-start.7) | collective-permute-done | bytes 32800 | tf_op jit(solution)/shard_map/ppermute | solution.py:23
  15.2 2.5 %collective-permute-start.10 = (bf16[4,2,32,256]{3,2,1,0:T(8,128)(2,1)S(1)}, bf16[4,2,32,256]{3,2,1,0:T(8,128)(2,1)S(1)}, u32[]{:S(2)}, u32[]{:S(2)}) collective-permute-start(bf16[4,2,32,256]{3,2,1,0:T(8,128)(2,1)S(1)} %pad_maximum_fusion.part), channel_id=1, source_target_pairs={{0,6},{1,7},{2,4},{3,5},{4,2},{5,3},{6,0},{7,1},{8,14},{9,15},{10,... | collective-permute-start | bytes 393224 | tf_op jit(solution)/shard_map/ppermute | solution.py:23
  18.8 2.6 %shard_map.61 = (bf16[2,32,256,256]{3,2,1,0:T(8,128)(2,1)S(1)}, bf16[2,2,256,256]{3,2,1,0:T(8,128)(2,1)S(1)}) custom-call(s32[3,1,16]{2,1,0:T(1,128)} %own_pattern.5, s32[3,1,16]{2,1,0:T(1,128)S(1)} %collective-permute-done.1.other_pattern, bf16[2,32,256]{2,1,0:T(8,128)(2,1)S(1)} %get-tuple-element.117.after.refs_0_.known, ...), custom_call_target="tpu_custom_call" | custom-call | flops 134217728 | tf_op jit(solution)/shard_map/pallas_call | solution.py:35
  21.5 0.7 shard_map.62.refs_0_
  22.2 0.7 shard_map.63.refs_0_
  23.1 0.7 shard_map.64.refs_1_
  23.9 0.8 shard_map.65.after.refs_1_.known
  24.8 2.6 %collective-permute-start.12 = (bf16[2,32,256]{2,1,0:T(8,128)(2,1)S(1)}, bf16[2,32,256]{2,1,0:T(8,128)(2,1)S(1)}, u32[]{:S(2)}, u32[]{:S(2)}) collective-permute-start(bf16[2,32,256]{2,1,0:T(8,128)(2,1)S(1)} %shard_map.65.after.refs_1_.known), channel_id=1, source_target_pairs={{0,16},{1,17},{2,18},{3,19},{4,20},{5,21},{6,22},{7,23},{8,24},{9,... | collective-permute-start | bytes 98312 | tf_op jit(solution)/shard_map/ppermute | solution.py:23
  27.4 1.7 %collective-permute-start.13 = (bf16[2,32,256]{2,1,0:T(8,128)(2,1)S(1)}, bf16[2,32,256]{2,1,0:T(8,128)(2,1)S(1)}, u32[]{:S(2)}, u32[]{:S(2)}) collective-permute-start(bf16[2,32,256]{2,1,0:T(8,128)(2,1)S(1)} %shard_map.65.after.refs_1_.known), channel_id=1, source_target_pairs={{0,24},{1,25},{2,26},{3,27},{4,28},{5,29},{6,30},{7,31},{8,16},{9,... | collective-permute-start | bytes 98312 | tf_op jit(solution)/shard_map/ppermute | solution.py:23
  29.1 2.6 %shard_map.66 = (bf16[2,32,256,256]{3,2,1,0:T(8,128)(2,1)S(1)}, bf16[1,2,256,256]{3,2,1,0:T(8,128)(2,1)S(1)}) custom-call(s32[3,1,16]{2,1,0:T(1,128)} %own_pattern.5, s32[3,1,16]{2,1,0:T(1,128)S(1)} %collective-permute-done.1.other_pattern, bf16[2,32,256]{2,1,0:T(8,128)(2,1)S(1)} %shard_map.65.after.refs_1_.known, bf16[3,1,16,256,256]{4,3,2,1,0:T(8,128)(2,1)} %tiles0.5, ...), custom_call_target="tpu_custom_call" | custom-call | flops 134217728 | tf_op jit(solution)/shard_map/pallas_call | solution.py:35
  31.8 1.4 %collective-permute-done.13 = bf16[2,32,256]{2,1,0:T(8,128)(2,1)S(1)} collective-permute-done((bf16[2,32,256]{2,1,0:T(8,128)(2,1)S(1)}, bf16[2,32,256]{2,1,0:T(8,128)(2,1)S(1)}, u32[]{:S(2)}, u32[]{:S(2)}) %collective-permute-start.13) | collective-permute-done | bytes 32800 | tf_op jit(solution)/shard_map/ppermute | solution.py:23
  33.2 1.9 %collective-permute-start.16 = (bf16[4,2,32,256]{3,2,1,0:T(8,128)(2,1)S(1)}, bf16[4,2,32,256]{3,2,1,0:T(8,128)(2,1)S(1)}, u32[]{:S(2)}, u32[]{:S(2)}) collective-permute-start(bf16[4,2,32,256]{3,2,1,0:T(8,128)(2,1)S(1)} %pad_maximum_fusion.1.part), channel_id=1, source_target_pairs={{0,6},{1,7},{2,4},{3,5},{4,2},{5,3},{6,0},{7,1},{8,14},{9,15},{10,... | collective-permute-start | bytes 393224 | tf_op jit(solution)/shard_map/ppermute | solution.py:23
  35.6 1.2 %collective-permute-start.14 = (bf16[4,2,32,256]{3,2,1,0:T(8,128)(2,1)S(1)}, bf16[4,2,32,256]{3,2,1,0:T(8,128)(2,1)S(1)}, u32[]{:S(2)}, u32[]{:S(2)}) collective-permute-start(bf16[4,2,32,256]{3,2,1,0:T(8,128)(2,1)S(1)} %pad_maximum_fusion.1.part), channel_id=1, source_target_pairs={{0,4},{1,5},{2,6},{3,7},{4,0},{5,1},{6,2},{7,3},{8,12},{9,13},{10,... | collective-permute-start | bytes 393224 | tf_op jit(solution)/shard_map/ppermute | solution.py:23
  36.7 0.7 shard_map.67.refs_0_
  37.4 1.9 %collective-permute-done.16.part = bf16[4,2,32,256]{3,2,1,0:T(8,128)(2,1)S(1)} collective-permute-done((bf16[4,2,32,256]{3,2,1,0:T(8,128)(2,1)S(1)}, bf16[4,2,32,256]{3,2,1,0:T(8,128)(2,1)S(1)}, u32[]{:S(2)}, u32[]{:S(2)}) %collective-permute-start.16) | collective-permute-done | bytes 131104 | tf_op jit(solution)/shard_map/ppermute | solution.py:23
  39.3 0.7 shard_map.68.refs_0_
  40.1 0.7 shard_map.69.refs_1_
  40.8 0.8 shard_map.70.after.refs_2_.known
  41.7 2.6 %collective-permute-start.18 = (bf16[2,32,256]{2,1,0:T(8,128)(2,1)S(1)}, bf16[2,32,256]{2,1,0:T(8,128)(2,1)S(1)}, u32[]{:S(2)}, u32[]{:S(2)}) collective-permute-start(bf16[2,32,256]{2,1,0:T(8,128)(2,1)S(1)} %shard_map.70.after.refs_2_.known), channel_id=1, source_target_pairs={{0,16},{1,17},{2,18},{3,19},{4,20},{5,21},{6,22},{7,23},{8,24},{9,... | collective-permute-start | bytes 98312 | tf_op jit(solution)/shard_map/ppermute | solution.py:23
  44.3 1.8 %collective-permute-start.19 = (bf16[2,32,256]{2,1,0:T(8,128)(2,1)S(1)}, bf16[2,32,256]{2,1,0:T(8,128)(2,1)S(1)}, u32[]{:S(2)}, u32[]{:S(2)}) collective-permute-start(bf16[2,32,256]{2,1,0:T(8,128)(2,1)S(1)} %shard_map.70.after.refs_2_.known), channel_id=1, source_target_pairs={{0,24},{1,25},{2,26},{3,27},{4,28},{5,29},{6,30},{7,31},{8,16},{9,... | collective-permute-start | bytes 98312 | tf_op jit(solution)/shard_map/ppermute | solution.py:23
  46.0 2.6 %shard_map.71 = (bf16[2,32,256,256]{3,2,1,0:T(8,128)(2,1)S(1)}, bf16[1,2,256,256]{3,2,1,0:T(8,128)(2,1)S(1)}) custom-call(s32[3,1,16]{2,1,0:T(1,128)} %own_pattern.5, s32[3,1,16]{2,1,0:T(1,128)S(1)} %collective-permute-done.1.other_pattern, bf16[2,32,256]{2,1,0:T(8,128)(2,1)S(1)} %shard_map.70.after.refs_2_.known, bf16[3,1,16,256,256]{4,3,2,1,0:T(8,128)(2,1)} %tiles0.5, ...), custom_call_target="tpu_custom_call" | custom-call | flops 134217728 | tf_op jit(solution)/shard_map/pallas_call | solution.py:35
  48.7 1.3 %collective-permute-done.19 = bf16[2,32,256]{2,1,0:T(8,128)(2,1)S(1)} collective-permute-done((bf16[2,32,256]{2,1,0:T(8,128)(2,1)S(1)}, bf16[2,32,256]{2,1,0:T(8,128)(2,1)S(1)}, u32[]{:S(2)}, u32[]{:S(2)}) %collective-permute-start.19) | collective-permute-done | bytes 32800 | tf_op jit(solution)/shard_map/ppermute | solution.py:23
  50.0 1.8 %collective-permute-start.22 = (bf16[4,2,32,256]{3,2,1,0:T(8,128)(2,1)S(1)}, bf16[4,2,32,256]{3,2,1,0:T(8,128)(2,1)S(1)}, u32[]{:S(2)}, u32[]{:S(2)}) collective-permute-start(bf16[4,2,32,256]{3,2,1,0:T(8,128)(2,1)S(1)} %pad_maximum_fusion.2.part), channel_id=1, source_target_pairs={{0,6},{1,7},{2,4},{3,5},{4,2},{5,3},{6,0},{7,1},{8,14},{9,15},{10,... | collective-permute-start | bytes 393224 | tf_op jit(solution)/shard_map/ppermute | solution.py:23
  52.3 1.3 %collective-permute-start.20 = (bf16[4,2,32,256]{3,2,1,0:T(8,128)(2,1)S(1)}, bf16[4,2,32,256]{3,2,1,0:T(8,128)(2,1)S(1)}, u32[]{:S(2)}, u32[]{:S(2)}) collective-permute-start(bf16[4,2,32,256]{3,2,1,0:T(8,128)(2,1)S(1)} %pad_maximum_fusion.2.part), channel_id=1, source_target_pairs={{0,4},{1,5},{2,6},{3,7},{4,0},{5,1},{6,2},{7,3},{8,12},{9,13},{10,... | collective-permute-start | bytes 393224 | tf_op jit(solution)/shard_map/ppermute | solution.py:23
  53.6 0.7 shard_map.72.refs_0_
  54.3 1.7 %collective-permute-done.22.part = bf16[4,2,32,256]{3,2,1,0:T(8,128)(2,1)S(1)} collective-permute-done((bf16[4,2,32,256]{3,2,1,0:T(8,128)(2,1)S(1)}, bf16[4,2,32,256]{3,2,1,0:T(8,128)(2,1)S(1)}, u32[]{:S(2)}, u32[]{:S(2)}) %collective-permute-start.22) | collective-permute-done | bytes 131104 | tf_op jit(solution)/shard_map/ppermute | solution.py:23
  55.9 0.7 shard_map.73.refs_0_
  56.7 0.7 shard_map.74.refs_1_
  57.5 2.1 %shard_map.75 = (bf16[2,32,256]{2,1,0:T(8,128)(2,1)S(1)}, bf16[2,32,256]{2,1,0:T(8,128)(2,1)S(1)}, bf16[4,2,32,256]{3,2,1,0:T(8,128)(2,1)S(1)}, bf16[4,2,32,256]...) custom-call(bf16[2,32,256,256]{3,2,1,0:T(8,128)(2,1)S(1)} %get-tuple-element.77.spread, ...), custom_call_target="tpu_custom_call" | custom-call | flops 268435456 | tf_op jit(solution)/shard_map/pallas_call | solution.py:35
  59.6 2.1 %collective-permute-start.24 = (bf16[4,2,32,256]{3,2,1,0:T(8,128)(2,1)S(1)}, bf16[4,2,32,256]{3,2,1,0:T(8,128)(2,1)S(1)}, u32[]{:S(2)}, u32[]{:S(2)}) collective-permute-start(bf16[4,2,32,256]{3,2,1,0:T(8,128)(2,1)S(1)} %get-tuple-element.87), channel_id=1, source_target_pairs={{0,6},{1,7},{2,4},{3,5},{4,2},{5,3},{6,0},{7,1},{8,14},{9,15},{10,... | collective-permute-start | bytes 393224 | tf_op jit(solution)/shard_map/ppermute | solution.py:23
  61.6 1.9 %collective-permute-start.25 = (bf16[4,2,32,256]{3,2,1,0:T(8,128)(2,1)S(1)}, bf16[4,2,32,256]{3,2,1,0:T(8,128)(2,1)S(1)}, u32[]{:S(2)}, u32[]{:S(2)}) collective-permute-start(bf16[4,2,32,256]{3,2,1,0:T(8,128)(2,1)S(1)} %get-tuple-element.88), channel_id=1, source_target_pairs={{0,2},{1,3},{2,0},{3,1},{4,6},{5,7},{6,4},{7,5},{8,10},{9,11},{10,... | collective-permute-start | bytes 393224 | tf_op jit(solution)/shard_map/ppermute | solution.py:23
  64.0 1.5 %collective-permute-done.24.a = bf16[4,2,32,256]{3,2,1,0:T(8,128)(2,1)S(1)} collective-permute-done((bf16[4,2,32,256]{3,2,1,0:T(8,128)(2,1)S(1)}, bf16[4,2,32,256]{3,2,1,0:T(8,128)(2,1)S(1)}, u32[]{:S(2)}, u32[]{:S(2)}) %collective-permute-start.24) | collective-permute-done | bytes 131104 | tf_op jit(solution)/shard_map/ppermute | solution.py:23
  65.5 2.4 %collective-permute-done.25.b = bf16[4,2,32,256]{3,2,1,0:T(8,128)(2,1)S(1)} collective-permute-done((bf16[4,2,32,256]{3,2,1,0:T(8,128)(2,1)S(1)}, bf16[4,2,32,256]{3,2,1,0:T(8,128)(2,1)S(1)}, u32[]{:S(2)}, u32[]{:S(2)}) %collective-permute-start.25) | collective-permute-done | bytes 131104 | tf_op jit(solution)/shard_map/ppermute | solution.py:23
  67.9 0.6 collective-permute-done.26.c
  68.6 1.1 %collective-permute-start.28 = (bf16[2,32,256]{2,1,0:T(8,128)(2,1)S(1)}, bf16[2,32,256]{2,1,0:T(8,128)(2,1)S(1)}, u32[]{:S(2)}, u32[]{:S(2)}) collective-permute-start(bf16[2,32,256]{2,1,0:T(8,128)(2,1)S(1)} %get-tuple-element.92), channel_id=1, source_target_pairs={{0,16},{1,17},{2,18},{3,19},{4,20},{5,21},{6,22},{7,23},{8,24},{9,... | collective-permute-start | bytes 98312 | tf_op jit(solution)/shard_map/ppermute | solution.py:23
  69.8 3.2 %collective-permute-start.29 = (bf16[2,32,256]{2,1,0:T(8,128)(2,1)S(1)}, bf16[2,32,256]{2,1,0:T(8,128)(2,1)S(1)}, u32[]{:S(2)}, u32[]{:S(2)}) collective-permute-start(bf16[2,32,256]{2,1,0:T(8,128)(2,1)S(1)} %get-tuple-element.93), channel_id=1, source_target_pairs={{0,24},{1,25},{2,26},{3,27},{4,28},{5,29},{6,30},{7,31},{8,16},{9,... | collective-permute-start | bytes 98312 | tf_op jit(solution)/shard_map/ppermute | solution.py:23
  73.5 2.0 %collective-permute-done.29.refs_2_ = bf16[2,32,256]{2,1,0:T(8,128)(2,1)S(1)} collective-permute-done((bf16[2,32,256]{2,1,0:T(8,128)(2,1)S(1)}, bf16[2,32,256]{2,1,0:T(8,128)(2,1)S(1)}, u32[]{:S(2)}, u32[]{:S(2)}) %collective-permute-start.29) | collective-permute-done | bytes 32800 | tf_op jit(solution)/shard_map/ppermute | solution.py:23
  75.5 1.3 %shard_map.80 = (bf16[2,32,256]{2,1,0:T(8,128)(2,1)S(1)}, bf16[4,2,32,256]{3,2,1,0:T(8,128)(2,1)S(1)}, bf16[4,2,32,256]{3,2,1,0:T(8,128)(2,1)S(1)}, bf16[4,2,32,256]{3,2,1,0:T(8,128)(2,1)S(1)}) custom-call(bf16[2,32,256,256]{3,2,1,0:T(8,128)(2,1)S(1)} %get-tuple-element.70.spread, f32[2,32,256]{2,1,0:T(8,128)S(1)} %get-tuple-element.90.own, ...), custom_call_target="tpu_custom_call" | custom-call | flops 201326592 | tf_op jit(solution)/shard_map/pallas_call | solution.py:35
  76.8 2.1 %collective-permute-start.30 = (bf16[4,2,32,256]{3,2,1,0:T(8,128)(2,1)S(1)}, bf16[4,2,32,256]{3,2,1,0:T(8,128)(2,1)S(1)}, u32[]{:S(2)}, u32[]{:S(2)}) collective-permute-start(bf16[4,2,32,256]{3,2,1,0:T(8,128)(2,1)S(1)} %get-tuple-element.95), channel_id=1, source_target_pairs={{0,6},{1,7},{2,4},{3,5},{4,2},{5,3},{6,0},{7,1},{8,14},{9,15},{10,... | collective-permute-start | bytes 393224 | tf_op jit(solution)/shard_map/ppermute | solution.py:23
  78.9 0.6 collective-permute-start.31
  79.5 0.8 collective-permute-start.32
  80.8 1.9 %collective-permute-done.30.a = bf16[4,2,32,256]{3,2,1,0:T(8,128)(2,1)S(1)} collective-permute-done((bf16[4,2,32,256]{3,2,1,0:T(8,128)(2,1)S(1)}, bf16[4,2,32,256]{3,2,1,0:T(8,128)(2,1)S(1)}, u32[]{:S(2)}, u32[]{:S(2)}) %collective-permute-start.30) | collective-permute-done | bytes 131104 | tf_op jit(solution)/shard_map/ppermute | solution.py:23
  82.7 1.1 %collective-permute-done.31.b = bf16[4,2,32,256]{3,2,1,0:T(8,128)(2,1)S(1)} collective-permute-done((bf16[4,2,32,256]{3,2,1,0:T(8,128)(2,1)S(1)}, bf16[4,2,32,256]{3,2,1,0:T(8,128)(2,1)S(1)}, u32[]{:S(2)}, u32[]{:S(2)}) %collective-permute-start.31) | collective-permute-done | bytes 131104 | tf_op jit(solution)/shard_map/ppermute | solution.py:23
  83.8 0.6 collective-permute-done.32.c
  84.6 3.4 %collective-permute-start.34 = (bf16[2,32,256]{2,1,0:T(8,128)(2,1)S(1)}, bf16[2,32,256]{2,1,0:T(8,128)(2,1)S(1)}, u32[]{:S(2)}, u32[]{:S(2)}) collective-permute-start(bf16[2,32,256]{2,1,0:T(8,128)(2,1)S(1)} %get-tuple-element.100), channel_id=1, source_target_pairs={{0,16},{1,17},{2,18},{3,19},{4,20},{5,21},{6,22},{7,23},{8,24},{9,... | collective-permute-start | bytes 98312 | tf_op jit(solution)/shard_map/ppermute | solution.py:23
  88.0 0.9 collective-permute-start.35
  89.0 1.0 collective-permute-done.34.refs_1_
  89.9 3.8 %collective-permute-done.35.refs_2_ = bf16[2,32,256]{2,1,0:T(8,128)(2,1)S(1)} collective-permute-done((bf16[2,32,256]{2,1,0:T(8,128)(2,1)S(1)}, bf16[2,32,256]{2,1,0:T(8,128)(2,1)S(1)}, u32[]{:S(2)}, u32[]{:S(2)}) %collective-permute-start.35) | collective-permute-done | bytes 32800 | tf_op jit(solution)/shard_map/ppermute | solution.py:23
  93.8 1.3 %shard_map.83 = (bf16[2,32,256]{2,1,0:T(8,128)(2,1)S(1)}, bf16[4,2,32,256]{3,2,1,0:T(8,128)(2,1)S(1)}, bf16[4,2,32,256]{3,2,1,0:T(8,128)(2,1)S(1)}, bf16[4,2,32,256]{3,2,1,0:T(8,128)(2,1)S(1)}) custom-call(bf16[2,32,256,256]{3,2,1,0:T(8,128)(2,1)S(1)} %get-tuple-element.65.spread, f32[2,32,256]{2,1,0:T(8,128)S(1)} %get-tuple-element.98.own, ...), custom_call_target="tpu_custom_call" | custom-call | flops 201326592 | tf_op jit(solution)/shard_map/pallas_call | solution.py:35
  95.1 0.8 collective-permute-start.36
  95.8 1.9 %collective-permute-start.37 = (bf16[4,2,32,256]{3,2,1,0:T(8,128)(2,1)S(1)}, bf16[4,2,32,256]{3,2,1,0:T(8,128)(2,1)S(1)}, u32[]{:S(2)}, u32[]{:S(2)}) collective-permute-start(bf16[4,2,32,256]{3,2,1,0:T(8,128)(2,1)S(1)} %get-tuple-element.104), channel_id=1, source_target_pairs={{0,2},{1,3},{2,0},{3,1},{4,6},{5,7},{6,4},{7,5},{8,10},{9,11},{10,... | collective-permute-start | bytes 393224 | tf_op jit(solution)/shard_map/ppermute | solution.py:23
  97.7 0.8 collective-permute-start.38
  99.1 1.8 %collective-permute-done.36.a = bf16[4,2,32,256]{3,2,1,0:T(8,128)(2,1)S(1)} collective-permute-done((bf16[4,2,32,256]{3,2,1,0:T(8,128)(2,1)S(1)}, bf16[4,2,32,256]{3,2,1,0:T(8,128)(2,1)S(1)}, u32[]{:S(2)}, u32[]{:S(2)}) %collective-permute-start.36) | collective-permute-done | bytes 131104 | tf_op jit(solution)/shard_map/ppermute | solution.py:23
  101.0 1.1 %collective-permute-done.37.b = bf16[4,2,32,256]{3,2,1,0:T(8,128)(2,1)S(1)} collective-permute-done((bf16[4,2,32,256]{3,2,1,0:T(8,128)(2,1)S(1)}, bf16[4,2,32,256]{3,2,1,0:T(8,128)(2,1)S(1)}, u32[]{:S(2)}, u32[]{:S(2)}) %collective-permute-start.37) | collective-permute-done | bytes 131104 | tf_op jit(solution)/shard_map/ppermute | solution.py:23
  102.9 1.1 %collective-permute-start.40 = (bf16[2,32,256]{2,1,0:T(8,128)(2,1)S(1)}, bf16[2,32,256]{2,1,0:T(8,128)(2,1)S(1)}, u32[]{:S(2)}, u32[]{:S(2)}) collective-permute-start(bf16[2,32,256]{2,1,0:T(8,128)(2,1)S(1)} %get-tuple-element.108), channel_id=1, source_target_pairs={{0,16},{1,17},{2,18},{3,19},{4,20},{5,21},{6,22},{7,23},{8,24},{9,... | collective-permute-start | bytes 98312 | tf_op jit(solution)/shard_map/ppermute | solution.py:23
  104.0 3.2 %collective-permute-start.41 = (bf16[2,32,256]{2,1,0:T(8,128)(2,1)S(1)}, bf16[2,32,256]{2,1,0:T(8,128)(2,1)S(1)}, u32[]{:S(2)}, u32[]{:S(2)}) collective-permute-start(bf16[2,32,256]{2,1,0:T(8,128)(2,1)S(1)} %get-tuple-element.109), channel_id=1, source_target_pairs={{0,24},{1,25},{2,26},{3,27},{4,28},{5,29},{6,30},{7,31},{8,16},{9,... | collective-permute-start | bytes 98312 | tf_op jit(solution)/shard_map/ppermute | solution.py:23
  107.7 2.0 %collective-permute-done.41.refs_2_ = bf16[2,32,256]{2,1,0:T(8,128)(2,1)S(1)} collective-permute-done((bf16[2,32,256]{2,1,0:T(8,128)(2,1)S(1)}, bf16[2,32,256]{2,1,0:T(8,128)(2,1)S(1)}, u32[]{:S(2)}, u32[]{:S(2)}) %collective-permute-start.41) | collective-permute-done | bytes 32800 | tf_op jit(solution)/shard_map/ppermute | solution.py:23
  109.9 0.7 shard_map.77
  111.1 0.7 shard_map.88
  (61 shorter events, 8.4 us)
Async XLA Ops:
  1.8 1.9 %collective-permute-start = (bf16[32,256]{1,0:T(8,128)(2,1)S(1)}, bf16[32,256]{1,0:T(8,128)(2,1)S(1)}, u32[]{:S(2)}, u32[]{:S(2)}) collective-permute-start(bf16[32,256]{1,0:T(8,128)(2,1)S(1)} %get-tuple-element.59.after), channel_id=1, source_target_pairs={{0,1},{1,0},{2,3},{3,2},{4,5},{5,4},{6,7},{7,6},{8,9},{9,8},{10,11... | collective-permute-start | bytes 49160 | tf_op jit(solution)/shard_map/ppermute | solution.py:23
  2.3 1.4 %collective-permute-start.1 = (s32[3,1,16]{2,1,0:T(1,128)}, s32[3,1,16]{2,1,0:T(1,128)S(1)}, u32[]{:S(2)}, u32[]{:S(2)}) collective-permute-start(s32[3,1,16]{2,1,0:T(1,128)} %own_pattern.5), channel_id=1, source_target_pairs={{0,1},{1,0},{2,3},{3,2},{4,5},{5,4},{6,7},{7,6},{8,9},{9,8},{10,11... | collective-permute-start | bytes 584 | tf_op jit(solution)/shard_map/ppermute | solution.py:23
  2.4 0.9 copy-start
  3.7 15.2 %collective-permute-start.2 = (bf16[3,1,16,256,256]{4,3,2,1,0:T(8,128)(2,1)}, bf16[3,1,16,256,256]{4,3,2,1,0:T(8,128)(2,1)S(1)}, u32[]{:S(2)}, u32[]{:S(2)}) collective-permute-start(bf16[3,1,16,256,256]{4,3,2,1,0:T(8,128)(2,1)} %tiles0.5), channel_id=1, source_target_pairs={{0,1},{1,0},{2,3},{3,2},{4,5},{5,4},{6,7},{7,6},{8,9},{9,8},{10,11... | collective-permute-start | bytes 18874376 | tf_op jit(solution)/shard_map/ppermute | solution.py:23
  3.8 14.5 %collective-permute-start.3 = (bf16[4,1,256,256]{3,2,1,0:T(8,128)(2,1)}, bf16[4,1,256,256]{3,2,1,0:T(8,128)(2,1)S(1)}, u32[]{:S(2)}, u32[]{:S(2)}) collective-permute-start(bf16[4,1,256,256]{3,2,1,0:T(8,128)(2,1)} %diag0.5), channel_id=1, source_target_pairs={{0,1},{1,0},{2,3},{3,2},{4,5},{5,4},{6,7},{7,6},{8,9},{9,8},{10,11... | collective-permute-start | bytes 1572872 | tf_op jit(solution)/shard_map/ppermute | solution.py:23
  4.2 5.3 %collective-permute-start.5 = (bf16[2,32,256]{2,1,0:T(8,128)(2,1)S(1)}, bf16[2,32,256]{2,1,0:T(8,128)(2,1)S(1)}, u32[]{:S(2)}, u32[]{:S(2)}) collective-permute-start(bf16[2,32,256]{2,1,0:T(8,128)(2,1)S(1)} %get-tuple-element.117.after.refs_0_.known), channel_id=1, source_target_pairs={{0,8},{1,9},{2,10},{3,11},{4,12},{5,13},{6,14},{7,15},{8,0},{9,1},... | collective-permute-start | bytes 98312 | tf_op jit(solution)/shard_map/ppermute | solution.py:23
  6.9 5.4 %collective-permute-start.6 = (bf16[2,32,256]{2,1,0:T(8,128)(2,1)S(1)}, bf16[2,32,256]{2,1,0:T(8,128)(2,1)S(1)}, u32[]{:S(2)}, u32[]{:S(2)}) collective-permute-start(bf16[2,32,256]{2,1,0:T(8,128)(2,1)S(1)} %get-tuple-element.117.after.refs_0_.known), channel_id=1, source_target_pairs={{0,16},{1,17},{2,18},{3,19},{4,20},{5,21},{6,22},{7,23},{8,24},{9,... | collective-permute-start | bytes 98312 | tf_op jit(solution)/shard_map/ppermute | solution.py:23
  9.5 5.7 %collective-permute-start.7 = (bf16[2,32,256]{2,1,0:T(8,128)(2,1)S(1)}, bf16[2,32,256]{2,1,0:T(8,128)(2,1)S(1)}, u32[]{:S(2)}, u32[]{:S(2)}) collective-permute-start(bf16[2,32,256]{2,1,0:T(8,128)(2,1)S(1)} %get-tuple-element.117.after.refs_0_.known), channel_id=1, source_target_pairs={{0,24},{1,25},{2,26},{3,27},{4,28},{5,29},{6,30},{7,31},{8,16},{9,... | collective-permute-start | bytes 98312 | tf_op jit(solution)/shard_map/ppermute | solution.py:23
  9.5 14.3 %collective-permute-start.4 = (bf16[4,32,256]{2,1,0:T(8,128)(2,1)S(1)}, bf16[4,32,256]{2,1,0:T(8,128)(2,1)S(1)}, u32[]{:S(2)}, u32[]{:S(2)}) collective-permute-start(bf16[4,32,256]{2,1,0:T(8,128)(2,1)S(1)} %get-tuple-element.67), channel_id=1, source_target_pairs={{0,1},{1,0},{2,3},{3,2},{4,5},{5,4},{6,7},{7,6},{8,9},{9,8},{10,11... | collective-permute-start | bytes 196616 | tf_op jit(solution)/shard_map/ppermute | solution.py:23
  15.2 6.9 %collective-permute-start.10 = (bf16[4,2,32,256]{3,2,1,0:T(8,128)(2,1)S(1)}, bf16[4,2,32,256]{3,2,1,0:T(8,128)(2,1)S(1)}, u32[]{:S(2)}, u32[]{:S(2)}) collective-permute-start(bf16[4,2,32,256]{3,2,1,0:T(8,128)(2,1)S(1)} %pad_maximum_fusion.part), channel_id=1, source_target_pairs={{0,6},{1,7},{2,4},{3,5},{4,2},{5,3},{6,0},{7,1},{8,14},{9,15},{10,... | collective-permute-start | bytes 393224 | tf_op jit(solution)/shard_map/ppermute | solution.py:23
  17.8 5.4 %collective-permute-start.9 = (bf16[4,2,32,256]{3,2,1,0:T(8,128)(2,1)S(1)}, bf16[4,2,32,256]{3,2,1,0:T(8,128)(2,1)S(1)}, u32[]{:S(2)}, u32[]{:S(2)}) collective-permute-start(bf16[4,2,32,256]{3,2,1,0:T(8,128)(2,1)S(1)} %pad_maximum_fusion.part), channel_id=1, source_target_pairs={{0,2},{1,3},{2,0},{3,1},{4,6},{5,7},{6,4},{7,5},{8,10},{9,11},{10,... | collective-permute-start | bytes 393224 | tf_op jit(solution)/shard_map/ppermute | solution.py:23
  18.3 5.6 %collective-permute-start.8 = (bf16[4,2,32,256]{3,2,1,0:T(8,128)(2,1)S(1)}, bf16[4,2,32,256]{3,2,1,0:T(8,128)(2,1)S(1)}, u32[]{:S(2)}, u32[]{:S(2)}) collective-permute-start(bf16[4,2,32,256]{3,2,1,0:T(8,128)(2,1)S(1)} %pad_maximum_fusion.part), channel_id=1, source_target_pairs={{0,4},{1,5},{2,6},{3,7},{4,0},{5,1},{6,2},{7,3},{8,12},{9,13},{10,... | collective-permute-start | bytes 393224 | tf_op jit(solution)/shard_map/ppermute | solution.py:23
  24.7 7.0 %collective-permute-start.11 = (bf16[2,32,256]{2,1,0:T(8,128)(2,1)S(1)}, bf16[2,32,256]{2,1,0:T(8,128)(2,1)S(1)}, u32[]{:S(2)}, u32[]{:S(2)}) collective-permute-start(bf16[2,32,256]{2,1,0:T(8,128)(2,1)S(1)} %shard_map.65.after.refs_1_.known), channel_id=1, source_target_pairs={{0,8},{1,9},{2,10},{3,11},{4,12},{5,13},{6,14},{7,15},{8,0},{9,1},... | collective-permute-start | bytes 98312 | tf_op jit(solution)/shard_map/ppermute | solution.py:23
  24.8 6.9 %collective-permute-start.12 = (bf16[2,32,256]{2,1,0:T(8,128)(2,1)S(1)}, bf16[2,32,256]{2,1,0:T(8,128)(2,1)S(1)}, u32[]{:S(2)}, u32[]{:S(2)}) collective-permute-start(bf16[2,32,256]{2,1,0:T(8,128)(2,1)S(1)} %shard_map.65.after.refs_1_.known), channel_id=1, source_target_pairs={{0,16},{1,17},{2,18},{3,19},{4,20},{5,21},{6,22},{7,23},{8,24},{9,... | collective-permute-start | bytes 98312 | tf_op jit(solution)/shard_map/ppermute | solution.py:23
  27.4 5.7 %collective-permute-start.13 = (bf16[2,32,256]{2,1,0:T(8,128)(2,1)S(1)}, bf16[2,32,256]{2,1,0:T(8,128)(2,1)S(1)}, u32[]{:S(2)}, u32[]{:S(2)}) collective-permute-start(bf16[2,32,256]{2,1,0:T(8,128)(2,1)S(1)} %shard_map.65.after.refs_1_.known), channel_id=1, source_target_pairs={{0,24},{1,25},{2,26},{3,27},{4,28},{5,29},{6,30},{7,31},{8,16},{9,... | collective-permute-start | bytes 98312 | tf_op jit(solution)/shard_map/ppermute | solution.py:23
  33.2 6.2 %collective-permute-start.16 = (bf16[4,2,32,256]{3,2,1,0:T(8,128)(2,1)S(1)}, bf16[4,2,32,256]{3,2,1,0:T(8,128)(2,1)S(1)}, u32[]{:S(2)}, u32[]{:S(2)}) collective-permute-start(bf16[4,2,32,256]{3,2,1,0:T(8,128)(2,1)S(1)} %pad_maximum_fusion.1.part), channel_id=1, source_target_pairs={{0,6},{1,7},{2,4},{3,5},{4,2},{5,3},{6,0},{7,1},{8,14},{9,15},{10,... | collective-permute-start | bytes 393224 | tf_op jit(solution)/shard_map/ppermute | solution.py:23
  35.0 5.0 %collective-permute-start.15 = (bf16[4,2,32,256]{3,2,1,0:T(8,128)(2,1)S(1)}, bf16[4,2,32,256]{3,2,1,0:T(8,128)(2,1)S(1)}, u32[]{:S(2)}, u32[]{:S(2)}) collective-permute-start(bf16[4,2,32,256]{3,2,1,0:T(8,128)(2,1)S(1)} %pad_maximum_fusion.1.part), channel_id=1, source_target_pairs={{0,2},{1,3},{2,0},{3,1},{4,6},{5,7},{6,4},{7,5},{8,10},{9,11},{10,... | collective-permute-start | bytes 393224 | tf_op jit(solution)/shard_map/ppermute | solution.py:23
  35.6 5.2 %collective-permute-start.14 = (bf16[4,2,32,256]{3,2,1,0:T(8,128)(2,1)S(1)}, bf16[4,2,32,256]{3,2,1,0:T(8,128)(2,1)S(1)}, u32[]{:S(2)}, u32[]{:S(2)}) collective-permute-start(bf16[4,2,32,256]{3,2,1,0:T(8,128)(2,1)S(1)} %pad_maximum_fusion.1.part), channel_id=1, source_target_pairs={{0,4},{1,5},{2,6},{3,7},{4,0},{5,1},{6,2},{7,3},{8,12},{9,13},{10,... | collective-permute-start | bytes 393224 | tf_op jit(solution)/shard_map/ppermute | solution.py:23
  41.6 7.0 %collective-permute-start.17 = (bf16[2,32,256]{2,1,0:T(8,128)(2,1)S(1)}, bf16[2,32,256]{2,1,0:T(8,128)(2,1)S(1)}, u32[]{:S(2)}, u32[]{:S(2)}) collective-permute-start(bf16[2,32,256]{2,1,0:T(8,128)(2,1)S(1)} %shard_map.70.after.refs_2_.known), channel_id=1, source_target_pairs={{0,8},{1,9},{2,10},{3,11},{4,12},{5,13},{6,14},{7,15},{8,0},{9,1},... | collective-permute-start | bytes 98312 | tf_op jit(solution)/shard_map/ppermute | solution.py:23
  41.7 7.0 %collective-permute-start.18 = (bf16[2,32,256]{2,1,0:T(8,128)(2,1)S(1)}, bf16[2,32,256]{2,1,0:T(8,128)(2,1)S(1)}, u32[]{:S(2)}, u32[]{:S(2)}) collective-permute-start(bf16[2,32,256]{2,1,0:T(8,128)(2,1)S(1)} %shard_map.70.after.refs_2_.known), channel_id=1, source_target_pairs={{0,16},{1,17},{2,18},{3,19},{4,20},{5,21},{6,22},{7,23},{8,24},{9,... | collective-permute-start | bytes 98312 | tf_op jit(solution)/shard_map/ppermute | solution.py:23
  44.3 5.7 %collective-permute-start.19 = (bf16[2,32,256]{2,1,0:T(8,128)(2,1)S(1)}, bf16[2,32,256]{2,1,0:T(8,128)(2,1)S(1)}, u32[]{:S(2)}, u32[]{:S(2)}) collective-permute-start(bf16[2,32,256]{2,1,0:T(8,128)(2,1)S(1)} %shard_map.70.after.refs_2_.known), channel_id=1, source_target_pairs={{0,24},{1,25},{2,26},{3,27},{4,28},{5,29},{6,30},{7,31},{8,16},{9,... | collective-permute-start | bytes 98312 | tf_op jit(solution)/shard_map/ppermute | solution.py:23
  50.0 5.9 %collective-permute-start.22 = (bf16[4,2,32,256]{3,2,1,0:T(8,128)(2,1)S(1)}, bf16[4,2,32,256]{3,2,1,0:T(8,128)(2,1)S(1)}, u32[]{:S(2)}, u32[]{:S(2)}) collective-permute-start(bf16[4,2,32,256]{3,2,1,0:T(8,128)(2,1)S(1)} %pad_maximum_fusion.2.part), channel_id=1, source_target_pairs={{0,6},{1,7},{2,4},{3,5},{4,2},{5,3},{6,0},{7,1},{8,14},{9,15},{10,... | collective-permute-start | bytes 393224 | tf_op jit(solution)/shard_map/ppermute | solution.py:23
  51.8 5.0 %collective-permute-start.21 = (bf16[4,2,32,256]{3,2,1,0:T(8,128)(2,1)S(1)}, bf16[4,2,32,256]{3,2,1,0:T(8,128)(2,1)S(1)}, u32[]{:S(2)}, u32[]{:S(2)}) collective-permute-start(bf16[4,2,32,256]{3,2,1,0:T(8,128)(2,1)S(1)} %pad_maximum_fusion.2.part), channel_id=1, source_target_pairs={{0,2},{1,3},{2,0},{3,1},{4,6},{5,7},{6,4},{7,5},{8,10},{9,11},{10,... | collective-permute-start | bytes 393224 | tf_op jit(solution)/shard_map/ppermute | solution.py:23
  52.3 5.1 %collective-permute-start.20 = (bf16[4,2,32,256]{3,2,1,0:T(8,128)(2,1)S(1)}, bf16[4,2,32,256]{3,2,1,0:T(8,128)(2,1)S(1)}, u32[]{:S(2)}, u32[]{:S(2)}) collective-permute-start(bf16[4,2,32,256]{3,2,1,0:T(8,128)(2,1)S(1)} %pad_maximum_fusion.2.part), channel_id=1, source_target_pairs={{0,4},{1,5},{2,6},{3,7},{4,0},{5,1},{6,2},{7,3},{8,12},{9,13},{10,... | collective-permute-start | bytes 393224 | tf_op jit(solution)/shard_map/ppermute | solution.py:23
  59.6 5.9 %collective-permute-start.24 = (bf16[4,2,32,256]{3,2,1,0:T(8,128)(2,1)S(1)}, bf16[4,2,32,256]{3,2,1,0:T(8,128)(2,1)S(1)}, u32[]{:S(2)}, u32[]{:S(2)}) collective-permute-start(bf16[4,2,32,256]{3,2,1,0:T(8,128)(2,1)S(1)} %get-tuple-element.87), channel_id=1, source_target_pairs={{0,6},{1,7},{2,4},{3,5},{4,2},{5,3},{6,0},{7,1},{8,14},{9,15},{10,... | collective-permute-start | bytes 393224 | tf_op jit(solution)/shard_map/ppermute | solution.py:23
  61.6 6.3 %collective-permute-start.25 = (bf16[4,2,32,256]{3,2,1,0:T(8,128)(2,1)S(1)}, bf16[4,2,32,256]{3,2,1,0:T(8,128)(2,1)S(1)}, u32[]{:S(2)}, u32[]{:S(2)}) collective-permute-start(bf16[4,2,32,256]{3,2,1,0:T(8,128)(2,1)S(1)} %get-tuple-element.88), channel_id=1, source_target_pairs={{0,2},{1,3},{2,0},{3,1},{4,6},{5,7},{6,4},{7,5},{8,10},{9,11},{10,... | collective-permute-start | bytes 393224 | tf_op jit(solution)/shard_map/ppermute | solution.py:23
  63.5 5.0 %collective-permute-start.26 = (bf16[4,2,32,256]{3,2,1,0:T(8,128)(2,1)S(1)}, bf16[4,2,32,256]{3,2,1,0:T(8,128)(2,1)S(1)}, u32[]{:S(2)}, u32[]{:S(2)}) collective-permute-start(bf16[4,2,32,256]{3,2,1,0:T(8,128)(2,1)S(1)} %get-tuple-element.89), channel_id=1, source_target_pairs={{0,4},{1,5},{2,6},{3,7},{4,0},{5,1},{6,2},{7,3},{8,12},{9,13},{10,... | collective-permute-start | bytes 393224 | tf_op jit(solution)/shard_map/ppermute | solution.py:23
  68.6 4.5 %collective-permute-start.27 = (bf16[2,32,256]{2,1,0:T(8,128)(2,1)S(1)}, bf16[2,32,256]{2,1,0:T(8,128)(2,1)S(1)}, u32[]{:S(2)}, u32[]{:S(2)}) collective-permute-start(bf16[2,32,256]{2,1,0:T(8,128)(2,1)S(1)} %get-tuple-element.91), channel_id=1, source_target_pairs={{0,8},{1,9},{2,10},{3,11},{4,12},{5,13},{6,14},{7,15},{8,0},{9,1},... | collective-permute-start | bytes 98312 | tf_op jit(solution)/shard_map/ppermute | solution.py:23
  68.6 4.9 %collective-permute-start.28 = (bf16[2,32,256]{2,1,0:T(8,128)(2,1)S(1)}, bf16[2,32,256]{2,1,0:T(8,128)(2,1)S(1)}, u32[]{:S(2)}, u32[]{:S(2)}) collective-permute-start(bf16[2,32,256]{2,1,0:T(8,128)(2,1)S(1)} %get-tuple-element.92), channel_id=1, source_target_pairs={{0,16},{1,17},{2,18},{3,19},{4,20},{5,21},{6,22},{7,23},{8,24},{9,... | collective-permute-start | bytes 98312 | tf_op jit(solution)/shard_map/ppermute | solution.py:23
  69.8 5.7 %collective-permute-start.29 = (bf16[2,32,256]{2,1,0:T(8,128)(2,1)S(1)}, bf16[2,32,256]{2,1,0:T(8,128)(2,1)S(1)}, u32[]{:S(2)}, u32[]{:S(2)}) collective-permute-start(bf16[2,32,256]{2,1,0:T(8,128)(2,1)S(1)} %get-tuple-element.93), channel_id=1, source_target_pairs={{0,24},{1,25},{2,26},{3,27},{4,28},{5,29},{6,30},{7,31},{8,16},{9,... | collective-permute-start | bytes 98312 | tf_op jit(solution)/shard_map/ppermute | solution.py:23
  76.8 5.9 %collective-permute-start.30 = (bf16[4,2,32,256]{3,2,1,0:T(8,128)(2,1)S(1)}, bf16[4,2,32,256]{3,2,1,0:T(8,128)(2,1)S(1)}, u32[]{:S(2)}, u32[]{:S(2)}) collective-permute-start(bf16[4,2,32,256]{3,2,1,0:T(8,128)(2,1)S(1)} %get-tuple-element.95), channel_id=1, source_target_pairs={{0,6},{1,7},{2,4},{3,5},{4,2},{5,3},{6,0},{7,1},{8,14},{9,15},{10,... | collective-permute-start | bytes 393224 | tf_op jit(solution)/shard_map/ppermute | solution.py:23
  78.9 5.0 %collective-permute-start.31 = (bf16[4,2,32,256]{3,2,1,0:T(8,128)(2,1)S(1)}, bf16[4,2,32,256]{3,2,1,0:T(8,128)(2,1)S(1)}, u32[]{:S(2)}, u32[]{:S(2)}) collective-permute-start(bf16[4,2,32,256]{3,2,1,0:T(8,128)(2,1)S(1)} %get-tuple-element.96), channel_id=1, source_target_pairs={{0,2},{1,3},{2,0},{3,1},{4,6},{5,7},{6,4},{7,5},{8,10},{9,11},{10,... | collective-permute-start | bytes 393224 | tf_op jit(solution)/shard_map/ppermute | solution.py:23
  79.5 5.0 %collective-permute-start.32 = (bf16[4,2,32,256]{3,2,1,0:T(8,128)(2,1)S(1)}, bf16[4,2,32,256]{3,2,1,0:T(8,128)(2,1)S(1)}, u32[]{:S(2)}, u32[]{:S(2)}) collective-permute-start(bf16[4,2,32,256]{3,2,1,0:T(8,128)(2,1)S(1)} %get-tuple-element.97), channel_id=1, source_target_pairs={{0,4},{1,5},{2,6},{3,7},{4,0},{5,1},{6,2},{7,3},{8,12},{9,13},{10,... | collective-permute-start | bytes 393224 | tf_op jit(solution)/shard_map/ppermute | solution.py:23
  84.5 4.5 %collective-permute-start.33 = (bf16[2,32,256]{2,1,0:T(8,128)(2,1)S(1)}, bf16[2,32,256]{2,1,0:T(8,128)(2,1)S(1)}, u32[]{:S(2)}, u32[]{:S(2)}) collective-permute-start(bf16[2,32,256]{2,1,0:T(8,128)(2,1)S(1)} %get-tuple-element.99), channel_id=1, source_target_pairs={{0,8},{1,9},{2,10},{3,11},{4,12},{5,13},{6,14},{7,15},{8,0},{9,1},... | collective-permute-start | bytes 98312 | tf_op jit(solution)/shard_map/ppermute | solution.py:23
  84.6 5.3 %collective-permute-start.34 = (bf16[2,32,256]{2,1,0:T(8,128)(2,1)S(1)}, bf16[2,32,256]{2,1,0:T(8,128)(2,1)S(1)}, u32[]{:S(2)}, u32[]{:S(2)}) collective-permute-start(bf16[2,32,256]{2,1,0:T(8,128)(2,1)S(1)} %get-tuple-element.100), channel_id=1, source_target_pairs={{0,16},{1,17},{2,18},{3,19},{4,20},{5,21},{6,22},{7,23},{8,24},{9,... | collective-permute-start | bytes 98312 | tf_op jit(solution)/shard_map/ppermute | solution.py:23
  88.0 5.7 %collective-permute-start.35 = (bf16[2,32,256]{2,1,0:T(8,128)(2,1)S(1)}, bf16[2,32,256]{2,1,0:T(8,128)(2,1)S(1)}, u32[]{:S(2)}, u32[]{:S(2)}) collective-permute-start(bf16[2,32,256]{2,1,0:T(8,128)(2,1)S(1)} %get-tuple-element.101), channel_id=1, source_target_pairs={{0,24},{1,25},{2,26},{3,27},{4,28},{5,29},{6,30},{7,31},{8,16},{9,... | collective-permute-start | bytes 98312 | tf_op jit(solution)/shard_map/ppermute | solution.py:23
  95.1 5.9 %collective-permute-start.36 = (bf16[4,2,32,256]{3,2,1,0:T(8,128)(2,1)S(1)}, bf16[4,2,32,256]{3,2,1,0:T(8,128)(2,1)S(1)}, u32[]{:S(2)}, u32[]{:S(2)}) collective-permute-start(bf16[4,2,32,256]{3,2,1,0:T(8,128)(2,1)S(1)} %get-tuple-element.103), channel_id=1, source_target_pairs={{0,6},{1,7},{2,4},{3,5},{4,2},{5,3},{6,0},{7,1},{8,14},{9,15},{10,... | collective-permute-start | bytes 393224 | tf_op jit(solution)/shard_map/ppermute | solution.py:23
  95.8 6.3 %collective-permute-start.37 = (bf16[4,2,32,256]{3,2,1,0:T(8,128)(2,1)S(1)}, bf16[4,2,32,256]{3,2,1,0:T(8,128)(2,1)S(1)}, u32[]{:S(2)}, u32[]{:S(2)}) collective-permute-start(bf16[4,2,32,256]{3,2,1,0:T(8,128)(2,1)S(1)} %get-tuple-element.104), channel_id=1, source_target_pairs={{0,2},{1,3},{2,0},{3,1},{4,6},{5,7},{6,4},{7,5},{8,10},{9,11},{10,... | collective-permute-start | bytes 393224 | tf_op jit(solution)/shard_map/ppermute | solution.py:23
  97.7 5.0 %collective-permute-start.38 = (bf16[4,2,32,256]{3,2,1,0:T(8,128)(2,1)S(1)}, bf16[4,2,32,256]{3,2,1,0:T(8,128)(2,1)S(1)}, u32[]{:S(2)}, u32[]{:S(2)}) collective-permute-start(bf16[4,2,32,256]{3,2,1,0:T(8,128)(2,1)S(1)} %get-tuple-element.105), channel_id=1, source_target_pairs={{0,4},{1,5},{2,6},{3,7},{4,0},{5,1},{6,2},{7,3},{8,12},{9,13},{10,... | collective-permute-start | bytes 393224 | tf_op jit(solution)/shard_map/ppermute | solution.py:23
  98.6 11.3 %collective-permute-start.23 = (bf16[4,32,256]{2,1,0:T(8,128)(2,1)S(1)}, bf16[4,32,256]{2,1,0:T(8,128)(2,1)S(1)}, u32[]{:S(2)}, u32[]{:S(2)}) collective-permute-start(bf16[4,32,256]{2,1,0:T(8,128)(2,1)S(1)} %get-tuple-element.85), channel_id=1, source_target_pairs={{0,1},{1,0},{2,3},{3,2},{4,5},{5,4},{6,7},{7,6},{8,9},{9,8},{10,11... | collective-permute-start | bytes 196616 | tf_op jit(solution)/shard_map/ppermute | solution.py:23
  102.8 4.5 %collective-permute-start.39 = (bf16[2,32,256]{2,1,0:T(8,128)(2,1)S(1)}, bf16[2,32,256]{2,1,0:T(8,128)(2,1)S(1)}, u32[]{:S(2)}, u32[]{:S(2)}) collective-permute-start(bf16[2,32,256]{2,1,0:T(8,128)(2,1)S(1)} %get-tuple-element.107), channel_id=1, source_target_pairs={{0,8},{1,9},{2,10},{3,11},{4,12},{5,13},{6,14},{7,15},{8,0},{9,1},... | collective-permute-start | bytes 98312 | tf_op jit(solution)/shard_map/ppermute | solution.py:23
  102.9 4.9 %collective-permute-start.40 = (bf16[2,32,256]{2,1,0:T(8,128)(2,1)S(1)}, bf16[2,32,256]{2,1,0:T(8,128)(2,1)S(1)}, u32[]{:S(2)}, u32[]{:S(2)}) collective-permute-start(bf16[2,32,256]{2,1,0:T(8,128)(2,1)S(1)} %get-tuple-element.108), channel_id=1, source_target_pairs={{0,16},{1,17},{2,18},{3,19},{4,20},{5,21},{6,22},{7,23},{8,24},{9,... | collective-permute-start | bytes 98312 | tf_op jit(solution)/shard_map/ppermute | solution.py:23
  104.0 5.7 %collective-permute-start.41 = (bf16[2,32,256]{2,1,0:T(8,128)(2,1)S(1)}, bf16[2,32,256]{2,1,0:T(8,128)(2,1)S(1)}, u32[]{:S(2)}, u32[]{:S(2)}) collective-permute-start(bf16[2,32,256]{2,1,0:T(8,128)(2,1)S(1)} %get-tuple-element.109), channel_id=1, source_target_pairs={{0,24},{1,25},{2,26},{3,27},{4,28},{5,29},{6,30},{7,31},{8,16},{9,... | collective-permute-start | bytes 98312 | tf_op jit(solution)/shard_map/ppermute | solution.py:23
  107.2 3.4 %collective-permute-start.43 = (bf16[3,32,256]{2,1,0:T(8,128)(2,1)S(1)}, bf16[3,32,256]{2,1,0:T(8,128)(2,1)S(1)}, u32[]{:S(2)}, u32[]{:S(2)}) collective-permute-start(bf16[3,32,256]{2,1,0:T(8,128)(2,1)S(1)} %get-tuple-element.113), channel_id=1, source_target_pairs={{0,1},{1,0},{2,3},{3,2},{4,5},{5,4},{6,7},{7,6},{8,9},{9,8},{10,11... | collective-permute-start | bytes 147464 | tf_op jit(solution)/shard_map/ppermute | solution.py:23
  109.9 1.2 %collective-permute-start.42 = (bf16[32,256]{1,0:T(8,128)(2,1)S(1)}, bf16[32,256]{1,0:T(8,128)(2,1)S(1)}, u32[]{:S(2)}, u32[]{:S(2)}) collective-permute-start(bf16[32,256]{1,0:T(8,128)(2,1)S(1)} %get-tuple-element.111), channel_id=1, source_target_pairs={{0,1},{1,0},{2,3},{3,2},{4,5},{5,4},{6,7},{7,6},{8,9},{9,8},{10,11... | collective-permute-start | bytes 49160 | tf_op jit(solution)/shard_map/ppermute | solution.py:23

commit v4 on v3

--- a/solution.py
+++ b/solution.py
@@ -16,6 +16,8 @@
 
 
 FIRST = 3
+ROUND = 6
+CROSS = (1,2,3)
 
 
 def swap(value, mask):
@@ -44,7 +46,9 @@
 
 
 def side(index):
-    return jnp.bitwise_and(index, 1)
+    for bit in CROSS:
+        index = index ^ ((index >> bit) & 1)
+    return index & 1
 
 
 def halves(width):
@@ -82,28 +86,58 @@
 ):
     me = lax.axis_index("rows")
     deep = spread.shape[1] // 8
+    patterns, tiles = (own_pattern, other_pattern), (tiles0, tiles1)
     loads = []
-    for i, (tiles, inverse) in enumerate(((tiles0, diag0), (tiles1, diag1))):
-        loads.append(pltpu.make_async_copy(tiles.at[level - 1, 0], held.at[i], arrived.at[i]))
+    for i, inverse in enumerate((diag0, diag1)):
         for n, l in enumerate(solve_levels):
             loads.append(pltpu.make_async_copy(inverse.at[l, 0], diag.at[n, i], arrived.at[2 + 2 * n + i]))
     for load in loads:
         load.start()
 
-    def clear(e, nothing):
+    def clear():
+        def clear_place(e, nothing):
+            for i in range(2):
+                spread[i, e] = jnp.zeros(spread.shape[2:], spread.dtype)
+            return nothing
+
+        lax.fori_loop(0, spread.shape[1], clear_place, 0)
+
+    def place_of(i, k):
+        away = jnp.bitwise_xor(patterns[i][level - 1, 0, k], me)
+        flat = jnp.bitwise_and(away, 6)
+        part = jnp.where(flat == PLANE[0], 1, jnp.where(flat == PLANE[1], 2, jnp.where(flat == PLANE[2], 3, 0)))
+        return part * (2 * deep) + (away >> 3) * 2 + side(away)
+
+    whole = [pltpu.make_async_copy(tiles[i].at[level - 1, 0], held.at[i], arrived.at[i]) for i in range(2)]
+
+    def place_all():
+        for load in whole:
+            load.start()
+        clear()
         for i in range(2):
-            spread[i, e] = jnp.zeros(spread.shape[2:], spread.dtype)
-        return nothing
-
-    lax.fori_loop(0, spread.shape[1], clear, 0)
+            whole[i].wait()
+            for k in range(held.shape[1]):
+                spread[i, place_of(i, k)] = held[i, k]
+
+    def place_few():
+        clear()
+        for i in range(2):
+            for start in range(0, held.shape[1], ROUND):
+                count = min(ROUND, held.shape[1] - start)
+                for k in range(start, start + count):
+                    tile = tiles[i].at[level - 1, 0, k]
+                    pltpu.make_async_copy(tile, spread.at[i, place_of(i, k)], arrived.at[i]).start()
+                some = tiles[i].at[level - 1, 0, pl.ds(start, count)]
+                pltpu.make_async_copy(some, spread.at[i, pl.ds(0, count)], arrived.at[i]).wait()
+
+    if level == 1:
+        group = side(me)
+        pl.when(group == 0)(place_all)
+        pl.when(group == 1)(place_few)
+    else:
+        place_all()
     for load in loads:
         load.wait()
-    for i, pattern in enumerate((own_pattern, other_pattern)):
-        for k in range(held.shape[1]):
-            away = jnp.bitwise_xor(pattern[level - 1, 0, k], me)
-            flat = jnp.bitwise_and(away, 6)
-            part = jnp.where(flat == PLANE[0], 1, jnp.where(flat == PLANE[1], 2, jnp.where(flat == PLANE[2], 3, 0)))
-            spread[i, part * (2 * deep) + (away >> 3) * 2 + side(away)] = held[i, k]
 
 
 def meet(part, spread, i, j):
@@ -189,34 +223,32 @@
         push(down, spread, j + 1, part)
 
 
-def last_kernel(own, known, diag, *refs):
-    arrived, (mine, sent) = refs[:-2], refs[-2:]
-    mine[...], sent[...] = backward_step(own, arrived, known, diag)
-
-
-def split_kernel(*refs):
-    blocks, (mine, sent) = refs[:-2], refs[-2:]
-    for l, block in enumerate(blocks):
-        mine[l] = block[0]
-        sent[l] = block[1]
-
-
-def join_kernel(*refs):
-    pairs, out = refs[:-1], refs[-1]
-    here, there = halves(out.shape[2])
-    l = 0
-    for mine, other in zip(pairs[0::2], pairs[1::2]):
-        for m in range(mine.shape[0]):
-            out[l, 0, here] = mine[m]
-            out[l, 0, there] = other[m]
-            l += 1
+def last_kernel(levels, own, known, diag, *refs):
+    split = len(refs) - 2 - (2 * levels - 1)
+    arrived, blocks, (mine, sent) = refs[:split], refs[split:-2], refs[-2:]
+    solved = backward_step(own, arrived, known, diag)
+    for n, block in enumerate(blocks):
+        n += n >= levels
+        mine[n] = block[0]
+        sent[n] = block[1]
+    mine[levels], sent[levels] = solved
+
+
+def join_kernel(mine, other, *outs):
+    here, there = halves(outs[0].shape[2])
+    levels = outs[0].shape[0]
+    for n, out in enumerate(outs):
+        for l in range(levels):
+            out[l, 0, here] = mine[n * levels + l]
+            out[l, 0, there] = other[n * levels + l]
 
 
 def body(rhs_block, diag_inv, off_tiles, pattern):
     levels, _, width, size = rhs_block.shape
     devices = lax.axis_size("rows")
     half = width // 2
-    line = [8 * j for j in range(1, devices // 8)]
+    line = [8 * j + side(8 * j) for j in range(1, devices // 8)]
+    plane = [m + side(m) for m in PLANE]
     deep = len(line) + 1
     if lax.axis_size("rhs") > 1:
         off_tiles = lax.all_gather(off_tiles, "rhs", axis=2, tiled=True)
@@ -275,7 +307,7 @@
 
     def met(level, arrived, spread, first):
         parts = [jnp.stack(arrived)]
-        parts += [swap(parts[0], m) for m in PLANE]
+        parts += [swap(parts[0], m) for m in plane]
         partial = []
         for j in range(first):
             kernel = functools.partial(more_kernel, j)
@@ -284,7 +316,7 @@
 
     def scattered(spread, back, outs):
         keep = call(keep_kernel, shape(deep, 2, dtype=jnp.float32), [spread, back], flops=work)
-        arrived = [swap(out, m) for out, m in zip(outs, PLANE)]
+        arrived = [swap(out, m) for out, m in zip(outs, plane)]
         summed = call(reduce_kernel, [shape(2, dtype=jnp.float32)] + [shape(2)] * (deep - 1), [keep] + arrived)
         return summed[0], [swap(part, m) for part, m in zip(summed[1:], line)]
 
@@ -315,13 +347,13 @@
         )
         backward.insert(0, back)
     own, arrived = scattered(spreads[0], back, outs)
-    last, last_sent = call(last_kernel, [shape()] * 2, [own, forward[0], diag[0]] + arrived)
-
+    mine, sent = call(
+        functools.partial(last_kernel, levels),
+        [shape(2 * levels)] * 2,
+        [own, forward[0], diag[0]] + arrived + forward + backward,
+    )
     whole = jax.ShapeDtypeStruct((levels, 1, width, size), jnp.bfloat16)
-    mine, sent = call(split_kernel, [shape(levels)] * 2, forward)
-    forward_sol = call(join_kernel, whole, [mine, swap(sent, 1)])
-    mine, sent = call(split_kernel, [shape(levels - 1)] * 2, backward)
-    backward_sol = call(join_kernel, whole, [last[None], swap(last_sent, 1)[None], mine, swap(sent, 1)])
+    forward_sol, backward_sol = call(join_kernel, [whole] * 2, [mine, swap(sent, 1)])
     return forward_sol, backward_sol
 
 

time: 112 us -> 111 us (level)
  waiting for transfers between devices: 34.7 us -> 33.5 us
    ppermute x44 -> x42, waiting for transfers between devices: 34.7 us -> 33.5 us  [swap(): return lax.ppermute(value, 'rows', [(i, i ^ mask) for i in range(size)])]
    pallas_call x30 -> x27, Pallas kernels: 24.7 us -> 24.9 us  [call(): pl.pallas_call(kernel, out_shape=out_shape, in_specs=[VMEM_SPEC] * len(op...]
    ppermute x44 -> x42, starting transfers between devices: 50.4 us -> 50.5 us  [swap(): return lax.ppermute(value, 'rows', [(i, i ^ mask) for i in range(size)])]
  transfers between devices with their start and end apart: 44 -> 42, of which waited for: 25 -> 25; matrix products, arithmetic and copies ran while one was open for 0% -> 0% of each run, Pallas kernels for 15% -> 15%
where the time goes in v4:
time: 111 us
  starting transfers between devices  50.5 us (45%)
  waiting for transfers between devices  33.5 us (30%)
  Pallas kernels  24.9 us (22%)
    ppermute x42, starting transfers between devices, swap(): return lax.ppermute(value, 'rows', [(i, i ^ mask) for i in range(size)])  50.5 us
    ppermute x42, waiting for transfers between devices, swap(): return lax.ppermute(value, 'rows', [(i, i ^ mask) for i in range(size)])  33.5 us
    pallas_call x27, Pallas kernels, call(): pl.pallas_call(kernel, out_shape=out_shape, in_specs=[VMEM_SPEC] * len(op...  24.9 us
  transfers between devices with their start and end apart: 42, of which 25 were waited for; matrix products, arithmetic and copies ran while one was open for 0% of the time, Pallas kernels for 15%

profile of v4, /device:TPU:0, one launch (start us, length us, event | category | flops | bytes accessed | tf_op | source)
XLA Modules:
  0.0 110.7 jit_solution(15252338995725746055)
XLA Ops:
  0.6 1.1 %shard_map.59 = (bf16[32,256]{1,0:T(8,128)(2,1)S(1)}, bf16[32,256]{1,0:T(8,128)(2,1)S(1)}) custom-call(bf16[4,1,64,256]{3,2,1,0:T(8,128)(2,1)} %rhs.3, bf16[4,1,256,256]{3,2,1,0:T(8,128)(2,1)} %diag0.5), custom_call_target="tpu_custom_call" | custom-call | tf_op jit(solution)/shard_map/pallas_call | solution.py:37
  2.4 0.9 copy-done
  4.2 2.7 %collective-permute-start.5 = (bf16[2,32,256]{2,1,0:T(8,128)(2,1)S(1)}, bf16[2,32,256]{2,1,0:T(8,128)(2,1)S(1)}, u32[]{:S(2)}, u32[]{:S(2)}) collective-permute-start(bf16[2,32,256]{2,1,0:T(8,128)(2,1)S(1)} %get-tuple-element.109.after.known.refs_3_), channel_id=1, source_target_pairs={{0,9},{1,8},{2,11},{3,10},{4,13},{5,12},{6,15},{7,14},{8,1},{9,0},... | collective-permute-start | bytes 98312 | tf_op jit(solution)/shard_map/ppermute | solution.py:25
  6.9 2.6 %collective-permute-start.6 = (bf16[2,32,256]{2,1,0:T(8,128)(2,1)S(1)}, bf16[2,32,256]{2,1,0:T(8,128)(2,1)S(1)}, u32[]{:S(2)}, u32[]{:S(2)}) collective-permute-start(bf16[2,32,256]{2,1,0:T(8,128)(2,1)S(1)} %get-tuple-element.109.after.known.refs_3_), channel_id=1, source_target_pairs={{0,16},{1,17},{2,18},{3,19},{4,20},{5,21},{6,22},{7,23},{8,24},{9,... | collective-permute-start | bytes 98312 | tf_op jit(solution)/shard_map/ppermute | solution.py:25
  9.5 2.5 %collective-permute-done.6 = bf16[2,32,256]{2,1,0:T(8,128)(2,1)S(1)} collective-permute-done((bf16[2,32,256]{2,1,0:T(8,128)(2,1)S(1)}, bf16[2,32,256]{2,1,0:T(8,128)(2,1)S(1)}, u32[]{:S(2)}, u32[]{:S(2)}) %collective-permute-start.6) | collective-permute-done | bytes 32800 | tf_op jit(solution)/shard_map/ppermute | solution.py:25
  12.0 2.8 %collective-permute-done.7 = bf16[2,32,256]{2,1,0:T(8,128)(2,1)S(1)} collective-permute-done((bf16[2,32,256]{2,1,0:T(8,128)(2,1)S(1)}, bf16[2,32,256]{2,1,0:T(8,128)(2,1)S(1)}, u32[]{:S(2)}, u32[]{:S(2)}) %collective-permute-start.7) | collective-permute-done | bytes 32800 | tf_op jit(solution)/shard_map/ppermute | solution.py:25
  14.9 2.5 %collective-permute-start.10 = (bf16[4,2,32,256]{3,2,1,0:T(8,128)(2,1)S(1)}, bf16[4,2,32,256]{3,2,1,0:T(8,128)(2,1)S(1)}, u32[]{:S(2)}, u32[]{:S(2)}) collective-permute-start(bf16[4,2,32,256]{3,2,1,0:T(8,128)(2,1)S(1)} %pad_maximum_fusion.part), channel_id=1, source_target_pairs={{0,6},{1,7},{2,4},{3,5},{4,2},{5,3},{6,0},{7,1},{8,14},{9,15},{10,... | collective-permute-start | bytes 393224 | tf_op jit(solution)/shard_map/ppermute | solution.py:25
  17.4 0.8 collective-permute-start.8
  18.2 3.0 %shard_map.61 = (bf16[2,32,256,256]{3,2,1,0:T(8,128)(2,1)S(1)}, bf16[2,2,256,256]{3,2,1,0:T(8,128)(2,1)S(1)}) custom-call(s32[3,1,16]{2,1,0:T(1,128)} %own_pattern.5, s32[3,1,16]{2,1,0:T(1,128)S(1)} %collective-permute-done.1.other_pattern, bf16[2,32,256]{2,1,0:T(8,128)(2,1)S(1)} %get-tuple-element.109.after.known.refs_3_, ...), custom_call_target="tpu_custom_call" | custom-call | flops 134217728 | tf_op jit(solution)/shard_map/pallas_call | solution.py:37
  21.2 0.7 shard_map.62.refs_0_
  22.2 0.7 shard_map.63.refs_0_
  23.4 0.7 shard_map.64.refs_1_
  24.1 0.8 shard_map.65.after.known.refs_4_
  25.0 2.6 %collective-permute-start.12 = (bf16[2,32,256]{2,1,0:T(8,128)(2,1)S(1)}, bf16[2,32,256]{2,1,0:T(8,128)(2,1)S(1)}, u32[]{:S(2)}, u32[]{:S(2)}) collective-permute-start(bf16[2,32,256]{2,1,0:T(8,128)(2,1)S(1)} %shard_map.65.after.known.refs_4_), channel_id=1, source_target_pairs={{0,16},{1,17},{2,18},{3,19},{4,20},{5,21},{6,22},{7,23},{8,24},{9,... | collective-permute-start | bytes 98312 | tf_op jit(solution)/shard_map/ppermute | solution.py:25
  27.6 1.2 %collective-permute-start.13 = (bf16[2,32,256]{2,1,0:T(8,128)(2,1)S(1)}, bf16[2,32,256]{2,1,0:T(8,128)(2,1)S(1)}, u32[]{:S(2)}, u32[]{:S(2)}) collective-permute-start(bf16[2,32,256]{2,1,0:T(8,128)(2,1)S(1)} %shard_map.65.after.known.refs_4_), channel_id=1, source_target_pairs={{0,25},{1,24},{2,27},{3,26},{4,29},{5,28},{6,31},{7,30},{8,17},{9,... | collective-permute-start | bytes 98312 | tf_op jit(solution)/shard_map/ppermute | solution.py:25
  28.8 2.8 %shard_map.66 = (bf16[2,32,256,256]{3,2,1,0:T(8,128)(2,1)S(1)}, bf16[1,2,256,256]{3,2,1,0:T(8,128)(2,1)S(1)}) custom-call(s32[3,1,16]{2,1,0:T(1,128)} %own_pattern.5, s32[3,1,16]{2,1,0:T(1,128)S(1)} %collective-permute-done.1.other_pattern, bf16[2,32,256]{2,1,0:T(8,128)(2,1)S(1)} %shard_map.65.after.known.refs_4_, bf16[3,1,16,256,256]{4,3,2,1,0:T(8,128)(2,1)} %tiles0.5, ...), custom_call_target="tpu_custom_call" | custom-call | flops 134217728 | tf_op jit(solution)/shard_map/pallas_call | solution.py:37
  31.6 1.2 %collective-permute-done.13 = bf16[2,32,256]{2,1,0:T(8,128)(2,1)S(1)} collective-permute-done((bf16[2,32,256]{2,1,0:T(8,128)(2,1)S(1)}, bf16[2,32,256]{2,1,0:T(8,128)(2,1)S(1)}, u32[]{:S(2)}, u32[]{:S(2)}) %collective-permute-start.13) | collective-permute-done | bytes 32800 | tf_op jit(solution)/shard_map/ppermute | solution.py:25
  32.8 1.4 %collective-permute-start.16 = (bf16[4,2,32,256]{3,2,1,0:T(8,128)(2,1)S(1)}, bf16[4,2,32,256]{3,2,1,0:T(8,128)(2,1)S(1)}, u32[]{:S(2)}, u32[]{:S(2)}) collective-permute-start(bf16[4,2,32,256]{3,2,1,0:T(8,128)(2,1)S(1)} %pad_maximum_fusion.1.part), channel_id=1, source_target_pairs={{0,6},{1,7},{2,4},{3,5},{4,2},{5,3},{6,0},{7,1},{8,14},{9,15},{10,... | collective-permute-start | bytes 393224 | tf_op jit(solution)/shard_map/ppermute | solution.py:25
  34.4 1.7 %collective-permute-start.14 = (bf16[4,2,32,256]{3,2,1,0:T(8,128)(2,1)S(1)}, bf16[4,2,32,256]{3,2,1,0:T(8,128)(2,1)S(1)}, u32[]{:S(2)}, u32[]{:S(2)}) collective-permute-start(bf16[4,2,32,256]{3,2,1,0:T(8,128)(2,1)S(1)} %pad_maximum_fusion.1.part), channel_id=1, source_target_pairs={{0,5},{1,4},{2,7},{3,6},{4,1},{5,0},{6,3},{7,2},{8,13},{9,12},{10,... | collective-permute-start | bytes 393224 | tf_op jit(solution)/shard_map/ppermute | solution.py:25
  36.1 0.7 shard_map.67.refs_0_
  36.8 2.1 %collective-permute-done.16.part = bf16[4,2,32,256]{3,2,1,0:T(8,128)(2,1)S(1)} collective-permute-done((bf16[4,2,32,256]{3,2,1,0:T(8,128)(2,1)S(1)}, bf16[4,2,32,256]{3,2,1,0:T(8,128)(2,1)S(1)}, u32[]{:S(2)}, u32[]{:S(2)}) %collective-permute-start.16) | collective-permute-done | bytes 131104 | tf_op jit(solution)/shard_map/ppermute | solution.py:25
  38.9 0.7 shard_map.68.refs_0_
  39.6 0.7 shard_map.69.refs_1_
  40.3 0.8 shard_map.70.after.known.refs_5_
  41.2 2.0 %collective-permute-start.18 = (bf16[2,32,256]{2,1,0:T(8,128)(2,1)S(1)}, bf16[2,32,256]{2,1,0:T(8,128)(2,1)S(1)}, u32[]{:S(2)}, u32[]{:S(2)}) collective-permute-start(bf16[2,32,256]{2,1,0:T(8,128)(2,1)S(1)} %shard_map.70.after.known.refs_5_), channel_id=1, source_target_pairs={{0,16},{1,17},{2,18},{3,19},{4,20},{5,21},{6,22},{7,23},{8,24},{9,... | collective-permute-start | bytes 98312 | tf_op jit(solution)/shard_map/ppermute | solution.py:25
  43.2 1.8 %collective-permute-start.19 = (bf16[2,32,256]{2,1,0:T(8,128)(2,1)S(1)}, bf16[2,32,256]{2,1,0:T(8,128)(2,1)S(1)}, u32[]{:S(2)}, u32[]{:S(2)}) collective-permute-start(bf16[2,32,256]{2,1,0:T(8,128)(2,1)S(1)} %shard_map.70.after.known.refs_5_), channel_id=1, source_target_pairs={{0,25},{1,24},{2,27},{3,26},{4,29},{5,28},{6,31},{7,30},{8,17},{9,... | collective-permute-start | bytes 98312 | tf_op jit(solution)/shard_map/ppermute | solution.py:25
  45.0 2.8 %shard_map.71 = (bf16[2,32,256,256]{3,2,1,0:T(8,128)(2,1)S(1)}, bf16[1,2,256,256]{3,2,1,0:T(8,128)(2,1)S(1)}) custom-call(s32[3,1,16]{2,1,0:T(1,128)} %own_pattern.5, s32[3,1,16]{2,1,0:T(1,128)S(1)} %collective-permute-done.1.other_pattern, bf16[2,32,256]{2,1,0:T(8,128)(2,1)S(1)} %shard_map.70.after.known.refs_5_, bf16[3,1,16,256,256]{4,3,2,1,0:T(8,128)(2,1)} %tiles0.5, ...), custom_call_target="tpu_custom_call" | custom-call | flops 134217728 | tf_op jit(solution)/shard_map/pallas_call | solution.py:37
  48.3 2.1 %collective-permute-start.22 = (bf16[4,2,32,256]{3,2,1,0:T(8,128)(2,1)S(1)}, bf16[4,2,32,256]{3,2,1,0:T(8,128)(2,1)S(1)}, u32[]{:S(2)}, u32[]{:S(2)}) collective-permute-start(bf16[4,2,32,256]{3,2,1,0:T(8,128)(2,1)S(1)} %pad_maximum_fusion.2.part), channel_id=1, source_target_pairs={{0,6},{1,7},{2,4},{3,5},{4,2},{5,3},{6,0},{7,1},{8,14},{9,15},{10,... | collective-permute-start | bytes 393224 | tf_op jit(solution)/shard_map/ppermute | solution.py:25
  50.5 1.1 %collective-permute-start.20 = (bf16[4,2,32,256]{3,2,1,0:T(8,128)(2,1)S(1)}, bf16[4,2,32,256]{3,2,1,0:T(8,128)(2,1)S(1)}, u32[]{:S(2)}, u32[]{:S(2)}) collective-permute-start(bf16[4,2,32,256]{3,2,1,0:T(8,128)(2,1)S(1)} %pad_maximum_fusion.2.part), channel_id=1, source_target_pairs={{0,5},{1,4},{2,7},{3,6},{4,1},{5,0},{6,3},{7,2},{8,13},{9,12},{10,... | collective-permute-start | bytes 393224 | tf_op jit(solution)/shard_map/ppermute | solution.py:25
  51.6 0.7 shard_map.72.refs_0_
  52.3 2.0 %collective-permute-done.22.part = bf16[4,2,32,256]{3,2,1,0:T(8,128)(2,1)S(1)} collective-permute-done((bf16[4,2,32,256]{3,2,1,0:T(8,128)(2,1)S(1)}, bf16[4,2,32,256]{3,2,1,0:T(8,128)(2,1)S(1)}, u32[]{:S(2)}, u32[]{:S(2)}) %collective-permute-start.22) | collective-permute-done | bytes 131104 | tf_op jit(solution)/shard_map/ppermute | solution.py:25
  54.3 0.7 shard_map.73.refs_0_
  55.1 0.7 shard_map.74.refs_1_
  55.8 2.1 %shard_map.75 = (bf16[2,32,256]{2,1,0:T(8,128)(2,1)S(1)}, bf16[2,32,256]{2,1,0:T(8,128)(2,1)S(1)}, bf16[4,2,32,256]{3,2,1,0:T(8,128)(2,1)S(1)}, bf16[4,2,32,256]...) custom-call(bf16[2,32,256,256]{3,2,1,0:T(8,128)(2,1)S(1)} %get-tuple-element.73.spread, ...), custom_call_target="tpu_custom_call" | custom-call | flops 268435456 | tf_op jit(solution)/shard_map/pallas_call | solution.py:37
  57.9 2.0 %collective-permute-start.23 = (bf16[4,2,32,256]{3,2,1,0:T(8,128)(2,1)S(1)}, bf16[4,2,32,256]{3,2,1,0:T(8,128)(2,1)S(1)}, u32[]{:S(2)}, u32[]{:S(2)}) collective-permute-start(bf16[4,2,32,256]{3,2,1,0:T(8,128)(2,1)S(1)} %get-tuple-element.80), channel_id=1, source_target_pairs={{0,6},{1,7},{2,4},{3,5},{4,2},{5,3},{6,0},{7,1},{8,14},{9,15},{10,... | collective-permute-start | bytes 393224 | tf_op jit(solution)/shard_map/ppermute | solution.py:25
  59.9 1.2 %collective-permute-start.25 = (bf16[4,2,32,256]{3,2,1,0:T(8,128)(2,1)S(1)}, bf16[4,2,32,256]{3,2,1,0:T(8,128)(2,1)S(1)}, u32[]{:S(2)}, u32[]{:S(2)}) collective-permute-start(bf16[4,2,32,256]{3,2,1,0:T(8,128)(2,1)S(1)} %get-tuple-element.82), channel_id=1, source_target_pairs={{0,5},{1,4},{2,7},{3,6},{4,1},{5,0},{6,3},{7,2},{8,13},{9,12},{10,... | collective-permute-start | bytes 393224 | tf_op jit(solution)/shard_map/ppermute | solution.py:25
  61.6 2.3 %collective-permute-done.23.a = bf16[4,2,32,256]{3,2,1,0:T(8,128)(2,1)S(1)} collective-permute-done((bf16[4,2,32,256]{3,2,1,0:T(8,128)(2,1)S(1)}, bf16[4,2,32,256]{3,2,1,0:T(8,128)(2,1)S(1)}, u32[]{:S(2)}, u32[]{:S(2)}) %collective-permute-start.23) | collective-permute-done | bytes 131104 | tf_op jit(solution)/shard_map/ppermute | solution.py:25
  64.3 0.9 collective-permute-done.25.c
  65.3 1.8 %collective-permute-start.27 = (bf16[2,32,256]{2,1,0:T(8,128)(2,1)S(1)}, bf16[2,32,256]{2,1,0:T(8,128)(2,1)S(1)}, u32[]{:S(2)}, u32[]{:S(2)}) collective-permute-start(bf16[2,32,256]{2,1,0:T(8,128)(2,1)S(1)} %get-tuple-element.85), channel_id=1, source_target_pairs={{0,16},{1,17},{2,18},{3,19},{4,20},{5,21},{6,22},{7,23},{8,24},{9,... | collective-permute-start | bytes 98312 | tf_op jit(solution)/shard_map/ppermute | solution.py:25
  67.1 2.0 %collective-permute-start.28 = (bf16[2,32,256]{2,1,0:T(8,128)(2,1)S(1)}, bf16[2,32,256]{2,1,0:T(8,128)(2,1)S(1)}, u32[]{:S(2)}, u32[]{:S(2)}) collective-permute-start(bf16[2,32,256]{2,1,0:T(8,128)(2,1)S(1)} %get-tuple-element.86), channel_id=1, source_target_pairs={{0,25},{1,24},{2,27},{3,26},{4,29},{5,28},{6,31},{7,30},{8,17},{9,... | collective-permute-start | bytes 98312 | tf_op jit(solution)/shard_map/ppermute | solution.py:25
  69.2 1.1 collective-permute-done.27.refs_1_
  70.2 2.0 %collective-permute-done.28.refs_2_ = bf16[2,32,256]{2,1,0:T(8,128)(2,1)S(1)} collective-permute-done((bf16[2,32,256]{2,1,0:T(8,128)(2,1)S(1)}, bf16[2,32,256]{2,1,0:T(8,128)(2,1)S(1)}, u32[]{:S(2)}, u32[]{:S(2)}) %collective-permute-start.28) | collective-permute-done | bytes 32800 | tf_op jit(solution)/shard_map/ppermute | solution.py:25
  72.3 1.3 %shard_map.78 = (bf16[2,32,256]{2,1,0:T(8,128)(2,1)S(1)}, bf16[4,2,32,256]{3,2,1,0:T(8,128)(2,1)S(1)}, bf16[4,2,32,256]{3,2,1,0:T(8,128)(2,1)S(1)}, bf16[4,2,32,256]{3,2,1,0:T(8,128)(2,1)S(1)}) custom-call(bf16[2,32,256,256]{3,2,1,0:T(8,128)(2,1)S(1)} %get-tuple-element.66.spread, f32[2,32,256]{2,1,0:T(8,128)S(1)} %get-tuple-element.83.own, ...), custom_call_target="tpu_custom_call" | custom-call | flops 201326592 | tf_op jit(solution)/shard_map/pallas_call | solution.py:37
  73.6 1.5 %collective-permute-start.29 = (bf16[4,2,32,256]{3,2,1,0:T(8,128)(2,1)S(1)}, bf16[4,2,32,256]{3,2,1,0:T(8,128)(2,1)S(1)}, u32[]{:S(2)}, u32[]{:S(2)}) collective-permute-start(bf16[4,2,32,256]{3,2,1,0:T(8,128)(2,1)S(1)} %get-tuple-element.88), channel_id=1, source_target_pairs={{0,6},{1,7},{2,4},{3,5},{4,2},{5,3},{6,0},{7,1},{8,14},{9,15},{10,... | collective-permute-start | bytes 393224 | tf_op jit(solution)/shard_map/ppermute | solution.py:25
  75.1 1.1 collective-permute-start.30
  77.3 2.2 %collective-permute-done.29.a = bf16[4,2,32,256]{3,2,1,0:T(8,128)(2,1)S(1)} collective-permute-done((bf16[4,2,32,256]{3,2,1,0:T(8,128)(2,1)S(1)}, bf16[4,2,32,256]{3,2,1,0:T(8,128)(2,1)S(1)}, u32[]{:S(2)}, u32[]{:S(2)}) %collective-permute-start.29) | collective-permute-done | bytes 131104 | tf_op jit(solution)/shard_map/ppermute | solution.py:25
  79.5 0.7 collective-permute-done.30.b
  80.2 0.6 collective-permute-done.31.c
  81.0 1.8 %collective-permute-start.33 = (bf16[2,32,256]{2,1,0:T(8,128)(2,1)S(1)}, bf16[2,32,256]{2,1,0:T(8,128)(2,1)S(1)}, u32[]{:S(2)}, u32[]{:S(2)}) collective-permute-start(bf16[2,32,256]{2,1,0:T(8,128)(2,1)S(1)} %get-tuple-element.93), channel_id=1, source_target_pairs={{0,16},{1,17},{2,18},{3,19},{4,20},{5,21},{6,22},{7,23},{8,24},{9,... | collective-permute-start | bytes 98312 | tf_op jit(solution)/shard_map/ppermute | solution.py:25
  82.8 2.0 %collective-permute-start.34 = (bf16[2,32,256]{2,1,0:T(8,128)(2,1)S(1)}, bf16[2,32,256]{2,1,0:T(8,128)(2,1)S(1)}, u32[]{:S(2)}, u32[]{:S(2)}) collective-permute-start(bf16[2,32,256]{2,1,0:T(8,128)(2,1)S(1)} %get-tuple-element.94), channel_id=1, source_target_pairs={{0,25},{1,24},{2,27},{3,26},{4,29},{5,28},{6,31},{7,30},{8,17},{9,... | collective-permute-start | bytes 98312 | tf_op jit(solution)/shard_map/ppermute | solution.py:25
  84.8 1.1 collective-permute-done.33.refs_1_
  85.9 2.0 %collective-permute-done.34.refs_2_ = bf16[2,32,256]{2,1,0:T(8,128)(2,1)S(1)} collective-permute-done((bf16[2,32,256]{2,1,0:T(8,128)(2,1)S(1)}, bf16[2,32,256]{2,1,0:T(8,128)(2,1)S(1)}, u32[]{:S(2)}, u32[]{:S(2)}) %collective-permute-start.34) | collective-permute-done | bytes 32800 | tf_op jit(solution)/shard_map/ppermute | solution.py:25
  87.9 1.3 %shard_map.81 = (bf16[2,32,256]{2,1,0:T(8,128)(2,1)S(1)}, bf16[4,2,32,256]{3,2,1,0:T(8,128)(2,1)S(1)}, bf16[4,2,32,256]{3,2,1,0:T(8,128)(2,1)S(1)}, bf16[4,2,32,256]{3,2,1,0:T(8,128)(2,1)S(1)}) custom-call(bf16[2,32,256,256]{3,2,1,0:T(8,128)(2,1)S(1)} %get-tuple-element.61.spread, f32[2,32,256]{2,1,0:T(8,128)S(1)} %get-tuple-element.91.own, ...), custom_call_target="tpu_custom_call" | custom-call | flops 201326592 | tf_op jit(solution)/shard_map/pallas_call | solution.py:37
  89.3 2.0 %collective-permute-start.35 = (bf16[4,2,32,256]{3,2,1,0:T(8,128)(2,1)S(1)}, bf16[4,2,32,256]{3,2,1,0:T(8,128)(2,1)S(1)}, u32[]{:S(2)}, u32[]{:S(2)}) collective-permute-start(bf16[4,2,32,256]{3,2,1,0:T(8,128)(2,1)S(1)} %get-tuple-element.96), channel_id=1, source_target_pairs={{0,6},{1,7},{2,4},{3,5},{4,2},{5,3},{6,0},{7,1},{8,14},{9,15},{10,... | collective-permute-start | bytes 393224 | tf_op jit(solution)/shard_map/ppermute | solution.py:25
  91.6 0.9 collective-permute-start.37
  93.0 2.3 %collective-permute-done.35.a = bf16[4,2,32,256]{3,2,1,0:T(8,128)(2,1)S(1)} collective-permute-done((bf16[4,2,32,256]{3,2,1,0:T(8,128)(2,1)S(1)}, bf16[4,2,32,256]{3,2,1,0:T(8,128)(2,1)S(1)}, u32[]{:S(2)}, u32[]{:S(2)}) %collective-permute-start.35) | collective-permute-done | bytes 131104 | tf_op jit(solution)/shard_map/ppermute | solution.py:25
  95.7 0.9 collective-permute-done.37.c
  96.7 1.8 %collective-permute-start.39 = (bf16[2,32,256]{2,1,0:T(8,128)(2,1)S(1)}, bf16[2,32,256]{2,1,0:T(8,128)(2,1)S(1)}, u32[]{:S(2)}, u32[]{:S(2)}) collective-permute-start(bf16[2,32,256]{2,1,0:T(8,128)(2,1)S(1)} %get-tuple-element.101), channel_id=1, source_target_pairs={{0,16},{1,17},{2,18},{3,19},{4,20},{5,21},{6,22},{7,23},{8,24},{9,... | collective-permute-start | bytes 98312 | tf_op jit(solution)/shard_map/ppermute | solution.py:25
  98.5 2.0 %collective-permute-start.40 = (bf16[2,32,256]{2,1,0:T(8,128)(2,1)S(1)}, bf16[2,32,256]{2,1,0:T(8,128)(2,1)S(1)}, u32[]{:S(2)}, u32[]{:S(2)}) collective-permute-start(bf16[2,32,256]{2,1,0:T(8,128)(2,1)S(1)} %get-tuple-element.102), channel_id=1, source_target_pairs={{0,25},{1,24},{2,27},{3,26},{4,29},{5,28},{6,31},{7,30},{8,17},{9,... | collective-permute-start | bytes 98312 | tf_op jit(solution)/shard_map/ppermute | solution.py:25
  100.5 1.1 collective-permute-done.39.refs_1_
  101.6 2.0 %collective-permute-done.40.refs_2_ = bf16[2,32,256]{2,1,0:T(8,128)(2,1)S(1)} collective-permute-done((bf16[2,32,256]{2,1,0:T(8,128)(2,1)S(1)}, bf16[2,32,256]{2,1,0:T(8,128)(2,1)S(1)}, u32[]{:S(2)}, u32[]{:S(2)}) %collective-permute-start.40) | collective-permute-done | bytes 32800 | tf_op jit(solution)/shard_map/ppermute | solution.py:25
  103.8 5.2 %collective-permute-start.41 = (bf16[8,32,256]{2,1,0:T(8,128)(2,1)S(1)}, bf16[8,32,256]{2,1,0:T(8,128)(2,1)S(1)}, u32[]{:S(2)}, u32[]{:S(2)}) collective-permute-start(bf16[8,32,256]{2,1,0:T(8,128)(2,1)S(1)} %get-tuple-element.105), channel_id=1, source_target_pairs={{0,1},{1,0},{2,3},{3,2},{4,5},{5,4},{6,7},{7,6},{8,9},{9,8},{10,11... | collective-permute-start | bytes 393224 | tf_op jit(solution)/shard_map/ppermute | solution.py:25
  109.0 1.0 collective-permute-done.41.other
  110.0 0.7 shard_map.85
  (54 shorter events, 7.0 us)
Async XLA Ops:
  1.8 1.9 %collective-permute-start = (bf16[32,256]{1,0:T(8,128)(2,1)S(1)}, bf16[32,256]{1,0:T(8,128)(2,1)S(1)}, u32[]{:S(2)}, u32[]{:S(2)}) collective-permute-start(bf16[32,256]{1,0:T(8,128)(2,1)S(1)} %get-tuple-element.54.after), channel_id=1, source_target_pairs={{0,1},{1,0},{2,3},{3,2},{4,5},{5,4},{6,7},{7,6},{8,9},{9,8},{10,11... | collective-permute-start | bytes 49160 | tf_op jit(solution)/shard_map/ppermute | solution.py:25
  2.3 1.4 %collective-permute-start.1 = (s32[3,1,16]{2,1,0:T(1,128)}, s32[3,1,16]{2,1,0:T(1,128)S(1)}, u32[]{:S(2)}, u32[]{:S(2)}) collective-permute-start(s32[3,1,16]{2,1,0:T(1,128)} %own_pattern.5), channel_id=1, source_target_pairs={{0,1},{1,0},{2,3},{3,2},{4,5},{5,4},{6,7},{7,6},{8,9},{9,8},{10,11... | collective-permute-start | bytes 584 | tf_op jit(solution)/shard_map/ppermute | solution.py:25
  2.4 0.9 copy-start
  3.7 14.5 %collective-permute-start.2 = (bf16[3,1,16,256,256]{4,3,2,1,0:T(8,128)(2,1)}, bf16[3,1,16,256,256]{4,3,2,1,0:T(8,128)(2,1)S(1)}, u32[]{:S(2)}, u32[]{:S(2)}) collective-permute-start(bf16[3,1,16,256,256]{4,3,2,1,0:T(8,128)(2,1)} %tiles0.5), channel_id=1, source_target_pairs={{0,1},{1,0},{2,3},{3,2},{4,5},{5,4},{6,7},{7,6},{8,9},{9,8},{10,11... | collective-permute-start | bytes 18874376 | tf_op jit(solution)/shard_map/ppermute | solution.py:25
  3.8 13.6 %collective-permute-start.3 = (bf16[4,1,256,256]{3,2,1,0:T(8,128)(2,1)}, bf16[4,1,256,256]{3,2,1,0:T(8,128)(2,1)S(1)}, u32[]{:S(2)}, u32[]{:S(2)}) collective-permute-start(bf16[4,1,256,256]{3,2,1,0:T(8,128)(2,1)} %diag0.5), channel_id=1, source_target_pairs={{0,1},{1,0},{2,3},{3,2},{4,5},{5,4},{6,7},{7,6},{8,9},{9,8},{10,11... | collective-permute-start | bytes 1572872 | tf_op jit(solution)/shard_map/ppermute | solution.py:25
  4.2 5.3 %collective-permute-start.5 = (bf16[2,32,256]{2,1,0:T(8,128)(2,1)S(1)}, bf16[2,32,256]{2,1,0:T(8,128)(2,1)S(1)}, u32[]{:S(2)}, u32[]{:S(2)}) collective-permute-start(bf16[2,32,256]{2,1,0:T(8,128)(2,1)S(1)} %get-tuple-element.109.after.known.refs_3_), channel_id=1, source_target_pairs={{0,9},{1,8},{2,11},{3,10},{4,13},{5,12},{6,15},{7,14},{8,1},{9,0},... | collective-permute-start | bytes 98312 | tf_op jit(solution)/shard_map/ppermute | solution.py:25
  6.9 5.2 %collective-permute-start.6 = (bf16[2,32,256]{2,1,0:T(8,128)(2,1)S(1)}, bf16[2,32,256]{2,1,0:T(8,128)(2,1)S(1)}, u32[]{:S(2)}, u32[]{:S(2)}) collective-permute-start(bf16[2,32,256]{2,1,0:T(8,128)(2,1)S(1)} %get-tuple-element.109.after.known.refs_3_), channel_id=1, source_target_pairs={{0,16},{1,17},{2,18},{3,19},{4,20},{5,21},{6,22},{7,23},{8,24},{9,... | collective-permute-start | bytes 98312 | tf_op jit(solution)/shard_map/ppermute | solution.py:25
  9.4 5.4 %collective-permute-start.7 = (bf16[2,32,256]{2,1,0:T(8,128)(2,1)S(1)}, bf16[2,32,256]{2,1,0:T(8,128)(2,1)S(1)}, u32[]{:S(2)}, u32[]{:S(2)}) collective-permute-start(bf16[2,32,256]{2,1,0:T(8,128)(2,1)S(1)} %get-tuple-element.109.after.known.refs_3_), channel_id=1, source_target_pairs={{0,25},{1,24},{2,27},{3,26},{4,29},{5,28},{6,31},{7,30},{8,17},{9,... | collective-permute-start | bytes 98312 | tf_op jit(solution)/shard_map/ppermute | solution.py:25
  9.5 14.7 %collective-permute-start.4 = (bf16[4,32,256]{2,1,0:T(8,128)(2,1)S(1)}, bf16[4,32,256]{2,1,0:T(8,128)(2,1)S(1)}, u32[]{:S(2)}, u32[]{:S(2)}) collective-permute-start(bf16[4,32,256]{2,1,0:T(8,128)(2,1)S(1)} %get-tuple-element.63), channel_id=1, source_target_pairs={{0,1},{1,0},{2,3},{3,2},{4,5},{5,4},{6,7},{7,6},{8,9},{9,8},{10,11... | collective-permute-start | bytes 196616 | tf_op jit(solution)/shard_map/ppermute | solution.py:25
  14.9 7.3 %collective-permute-start.10 = (bf16[4,2,32,256]{3,2,1,0:T(8,128)(2,1)S(1)}, bf16[4,2,32,256]{3,2,1,0:T(8,128)(2,1)S(1)}, u32[]{:S(2)}, u32[]{:S(2)}) collective-permute-start(bf16[4,2,32,256]{3,2,1,0:T(8,128)(2,1)S(1)} %pad_maximum_fusion.part), channel_id=1, source_target_pairs={{0,6},{1,7},{2,4},{3,5},{4,2},{5,3},{6,0},{7,1},{8,14},{9,15},{10,... | collective-permute-start | bytes 393224 | tf_op jit(solution)/shard_map/ppermute | solution.py:25
  17.4 6.0 %collective-permute-start.9 = (bf16[4,2,32,256]{3,2,1,0:T(8,128)(2,1)S(1)}, bf16[4,2,32,256]{3,2,1,0:T(8,128)(2,1)S(1)}, u32[]{:S(2)}, u32[]{:S(2)}) collective-permute-start(bf16[4,2,32,256]{3,2,1,0:T(8,128)(2,1)S(1)} %pad_maximum_fusion.part), channel_id=1, source_target_pairs={{0,3},{1,2},{2,1},{3,0},{4,7},{5,6},{6,5},{7,4},{8,11},{9,10},{10,... | collective-permute-start | bytes 393224 | tf_op jit(solution)/shard_map/ppermute | solution.py:25
  17.4 6.7 %collective-permute-start.8 = (bf16[4,2,32,256]{3,2,1,0:T(8,128)(2,1)S(1)}, bf16[4,2,32,256]{3,2,1,0:T(8,128)(2,1)S(1)}, u32[]{:S(2)}, u32[]{:S(2)}) collective-permute-start(bf16[4,2,32,256]{3,2,1,0:T(8,128)(2,1)S(1)} %pad_maximum_fusion.part), channel_id=1, source_target_pairs={{0,5},{1,4},{2,7},{3,6},{4,1},{5,0},{6,3},{7,2},{8,13},{9,12},{10,... | collective-permute-start | bytes 393224 | tf_op jit(solution)/shard_map/ppermute | solution.py:25
  25.0 6.7 %collective-permute-start.11 = (bf16[2,32,256]{2,1,0:T(8,128)(2,1)S(1)}, bf16[2,32,256]{2,1,0:T(8,128)(2,1)S(1)}, u32[]{:S(2)}, u32[]{:S(2)}) collective-permute-start(bf16[2,32,256]{2,1,0:T(8,128)(2,1)S(1)} %shard_map.65.after.known.refs_4_), channel_id=1, source_target_pairs={{0,9},{1,8},{2,11},{3,10},{4,13},{5,12},{6,15},{7,14},{8,1},{9,0},... | collective-permute-start | bytes 98312 | tf_op jit(solution)/shard_map/ppermute | solution.py:25
  25.0 6.6 %collective-permute-start.12 = (bf16[2,32,256]{2,1,0:T(8,128)(2,1)S(1)}, bf16[2,32,256]{2,1,0:T(8,128)(2,1)S(1)}, u32[]{:S(2)}, u32[]{:S(2)}) collective-permute-start(bf16[2,32,256]{2,1,0:T(8,128)(2,1)S(1)} %shard_map.65.after.known.refs_4_), channel_id=1, source_target_pairs={{0,16},{1,17},{2,18},{3,19},{4,20},{5,21},{6,22},{7,23},{8,24},{9,... | collective-permute-start | bytes 98312 | tf_op jit(solution)/shard_map/ppermute | solution.py:25
  27.6 5.2 %collective-permute-start.13 = (bf16[2,32,256]{2,1,0:T(8,128)(2,1)S(1)}, bf16[2,32,256]{2,1,0:T(8,128)(2,1)S(1)}, u32[]{:S(2)}, u32[]{:S(2)}) collective-permute-start(bf16[2,32,256]{2,1,0:T(8,128)(2,1)S(1)} %shard_map.65.after.known.refs_4_), channel_id=1, source_target_pairs={{0,25},{1,24},{2,27},{3,26},{4,29},{5,28},{6,31},{7,30},{8,17},{9,... | collective-permute-start | bytes 98312 | tf_op jit(solution)/shard_map/ppermute | solution.py:25
  32.8 6.0 %collective-permute-start.16 = (bf16[4,2,32,256]{3,2,1,0:T(8,128)(2,1)S(1)}, bf16[4,2,32,256]{3,2,1,0:T(8,128)(2,1)S(1)}, u32[]{:S(2)}, u32[]{:S(2)}) collective-permute-start(bf16[4,2,32,256]{3,2,1,0:T(8,128)(2,1)S(1)} %pad_maximum_fusion.1.part), channel_id=1, source_target_pairs={{0,6},{1,7},{2,4},{3,5},{4,2},{5,3},{6,0},{7,1},{8,14},{9,15},{10,... | collective-permute-start | bytes 393224 | tf_op jit(solution)/shard_map/ppermute | solution.py:25
  34.2 5.3 %collective-permute-start.15 = (bf16[4,2,32,256]{3,2,1,0:T(8,128)(2,1)S(1)}, bf16[4,2,32,256]{3,2,1,0:T(8,128)(2,1)S(1)}, u32[]{:S(2)}, u32[]{:S(2)}) collective-permute-start(bf16[4,2,32,256]{3,2,1,0:T(8,128)(2,1)S(1)} %pad_maximum_fusion.1.part), channel_id=1, source_target_pairs={{0,3},{1,2},{2,1},{3,0},{4,7},{5,6},{6,5},{7,4},{8,11},{9,10},{10,... | collective-permute-start | bytes 393224 | tf_op jit(solution)/shard_map/ppermute | solution.py:25
  34.4 5.9 %collective-permute-start.14 = (bf16[4,2,32,256]{3,2,1,0:T(8,128)(2,1)S(1)}, bf16[4,2,32,256]{3,2,1,0:T(8,128)(2,1)S(1)}, u32[]{:S(2)}, u32[]{:S(2)}) collective-permute-start(bf16[4,2,32,256]{3,2,1,0:T(8,128)(2,1)S(1)} %pad_maximum_fusion.1.part), channel_id=1, source_target_pairs={{0,5},{1,4},{2,7},{3,6},{4,1},{5,0},{6,3},{7,2},{8,13},{9,12},{10,... | collective-permute-start | bytes 393224 | tf_op jit(solution)/shard_map/ppermute | solution.py:25
  41.2 6.7 %collective-permute-start.17 = (bf16[2,32,256]{2,1,0:T(8,128)(2,1)S(1)}, bf16[2,32,256]{2,1,0:T(8,128)(2,1)S(1)}, u32[]{:S(2)}, u32[]{:S(2)}) collective-permute-start(bf16[2,32,256]{2,1,0:T(8,128)(2,1)S(1)} %shard_map.70.after.known.refs_5_), channel_id=1, source_target_pairs={{0,9},{1,8},{2,11},{3,10},{4,13},{5,12},{6,15},{7,14},{8,1},{9,0},... | collective-permute-start | bytes 98312 | tf_op jit(solution)/shard_map/ppermute | solution.py:25
  41.2 6.6 %collective-permute-start.18 = (bf16[2,32,256]{2,1,0:T(8,128)(2,1)S(1)}, bf16[2,32,256]{2,1,0:T(8,128)(2,1)S(1)}, u32[]{:S(2)}, u32[]{:S(2)}) collective-permute-start(bf16[2,32,256]{2,1,0:T(8,128)(2,1)S(1)} %shard_map.70.after.known.refs_5_), channel_id=1, source_target_pairs={{0,16},{1,17},{2,18},{3,19},{4,20},{5,21},{6,22},{7,23},{8,24},{9,... | collective-permute-start | bytes 98312 | tf_op jit(solution)/shard_map/ppermute | solution.py:25
  43.2 5.1 %collective-permute-start.19 = (bf16[2,32,256]{2,1,0:T(8,128)(2,1)S(1)}, bf16[2,32,256]{2,1,0:T(8,128)(2,1)S(1)}, u32[]{:S(2)}, u32[]{:S(2)}) collective-permute-start(bf16[2,32,256]{2,1,0:T(8,128)(2,1)S(1)} %shard_map.70.after.known.refs_5_), channel_id=1, source_target_pairs={{0,25},{1,24},{2,27},{3,26},{4,29},{5,28},{6,31},{7,30},{8,17},{9,... | collective-permute-start | bytes 98312 | tf_op jit(solution)/shard_map/ppermute | solution.py:25
  48.3 6.0 %collective-permute-start.22 = (bf16[4,2,32,256]{3,2,1,0:T(8,128)(2,1)S(1)}, bf16[4,2,32,256]{3,2,1,0:T(8,128)(2,1)S(1)}, u32[]{:S(2)}, u32[]{:S(2)}) collective-permute-start(bf16[4,2,32,256]{3,2,1,0:T(8,128)(2,1)S(1)} %pad_maximum_fusion.2.part), channel_id=1, source_target_pairs={{0,6},{1,7},{2,4},{3,5},{4,2},{5,3},{6,0},{7,1},{8,14},{9,15},{10,... | collective-permute-start | bytes 393224 | tf_op jit(solution)/shard_map/ppermute | solution.py:25
  50.4 4.7 %collective-permute-start.21 = (bf16[4,2,32,256]{3,2,1,0:T(8,128)(2,1)S(1)}, bf16[4,2,32,256]{3,2,1,0:T(8,128)(2,1)S(1)}, u32[]{:S(2)}, u32[]{:S(2)}) collective-permute-start(bf16[4,2,32,256]{3,2,1,0:T(8,128)(2,1)S(1)} %pad_maximum_fusion.2.part), channel_id=1, source_target_pairs={{0,3},{1,2},{2,1},{3,0},{4,7},{5,6},{6,5},{7,4},{8,11},{9,10},{10,... | collective-permute-start | bytes 393224 | tf_op jit(solution)/shard_map/ppermute | solution.py:25
  50.5 5.3 %collective-permute-start.20 = (bf16[4,2,32,256]{3,2,1,0:T(8,128)(2,1)S(1)}, bf16[4,2,32,256]{3,2,1,0:T(8,128)(2,1)S(1)}, u32[]{:S(2)}, u32[]{:S(2)}) collective-permute-start(bf16[4,2,32,256]{3,2,1,0:T(8,128)(2,1)S(1)} %pad_maximum_fusion.2.part), channel_id=1, source_target_pairs={{0,5},{1,4},{2,7},{3,6},{4,1},{5,0},{6,3},{7,2},{8,13},{9,12},{10,... | collective-permute-start | bytes 393224 | tf_op jit(solution)/shard_map/ppermute | solution.py:25
  57.9 6.0 %collective-permute-start.23 = (bf16[4,2,32,256]{3,2,1,0:T(8,128)(2,1)S(1)}, bf16[4,2,32,256]{3,2,1,0:T(8,128)(2,1)S(1)}, u32[]{:S(2)}, u32[]{:S(2)}) collective-permute-start(bf16[4,2,32,256]{3,2,1,0:T(8,128)(2,1)S(1)} %get-tuple-element.80), channel_id=1, source_target_pairs={{0,6},{1,7},{2,4},{3,5},{4,2},{5,3},{6,0},{7,1},{8,14},{9,15},{10,... | collective-permute-start | bytes 393224 | tf_op jit(solution)/shard_map/ppermute | solution.py:25
  59.9 4.4 %collective-permute-start.24 = (bf16[4,2,32,256]{3,2,1,0:T(8,128)(2,1)S(1)}, bf16[4,2,32,256]{3,2,1,0:T(8,128)(2,1)S(1)}, u32[]{:S(2)}, u32[]{:S(2)}) collective-permute-start(bf16[4,2,32,256]{3,2,1,0:T(8,128)(2,1)S(1)} %get-tuple-element.81), channel_id=1, source_target_pairs={{0,3},{1,2},{2,1},{3,0},{4,7},{5,6},{6,5},{7,4},{8,11},{9,10},{10,... | collective-permute-start | bytes 393224 | tf_op jit(solution)/shard_map/ppermute | solution.py:25
  59.9 5.3 %collective-permute-start.25 = (bf16[4,2,32,256]{3,2,1,0:T(8,128)(2,1)S(1)}, bf16[4,2,32,256]{3,2,1,0:T(8,128)(2,1)S(1)}, u32[]{:S(2)}, u32[]{:S(2)}) collective-permute-start(bf16[4,2,32,256]{3,2,1,0:T(8,128)(2,1)S(1)} %get-tuple-element.82), channel_id=1, source_target_pairs={{0,5},{1,4},{2,7},{3,6},{4,1},{5,0},{6,3},{7,2},{8,13},{9,12},{10,... | collective-permute-start | bytes 393224 | tf_op jit(solution)/shard_map/ppermute | solution.py:25
  65.3 3.9 %collective-permute-start.26 = (bf16[2,32,256]{2,1,0:T(8,128)(2,1)S(1)}, bf16[2,32,256]{2,1,0:T(8,128)(2,1)S(1)}, u32[]{:S(2)}, u32[]{:S(2)}) collective-permute-start(bf16[2,32,256]{2,1,0:T(8,128)(2,1)S(1)} %get-tuple-element.84), channel_id=1, source_target_pairs={{0,9},{1,8},{2,11},{3,10},{4,13},{5,12},{6,15},{7,14},{8,1},{9,0},... | collective-permute-start | bytes 98312 | tf_op jit(solution)/shard_map/ppermute | solution.py:25
  65.3 4.9 %collective-permute-start.27 = (bf16[2,32,256]{2,1,0:T(8,128)(2,1)S(1)}, bf16[2,32,256]{2,1,0:T(8,128)(2,1)S(1)}, u32[]{:S(2)}, u32[]{:S(2)}) collective-permute-start(bf16[2,32,256]{2,1,0:T(8,128)(2,1)S(1)} %get-tuple-element.85), channel_id=1, source_target_pairs={{0,16},{1,17},{2,18},{3,19},{4,20},{5,21},{6,22},{7,23},{8,24},{9,... | collective-permute-start | bytes 98312 | tf_op jit(solution)/shard_map/ppermute | solution.py:25
  67.1 5.1 %collective-permute-start.28 = (bf16[2,32,256]{2,1,0:T(8,128)(2,1)S(1)}, bf16[2,32,256]{2,1,0:T(8,128)(2,1)S(1)}, u32[]{:S(2)}, u32[]{:S(2)}) collective-permute-start(bf16[2,32,256]{2,1,0:T(8,128)(2,1)S(1)} %get-tuple-element.86), channel_id=1, source_target_pairs={{0,25},{1,24},{2,27},{3,26},{4,29},{5,28},{6,31},{7,30},{8,17},{9,... | collective-permute-start | bytes 98312 | tf_op jit(solution)/shard_map/ppermute | solution.py:25
  73.6 5.9 %collective-permute-start.29 = (bf16[4,2,32,256]{3,2,1,0:T(8,128)(2,1)S(1)}, bf16[4,2,32,256]{3,2,1,0:T(8,128)(2,1)S(1)}, u32[]{:S(2)}, u32[]{:S(2)}) collective-permute-start(bf16[4,2,32,256]{3,2,1,0:T(8,128)(2,1)S(1)} %get-tuple-element.88), channel_id=1, source_target_pairs={{0,6},{1,7},{2,4},{3,5},{4,2},{5,3},{6,0},{7,1},{8,14},{9,15},{10,... | collective-permute-start | bytes 393224 | tf_op jit(solution)/shard_map/ppermute | solution.py:25
  75.1 5.1 %collective-permute-start.30 = (bf16[4,2,32,256]{3,2,1,0:T(8,128)(2,1)S(1)}, bf16[4,2,32,256]{3,2,1,0:T(8,128)(2,1)S(1)}, u32[]{:S(2)}, u32[]{:S(2)}) collective-permute-start(bf16[4,2,32,256]{3,2,1,0:T(8,128)(2,1)S(1)} %get-tuple-element.89), channel_id=1, source_target_pairs={{0,3},{1,2},{2,1},{3,0},{4,7},{5,6},{6,5},{7,4},{8,11},{9,10},{10,... | collective-permute-start | bytes 393224 | tf_op jit(solution)/shard_map/ppermute | solution.py:25
  76.2 4.7 %collective-permute-start.31 = (bf16[4,2,32,256]{3,2,1,0:T(8,128)(2,1)S(1)}, bf16[4,2,32,256]{3,2,1,0:T(8,128)(2,1)S(1)}, u32[]{:S(2)}, u32[]{:S(2)}) collective-permute-start(bf16[4,2,32,256]{3,2,1,0:T(8,128)(2,1)S(1)} %get-tuple-element.90), channel_id=1, source_target_pairs={{0,5},{1,4},{2,7},{3,6},{4,1},{5,0},{6,3},{7,2},{8,13},{9,12},{10,... | collective-permute-start | bytes 393224 | tf_op jit(solution)/shard_map/ppermute | solution.py:25
  80.9 3.9 %collective-permute-start.32 = (bf16[2,32,256]{2,1,0:T(8,128)(2,1)S(1)}, bf16[2,32,256]{2,1,0:T(8,128)(2,1)S(1)}, u32[]{:S(2)}, u32[]{:S(2)}) collective-permute-start(bf16[2,32,256]{2,1,0:T(8,128)(2,1)S(1)} %get-tuple-element.92), channel_id=1, source_target_pairs={{0,9},{1,8},{2,11},{3,10},{4,13},{5,12},{6,15},{7,14},{8,1},{9,0},... | collective-permute-start | bytes 98312 | tf_op jit(solution)/shard_map/ppermute | solution.py:25
  81.0 4.9 %collective-permute-start.33 = (bf16[2,32,256]{2,1,0:T(8,128)(2,1)S(1)}, bf16[2,32,256]{2,1,0:T(8,128)(2,1)S(1)}, u32[]{:S(2)}, u32[]{:S(2)}) collective-permute-start(bf16[2,32,256]{2,1,0:T(8,128)(2,1)S(1)} %get-tuple-element.93), channel_id=1, source_target_pairs={{0,16},{1,17},{2,18},{3,19},{4,20},{5,21},{6,22},{7,23},{8,24},{9,... | collective-permute-start | bytes 98312 | tf_op jit(solution)/shard_map/ppermute | solution.py:25
  82.8 5.1 %collective-permute-start.34 = (bf16[2,32,256]{2,1,0:T(8,128)(2,1)S(1)}, bf16[2,32,256]{2,1,0:T(8,128)(2,1)S(1)}, u32[]{:S(2)}, u32[]{:S(2)}) collective-permute-start(bf16[2,32,256]{2,1,0:T(8,128)(2,1)S(1)} %get-tuple-element.94), channel_id=1, source_target_pairs={{0,25},{1,24},{2,27},{3,26},{4,29},{5,28},{6,31},{7,30},{8,17},{9,... | collective-permute-start | bytes 98312 | tf_op jit(solution)/shard_map/ppermute | solution.py:25
  89.3 6.0 %collective-permute-start.35 = (bf16[4,2,32,256]{3,2,1,0:T(8,128)(2,1)S(1)}, bf16[4,2,32,256]{3,2,1,0:T(8,128)(2,1)S(1)}, u32[]{:S(2)}, u32[]{:S(2)}) collective-permute-start(bf16[4,2,32,256]{3,2,1,0:T(8,128)(2,1)S(1)} %get-tuple-element.96), channel_id=1, source_target_pairs={{0,6},{1,7},{2,4},{3,5},{4,2},{5,3},{6,0},{7,1},{8,14},{9,15},{10,... | collective-permute-start | bytes 393224 | tf_op jit(solution)/shard_map/ppermute | solution.py:25
  91.3 4.4 %collective-permute-start.36 = (bf16[4,2,32,256]{3,2,1,0:T(8,128)(2,1)S(1)}, bf16[4,2,32,256]{3,2,1,0:T(8,128)(2,1)S(1)}, u32[]{:S(2)}, u32[]{:S(2)}) collective-permute-start(bf16[4,2,32,256]{3,2,1,0:T(8,128)(2,1)S(1)} %get-tuple-element.97), channel_id=1, source_target_pairs={{0,3},{1,2},{2,1},{3,0},{4,7},{5,6},{6,5},{7,4},{8,11},{9,10},{10,... | collective-permute-start | bytes 393224 | tf_op jit(solution)/shard_map/ppermute | solution.py:25
  91.6 5.0 %collective-permute-start.37 = (bf16[4,2,32,256]{3,2,1,0:T(8,128)(2,1)S(1)}, bf16[4,2,32,256]{3,2,1,0:T(8,128)(2,1)S(1)}, u32[]{:S(2)}, u32[]{:S(2)}) collective-permute-start(bf16[4,2,32,256]{3,2,1,0:T(8,128)(2,1)S(1)} %get-tuple-element.98), channel_id=1, source_target_pairs={{0,5},{1,4},{2,7},{3,6},{4,1},{5,0},{6,3},{7,2},{8,13},{9,12},{10,... | collective-permute-start | bytes 393224 | tf_op jit(solution)/shard_map/ppermute | solution.py:25
  96.6 3.9 %collective-permute-start.38 = (bf16[2,32,256]{2,1,0:T(8,128)(2,1)S(1)}, bf16[2,32,256]{2,1,0:T(8,128)(2,1)S(1)}, u32[]{:S(2)}, u32[]{:S(2)}) collective-permute-start(bf16[2,32,256]{2,1,0:T(8,128)(2,1)S(1)} %get-tuple-element.100), channel_id=1, source_target_pairs={{0,9},{1,8},{2,11},{3,10},{4,13},{5,12},{6,15},{7,14},{8,1},{9,0},... | collective-permute-start | bytes 98312 | tf_op jit(solution)/shard_map/ppermute | solution.py:25
  96.7 4.9 %collective-permute-start.39 = (bf16[2,32,256]{2,1,0:T(8,128)(2,1)S(1)}, bf16[2,32,256]{2,1,0:T(8,128)(2,1)S(1)}, u32[]{:S(2)}, u32[]{:S(2)}) collective-permute-start(bf16[2,32,256]{2,1,0:T(8,128)(2,1)S(1)} %get-tuple-element.101), channel_id=1, source_target_pairs={{0,16},{1,17},{2,18},{3,19},{4,20},{5,21},{6,22},{7,23},{8,24},{9,... | collective-permute-start | bytes 98312 | tf_op jit(solution)/shard_map/ppermute | solution.py:25
  98.5 5.1 %collective-permute-start.40 = (bf16[2,32,256]{2,1,0:T(8,128)(2,1)S(1)}, bf16[2,32,256]{2,1,0:T(8,128)(2,1)S(1)}, u32[]{:S(2)}, u32[]{:S(2)}) collective-permute-start(bf16[2,32,256]{2,1,0:T(8,128)(2,1)S(1)} %get-tuple-element.102), channel_id=1, source_target_pairs={{0,25},{1,24},{2,27},{3,26},{4,29},{5,28},{6,31},{7,30},{8,17},{9,... | collective-permute-start | bytes 98312 | tf_op jit(solution)/shard_map/ppermute | solution.py:25
  103.8 6.2 %collective-permute-start.41 = (bf16[8,32,256]{2,1,0:T(8,128)(2,1)S(1)}, bf16[8,32,256]{2,1,0:T(8,128)(2,1)S(1)}, u32[]{:S(2)}, u32[]{:S(2)}) collective-permute-start(bf16[8,32,256]{2,1,0:T(8,128)(2,1)S(1)} %get-tuple-element.105), channel_id=1, source_target_pairs={{0,1},{1,0},{2,3},{3,2},{4,5},{5,4},{6,7},{7,6},{8,9},{9,8},{10,11... | collective-permute-start | bytes 393224 | tf_op jit(solution)/shard_map/ppermute | solution.py:25

commit v5 on v4

--- a/solution.py
+++ b/solution.py
@@ -17,7 +17,7 @@
 
 FIRST = 3
 ROUND = 6
-CROSS = (1,2,3)
+CROSS = (2,3)
 
 
 def swap(value, mask):
@@ -223,24 +223,27 @@
         push(down, spread, j + 1, part)
 
 
-def last_kernel(levels, own, known, diag, *refs):
-    split = len(refs) - 2 - (2 * levels - 1)
-    arrived, blocks, (mine, sent) = refs[:split], refs[split:-2], refs[-2:]
-    solved = backward_step(own, arrived, known, diag)
-    for n, block in enumerate(blocks):
-        n += n >= levels
-        mine[n] = block[0]
-        sent[n] = block[1]
-    mine[levels], sent[levels] = solved
-
-
-def join_kernel(mine, other, *outs):
-    here, there = halves(outs[0].shape[2])
-    levels = outs[0].shape[0]
-    for n, out in enumerate(outs):
-        for l in range(levels):
-            out[l, 0, here] = mine[n * levels + l]
-            out[l, 0, there] = other[n * levels + l]
+def last_kernel(own, known, diag, *refs):
+    arrived, (mine, sent) = refs[:-2], refs[-2:]
+    mine[...], sent[...] = backward_step(own, arrived, known, diag)
+
+
+def split_kernel(*refs):
+    blocks, (mine, sent) = refs[:-2], refs[-2:]
+    for l, block in enumerate(blocks):
+        mine[l] = block[0]
+        sent[l] = block[1]
+
+
+def join_kernel(*refs):
+    pairs, out = refs[:-1], refs[-1]
+    here, there = halves(out.shape[2])
+    l = 0
+    for mine, other in zip(pairs[0::2], pairs[1::2]):
+        for m in range(mine.shape[0]):
+            out[l, 0, here] = mine[m]
+            out[l, 0, there] = other[m]
+            l += 1
 
 
 def body(rhs_block, diag_inv, off_tiles, pattern):
@@ -347,13 +350,13 @@
         )
         backward.insert(0, back)
     own, arrived = scattered(spreads[0], back, outs)
-    mine, sent = call(
-        functools.partial(last_kernel, levels),
-        [shape(2 * levels)] * 2,
-        [own, forward[0], diag[0]] + arrived + forward + backward,
-    )
+    last, last_sent = call(last_kernel, [shape()] * 2, [own, forward[0], diag[0]] + arrived)
+
     whole = jax.ShapeDtypeStruct((levels, 1, width, size), jnp.bfloat16)
-    forward_sol, backward_sol = call(join_kernel, [whole] * 2, [mine, swap(sent, 1)])
+    mine, sent = call(split_kernel, [shape(levels)] * 2, forward)
+    forward_sol = call(join_kernel, whole, [mine, swap(sent, 1)])
+    mine, sent = call(split_kernel, [shape(levels - 1)] * 2, backward)
+    backward_sol = call(join_kernel, whole, [last[None], swap(last_sent, 1)[None], mine, swap(sent, 1)])
     return forward_sol, backward_sol
 
 

time: 111 us -> 110 us (level)
  waiting for transfers between devices: 33.5 us -> 29.2 us
  starting transfers between devices: 50.5 us -> 53.5 us
    ppermute x42 -> x44, waiting for transfers between devices: 33.5 us -> 29.2 us  [swap(): return lax.ppermute(value, 'rows', [(i, i ^ mask) for i in range(size)])]
    ppermute x42 -> x44, starting transfers between devices: 50.5 us -> 53.5 us  [swap(): return lax.ppermute(value, 'rows', [(i, i ^ mask) for i in range(size)])]
    pallas_call x27 -> x30, Pallas kernels: 24.9 us -> 25.5 us  [call(): pl.pallas_call(kernel, out_shape=out_shape, in_specs=[VMEM_SPEC] * len(op...]
  transfers between devices with their start and end apart: 42 -> 44, of which waited for: 25 -> 20; matrix products, arithmetic and copies ran while one was open for 0% -> 0% of each run, Pallas kernels for 15% -> 16%
where the time goes in v5:
time: 110 us
  starting transfers between devices  53.5 us (49%)
  waiting for transfers between devices  29.2 us (27%)
  Pallas kernels  25.5 us (23%)
    ppermute x44, starting transfers between devices, swap(): return lax.ppermute(value, 'rows', [(i, i ^ mask) for i in range(size)])  53.5 us
    ppermute x44, waiting for transfers between devices, swap(): return lax.ppermute(value, 'rows', [(i, i ^ mask) for i in range(size)])  29.2 us
    pallas_call x30, Pallas kernels, call(): pl.pallas_call(kernel, out_shape=out_shape, in_specs=[VMEM_SPEC] * len(op...  25.5 us
  transfers between devices with their start and end apart: 44, of which 20 were waited for; matrix products, arithmetic and copies ran while one was open for 0% of the time, Pallas kernels for 16%

profile of v5, /device:TPU:0, one launch (start us, length us, event | category | flops | bytes accessed | tf_op | source)
XLA Modules:
  0.0 110.0 jit_solution(16584316116640949449)
XLA Ops:
  0.6 1.1 %shard_map.59 = (bf16[32,256]{1,0:T(8,128)(2,1)S(1)}, bf16[32,256]{1,0:T(8,128)(2,1)S(1)}) custom-call(bf16[4,1,64,256]{3,2,1,0:T(8,128)(2,1)} %rhs.3, bf16[4,1,256,256]{3,2,1,0:T(8,128)(2,1)} %diag0.5), custom_call_target="tpu_custom_call" | custom-call | tf_op jit(solution)/shard_map/pallas_call | solution.py:37
  2.4 0.9 copy-done
  4.2 2.7 %collective-permute-start.5 = (bf16[2,32,256]{2,1,0:T(8,128)(2,1)S(1)}, bf16[2,32,256]{2,1,0:T(8,128)(2,1)S(1)}, u32[]{:S(2)}, u32[]{:S(2)}) collective-permute-start(bf16[2,32,256]{2,1,0:T(8,128)(2,1)S(1)} %get-tuple-element.117.after.refs_0_.known), channel_id=1, source_target_pairs={{0,9},{1,8},{2,11},{3,10},{4,13},{5,12},{6,15},{7,14},{8,1},{9,0},... | collective-permute-start | bytes 98312 | tf_op jit(solution)/shard_map/ppermute | solution.py:25
  6.9 2.6 %collective-permute-start.6 = (bf16[2,32,256]{2,1,0:T(8,128)(2,1)S(1)}, bf16[2,32,256]{2,1,0:T(8,128)(2,1)S(1)}, u32[]{:S(2)}, u32[]{:S(2)}) collective-permute-start(bf16[2,32,256]{2,1,0:T(8,128)(2,1)S(1)} %get-tuple-element.117.after.refs_0_.known), channel_id=1, source_target_pairs={{0,16},{1,17},{2,18},{3,19},{4,20},{5,21},{6,22},{7,23},{8,24},{9,... | collective-permute-start | bytes 98312 | tf_op jit(solution)/shard_map/ppermute | solution.py:25
  9.5 2.5 %collective-permute-done.6 = bf16[2,32,256]{2,1,0:T(8,128)(2,1)S(1)} collective-permute-done((bf16[2,32,256]{2,1,0:T(8,128)(2,1)S(1)}, bf16[2,32,256]{2,1,0:T(8,128)(2,1)S(1)}, u32[]{:S(2)}, u32[]{:S(2)}) %collective-permute-start.6) | collective-permute-done | bytes 32800 | tf_op jit(solution)/shard_map/ppermute | solution.py:25
  12.0 2.8 %collective-permute-done.7 = bf16[2,32,256]{2,1,0:T(8,128)(2,1)S(1)} collective-permute-done((bf16[2,32,256]{2,1,0:T(8,128)(2,1)S(1)}, bf16[2,32,256]{2,1,0:T(8,128)(2,1)S(1)}, u32[]{:S(2)}, u32[]{:S(2)}) %collective-permute-start.7) | collective-permute-done | bytes 32800 | tf_op jit(solution)/shard_map/ppermute | solution.py:25
  14.9 2.2 %collective-permute-start.10 = (bf16[4,2,32,256]{3,2,1,0:T(8,128)(2,1)S(1)}, bf16[4,2,32,256]{3,2,1,0:T(8,128)(2,1)S(1)}, u32[]{:S(2)}, u32[]{:S(2)}) collective-permute-start(bf16[4,2,32,256]{3,2,1,0:T(8,128)(2,1)S(1)} %pad_maximum_fusion.part), channel_id=1, source_target_pairs={{0,7},{1,6},{2,5},{3,4},{4,3},{5,2},{6,1},{7,0},{8,15},{9,14},{10,... | collective-permute-start | bytes 393224 | tf_op jit(solution)/shard_map/ppermute | solution.py:25
  17.9 3.0 %shard_map.61 = (bf16[2,32,256,256]{3,2,1,0:T(8,128)(2,1)S(1)}, bf16[2,2,256,256]{3,2,1,0:T(8,128)(2,1)S(1)}) custom-call(s32[3,1,16]{2,1,0:T(1,128)} %own_pattern.5, s32[3,1,16]{2,1,0:T(1,128)S(1)} %collective-permute-done.1.other_pattern, bf16[2,32,256]{2,1,0:T(8,128)(2,1)S(1)} %get-tuple-element.117.after.refs_0_.known, ...), custom_call_target="tpu_custom_call" | custom-call | flops 134217728 | tf_op jit(solution)/shard_map/pallas_call | solution.py:37
  21.0 0.7 shard_map.62.refs_0_
  21.7 0.7 shard_map.63.refs_0_
  22.4 2.1 %collective-permute-done.9.part = bf16[4,2,32,256]{3,2,1,0:T(8,128)(2,1)S(1)} collective-permute-done((bf16[4,2,32,256]{3,2,1,0:T(8,128)(2,1)S(1)}, bf16[4,2,32,256]{3,2,1,0:T(8,128)(2,1)S(1)}, u32[]{:S(2)}, u32[]{:S(2)}) %collective-permute-start.9) | collective-permute-done | bytes 131104 | tf_op jit(solution)/shard_map/ppermute | solution.py:25
  24.5 0.7 shard_map.64.refs_1_
  25.3 0.8 shard_map.65.after.refs_1_.known
  26.1 1.4 %collective-permute-start.12 = (bf16[2,32,256]{2,1,0:T(8,128)(2,1)S(1)}, bf16[2,32,256]{2,1,0:T(8,128)(2,1)S(1)}, u32[]{:S(2)}, u32[]{:S(2)}) collective-permute-start(bf16[2,32,256]{2,1,0:T(8,128)(2,1)S(1)} %shard_map.65.after.refs_1_.known), channel_id=1, source_target_pairs={{0,16},{1,17},{2,18},{3,19},{4,20},{5,21},{6,22},{7,23},{8,24},{9,... | collective-permute-start | bytes 98312 | tf_op jit(solution)/shard_map/ppermute | solution.py:25
  27.6 2.4 %collective-permute-start.13 = (bf16[2,32,256]{2,1,0:T(8,128)(2,1)S(1)}, bf16[2,32,256]{2,1,0:T(8,128)(2,1)S(1)}, u32[]{:S(2)}, u32[]{:S(2)}) collective-permute-start(bf16[2,32,256]{2,1,0:T(8,128)(2,1)S(1)} %shard_map.65.after.refs_1_.known), channel_id=1, source_target_pairs={{0,25},{1,24},{2,27},{3,26},{4,29},{5,28},{6,31},{7,30},{8,17},{9,... | collective-permute-start | bytes 98312 | tf_op jit(solution)/shard_map/ppermute | solution.py:25
  29.9 2.8 %shard_map.66 = (bf16[2,32,256,256]{3,2,1,0:T(8,128)(2,1)S(1)}, bf16[1,2,256,256]{3,2,1,0:T(8,128)(2,1)S(1)}) custom-call(s32[3,1,16]{2,1,0:T(1,128)} %own_pattern.5, s32[3,1,16]{2,1,0:T(1,128)S(1)} %collective-permute-done.1.other_pattern, bf16[2,32,256]{2,1,0:T(8,128)(2,1)S(1)} %shard_map.65.after.refs_1_.known, bf16[3,1,16,256,256]{4,3,2,1,0:T(8,128)(2,1)} %tiles0.5, ...), custom_call_target="tpu_custom_call" | custom-call | flops 134217728 | tf_op jit(solution)/shard_map/pallas_call | solution.py:37
  32.8 1.7 %collective-permute-start.16 = (bf16[4,2,32,256]{3,2,1,0:T(8,128)(2,1)S(1)}, bf16[4,2,32,256]{3,2,1,0:T(8,128)(2,1)S(1)}, u32[]{:S(2)}, u32[]{:S(2)}) collective-permute-start(bf16[4,2,32,256]{3,2,1,0:T(8,128)(2,1)S(1)} %pad_maximum_fusion.1.part), channel_id=1, source_target_pairs={{0,7},{1,6},{2,5},{3,4},{4,3},{5,2},{6,1},{7,0},{8,15},{9,14},{10,... | collective-permute-start | bytes 393224 | tf_op jit(solution)/shard_map/ppermute | solution.py:25
  35.0 0.8 collective-permute-start.14
  35.8 0.7 shard_map.67.refs_0_
  36.5 1.7 %collective-permute-done.16.part = bf16[4,2,32,256]{3,2,1,0:T(8,128)(2,1)S(1)} collective-permute-done((bf16[4,2,32,256]{3,2,1,0:T(8,128)(2,1)S(1)}, bf16[4,2,32,256]{3,2,1,0:T(8,128)(2,1)S(1)}, u32[]{:S(2)}, u32[]{:S(2)}) %collective-permute-start.16) | collective-permute-done | bytes 131104 | tf_op jit(solution)/shard_map/ppermute | solution.py:25
  38.2 0.7 shard_map.68.refs_0_
  39.4 0.7 shard_map.69.refs_1_
  40.2 0.8 shard_map.70.after.refs_2_.known
  41.0 2.5 %collective-permute-start.18 = (bf16[2,32,256]{2,1,0:T(8,128)(2,1)S(1)}, bf16[2,32,256]{2,1,0:T(8,128)(2,1)S(1)}, u32[]{:S(2)}, u32[]{:S(2)}) collective-permute-start(bf16[2,32,256]{2,1,0:T(8,128)(2,1)S(1)} %shard_map.70.after.refs_2_.known), channel_id=1, source_target_pairs={{0,16},{1,17},{2,18},{3,19},{4,20},{5,21},{6,22},{7,23},{8,24},{9,... | collective-permute-start | bytes 98312 | tf_op jit(solution)/shard_map/ppermute | solution.py:25
  43.5 1.4 %collective-permute-start.19 = (bf16[2,32,256]{2,1,0:T(8,128)(2,1)S(1)}, bf16[2,32,256]{2,1,0:T(8,128)(2,1)S(1)}, u32[]{:S(2)}, u32[]{:S(2)}) collective-permute-start(bf16[2,32,256]{2,1,0:T(8,128)(2,1)S(1)} %shard_map.70.after.refs_2_.known), channel_id=1, source_target_pairs={{0,25},{1,24},{2,27},{3,26},{4,29},{5,28},{6,31},{7,30},{8,17},{9,... | collective-permute-start | bytes 98312 | tf_op jit(solution)/shard_map/ppermute | solution.py:25
  44.8 2.8 %shard_map.71 = (bf16[2,32,256,256]{3,2,1,0:T(8,128)(2,1)S(1)}, bf16[1,2,256,256]{3,2,1,0:T(8,128)(2,1)S(1)}) custom-call(s32[3,1,16]{2,1,0:T(1,128)} %own_pattern.5, s32[3,1,16]{2,1,0:T(1,128)S(1)} %collective-permute-done.1.other_pattern, bf16[2,32,256]{2,1,0:T(8,128)(2,1)S(1)} %shard_map.70.after.refs_2_.known, bf16[3,1,16,256,256]{4,3,2,1,0:T(8,128)(2,1)} %tiles0.5, ...), custom_call_target="tpu_custom_call" | custom-call | flops 134217728 | tf_op jit(solution)/shard_map/pallas_call | solution.py:37
  47.7 1.0 collective-permute-done.19
  48.7 2.3 %collective-permute-start.22 = (bf16[4,2,32,256]{3,2,1,0:T(8,128)(2,1)S(1)}, bf16[4,2,32,256]{3,2,1,0:T(8,128)(2,1)S(1)}, u32[]{:S(2)}, u32[]{:S(2)}) collective-permute-start(bf16[4,2,32,256]{3,2,1,0:T(8,128)(2,1)S(1)} %pad_maximum_fusion.2.part), channel_id=1, source_target_pairs={{0,7},{1,6},{2,5},{3,4},{4,3},{5,2},{6,1},{7,0},{8,15},{9,14},{10,... | collective-permute-start | bytes 393224 | tf_op jit(solution)/shard_map/ppermute | solution.py:25
  51.7 0.7 shard_map.72.refs_0_
  52.4 1.7 %collective-permute-done.22.part = bf16[4,2,32,256]{3,2,1,0:T(8,128)(2,1)S(1)} collective-permute-done((bf16[4,2,32,256]{3,2,1,0:T(8,128)(2,1)S(1)}, bf16[4,2,32,256]{3,2,1,0:T(8,128)(2,1)S(1)}, u32[]{:S(2)}, u32[]{:S(2)}) %collective-permute-start.22) | collective-permute-done | bytes 131104 | tf_op jit(solution)/shard_map/ppermute | solution.py:25
  54.0 0.7 shard_map.73.refs_0_
  54.7 1.2 %collective-permute-done.21.part = bf16[4,2,32,256]{3,2,1,0:T(8,128)(2,1)S(1)} collective-permute-done((bf16[4,2,32,256]{3,2,1,0:T(8,128)(2,1)S(1)}, bf16[4,2,32,256]{3,2,1,0:T(8,128)(2,1)S(1)}, u32[]{:S(2)}, u32[]{:S(2)}) %collective-permute-start.21) | collective-permute-done | bytes 131104 | tf_op jit(solution)/shard_map/ppermute | solution.py:25
  55.9 0.7 shard_map.74.refs_1_
  56.7 2.1 %shard_map.75 = (bf16[2,32,256]{2,1,0:T(8,128)(2,1)S(1)}, bf16[2,32,256]{2,1,0:T(8,128)(2,1)S(1)}, bf16[4,2,32,256]{3,2,1,0:T(8,128)(2,1)S(1)}, bf16[4,2,32,256]...) custom-call(bf16[2,32,256,256]{3,2,1,0:T(8,128)(2,1)S(1)} %get-tuple-element.77.spread, ...), custom_call_target="tpu_custom_call" | custom-call | flops 268435456 | tf_op jit(solution)/shard_map/pallas_call | solution.py:37
  58.8 1.1 %collective-permute-start.24 = (bf16[4,2,32,256]{3,2,1,0:T(8,128)(2,1)S(1)}, bf16[4,2,32,256]{3,2,1,0:T(8,128)(2,1)S(1)}, u32[]{:S(2)}, u32[]{:S(2)}) collective-permute-start(bf16[4,2,32,256]{3,2,1,0:T(8,128)(2,1)S(1)} %get-tuple-element.87), channel_id=1, source_target_pairs={{0,7},{1,6},{2,5},{3,4},{4,3},{5,2},{6,1},{7,0},{8,15},{9,14},{10,... | collective-permute-start | bytes 393224 | tf_op jit(solution)/shard_map/ppermute | solution.py:25
  59.9 0.6 collective-permute-start.25
  60.6 1.2 %collective-permute-start.26 = (bf16[4,2,32,256]{3,2,1,0:T(8,128)(2,1)S(1)}, bf16[4,2,32,256]{3,2,1,0:T(8,128)(2,1)S(1)}, u32[]{:S(2)}, u32[]{:S(2)}) collective-permute-start(bf16[4,2,32,256]{3,2,1,0:T(8,128)(2,1)S(1)} %get-tuple-element.89), channel_id=1, source_target_pairs={{0,5},{1,4},{2,7},{3,6},{4,1},{5,0},{6,3},{7,2},{8,13},{9,12},{10,... | collective-permute-start | bytes 393224 | tf_op jit(solution)/shard_map/ppermute | solution.py:25
  62.2 2.0 %collective-permute-done.24.a = bf16[4,2,32,256]{3,2,1,0:T(8,128)(2,1)S(1)} collective-permute-done((bf16[4,2,32,256]{3,2,1,0:T(8,128)(2,1)S(1)}, bf16[4,2,32,256]{3,2,1,0:T(8,128)(2,1)S(1)}, u32[]{:S(2)}, u32[]{:S(2)}) %collective-permute-start.24) | collective-permute-done | bytes 131104 | tf_op jit(solution)/shard_map/ppermute | solution.py:25
  64.1 0.8 collective-permute-done.25.b
  65.6 1.4 %collective-permute-start.28 = (bf16[2,32,256]{2,1,0:T(8,128)(2,1)S(1)}, bf16[2,32,256]{2,1,0:T(8,128)(2,1)S(1)}, u32[]{:S(2)}, u32[]{:S(2)}) collective-permute-start(bf16[2,32,256]{2,1,0:T(8,128)(2,1)S(1)} %get-tuple-element.92), channel_id=1, source_target_pairs={{0,16},{1,17},{2,18},{3,19},{4,20},{5,21},{6,22},{7,23},{8,24},{9,... | collective-permute-start | bytes 98312 | tf_op jit(solution)/shard_map/ppermute | solution.py:25
  67.1 2.4 %collective-permute-start.29 = (bf16[2,32,256]{2,1,0:T(8,128)(2,1)S(1)}, bf16[2,32,256]{2,1,0:T(8,128)(2,1)S(1)}, u32[]{:S(2)}, u32[]{:S(2)}) collective-permute-start(bf16[2,32,256]{2,1,0:T(8,128)(2,1)S(1)} %get-tuple-element.93), channel_id=1, source_target_pairs={{0,25},{1,24},{2,27},{3,26},{4,29},{5,28},{6,31},{7,30},{8,17},{9,... | collective-permute-start | bytes 98312 | tf_op jit(solution)/shard_map/ppermute | solution.py:25
  69.5 1.1 collective-permute-done.28.refs_1_
  70.5 1.7 %collective-permute-done.29.refs_2_ = bf16[2,32,256]{2,1,0:T(8,128)(2,1)S(1)} collective-permute-done((bf16[2,32,256]{2,1,0:T(8,128)(2,1)S(1)}, bf16[2,32,256]{2,1,0:T(8,128)(2,1)S(1)}, u32[]{:S(2)}, u32[]{:S(2)}) %collective-permute-start.29) | collective-permute-done | bytes 32800 | tf_op jit(solution)/shard_map/ppermute | solution.py:25
  72.2 1.3 %shard_map.80 = (bf16[2,32,256]{2,1,0:T(8,128)(2,1)S(1)}, bf16[4,2,32,256]{3,2,1,0:T(8,128)(2,1)S(1)}, bf16[4,2,32,256]{3,2,1,0:T(8,128)(2,1)S(1)}, bf16[4,2,32,256]{3,2,1,0:T(8,128)(2,1)S(1)}) custom-call(bf16[2,32,256,256]{3,2,1,0:T(8,128)(2,1)S(1)} %get-tuple-element.70.spread, f32[2,32,256]{2,1,0:T(8,128)S(1)} %get-tuple-element.90.own, ...), custom_call_target="tpu_custom_call" | custom-call | flops 201326592 | tf_op jit(solution)/shard_map/pallas_call | solution.py:37
  73.5 1.7 %collective-permute-start.30 = (bf16[4,2,32,256]{3,2,1,0:T(8,128)(2,1)S(1)}, bf16[4,2,32,256]{3,2,1,0:T(8,128)(2,1)S(1)}, u32[]{:S(2)}, u32[]{:S(2)}) collective-permute-start(bf16[4,2,32,256]{3,2,1,0:T(8,128)(2,1)S(1)} %get-tuple-element.95), channel_id=1, source_target_pairs={{0,7},{1,6},{2,5},{3,4},{4,3},{5,2},{6,1},{7,0},{8,15},{9,14},{10,... | collective-permute-start | bytes 393224 | tf_op jit(solution)/shard_map/ppermute | solution.py:25
  75.2 0.6 collective-permute-start.31
  75.9 0.6 collective-permute-start.32
  76.9 1.9 %collective-permute-done.30.a = bf16[4,2,32,256]{3,2,1,0:T(8,128)(2,1)S(1)} collective-permute-done((bf16[4,2,32,256]{3,2,1,0:T(8,128)(2,1)S(1)}, bf16[4,2,32,256]{3,2,1,0:T(8,128)(2,1)S(1)}, u32[]{:S(2)}, u32[]{:S(2)}) %collective-permute-start.30) | collective-permute-done | bytes 131104 | tf_op jit(solution)/shard_map/ppermute | solution.py:25
  78.8 1.4 %collective-permute-done.31.b = bf16[4,2,32,256]{3,2,1,0:T(8,128)(2,1)S(1)} collective-permute-done((bf16[4,2,32,256]{3,2,1,0:T(8,128)(2,1)S(1)}, bf16[4,2,32,256]{3,2,1,0:T(8,128)(2,1)S(1)}, u32[]{:S(2)}, u32[]{:S(2)}) %collective-permute-start.31) | collective-permute-done | bytes 131104 | tf_op jit(solution)/shard_map/ppermute | solution.py:25
  80.4 2.9 %collective-permute-start.34 = (bf16[2,32,256]{2,1,0:T(8,128)(2,1)S(1)}, bf16[2,32,256]{2,1,0:T(8,128)(2,1)S(1)}, u32[]{:S(2)}, u32[]{:S(2)}) collective-permute-start(bf16[2,32,256]{2,1,0:T(8,128)(2,1)S(1)} %get-tuple-element.100), channel_id=1, source_target_pairs={{0,16},{1,17},{2,18},{3,19},{4,20},{5,21},{6,22},{7,23},{8,24},{9,... | collective-permute-start | bytes 98312 | tf_op jit(solution)/shard_map/ppermute | solution.py:25
  83.3 0.9 collective-permute-start.35
  84.2 1.1 collective-permute-done.34.refs_1_
  85.3 3.4 %collective-permute-done.35.refs_2_ = bf16[2,32,256]{2,1,0:T(8,128)(2,1)S(1)} collective-permute-done((bf16[2,32,256]{2,1,0:T(8,128)(2,1)S(1)}, bf16[2,32,256]{2,1,0:T(8,128)(2,1)S(1)}, u32[]{:S(2)}, u32[]{:S(2)}) %collective-permute-start.35) | collective-permute-done | bytes 32800 | tf_op jit(solution)/shard_map/ppermute | solution.py:25
  88.6 1.3 %shard_map.83 = (bf16[2,32,256]{2,1,0:T(8,128)(2,1)S(1)}, bf16[4,2,32,256]{3,2,1,0:T(8,128)(2,1)S(1)}, bf16[4,2,32,256]{3,2,1,0:T(8,128)(2,1)S(1)}, bf16[4,2,32,256]{3,2,1,0:T(8,128)(2,1)S(1)}) custom-call(bf16[2,32,256,256]{3,2,1,0:T(8,128)(2,1)S(1)} %get-tuple-element.65.spread, f32[2,32,256]{2,1,0:T(8,128)S(1)} %get-tuple-element.98.own, ...), custom_call_target="tpu_custom_call" | custom-call | flops 201326592 | tf_op jit(solution)/shard_map/pallas_call | solution.py:37
  90.0 1.5 %collective-permute-start.36 = (bf16[4,2,32,256]{3,2,1,0:T(8,128)(2,1)S(1)}, bf16[4,2,32,256]{3,2,1,0:T(8,128)(2,1)S(1)}, u32[]{:S(2)}, u32[]{:S(2)}) collective-permute-start(bf16[4,2,32,256]{3,2,1,0:T(8,128)(2,1)S(1)} %get-tuple-element.103), channel_id=1, source_target_pairs={{0,7},{1,6},{2,5},{3,4},{4,3},{5,2},{6,1},{7,0},{8,15},{9,14},{10,... | collective-permute-start | bytes 393224 | tf_op jit(solution)/shard_map/ppermute | solution.py:25
  92.1 0.8 collective-permute-start.38
  92.9 3.6 %collective-permute-start.23 = (bf16[4,32,256]{2,1,0:T(8,128)(2,1)S(1)}, bf16[4,32,256]{2,1,0:T(8,128)(2,1)S(1)}, u32[]{:S(2)}, u32[]{:S(2)}) collective-permute-start(bf16[4,32,256]{2,1,0:T(8,128)(2,1)S(1)} %get-tuple-element.85), channel_id=1, source_target_pairs={{0,1},{1,0},{2,3},{3,2},{4,5},{5,4},{6,7},{7,6},{8,9},{9,8},{10,11... | collective-permute-start | bytes 196616 | tf_op jit(solution)/shard_map/ppermute | solution.py:25
  97.2 3.1 %collective-permute-start.40 = (bf16[2,32,256]{2,1,0:T(8,128)(2,1)S(1)}, bf16[2,32,256]{2,1,0:T(8,128)(2,1)S(1)}, u32[]{:S(2)}, u32[]{:S(2)}) collective-permute-start(bf16[2,32,256]{2,1,0:T(8,128)(2,1)S(1)} %get-tuple-element.108), channel_id=1, source_target_pairs={{0,16},{1,17},{2,18},{3,19},{4,20},{5,21},{6,22},{7,23},{8,24},{9,... | collective-permute-start | bytes 98312 | tf_op jit(solution)/shard_map/ppermute | solution.py:25
  100.3 0.7 collective-permute-start.41
  101.0 3.3 %collective-permute-start.43 = (bf16[3,32,256]{2,1,0:T(8,128)(2,1)S(1)}, bf16[3,32,256]{2,1,0:T(8,128)(2,1)S(1)}, u32[]{:S(2)}, u32[]{:S(2)}) collective-permute-start(bf16[3,32,256]{2,1,0:T(8,128)(2,1)S(1)} %get-tuple-element.113), channel_id=1, source_target_pairs={{0,1},{1,0},{2,3},{3,2},{4,5},{5,4},{6,7},{7,6},{8,9},{9,8},{10,11... | collective-permute-start | bytes 147464 | tf_op jit(solution)/shard_map/ppermute | solution.py:25
  104.3 1.1 %collective-permute-done.41.refs_2_ = bf16[2,32,256]{2,1,0:T(8,128)(2,1)S(1)} collective-permute-done((bf16[2,32,256]{2,1,0:T(8,128)(2,1)S(1)}, bf16[2,32,256]{2,1,0:T(8,128)(2,1)S(1)}, u32[]{:S(2)}, u32[]{:S(2)}) %collective-permute-start.41) | collective-permute-done | bytes 32800 | tf_op jit(solution)/shard_map/ppermute | solution.py:25
  105.6 2.9 %collective-permute-start.42 = (bf16[32,256]{1,0:T(8,128)(2,1)S(1)}, bf16[32,256]{1,0:T(8,128)(2,1)S(1)}, u32[]{:S(2)}, u32[]{:S(2)}) collective-permute-start(bf16[32,256]{1,0:T(8,128)(2,1)S(1)} %get-tuple-element.111), channel_id=1, source_target_pairs={{0,1},{1,0},{2,3},{3,2},{4,5},{5,4},{6,7},{7,6},{8,9},{9,8},{10,11... | collective-permute-start | bytes 49160 | tf_op jit(solution)/shard_map/ppermute | solution.py:25
  108.5 0.7 shard_map.77
  109.4 0.7 shard_map.88
  (61 shorter events, 7.7 us)
Async XLA Ops:
  1.8 1.9 %collective-permute-start = (bf16[32,256]{1,0:T(8,128)(2,1)S(1)}, bf16[32,256]{1,0:T(8,128)(2,1)S(1)}, u32[]{:S(2)}, u32[]{:S(2)}) collective-permute-start(bf16[32,256]{1,0:T(8,128)(2,1)S(1)} %get-tuple-element.59.after), channel_id=1, source_target_pairs={{0,1},{1,0},{2,3},{3,2},{4,5},{5,4},{6,7},{7,6},{8,9},{9,8},{10,11... | collective-permute-start | bytes 49160 | tf_op jit(solution)/shard_map/ppermute | solution.py:25
  2.3 1.4 %collective-permute-start.1 = (s32[3,1,16]{2,1,0:T(1,128)}, s32[3,1,16]{2,1,0:T(1,128)S(1)}, u32[]{:S(2)}, u32[]{:S(2)}) collective-permute-start(s32[3,1,16]{2,1,0:T(1,128)} %own_pattern.5), channel_id=1, source_target_pairs={{0,1},{1,0},{2,3},{3,2},{4,5},{5,4},{6,7},{7,6},{8,9},{9,8},{10,11... | collective-permute-start | bytes 584 | tf_op jit(solution)/shard_map/ppermute | solution.py:25
  2.4 0.9 copy-start
  3.7 14.3 %collective-permute-start.2 = (bf16[3,1,16,256,256]{4,3,2,1,0:T(8,128)(2,1)}, bf16[3,1,16,256,256]{4,3,2,1,0:T(8,128)(2,1)S(1)}, u32[]{:S(2)}, u32[]{:S(2)}) collective-permute-start(bf16[3,1,16,256,256]{4,3,2,1,0:T(8,128)(2,1)} %tiles0.5), channel_id=1, source_target_pairs={{0,1},{1,0},{2,3},{3,2},{4,5},{5,4},{6,7},{7,6},{8,9},{9,8},{10,11... | collective-permute-start | bytes 18874376 | tf_op jit(solution)/shard_map/ppermute | solution.py:25
  3.8 13.8 %collective-permute-start.3 = (bf16[4,1,256,256]{3,2,1,0:T(8,128)(2,1)}, bf16[4,1,256,256]{3,2,1,0:T(8,128)(2,1)S(1)}, u32[]{:S(2)}, u32[]{:S(2)}) collective-permute-start(bf16[4,1,256,256]{3,2,1,0:T(8,128)(2,1)} %diag0.5), channel_id=1, source_target_pairs={{0,1},{1,0},{2,3},{3,2},{4,5},{5,4},{6,7},{7,6},{8,9},{9,8},{10,11... | collective-permute-start | bytes 1572872 | tf_op jit(solution)/shard_map/ppermute | solution.py:25
  4.2 5.3 %collective-permute-start.5 = (bf16[2,32,256]{2,1,0:T(8,128)(2,1)S(1)}, bf16[2,32,256]{2,1,0:T(8,128)(2,1)S(1)}, u32[]{:S(2)}, u32[]{:S(2)}) collective-permute-start(bf16[2,32,256]{2,1,0:T(8,128)(2,1)S(1)} %get-tuple-element.117.after.refs_0_.known), channel_id=1, source_target_pairs={{0,9},{1,8},{2,11},{3,10},{4,13},{5,12},{6,15},{7,14},{8,1},{9,0},... | collective-permute-start | bytes 98312 | tf_op jit(solution)/shard_map/ppermute | solution.py:25
  6.9 5.2 %collective-permute-start.6 = (bf16[2,32,256]{2,1,0:T(8,128)(2,1)S(1)}, bf16[2,32,256]{2,1,0:T(8,128)(2,1)S(1)}, u32[]{:S(2)}, u32[]{:S(2)}) collective-permute-start(bf16[2,32,256]{2,1,0:T(8,128)(2,1)S(1)} %get-tuple-element.117.after.refs_0_.known), channel_id=1, source_target_pairs={{0,16},{1,17},{2,18},{3,19},{4,20},{5,21},{6,22},{7,23},{8,24},{9,... | collective-permute-start | bytes 98312 | tf_op jit(solution)/shard_map/ppermute | solution.py:25
  9.4 5.4 %collective-permute-start.7 = (bf16[2,32,256]{2,1,0:T(8,128)(2,1)S(1)}, bf16[2,32,256]{2,1,0:T(8,128)(2,1)S(1)}, u32[]{:S(2)}, u32[]{:S(2)}) collective-permute-start(bf16[2,32,256]{2,1,0:T(8,128)(2,1)S(1)} %get-tuple-element.117.after.refs_0_.known), channel_id=1, source_target_pairs={{0,25},{1,24},{2,27},{3,26},{4,29},{5,28},{6,31},{7,30},{8,17},{9,... | collective-permute-start | bytes 98312 | tf_op jit(solution)/shard_map/ppermute | solution.py:25
  9.5 15.8 %collective-permute-start.4 = (bf16[4,32,256]{2,1,0:T(8,128)(2,1)S(1)}, bf16[4,32,256]{2,1,0:T(8,128)(2,1)S(1)}, u32[]{:S(2)}, u32[]{:S(2)}) collective-permute-start(bf16[4,32,256]{2,1,0:T(8,128)(2,1)S(1)} %get-tuple-element.67), channel_id=1, source_target_pairs={{0,1},{1,0},{2,3},{3,2},{4,5},{5,4},{6,7},{7,6},{8,9},{9,8},{10,11... | collective-permute-start | bytes 196616 | tf_op jit(solution)/shard_map/ppermute | solution.py:25
  14.9 6.8 %collective-permute-start.10 = (bf16[4,2,32,256]{3,2,1,0:T(8,128)(2,1)S(1)}, bf16[4,2,32,256]{3,2,1,0:T(8,128)(2,1)S(1)}, u32[]{:S(2)}, u32[]{:S(2)}) collective-permute-start(bf16[4,2,32,256]{3,2,1,0:T(8,128)(2,1)S(1)} %pad_maximum_fusion.part), channel_id=1, source_target_pairs={{0,7},{1,6},{2,5},{3,4},{4,3},{5,2},{6,1},{7,0},{8,15},{9,14},{10,... | collective-permute-start | bytes 393224 | tf_op jit(solution)/shard_map/ppermute | solution.py:25
  17.1 7.4 %collective-permute-start.9 = (bf16[4,2,32,256]{3,2,1,0:T(8,128)(2,1)S(1)}, bf16[4,2,32,256]{3,2,1,0:T(8,128)(2,1)S(1)}, u32[]{:S(2)}, u32[]{:S(2)}) collective-permute-start(bf16[4,2,32,256]{3,2,1,0:T(8,128)(2,1)S(1)} %pad_maximum_fusion.part), channel_id=1, source_target_pairs={{0,2},{1,3},{2,0},{3,1},{4,6},{5,7},{6,4},{7,5},{8,10},{9,11},{10,... | collective-permute-start | bytes 393224 | tf_op jit(solution)/shard_map/ppermute | solution.py:25
  17.6 7.6 %collective-permute-start.8 = (bf16[4,2,32,256]{3,2,1,0:T(8,128)(2,1)S(1)}, bf16[4,2,32,256]{3,2,1,0:T(8,128)(2,1)S(1)}, u32[]{:S(2)}, u32[]{:S(2)}) collective-permute-start(bf16[4,2,32,256]{3,2,1,0:T(8,128)(2,1)S(1)} %pad_maximum_fusion.part), channel_id=1, source_target_pairs={{0,5},{1,4},{2,7},{3,6},{4,1},{5,0},{6,3},{7,2},{8,13},{9,12},{10,... | collective-permute-start | bytes 393224 | tf_op jit(solution)/shard_map/ppermute | solution.py:25
  26.1 6.7 %collective-permute-start.11 = (bf16[2,32,256]{2,1,0:T(8,128)(2,1)S(1)}, bf16[2,32,256]{2,1,0:T(8,128)(2,1)S(1)}, u32[]{:S(2)}, u32[]{:S(2)}) collective-permute-start(bf16[2,32,256]{2,1,0:T(8,128)(2,1)S(1)} %shard_map.65.after.refs_1_.known), channel_id=1, source_target_pairs={{0,9},{1,8},{2,11},{3,10},{4,13},{5,12},{6,15},{7,14},{8,1},{9,0},... | collective-permute-start | bytes 98312 | tf_op jit(solution)/shard_map/ppermute | solution.py:25
  26.1 6.6 %collective-permute-start.12 = (bf16[2,32,256]{2,1,0:T(8,128)(2,1)S(1)}, bf16[2,32,256]{2,1,0:T(8,128)(2,1)S(1)}, u32[]{:S(2)}, u32[]{:S(2)}) collective-permute-start(bf16[2,32,256]{2,1,0:T(8,128)(2,1)S(1)} %shard_map.65.after.refs_1_.known), channel_id=1, source_target_pairs={{0,16},{1,17},{2,18},{3,19},{4,20},{5,21},{6,22},{7,23},{8,24},{9,... | collective-permute-start | bytes 98312 | tf_op jit(solution)/shard_map/ppermute | solution.py:25
  27.6 5.2 %collective-permute-start.13 = (bf16[2,32,256]{2,1,0:T(8,128)(2,1)S(1)}, bf16[2,32,256]{2,1,0:T(8,128)(2,1)S(1)}, u32[]{:S(2)}, u32[]{:S(2)}) collective-permute-start(bf16[2,32,256]{2,1,0:T(8,128)(2,1)S(1)} %shard_map.65.after.refs_1_.known), channel_id=1, source_target_pairs={{0,25},{1,24},{2,27},{3,26},{4,29},{5,28},{6,31},{7,30},{8,17},{9,... | collective-permute-start | bytes 98312 | tf_op jit(solution)/shard_map/ppermute | solution.py:25
  32.8 5.4 %collective-permute-start.16 = (bf16[4,2,32,256]{3,2,1,0:T(8,128)(2,1)S(1)}, bf16[4,2,32,256]{3,2,1,0:T(8,128)(2,1)S(1)}, u32[]{:S(2)}, u32[]{:S(2)}) collective-permute-start(bf16[4,2,32,256]{3,2,1,0:T(8,128)(2,1)S(1)} %pad_maximum_fusion.1.part), channel_id=1, source_target_pairs={{0,7},{1,6},{2,5},{3,4},{4,3},{5,2},{6,1},{7,0},{8,15},{9,14},{10,... | collective-permute-start | bytes 393224 | tf_op jit(solution)/shard_map/ppermute | solution.py:25
  34.5 5.0 %collective-permute-start.15 = (bf16[4,2,32,256]{3,2,1,0:T(8,128)(2,1)S(1)}, bf16[4,2,32,256]{3,2,1,0:T(8,128)(2,1)S(1)}, u32[]{:S(2)}, u32[]{:S(2)}) collective-permute-start(bf16[4,2,32,256]{3,2,1,0:T(8,128)(2,1)S(1)} %pad_maximum_fusion.1.part), channel_id=1, source_target_pairs={{0,2},{1,3},{2,0},{3,1},{4,6},{5,7},{6,4},{7,5},{8,10},{9,11},{10,... | collective-permute-start | bytes 393224 | tf_op jit(solution)/shard_map/ppermute | solution.py:25
  35.0 5.1 %collective-permute-start.14 = (bf16[4,2,32,256]{3,2,1,0:T(8,128)(2,1)S(1)}, bf16[4,2,32,256]{3,2,1,0:T(8,128)(2,1)S(1)}, u32[]{:S(2)}, u32[]{:S(2)}) collective-permute-start(bf16[4,2,32,256]{3,2,1,0:T(8,128)(2,1)S(1)} %pad_maximum_fusion.1.part), channel_id=1, source_target_pairs={{0,5},{1,4},{2,7},{3,6},{4,1},{5,0},{6,3},{7,2},{8,13},{9,12},{10,... | collective-permute-start | bytes 393224 | tf_op jit(solution)/shard_map/ppermute | solution.py:25
  41.0 6.7 %collective-permute-start.17 = (bf16[2,32,256]{2,1,0:T(8,128)(2,1)S(1)}, bf16[2,32,256]{2,1,0:T(8,128)(2,1)S(1)}, u32[]{:S(2)}, u32[]{:S(2)}) collective-permute-start(bf16[2,32,256]{2,1,0:T(8,128)(2,1)S(1)} %shard_map.70.after.refs_2_.known), channel_id=1, source_target_pairs={{0,9},{1,8},{2,11},{3,10},{4,13},{5,12},{6,15},{7,14},{8,1},{9,0},... | collective-permute-start | bytes 98312 | tf_op jit(solution)/shard_map/ppermute | solution.py:25
  41.0 6.6 %collective-permute-start.18 = (bf16[2,32,256]{2,1,0:T(8,128)(2,1)S(1)}, bf16[2,32,256]{2,1,0:T(8,128)(2,1)S(1)}, u32[]{:S(2)}, u32[]{:S(2)}) collective-permute-start(bf16[2,32,256]{2,1,0:T(8,128)(2,1)S(1)} %shard_map.70.after.refs_2_.known), channel_id=1, source_target_pairs={{0,16},{1,17},{2,18},{3,19},{4,20},{5,21},{6,22},{7,23},{8,24},{9,... | collective-permute-start | bytes 98312 | tf_op jit(solution)/shard_map/ppermute | solution.py:25
  43.5 5.2 %collective-permute-start.19 = (bf16[2,32,256]{2,1,0:T(8,128)(2,1)S(1)}, bf16[2,32,256]{2,1,0:T(8,128)(2,1)S(1)}, u32[]{:S(2)}, u32[]{:S(2)}) collective-permute-start(bf16[2,32,256]{2,1,0:T(8,128)(2,1)S(1)} %shard_map.70.after.refs_2_.known), channel_id=1, source_target_pairs={{0,25},{1,24},{2,27},{3,26},{4,29},{5,28},{6,31},{7,30},{8,17},{9,... | collective-permute-start | bytes 98312 | tf_op jit(solution)/shard_map/ppermute | solution.py:25
  48.7 5.4 %collective-permute-start.22 = (bf16[4,2,32,256]{3,2,1,0:T(8,128)(2,1)S(1)}, bf16[4,2,32,256]{3,2,1,0:T(8,128)(2,1)S(1)}, u32[]{:S(2)}, u32[]{:S(2)}) collective-permute-start(bf16[4,2,32,256]{3,2,1,0:T(8,128)(2,1)S(1)} %pad_maximum_fusion.2.part), channel_id=1, source_target_pairs={{0,7},{1,6},{2,5},{3,4},{4,3},{5,2},{6,1},{7,0},{8,15},{9,14},{10,... | collective-permute-start | bytes 393224 | tf_op jit(solution)/shard_map/ppermute | solution.py:25
  51.0 5.0 %collective-permute-start.21 = (bf16[4,2,32,256]{3,2,1,0:T(8,128)(2,1)S(1)}, bf16[4,2,32,256]{3,2,1,0:T(8,128)(2,1)S(1)}, u32[]{:S(2)}, u32[]{:S(2)}) collective-permute-start(bf16[4,2,32,256]{3,2,1,0:T(8,128)(2,1)S(1)} %pad_maximum_fusion.2.part), channel_id=1, source_target_pairs={{0,2},{1,3},{2,0},{3,1},{4,6},{5,7},{6,4},{7,5},{8,10},{9,11},{10,... | collective-permute-start | bytes 393224 | tf_op jit(solution)/shard_map/ppermute | solution.py:25
  51.6 5.1 %collective-permute-start.20 = (bf16[4,2,32,256]{3,2,1,0:T(8,128)(2,1)S(1)}, bf16[4,2,32,256]{3,2,1,0:T(8,128)(2,1)S(1)}, u32[]{:S(2)}, u32[]{:S(2)}) collective-permute-start(bf16[4,2,32,256]{3,2,1,0:T(8,128)(2,1)S(1)} %pad_maximum_fusion.2.part), channel_id=1, source_target_pairs={{0,5},{1,4},{2,7},{3,6},{4,1},{5,0},{6,3},{7,2},{8,13},{9,12},{10,... | collective-permute-start | bytes 393224 | tf_op jit(solution)/shard_map/ppermute | solution.py:25
  58.8 5.4 %collective-permute-start.24 = (bf16[4,2,32,256]{3,2,1,0:T(8,128)(2,1)S(1)}, bf16[4,2,32,256]{3,2,1,0:T(8,128)(2,1)S(1)}, u32[]{:S(2)}, u32[]{:S(2)}) collective-permute-start(bf16[4,2,32,256]{3,2,1,0:T(8,128)(2,1)S(1)} %get-tuple-element.87), channel_id=1, source_target_pairs={{0,7},{1,6},{2,5},{3,4},{4,3},{5,2},{6,1},{7,0},{8,15},{9,14},{10,... | collective-permute-start | bytes 393224 | tf_op jit(solution)/shard_map/ppermute | solution.py:25
  59.9 5.0 %collective-permute-start.25 = (bf16[4,2,32,256]{3,2,1,0:T(8,128)(2,1)S(1)}, bf16[4,2,32,256]{3,2,1,0:T(8,128)(2,1)S(1)}, u32[]{:S(2)}, u32[]{:S(2)}) collective-permute-start(bf16[4,2,32,256]{3,2,1,0:T(8,128)(2,1)S(1)} %get-tuple-element.88), channel_id=1, source_target_pairs={{0,2},{1,3},{2,0},{3,1},{4,6},{5,7},{6,4},{7,5},{8,10},{9,11},{10,... | collective-permute-start | bytes 393224 | tf_op jit(solution)/shard_map/ppermute | solution.py:25
  60.6 4.9 %collective-permute-start.26 = (bf16[4,2,32,256]{3,2,1,0:T(8,128)(2,1)S(1)}, bf16[4,2,32,256]{3,2,1,0:T(8,128)(2,1)S(1)}, u32[]{:S(2)}, u32[]{:S(2)}) collective-permute-start(bf16[4,2,32,256]{3,2,1,0:T(8,128)(2,1)S(1)} %get-tuple-element.89), channel_id=1, source_target_pairs={{0,5},{1,4},{2,7},{3,6},{4,1},{5,0},{6,3},{7,2},{8,13},{9,12},{10,... | collective-permute-start | bytes 393224 | tf_op jit(solution)/shard_map/ppermute | solution.py:25
  65.6 3.9 %collective-permute-start.27 = (bf16[2,32,256]{2,1,0:T(8,128)(2,1)S(1)}, bf16[2,32,256]{2,1,0:T(8,128)(2,1)S(1)}, u32[]{:S(2)}, u32[]{:S(2)}) collective-permute-start(bf16[2,32,256]{2,1,0:T(8,128)(2,1)S(1)} %get-tuple-element.91), channel_id=1, source_target_pairs={{0,9},{1,8},{2,11},{3,10},{4,13},{5,12},{6,15},{7,14},{8,1},{9,0},... | collective-permute-start | bytes 98312 | tf_op jit(solution)/shard_map/ppermute | solution.py:25
  65.6 4.9 %collective-permute-start.28 = (bf16[2,32,256]{2,1,0:T(8,128)(2,1)S(1)}, bf16[2,32,256]{2,1,0:T(8,128)(2,1)S(1)}, u32[]{:S(2)}, u32[]{:S(2)}) collective-permute-start(bf16[2,32,256]{2,1,0:T(8,128)(2,1)S(1)} %get-tuple-element.92), channel_id=1, source_target_pairs={{0,16},{1,17},{2,18},{3,19},{4,20},{5,21},{6,22},{7,23},{8,24},{9,... | collective-permute-start | bytes 98312 | tf_op jit(solution)/shard_map/ppermute | solution.py:25
  67.1 5.1 %collective-permute-start.29 = (bf16[2,32,256]{2,1,0:T(8,128)(2,1)S(1)}, bf16[2,32,256]{2,1,0:T(8,128)(2,1)S(1)}, u32[]{:S(2)}, u32[]{:S(2)}) collective-permute-start(bf16[2,32,256]{2,1,0:T(8,128)(2,1)S(1)} %get-tuple-element.93), channel_id=1, source_target_pairs={{0,25},{1,24},{2,27},{3,26},{4,29},{5,28},{6,31},{7,30},{8,17},{9,... | collective-permute-start | bytes 98312 | tf_op jit(solution)/shard_map/ppermute | solution.py:25
  73.5 5.3 %collective-permute-start.30 = (bf16[4,2,32,256]{3,2,1,0:T(8,128)(2,1)S(1)}, bf16[4,2,32,256]{3,2,1,0:T(8,128)(2,1)S(1)}, u32[]{:S(2)}, u32[]{:S(2)}) collective-permute-start(bf16[4,2,32,256]{3,2,1,0:T(8,128)(2,1)S(1)} %get-tuple-element.95), channel_id=1, source_target_pairs={{0,7},{1,6},{2,5},{3,4},{4,3},{5,2},{6,1},{7,0},{8,15},{9,14},{10,... | collective-permute-start | bytes 393224 | tf_op jit(solution)/shard_map/ppermute | solution.py:25
  75.2 5.0 %collective-permute-start.31 = (bf16[4,2,32,256]{3,2,1,0:T(8,128)(2,1)S(1)}, bf16[4,2,32,256]{3,2,1,0:T(8,128)(2,1)S(1)}, u32[]{:S(2)}, u32[]{:S(2)}) collective-permute-start(bf16[4,2,32,256]{3,2,1,0:T(8,128)(2,1)S(1)} %get-tuple-element.96), channel_id=1, source_target_pairs={{0,2},{1,3},{2,0},{3,1},{4,6},{5,7},{6,4},{7,5},{8,10},{9,11},{10,... | collective-permute-start | bytes 393224 | tf_op jit(solution)/shard_map/ppermute | solution.py:25
  75.9 4.4 %collective-permute-start.32 = (bf16[4,2,32,256]{3,2,1,0:T(8,128)(2,1)S(1)}, bf16[4,2,32,256]{3,2,1,0:T(8,128)(2,1)S(1)}, u32[]{:S(2)}, u32[]{:S(2)}) collective-permute-start(bf16[4,2,32,256]{3,2,1,0:T(8,128)(2,1)S(1)} %get-tuple-element.97), channel_id=1, source_target_pairs={{0,5},{1,4},{2,7},{3,6},{4,1},{5,0},{6,3},{7,2},{8,13},{9,12},{10,... | collective-permute-start | bytes 393224 | tf_op jit(solution)/shard_map/ppermute | solution.py:25
  80.3 3.9 %collective-permute-start.33 = (bf16[2,32,256]{2,1,0:T(8,128)(2,1)S(1)}, bf16[2,32,256]{2,1,0:T(8,128)(2,1)S(1)}, u32[]{:S(2)}, u32[]{:S(2)}) collective-permute-start(bf16[2,32,256]{2,1,0:T(8,128)(2,1)S(1)} %get-tuple-element.99), channel_id=1, source_target_pairs={{0,9},{1,8},{2,11},{3,10},{4,13},{5,12},{6,15},{7,14},{8,1},{9,0},... | collective-permute-start | bytes 98312 | tf_op jit(solution)/shard_map/ppermute | solution.py:25
  80.4 4.9 %collective-permute-start.34 = (bf16[2,32,256]{2,1,0:T(8,128)(2,1)S(1)}, bf16[2,32,256]{2,1,0:T(8,128)(2,1)S(1)}, u32[]{:S(2)}, u32[]{:S(2)}) collective-permute-start(bf16[2,32,256]{2,1,0:T(8,128)(2,1)S(1)} %get-tuple-element.100), channel_id=1, source_target_pairs={{0,16},{1,17},{2,18},{3,19},{4,20},{5,21},{6,22},{7,23},{8,24},{9,... | collective-permute-start | bytes 98312 | tf_op jit(solution)/shard_map/ppermute | solution.py:25
  83.3 5.3 %collective-permute-start.35 = (bf16[2,32,256]{2,1,0:T(8,128)(2,1)S(1)}, bf16[2,32,256]{2,1,0:T(8,128)(2,1)S(1)}, u32[]{:S(2)}, u32[]{:S(2)}) collective-permute-start(bf16[2,32,256]{2,1,0:T(8,128)(2,1)S(1)} %get-tuple-element.101), channel_id=1, source_target_pairs={{0,25},{1,24},{2,27},{3,26},{4,29},{5,28},{6,31},{7,30},{8,17},{9,... | collective-permute-start | bytes 98312 | tf_op jit(solution)/shard_map/ppermute | solution.py:25
  90.0 7.1 %collective-permute-start.36 = (bf16[4,2,32,256]{3,2,1,0:T(8,128)(2,1)S(1)}, bf16[4,2,32,256]{3,2,1,0:T(8,128)(2,1)S(1)}, u32[]{:S(2)}, u32[]{:S(2)}) collective-permute-start(bf16[4,2,32,256]{3,2,1,0:T(8,128)(2,1)S(1)} %get-tuple-element.103), channel_id=1, source_target_pairs={{0,7},{1,6},{2,5},{3,4},{4,3},{5,2},{6,1},{7,0},{8,15},{9,14},{10,... | collective-permute-start | bytes 393224 | tf_op jit(solution)/shard_map/ppermute | solution.py:25
  91.5 5.6 %collective-permute-start.37 = (bf16[4,2,32,256]{3,2,1,0:T(8,128)(2,1)S(1)}, bf16[4,2,32,256]{3,2,1,0:T(8,128)(2,1)S(1)}, u32[]{:S(2)}, u32[]{:S(2)}) collective-permute-start(bf16[4,2,32,256]{3,2,1,0:T(8,128)(2,1)S(1)} %get-tuple-element.104), channel_id=1, source_target_pairs={{0,2},{1,3},{2,0},{3,1},{4,6},{5,7},{6,4},{7,5},{8,10},{9,11},{10,... | collective-permute-start | bytes 393224 | tf_op jit(solution)/shard_map/ppermute | solution.py:25
  92.1 4.9 %collective-permute-start.38 = (bf16[4,2,32,256]{3,2,1,0:T(8,128)(2,1)S(1)}, bf16[4,2,32,256]{3,2,1,0:T(8,128)(2,1)S(1)}, u32[]{:S(2)}, u32[]{:S(2)}) collective-permute-start(bf16[4,2,32,256]{3,2,1,0:T(8,128)(2,1)S(1)} %get-tuple-element.105), channel_id=1, source_target_pairs={{0,5},{1,4},{2,7},{3,6},{4,1},{5,0},{6,3},{7,2},{8,13},{9,12},{10,... | collective-permute-start | bytes 393224 | tf_op jit(solution)/shard_map/ppermute | solution.py:25
  92.9 15.6 %collective-permute-start.23 = (bf16[4,32,256]{2,1,0:T(8,128)(2,1)S(1)}, bf16[4,32,256]{2,1,0:T(8,128)(2,1)S(1)}, u32[]{:S(2)}, u32[]{:S(2)}) collective-permute-start(bf16[4,32,256]{2,1,0:T(8,128)(2,1)S(1)} %get-tuple-element.85), channel_id=1, source_target_pairs={{0,1},{1,0},{2,3},{3,2},{4,5},{5,4},{6,7},{7,6},{8,9},{9,8},{10,11... | collective-permute-start | bytes 196616 | tf_op jit(solution)/shard_map/ppermute | solution.py:25
  97.1 7.2 %collective-permute-start.39 = (bf16[2,32,256]{2,1,0:T(8,128)(2,1)S(1)}, bf16[2,32,256]{2,1,0:T(8,128)(2,1)S(1)}, u32[]{:S(2)}, u32[]{:S(2)}) collective-permute-start(bf16[2,32,256]{2,1,0:T(8,128)(2,1)S(1)} %get-tuple-element.107), channel_id=1, source_target_pairs={{0,9},{1,8},{2,11},{3,10},{4,13},{5,12},{6,15},{7,14},{8,1},{9,0},... | collective-permute-start | bytes 98312 | tf_op jit(solution)/shard_map/ppermute | solution.py:25
  97.2 7.1 %collective-permute-start.40 = (bf16[2,32,256]{2,1,0:T(8,128)(2,1)S(1)}, bf16[2,32,256]{2,1,0:T(8,128)(2,1)S(1)}, u32[]{:S(2)}, u32[]{:S(2)}) collective-permute-start(bf16[2,32,256]{2,1,0:T(8,128)(2,1)S(1)} %get-tuple-element.108), channel_id=1, source_target_pairs={{0,16},{1,17},{2,18},{3,19},{4,20},{5,21},{6,22},{7,23},{8,24},{9,... | collective-permute-start | bytes 98312 | tf_op jit(solution)/shard_map/ppermute | solution.py:25
  100.3 5.1 %collective-permute-start.41 = (bf16[2,32,256]{2,1,0:T(8,128)(2,1)S(1)}, bf16[2,32,256]{2,1,0:T(8,128)(2,1)S(1)}, u32[]{:S(2)}, u32[]{:S(2)}) collective-permute-start(bf16[2,32,256]{2,1,0:T(8,128)(2,1)S(1)} %get-tuple-element.109), channel_id=1, source_target_pairs={{0,25},{1,24},{2,27},{3,26},{4,29},{5,28},{6,31},{7,30},{8,17},{9,... | collective-permute-start | bytes 98312 | tf_op jit(solution)/shard_map/ppermute | solution.py:25
  101.0 8.2 %collective-permute-start.43 = (bf16[3,32,256]{2,1,0:T(8,128)(2,1)S(1)}, bf16[3,32,256]{2,1,0:T(8,128)(2,1)S(1)}, u32[]{:S(2)}, u32[]{:S(2)}) collective-permute-start(bf16[3,32,256]{2,1,0:T(8,128)(2,1)S(1)} %get-tuple-element.113), channel_id=1, source_target_pairs={{0,1},{1,0},{2,3},{3,2},{4,5},{5,4},{6,7},{7,6},{8,9},{9,8},{10,11... | collective-permute-start | bytes 147464 | tf_op jit(solution)/shard_map/ppermute | solution.py:25
  105.6 3.8 %collective-permute-start.42 = (bf16[32,256]{1,0:T(8,128)(2,1)S(1)}, bf16[32,256]{1,0:T(8,128)(2,1)S(1)}, u32[]{:S(2)}, u32[]{:S(2)}) collective-permute-start(bf16[32,256]{1,0:T(8,128)(2,1)S(1)} %get-tuple-element.111), channel_id=1, source_target_pairs={{0,1},{1,0},{2,3},{3,2},{4,5},{5,4},{6,7},{7,6},{8,9},{9,8},{10,11... | collective-permute-start | bytes 49160 | tf_op jit(solution)/shard_map/ppermute | solution.py:25

commit v6 on v5

--- a/solution.py
+++ b/solution.py
@@ -154,6 +154,16 @@
     terms = [meet(part, spread, i, j) for i in range(2)]
     for i in range(2):
         refs[-1][i] = refs[0][i] + terms[i] if len(refs) > 1 else terms[i]
+
+
+def early_kernel(spread, *refs):
+    parts, out = refs[:-1], refs[-1]
+    totals = []
+    for i in range(2):
+        terms = [meet(part, spread, i, j) for j, part in enumerate(parts)]
+        totals.append(sum(terms[1:], terms[0]))
+    for i in range(2):
+        out[i] = totals[i]
 
 
 def finish(spread, late, partial, rhs, diag):
@@ -312,7 +322,9 @@
         parts = [jnp.stack(arrived)]
         parts += [swap(parts[0], m) for m in plane]
         partial = []
-        for j in range(first):
+        if level == 1:
+            partial = [call(early_kernel, shape(2, dtype=jnp.float32), [spread] + parts[:first], flops=first * work)]
+        for j in range(first if level > 1 else 0):
             kernel = functools.partial(more_kernel, j)
             partial = [call(kernel, shape(2, dtype=jnp.float32), [spread, parts[j]] + partial, flops=work)]
         return [spread, rhs_own, rhs_other, diag[level]] + parts[first:] + partial

time: 110 us -> 110 us (level)
    pallas_call x30 -> x28, Pallas kernels: 25.5 us -> 25.3 us  [call(): pl.pallas_call(kernel, out_shape=out_shape, in_specs=[VMEM_SPEC] * len(op...]
  transfers between devices with their start and end apart: 44 -> 44, of which waited for: 20 -> 22; matrix products, arithmetic and copies ran while one was open for 0% -> 0% of each run, Pallas kernels for 16% -> 16%
where the time goes in v6:
time: 110 us
  starting transfers between devices  54 us (49%)
  waiting for transfers between devices  28.3 us (26%)
  Pallas kernels  25.3 us (23%)
    ppermute x44, starting transfers between devices, swap(): return lax.ppermute(value, 'rows', [(i, i ^ mask) for i in range(size)])  54 us
    ppermute x44, waiting for transfers between devices, swap(): return lax.ppermute(value, 'rows', [(i, i ^ mask) for i in range(size)])  28.3 us
    pallas_call x28, Pallas kernels, call(): pl.pallas_call(kernel, out_shape=out_shape, in_specs=[VMEM_SPEC] * len(op...  25.3 us
  transfers between devices with their start and end apart: 44, of which 22 were waited for; matrix products, arithmetic and copies ran while one was open for 0% of the time, Pallas kernels for 16%

profile of v6, /device:TPU:0, one launch (start us, length us, event | category | flops | bytes accessed | tf_op | source)
XLA Modules:
  0.0 109.5 jit_solution(16021234437177589727)
XLA Ops:
  0.6 1.1 %shard_map.59 = (bf16[32,256]{1,0:T(8,128)(2,1)S(1)}, bf16[32,256]{1,0:T(8,128)(2,1)S(1)}) custom-call(bf16[4,1,64,256]{3,2,1,0:T(8,128)(2,1)} %rhs.3, bf16[4,1,256,256]{3,2,1,0:T(8,128)(2,1)} %diag0.5), custom_call_target="tpu_custom_call" | custom-call | tf_op jit(solution)/shard_map/pallas_call | solution.py:37
  2.4 0.9 copy-done
  4.2 2.7 %collective-permute-start.5 = (bf16[2,32,256]{2,1,0:T(8,128)(2,1)S(1)}, bf16[2,32,256]{2,1,0:T(8,128)(2,1)S(1)}, u32[]{:S(2)}, u32[]{:S(2)}) collective-permute-start(bf16[2,32,256]{2,1,0:T(8,128)(2,1)S(1)} %get-tuple-element.117.after.refs_0_.known), channel_id=1, source_target_pairs={{0,9},{1,8},{2,11},{3,10},{4,13},{5,12},{6,15},{7,14},{8,1},{9,0},... | collective-permute-start | bytes 98312 | tf_op jit(solution)/shard_map/ppermute | solution.py:25
  6.9 2.6 %collective-permute-start.6 = (bf16[2,32,256]{2,1,0:T(8,128)(2,1)S(1)}, bf16[2,32,256]{2,1,0:T(8,128)(2,1)S(1)}, u32[]{:S(2)}, u32[]{:S(2)}) collective-permute-start(bf16[2,32,256]{2,1,0:T(8,128)(2,1)S(1)} %get-tuple-element.117.after.refs_0_.known), channel_id=1, source_target_pairs={{0,16},{1,17},{2,18},{3,19},{4,20},{5,21},{6,22},{7,23},{8,24},{9,... | collective-permute-start | bytes 98312 | tf_op jit(solution)/shard_map/ppermute | solution.py:25
  9.5 2.5 %collective-permute-done.6 = bf16[2,32,256]{2,1,0:T(8,128)(2,1)S(1)} collective-permute-done((bf16[2,32,256]{2,1,0:T(8,128)(2,1)S(1)}, bf16[2,32,256]{2,1,0:T(8,128)(2,1)S(1)}, u32[]{:S(2)}, u32[]{:S(2)}) %collective-permute-start.6) | collective-permute-done | bytes 32800 | tf_op jit(solution)/shard_map/ppermute | solution.py:25
  12.0 2.8 %collective-permute-done.7 = bf16[2,32,256]{2,1,0:T(8,128)(2,1)S(1)} collective-permute-done((bf16[2,32,256]{2,1,0:T(8,128)(2,1)S(1)}, bf16[2,32,256]{2,1,0:T(8,128)(2,1)S(1)}, u32[]{:S(2)}, u32[]{:S(2)}) %collective-permute-start.7) | collective-permute-done | bytes 32800 | tf_op jit(solution)/shard_map/ppermute | solution.py:25
  14.9 1.6 %collective-permute-start.10 = (bf16[4,2,32,256]{3,2,1,0:T(8,128)(2,1)S(1)}, bf16[4,2,32,256]{3,2,1,0:T(8,128)(2,1)S(1)}, u32[]{:S(2)}, u32[]{:S(2)}) collective-permute-start(bf16[4,2,32,256]{3,2,1,0:T(8,128)(2,1)S(1)} %pad_maximum_fusion.refs_0_), channel_id=1, source_target_pairs={{0,2},{1,3},{2,0},{3,1},{4,6},{5,7},{6,4},{7,5},{8,10},{9,11},{10,... | collective-permute-start | bytes 393224 | tf_op jit(solution)/shard_map/ppermute | solution.py:25
  16.4 0.9 collective-permute-start.9
  17.4 0.8 collective-permute-start.8
  18.2 3.0 %shard_map.61 = (bf16[2,32,256,256]{3,2,1,0:T(8,128)(2,1)S(1)}, bf16[2,2,256,256]{3,2,1,0:T(8,128)(2,1)S(1)}) custom-call(s32[3,1,16]{2,1,0:T(1,128)} %own_pattern.5, s32[3,1,16]{2,1,0:T(1,128)S(1)} %collective-permute-done.1.other_pattern, bf16[2,32,256]{2,1,0:T(8,128)(2,1)S(1)} %get-tuple-element.117.after.refs_0_.known, ...), custom_call_target="tpu_custom_call" | custom-call | flops 134217728 | tf_op jit(solution)/shard_map/pallas_call | solution.py:37
  21.2 2.3 %collective-permute-done.9.refs_1_ = bf16[4,2,32,256]{3,2,1,0:T(8,128)(2,1)S(1)} collective-permute-done((bf16[4,2,32,256]{3,2,1,0:T(8,128)(2,1)S(1)}, bf16[4,2,32,256]{3,2,1,0:T(8,128)(2,1)S(1)}, u32[]{:S(2)}, u32[]{:S(2)}) %collective-permute-start.9) | collective-permute-done | bytes 131104 | tf_op jit(solution)/shard_map/ppermute | solution.py:25
  23.5 1.9 %shard_map.62.refs_1_ = f32[2,32,256]{2,1,0:T(8,128)S(1)} custom-call(bf16[2,32,256,256]{3,2,1,0:T(8,128)(2,1)S(1)} %get-tuple-element.65.spread, bf16[4,2,32,256]{3,2,1,0:T(8,128)(2,1)S(1)} %pad_maximum_fusion.refs_0_, bf16[4,2,32,256]{3,2,1,0:T(8,128)(2,1)S(1)} %collective-permute-done.9.refs_1_, bf16[4,2,32,256]{3,2,1,0:T(8,128)(2,1)S(1)} %collective-permute-done.10.refs_2_), custom_call_target="tpu_custom_call" | custom-call | flops 201326592 | tf_op jit(solution)/shard_map/pallas_call | solution.py:37
  25.5 0.8 shard_map.63.after.refs_1_.known
  26.3 2.2 %collective-permute-start.12 = (bf16[2,32,256]{2,1,0:T(8,128)(2,1)S(1)}, bf16[2,32,256]{2,1,0:T(8,128)(2,1)S(1)}, u32[]{:S(2)}, u32[]{:S(2)}) collective-permute-start(bf16[2,32,256]{2,1,0:T(8,128)(2,1)S(1)} %shard_map.63.after.refs_1_.known), channel_id=1, source_target_pairs={{0,16},{1,17},{2,18},{3,19},{4,20},{5,21},{6,22},{7,23},{8,24},{9,... | collective-permute-start | bytes 98312 | tf_op jit(solution)/shard_map/ppermute | solution.py:25
  28.5 1.6 %collective-permute-start.13 = (bf16[2,32,256]{2,1,0:T(8,128)(2,1)S(1)}, bf16[2,32,256]{2,1,0:T(8,128)(2,1)S(1)}, u32[]{:S(2)}, u32[]{:S(2)}) collective-permute-start(bf16[2,32,256]{2,1,0:T(8,128)(2,1)S(1)} %shard_map.63.after.refs_1_.known), channel_id=1, source_target_pairs={{0,25},{1,24},{2,27},{3,26},{4,29},{5,28},{6,31},{7,30},{8,17},{9,... | collective-permute-start | bytes 98312 | tf_op jit(solution)/shard_map/ppermute | solution.py:25
  30.1 2.8 %shard_map.64 = (bf16[2,32,256,256]{3,2,1,0:T(8,128)(2,1)S(1)}, bf16[1,2,256,256]{3,2,1,0:T(8,128)(2,1)S(1)}) custom-call(s32[3,1,16]{2,1,0:T(1,128)} %own_pattern.5, s32[3,1,16]{2,1,0:T(1,128)S(1)} %collective-permute-done.1.other_pattern, bf16[2,32,256]{2,1,0:T(8,128)(2,1)S(1)} %shard_map.63.after.refs_1_.known, bf16[3,1,16,256,256]{4,3,2,1,0:T(8,128)(2,1)} %tiles0.5, ...), custom_call_target="tpu_custom_call" | custom-call | flops 134217728 | tf_op jit(solution)/shard_map/pallas_call | solution.py:37
  33.0 0.7 collective-permute-done.13
  33.7 1.4 %collective-permute-start.16 = (bf16[4,2,32,256]{3,2,1,0:T(8,128)(2,1)S(1)}, bf16[4,2,32,256]{3,2,1,0:T(8,128)(2,1)S(1)}, u32[]{:S(2)}, u32[]{:S(2)}) collective-permute-start(bf16[4,2,32,256]{3,2,1,0:T(8,128)(2,1)S(1)} %pad_maximum_fusion.1.part), channel_id=1, source_target_pairs={{0,7},{1,6},{2,5},{3,4},{4,3},{5,2},{6,1},{7,0},{8,15},{9,14},{10,... | collective-permute-start | bytes 393224 | tf_op jit(solution)/shard_map/ppermute | solution.py:25
  35.0 0.7 collective-permute-start.15
  35.8 0.9 collective-permute-start.14
  36.7 0.7 shard_map.65.refs_0_
  37.4 1.7 %collective-permute-done.16.part = bf16[4,2,32,256]{3,2,1,0:T(8,128)(2,1)S(1)} collective-permute-done((bf16[4,2,32,256]{3,2,1,0:T(8,128)(2,1)S(1)}, bf16[4,2,32,256]{3,2,1,0:T(8,128)(2,1)S(1)}, u32[]{:S(2)}, u32[]{:S(2)}) %collective-permute-start.16) | collective-permute-done | bytes 131104 | tf_op jit(solution)/shard_map/ppermute | solution.py:25
  39.0 0.7 shard_map.66.refs_0_
  40.1 0.7 shard_map.67.refs_1_
  40.8 0.8 shard_map.68.after.refs_2_.known
  41.7 2.2 %collective-permute-start.18 = (bf16[2,32,256]{2,1,0:T(8,128)(2,1)S(1)}, bf16[2,32,256]{2,1,0:T(8,128)(2,1)S(1)}, u32[]{:S(2)}, u32[]{:S(2)}) collective-permute-start(bf16[2,32,256]{2,1,0:T(8,128)(2,1)S(1)} %shard_map.68.after.refs_2_.known), channel_id=1, source_target_pairs={{0,16},{1,17},{2,18},{3,19},{4,20},{5,21},{6,22},{7,23},{8,24},{9,... | collective-permute-start | bytes 98312 | tf_op jit(solution)/shard_map/ppermute | solution.py:25
  44.0 1.6 %collective-permute-start.19 = (bf16[2,32,256]{2,1,0:T(8,128)(2,1)S(1)}, bf16[2,32,256]{2,1,0:T(8,128)(2,1)S(1)}, u32[]{:S(2)}, u32[]{:S(2)}) collective-permute-start(bf16[2,32,256]{2,1,0:T(8,128)(2,1)S(1)} %shard_map.68.after.refs_2_.known), channel_id=1, source_target_pairs={{0,25},{1,24},{2,27},{3,26},{4,29},{5,28},{6,31},{7,30},{8,17},{9,... | collective-permute-start | bytes 98312 | tf_op jit(solution)/shard_map/ppermute | solution.py:25
  45.5 2.8 %shard_map.69 = (bf16[2,32,256,256]{3,2,1,0:T(8,128)(2,1)S(1)}, bf16[1,2,256,256]{3,2,1,0:T(8,128)(2,1)S(1)}) custom-call(s32[3,1,16]{2,1,0:T(1,128)} %own_pattern.5, s32[3,1,16]{2,1,0:T(1,128)S(1)} %collective-permute-done.1.other_pattern, bf16[2,32,256]{2,1,0:T(8,128)(2,1)S(1)} %shard_map.68.after.refs_2_.known, bf16[3,1,16,256,256]{4,3,2,1,0:T(8,128)(2,1)} %tiles0.5, ...), custom_call_target="tpu_custom_call" | custom-call | flops 134217728 | tf_op jit(solution)/shard_map/pallas_call | solution.py:37
  48.4 1.1 collective-permute-done.19
  49.4 1.5 %collective-permute-start.22 = (bf16[4,2,32,256]{3,2,1,0:T(8,128)(2,1)S(1)}, bf16[4,2,32,256]{3,2,1,0:T(8,128)(2,1)S(1)}, u32[]{:S(2)}, u32[]{:S(2)}) collective-permute-start(bf16[4,2,32,256]{3,2,1,0:T(8,128)(2,1)S(1)} %pad_maximum_fusion.2.part), channel_id=1, source_target_pairs={{0,7},{1,6},{2,5},{3,4},{4,3},{5,2},{6,1},{7,0},{8,15},{9,14},{10,... | collective-permute-start | bytes 393224 | tf_op jit(solution)/shard_map/ppermute | solution.py:25
  51.6 0.9 collective-permute-start.20
  52.4 0.7 shard_map.70.refs_0_
  53.1 1.7 %collective-permute-done.22.part = bf16[4,2,32,256]{3,2,1,0:T(8,128)(2,1)S(1)} collective-permute-done((bf16[4,2,32,256]{3,2,1,0:T(8,128)(2,1)S(1)}, bf16[4,2,32,256]{3,2,1,0:T(8,128)(2,1)S(1)}, u32[]{:S(2)}, u32[]{:S(2)}) %collective-permute-start.22) | collective-permute-done | bytes 131104 | tf_op jit(solution)/shard_map/ppermute | solution.py:25
  54.8 0.7 shard_map.71.refs_0_
  55.9 0.7 shard_map.72.refs_1_
  56.7 2.1 %shard_map.73 = (bf16[2,32,256]{2,1,0:T(8,128)(2,1)S(1)}, bf16[2,32,256]{2,1,0:T(8,128)(2,1)S(1)}, bf16[4,2,32,256]{3,2,1,0:T(8,128)(2,1)S(1)}, bf16[4,2,32,256]...) custom-call(bf16[2,32,256,256]{3,2,1,0:T(8,128)(2,1)S(1)} %get-tuple-element.77.spread, ...), custom_call_target="tpu_custom_call" | custom-call | flops 268435456 | tf_op jit(solution)/shard_map/pallas_call | solution.py:37
  58.8 1.1 %collective-permute-start.24 = (bf16[4,2,32,256]{3,2,1,0:T(8,128)(2,1)S(1)}, bf16[4,2,32,256]{3,2,1,0:T(8,128)(2,1)S(1)}, u32[]{:S(2)}, u32[]{:S(2)}) collective-permute-start(bf16[4,2,32,256]{3,2,1,0:T(8,128)(2,1)S(1)} %get-tuple-element.87), channel_id=1, source_target_pairs={{0,7},{1,6},{2,5},{3,4},{4,3},{5,2},{6,1},{7,0},{8,15},{9,14},{10,... | collective-permute-start | bytes 393224 | tf_op jit(solution)/shard_map/ppermute | solution.py:25
  59.9 0.9 collective-permute-start.25
  60.7 1.0 collective-permute-start.26
  62.2 1.9 %collective-permute-done.24.a = bf16[4,2,32,256]{3,2,1,0:T(8,128)(2,1)S(1)} collective-permute-done((bf16[4,2,32,256]{3,2,1,0:T(8,128)(2,1)S(1)}, bf16[4,2,32,256]{3,2,1,0:T(8,128)(2,1)S(1)}, u32[]{:S(2)}, u32[]{:S(2)}) %collective-permute-start.24) | collective-permute-done | bytes 131104 | tf_op jit(solution)/shard_map/ppermute | solution.py:25
  64.1 1.0 collective-permute-done.25.b
  65.6 1.8 %collective-permute-start.28 = (bf16[2,32,256]{2,1,0:T(8,128)(2,1)S(1)}, bf16[2,32,256]{2,1,0:T(8,128)(2,1)S(1)}, u32[]{:S(2)}, u32[]{:S(2)}) collective-permute-start(bf16[2,32,256]{2,1,0:T(8,128)(2,1)S(1)} %get-tuple-element.92), channel_id=1, source_target_pairs={{0,16},{1,17},{2,18},{3,19},{4,20},{5,21},{6,22},{7,23},{8,24},{9,... | collective-permute-start | bytes 98312 | tf_op jit(solution)/shard_map/ppermute | solution.py:25
  67.4 2.0 %collective-permute-start.29 = (bf16[2,32,256]{2,1,0:T(8,128)(2,1)S(1)}, bf16[2,32,256]{2,1,0:T(8,128)(2,1)S(1)}, u32[]{:S(2)}, u32[]{:S(2)}) collective-permute-start(bf16[2,32,256]{2,1,0:T(8,128)(2,1)S(1)} %get-tuple-element.93), channel_id=1, source_target_pairs={{0,25},{1,24},{2,27},{3,26},{4,29},{5,28},{6,31},{7,30},{8,17},{9,... | collective-permute-start | bytes 98312 | tf_op jit(solution)/shard_map/ppermute | solution.py:25
  69.5 1.1 collective-permute-done.28.refs_1_
  70.5 2.1 %collective-permute-done.29.refs_2_ = bf16[2,32,256]{2,1,0:T(8,128)(2,1)S(1)} collective-permute-done((bf16[2,32,256]{2,1,0:T(8,128)(2,1)S(1)}, bf16[2,32,256]{2,1,0:T(8,128)(2,1)S(1)}, u32[]{:S(2)}, u32[]{:S(2)}) %collective-permute-start.29) | collective-permute-done | bytes 32800 | tf_op jit(solution)/shard_map/ppermute | solution.py:25
  72.6 1.3 %shard_map.78 = (bf16[2,32,256]{2,1,0:T(8,128)(2,1)S(1)}, bf16[4,2,32,256]{3,2,1,0:T(8,128)(2,1)S(1)}, bf16[4,2,32,256]{3,2,1,0:T(8,128)(2,1)S(1)}, bf16[4,2,32,256]{3,2,1,0:T(8,128)(2,1)S(1)}) custom-call(bf16[2,32,256,256]{3,2,1,0:T(8,128)(2,1)S(1)} %get-tuple-element.70.spread, f32[2,32,256]{2,1,0:T(8,128)S(1)} %get-tuple-element.90.own, ...), custom_call_target="tpu_custom_call" | custom-call | flops 201326592 | tf_op jit(solution)/shard_map/pallas_call | solution.py:37
  73.9 1.6 %collective-permute-start.30 = (bf16[4,2,32,256]{3,2,1,0:T(8,128)(2,1)S(1)}, bf16[4,2,32,256]{3,2,1,0:T(8,128)(2,1)S(1)}, u32[]{:S(2)}, u32[]{:S(2)}) collective-permute-start(bf16[4,2,32,256]{3,2,1,0:T(8,128)(2,1)S(1)} %get-tuple-element.95), channel_id=1, source_target_pairs={{0,7},{1,6},{2,5},{3,4},{4,3},{5,2},{6,1},{7,0},{8,15},{9,14},{10,... | collective-permute-start | bytes 393224 | tf_op jit(solution)/shard_map/ppermute | solution.py:25
  75.5 0.7 collective-permute-start.31
  77.3 1.9 %collective-permute-done.30.a = bf16[4,2,32,256]{3,2,1,0:T(8,128)(2,1)S(1)} collective-permute-done((bf16[4,2,32,256]{3,2,1,0:T(8,128)(2,1)S(1)}, bf16[4,2,32,256]{3,2,1,0:T(8,128)(2,1)S(1)}, u32[]{:S(2)}, u32[]{:S(2)}) %collective-permute-start.30) | collective-permute-done | bytes 131104 | tf_op jit(solution)/shard_map/ppermute | solution.py:25
  79.2 1.3 %collective-permute-done.31.b = bf16[4,2,32,256]{3,2,1,0:T(8,128)(2,1)S(1)} collective-permute-done((bf16[4,2,32,256]{3,2,1,0:T(8,128)(2,1)S(1)}, bf16[4,2,32,256]{3,2,1,0:T(8,128)(2,1)S(1)}, u32[]{:S(2)}, u32[]{:S(2)}) %collective-permute-start.31) | collective-permute-done | bytes 131104 | tf_op jit(solution)/shard_map/ppermute | solution.py:25
  80.8 2.6 %collective-permute-start.34 = (bf16[2,32,256]{2,1,0:T(8,128)(2,1)S(1)}, bf16[2,32,256]{2,1,0:T(8,128)(2,1)S(1)}, u32[]{:S(2)}, u32[]{:S(2)}) collective-permute-start(bf16[2,32,256]{2,1,0:T(8,128)(2,1)S(1)} %get-tuple-element.100), channel_id=1, source_target_pairs={{0,16},{1,17},{2,18},{3,19},{4,20},{5,21},{6,22},{7,23},{8,24},{9,... | collective-permute-start | bytes 98312 | tf_op jit(solution)/shard_map/ppermute | solution.py:25
  83.3 1.3 %collective-permute-start.35 = (bf16[2,32,256]{2,1,0:T(8,128)(2,1)S(1)}, bf16[2,32,256]{2,1,0:T(8,128)(2,1)S(1)}, u32[]{:S(2)}, u32[]{:S(2)}) collective-permute-start(bf16[2,32,256]{2,1,0:T(8,128)(2,1)S(1)} %get-tuple-element.101), channel_id=1, source_target_pairs={{0,25},{1,24},{2,27},{3,26},{4,29},{5,28},{6,31},{7,30},{8,17},{9,... | collective-permute-start | bytes 98312 | tf_op jit(solution)/shard_map/ppermute | solution.py:25
  84.6 1.1 collective-permute-done.34.refs_1_
  85.7 3.1 %collective-permute-done.35.refs_2_ = bf16[2,32,256]{2,1,0:T(8,128)(2,1)S(1)} collective-permute-done((bf16[2,32,256]{2,1,0:T(8,128)(2,1)S(1)}, bf16[2,32,256]{2,1,0:T(8,128)(2,1)S(1)}, u32[]{:S(2)}, u32[]{:S(2)}) %collective-permute-start.35) | collective-permute-done | bytes 32800 | tf_op jit(solution)/shard_map/ppermute | solution.py:25
  88.8 1.3 %shard_map.81 = (bf16[2,32,256]{2,1,0:T(8,128)(2,1)S(1)}, bf16[4,2,32,256]{3,2,1,0:T(8,128)(2,1)S(1)}, bf16[4,2,32,256]{3,2,1,0:T(8,128)(2,1)S(1)}, bf16[4,2,32,256]{3,2,1,0:T(8,128)(2,1)S(1)}) custom-call(bf16[2,32,256,256]{3,2,1,0:T(8,128)(2,1)S(1)} %get-tuple-element.65.spread, f32[2,32,256]{2,1,0:T(8,128)S(1)} %get-tuple-element.98.own, ...), custom_call_target="tpu_custom_call" | custom-call | flops 201326592 | tf_op jit(solution)/shard_map/pallas_call | solution.py:37
  90.1 1.4 %collective-permute-start.36 = (bf16[4,2,32,256]{3,2,1,0:T(8,128)(2,1)S(1)}, bf16[4,2,32,256]{3,2,1,0:T(8,128)(2,1)S(1)}, u32[]{:S(2)}, u32[]{:S(2)}) collective-permute-start(bf16[4,2,32,256]{3,2,1,0:T(8,128)(2,1)S(1)} %get-tuple-element.103), channel_id=1, source_target_pairs={{0,7},{1,6},{2,5},{3,4},{4,3},{5,2},{6,1},{7,0},{8,15},{9,14},{10,... | collective-permute-start | bytes 393224 | tf_op jit(solution)/shard_map/ppermute | solution.py:25
  92.1 0.9 collective-permute-start.38
  93.1 3.5 %collective-permute-start.23 = (bf16[4,32,256]{2,1,0:T(8,128)(2,1)S(1)}, bf16[4,32,256]{2,1,0:T(8,128)(2,1)S(1)}, u32[]{:S(2)}, u32[]{:S(2)}) collective-permute-start(bf16[4,32,256]{2,1,0:T(8,128)(2,1)S(1)} %get-tuple-element.85), channel_id=1, source_target_pairs={{0,1},{1,0},{2,3},{3,2},{4,5},{5,4},{6,7},{7,6},{8,9},{9,8},{10,11... | collective-permute-start | bytes 196616 | tf_op jit(solution)/shard_map/ppermute | solution.py:25
  97.2 2.5 %collective-permute-start.40 = (bf16[2,32,256]{2,1,0:T(8,128)(2,1)S(1)}, bf16[2,32,256]{2,1,0:T(8,128)(2,1)S(1)}, u32[]{:S(2)}, u32[]{:S(2)}) collective-permute-start(bf16[2,32,256]{2,1,0:T(8,128)(2,1)S(1)} %get-tuple-element.108), channel_id=1, source_target_pairs={{0,16},{1,17},{2,18},{3,19},{4,20},{5,21},{6,22},{7,23},{8,24},{9,... | collective-permute-start | bytes 98312 | tf_op jit(solution)/shard_map/ppermute | solution.py:25
  99.7 1.3 %collective-permute-start.41 = (bf16[2,32,256]{2,1,0:T(8,128)(2,1)S(1)}, bf16[2,32,256]{2,1,0:T(8,128)(2,1)S(1)}, u32[]{:S(2)}, u32[]{:S(2)}) collective-permute-start(bf16[2,32,256]{2,1,0:T(8,128)(2,1)S(1)} %get-tuple-element.109), channel_id=1, source_target_pairs={{0,25},{1,24},{2,27},{3,26},{4,29},{5,28},{6,31},{7,30},{8,17},{9,... | collective-permute-start | bytes 98312 | tf_op jit(solution)/shard_map/ppermute | solution.py:25
  101.1 3.6 %collective-permute-start.43 = (bf16[3,32,256]{2,1,0:T(8,128)(2,1)S(1)}, bf16[3,32,256]{2,1,0:T(8,128)(2,1)S(1)}, u32[]{:S(2)}, u32[]{:S(2)}) collective-permute-start(bf16[3,32,256]{2,1,0:T(8,128)(2,1)S(1)} %get-tuple-element.113), channel_id=1, source_target_pairs={{0,1},{1,0},{2,3},{3,2},{4,5},{5,4},{6,7},{7,6},{8,9},{9,8},{10,11... | collective-permute-start | bytes 147464 | tf_op jit(solution)/shard_map/ppermute | solution.py:25
  105.0 2.9 %collective-permute-start.42 = (bf16[32,256]{1,0:T(8,128)(2,1)S(1)}, bf16[32,256]{1,0:T(8,128)(2,1)S(1)}, u32[]{:S(2)}, u32[]{:S(2)}) collective-permute-start(bf16[32,256]{1,0:T(8,128)(2,1)S(1)} %get-tuple-element.111), channel_id=1, source_target_pairs={{0,1},{1,0},{2,3},{3,2},{4,5},{5,4},{6,7},{7,6},{8,9},{9,8},{10,11... | collective-permute-start | bytes 49160 | tf_op jit(solution)/shard_map/ppermute | solution.py:25
  108.0 0.7 shard_map.75
  108.8 0.7 shard_map.86
  (59 shorter events, 7.3 us)
Async XLA Ops:
  1.8 1.9 %collective-permute-start = (bf16[32,256]{1,0:T(8,128)(2,1)S(1)}, bf16[32,256]{1,0:T(8,128)(2,1)S(1)}, u32[]{:S(2)}, u32[]{:S(2)}) collective-permute-start(bf16[32,256]{1,0:T(8,128)(2,1)S(1)} %get-tuple-element.59.after), channel_id=1, source_target_pairs={{0,1},{1,0},{2,3},{3,2},{4,5},{5,4},{6,7},{7,6},{8,9},{9,8},{10,11... | collective-permute-start | bytes 49160 | tf_op jit(solution)/shard_map/ppermute | solution.py:25
  2.3 1.4 %collective-permute-start.1 = (s32[3,1,16]{2,1,0:T(1,128)}, s32[3,1,16]{2,1,0:T(1,128)S(1)}, u32[]{:S(2)}, u32[]{:S(2)}) collective-permute-start(s32[3,1,16]{2,1,0:T(1,128)} %own_pattern.5), channel_id=1, source_target_pairs={{0,1},{1,0},{2,3},{3,2},{4,5},{5,4},{6,7},{7,6},{8,9},{9,8},{10,11... | collective-permute-start | bytes 584 | tf_op jit(solution)/shard_map/ppermute | solution.py:25
  2.4 0.9 copy-start
  3.7 14.5 %collective-permute-start.2 = (bf16[3,1,16,256,256]{4,3,2,1,0:T(8,128)(2,1)}, bf16[3,1,16,256,256]{4,3,2,1,0:T(8,128)(2,1)S(1)}, u32[]{:S(2)}, u32[]{:S(2)}) collective-permute-start(bf16[3,1,16,256,256]{4,3,2,1,0:T(8,128)(2,1)} %tiles0.5), channel_id=1, source_target_pairs={{0,1},{1,0},{2,3},{3,2},{4,5},{5,4},{6,7},{7,6},{8,9},{9,8},{10,11... | collective-permute-start | bytes 18874376 | tf_op jit(solution)/shard_map/ppermute | solution.py:25
  3.8 13.5 %collective-permute-start.3 = (bf16[4,1,256,256]{3,2,1,0:T(8,128)(2,1)}, bf16[4,1,256,256]{3,2,1,0:T(8,128)(2,1)S(1)}, u32[]{:S(2)}, u32[]{:S(2)}) collective-permute-start(bf16[4,1,256,256]{3,2,1,0:T(8,128)(2,1)} %diag0.5), channel_id=1, source_target_pairs={{0,1},{1,0},{2,3},{3,2},{4,5},{5,4},{6,7},{7,6},{8,9},{9,8},{10,11... | collective-permute-start | bytes 1572872 | tf_op jit(solution)/shard_map/ppermute | solution.py:25
  4.2 5.3 %collective-permute-start.5 = (bf16[2,32,256]{2,1,0:T(8,128)(2,1)S(1)}, bf16[2,32,256]{2,1,0:T(8,128)(2,1)S(1)}, u32[]{:S(2)}, u32[]{:S(2)}) collective-permute-start(bf16[2,32,256]{2,1,0:T(8,128)(2,1)S(1)} %get-tuple-element.117.after.refs_0_.known), channel_id=1, source_target_pairs={{0,9},{1,8},{2,11},{3,10},{4,13},{5,12},{6,15},{7,14},{8,1},{9,0},... | collective-permute-start | bytes 98312 | tf_op jit(solution)/shard_map/ppermute | solution.py:25
  6.9 5.2 %collective-permute-start.6 = (bf16[2,32,256]{2,1,0:T(8,128)(2,1)S(1)}, bf16[2,32,256]{2,1,0:T(8,128)(2,1)S(1)}, u32[]{:S(2)}, u32[]{:S(2)}) collective-permute-start(bf16[2,32,256]{2,1,0:T(8,128)(2,1)S(1)} %get-tuple-element.117.after.refs_0_.known), channel_id=1, source_target_pairs={{0,16},{1,17},{2,18},{3,19},{4,20},{5,21},{6,22},{7,23},{8,24},{9,... | collective-permute-start | bytes 98312 | tf_op jit(solution)/shard_map/ppermute | solution.py:25
  9.4 5.4 %collective-permute-start.7 = (bf16[2,32,256]{2,1,0:T(8,128)(2,1)S(1)}, bf16[2,32,256]{2,1,0:T(8,128)(2,1)S(1)}, u32[]{:S(2)}, u32[]{:S(2)}) collective-permute-start(bf16[2,32,256]{2,1,0:T(8,128)(2,1)S(1)} %get-tuple-element.117.after.refs_0_.known), channel_id=1, source_target_pairs={{0,25},{1,24},{2,27},{3,26},{4,29},{5,28},{6,31},{7,30},{8,17},{9,... | collective-permute-start | bytes 98312 | tf_op jit(solution)/shard_map/ppermute | solution.py:25
  9.5 15.9 %collective-permute-start.4 = (bf16[4,32,256]{2,1,0:T(8,128)(2,1)S(1)}, bf16[4,32,256]{2,1,0:T(8,128)(2,1)S(1)}, u32[]{:S(2)}, u32[]{:S(2)}) collective-permute-start(bf16[4,32,256]{2,1,0:T(8,128)(2,1)S(1)} %get-tuple-element.67), channel_id=1, source_target_pairs={{0,1},{1,0},{2,3},{3,2},{4,5},{5,4},{6,7},{7,6},{8,9},{9,8},{10,11... | collective-permute-start | bytes 196616 | tf_op jit(solution)/shard_map/ppermute | solution.py:25
  14.9 6.3 %collective-permute-start.10 = (bf16[4,2,32,256]{3,2,1,0:T(8,128)(2,1)S(1)}, bf16[4,2,32,256]{3,2,1,0:T(8,128)(2,1)S(1)}, u32[]{:S(2)}, u32[]{:S(2)}) collective-permute-start(bf16[4,2,32,256]{3,2,1,0:T(8,128)(2,1)S(1)} %pad_maximum_fusion.refs_0_), channel_id=1, source_target_pairs={{0,2},{1,3},{2,0},{3,1},{4,6},{5,7},{6,4},{7,5},{8,10},{9,11},{10,... | collective-permute-start | bytes 393224 | tf_op jit(solution)/shard_map/ppermute | solution.py:25
  16.4 7.1 %collective-permute-start.9 = (bf16[4,2,32,256]{3,2,1,0:T(8,128)(2,1)S(1)}, bf16[4,2,32,256]{3,2,1,0:T(8,128)(2,1)S(1)}, u32[]{:S(2)}, u32[]{:S(2)}) collective-permute-start(bf16[4,2,32,256]{3,2,1,0:T(8,128)(2,1)S(1)} %pad_maximum_fusion.refs_0_), channel_id=1, source_target_pairs={{0,7},{1,6},{2,5},{3,4},{4,3},{5,2},{6,1},{7,0},{8,15},{9,14},{10,... | collective-permute-start | bytes 393224 | tf_op jit(solution)/shard_map/ppermute | solution.py:25
  17.4 8.1 %collective-permute-start.8 = (bf16[4,2,32,256]{3,2,1,0:T(8,128)(2,1)S(1)}, bf16[4,2,32,256]{3,2,1,0:T(8,128)(2,1)S(1)}, u32[]{:S(2)}, u32[]{:S(2)}) collective-permute-start(bf16[4,2,32,256]{3,2,1,0:T(8,128)(2,1)S(1)} %pad_maximum_fusion.refs_0_), channel_id=1, source_target_pairs={{0,5},{1,4},{2,7},{3,6},{4,1},{5,0},{6,3},{7,2},{8,13},{9,12},{10,... | collective-permute-start | bytes 393224 | tf_op jit(solution)/shard_map/ppermute | solution.py:25
  26.3 6.7 %collective-permute-start.11 = (bf16[2,32,256]{2,1,0:T(8,128)(2,1)S(1)}, bf16[2,32,256]{2,1,0:T(8,128)(2,1)S(1)}, u32[]{:S(2)}, u32[]{:S(2)}) collective-permute-start(bf16[2,32,256]{2,1,0:T(8,128)(2,1)S(1)} %shard_map.63.after.refs_1_.known), channel_id=1, source_target_pairs={{0,9},{1,8},{2,11},{3,10},{4,13},{5,12},{6,15},{7,14},{8,1},{9,0},... | collective-permute-start | bytes 98312 | tf_op jit(solution)/shard_map/ppermute | solution.py:25
  26.3 6.6 %collective-permute-start.12 = (bf16[2,32,256]{2,1,0:T(8,128)(2,1)S(1)}, bf16[2,32,256]{2,1,0:T(8,128)(2,1)S(1)}, u32[]{:S(2)}, u32[]{:S(2)}) collective-permute-start(bf16[2,32,256]{2,1,0:T(8,128)(2,1)S(1)} %shard_map.63.after.refs_1_.known), channel_id=1, source_target_pairs={{0,16},{1,17},{2,18},{3,19},{4,20},{5,21},{6,22},{7,23},{8,24},{9,... | collective-permute-start | bytes 98312 | tf_op jit(solution)/shard_map/ppermute | solution.py:25
  28.5 5.1 %collective-permute-start.13 = (bf16[2,32,256]{2,1,0:T(8,128)(2,1)S(1)}, bf16[2,32,256]{2,1,0:T(8,128)(2,1)S(1)}, u32[]{:S(2)}, u32[]{:S(2)}) collective-permute-start(bf16[2,32,256]{2,1,0:T(8,128)(2,1)S(1)} %shard_map.63.after.refs_1_.known), channel_id=1, source_target_pairs={{0,25},{1,24},{2,27},{3,26},{4,29},{5,28},{6,31},{7,30},{8,17},{9,... | collective-permute-start | bytes 98312 | tf_op jit(solution)/shard_map/ppermute | solution.py:25
  33.7 5.4 %collective-permute-start.16 = (bf16[4,2,32,256]{3,2,1,0:T(8,128)(2,1)S(1)}, bf16[4,2,32,256]{3,2,1,0:T(8,128)(2,1)S(1)}, u32[]{:S(2)}, u32[]{:S(2)}) collective-permute-start(bf16[4,2,32,256]{3,2,1,0:T(8,128)(2,1)S(1)} %pad_maximum_fusion.1.part), channel_id=1, source_target_pairs={{0,7},{1,6},{2,5},{3,4},{4,3},{5,2},{6,1},{7,0},{8,15},{9,14},{10,... | collective-permute-start | bytes 393224 | tf_op jit(solution)/shard_map/ppermute | solution.py:25
  35.0 5.1 %collective-permute-start.15 = (bf16[4,2,32,256]{3,2,1,0:T(8,128)(2,1)S(1)}, bf16[4,2,32,256]{3,2,1,0:T(8,128)(2,1)S(1)}, u32[]{:S(2)}, u32[]{:S(2)}) collective-permute-start(bf16[4,2,32,256]{3,2,1,0:T(8,128)(2,1)S(1)} %pad_maximum_fusion.1.part), channel_id=1, source_target_pairs={{0,2},{1,3},{2,0},{3,1},{4,6},{5,7},{6,4},{7,5},{8,10},{9,11},{10,... | collective-permute-start | bytes 393224 | tf_op jit(solution)/shard_map/ppermute | solution.py:25
  35.8 5.1 %collective-permute-start.14 = (bf16[4,2,32,256]{3,2,1,0:T(8,128)(2,1)S(1)}, bf16[4,2,32,256]{3,2,1,0:T(8,128)(2,1)S(1)}, u32[]{:S(2)}, u32[]{:S(2)}) collective-permute-start(bf16[4,2,32,256]{3,2,1,0:T(8,128)(2,1)S(1)} %pad_maximum_fusion.1.part), channel_id=1, source_target_pairs={{0,5},{1,4},{2,7},{3,6},{4,1},{5,0},{6,3},{7,2},{8,13},{9,12},{10,... | collective-permute-start | bytes 393224 | tf_op jit(solution)/shard_map/ppermute | solution.py:25
  41.7 6.7 %collective-permute-start.17 = (bf16[2,32,256]{2,1,0:T(8,128)(2,1)S(1)}, bf16[2,32,256]{2,1,0:T(8,128)(2,1)S(1)}, u32[]{:S(2)}, u32[]{:S(2)}) collective-permute-start(bf16[2,32,256]{2,1,0:T(8,128)(2,1)S(1)} %shard_map.68.after.refs_2_.known), channel_id=1, source_target_pairs={{0,9},{1,8},{2,11},{3,10},{4,13},{5,12},{6,15},{7,14},{8,1},{9,0},... | collective-permute-start | bytes 98312 | tf_op jit(solution)/shard_map/ppermute | solution.py:25
  41.7 6.6 %collective-permute-start.18 = (bf16[2,32,256]{2,1,0:T(8,128)(2,1)S(1)}, bf16[2,32,256]{2,1,0:T(8,128)(2,1)S(1)}, u32[]{:S(2)}, u32[]{:S(2)}) collective-permute-start(bf16[2,32,256]{2,1,0:T(8,128)(2,1)S(1)} %shard_map.68.after.refs_2_.known), channel_id=1, source_target_pairs={{0,16},{1,17},{2,18},{3,19},{4,20},{5,21},{6,22},{7,23},{8,24},{9,... | collective-permute-start | bytes 98312 | tf_op jit(solution)/shard_map/ppermute | solution.py:25
  44.0 5.5 %collective-permute-start.19 = (bf16[2,32,256]{2,1,0:T(8,128)(2,1)S(1)}, bf16[2,32,256]{2,1,0:T(8,128)(2,1)S(1)}, u32[]{:S(2)}, u32[]{:S(2)}) collective-permute-start(bf16[2,32,256]{2,1,0:T(8,128)(2,1)S(1)} %shard_map.68.after.refs_2_.known), channel_id=1, source_target_pairs={{0,25},{1,24},{2,27},{3,26},{4,29},{5,28},{6,31},{7,30},{8,17},{9,... | collective-permute-start | bytes 98312 | tf_op jit(solution)/shard_map/ppermute | solution.py:25
  49.4 5.4 %collective-permute-start.22 = (bf16[4,2,32,256]{3,2,1,0:T(8,128)(2,1)S(1)}, bf16[4,2,32,256]{3,2,1,0:T(8,128)(2,1)S(1)}, u32[]{:S(2)}, u32[]{:S(2)}) collective-permute-start(bf16[4,2,32,256]{3,2,1,0:T(8,128)(2,1)S(1)} %pad_maximum_fusion.2.part), channel_id=1, source_target_pairs={{0,7},{1,6},{2,5},{3,4},{4,3},{5,2},{6,1},{7,0},{8,15},{9,14},{10,... | collective-permute-start | bytes 393224 | tf_op jit(solution)/shard_map/ppermute | solution.py:25
  50.9 5.0 %collective-permute-start.21 = (bf16[4,2,32,256]{3,2,1,0:T(8,128)(2,1)S(1)}, bf16[4,2,32,256]{3,2,1,0:T(8,128)(2,1)S(1)}, u32[]{:S(2)}, u32[]{:S(2)}) collective-permute-start(bf16[4,2,32,256]{3,2,1,0:T(8,128)(2,1)S(1)} %pad_maximum_fusion.2.part), channel_id=1, source_target_pairs={{0,2},{1,3},{2,0},{3,1},{4,6},{5,7},{6,4},{7,5},{8,10},{9,11},{10,... | collective-permute-start | bytes 393224 | tf_op jit(solution)/shard_map/ppermute | solution.py:25
  51.6 5.1 %collective-permute-start.20 = (bf16[4,2,32,256]{3,2,1,0:T(8,128)(2,1)S(1)}, bf16[4,2,32,256]{3,2,1,0:T(8,128)(2,1)S(1)}, u32[]{:S(2)}, u32[]{:S(2)}) collective-permute-start(bf16[4,2,32,256]{3,2,1,0:T(8,128)(2,1)S(1)} %pad_maximum_fusion.2.part), channel_id=1, source_target_pairs={{0,5},{1,4},{2,7},{3,6},{4,1},{5,0},{6,3},{7,2},{8,13},{9,12},{10,... | collective-permute-start | bytes 393224 | tf_op jit(solution)/shard_map/ppermute | solution.py:25
  58.8 5.4 %collective-permute-start.24 = (bf16[4,2,32,256]{3,2,1,0:T(8,128)(2,1)S(1)}, bf16[4,2,32,256]{3,2,1,0:T(8,128)(2,1)S(1)}, u32[]{:S(2)}, u32[]{:S(2)}) collective-permute-start(bf16[4,2,32,256]{3,2,1,0:T(8,128)(2,1)S(1)} %get-tuple-element.87), channel_id=1, source_target_pairs={{0,7},{1,6},{2,5},{3,4},{4,3},{5,2},{6,1},{7,0},{8,15},{9,14},{10,... | collective-permute-start | bytes 393224 | tf_op jit(solution)/shard_map/ppermute | solution.py:25
  59.9 5.2 %collective-permute-start.25 = (bf16[4,2,32,256]{3,2,1,0:T(8,128)(2,1)S(1)}, bf16[4,2,32,256]{3,2,1,0:T(8,128)(2,1)S(1)}, u32[]{:S(2)}, u32[]{:S(2)}) collective-permute-start(bf16[4,2,32,256]{3,2,1,0:T(8,128)(2,1)S(1)} %get-tuple-element.88), channel_id=1, source_target_pairs={{0,2},{1,3},{2,0},{3,1},{4,6},{5,7},{6,4},{7,5},{8,10},{9,11},{10,... | collective-permute-start | bytes 393224 | tf_op jit(solution)/shard_map/ppermute | solution.py:25
  60.7 4.8 %collective-permute-start.26 = (bf16[4,2,32,256]{3,2,1,0:T(8,128)(2,1)S(1)}, bf16[4,2,32,256]{3,2,1,0:T(8,128)(2,1)S(1)}, u32[]{:S(2)}, u32[]{:S(2)}) collective-permute-start(bf16[4,2,32,256]{3,2,1,0:T(8,128)(2,1)S(1)} %get-tuple-element.89), channel_id=1, source_target_pairs={{0,5},{1,4},{2,7},{3,6},{4,1},{5,0},{6,3},{7,2},{8,13},{9,12},{10,... | collective-permute-start | bytes 393224 | tf_op jit(solution)/shard_map/ppermute | solution.py:25
  65.6 3.9 %collective-permute-start.27 = (bf16[2,32,256]{2,1,0:T(8,128)(2,1)S(1)}, bf16[2,32,256]{2,1,0:T(8,128)(2,1)S(1)}, u32[]{:S(2)}, u32[]{:S(2)}) collective-permute-start(bf16[2,32,256]{2,1,0:T(8,128)(2,1)S(1)} %get-tuple-element.91), channel_id=1, source_target_pairs={{0,9},{1,8},{2,11},{3,10},{4,13},{5,12},{6,15},{7,14},{8,1},{9,0},... | collective-permute-start | bytes 98312 | tf_op jit(solution)/shard_map/ppermute | solution.py:25
  65.6 4.9 %collective-permute-start.28 = (bf16[2,32,256]{2,1,0:T(8,128)(2,1)S(1)}, bf16[2,32,256]{2,1,0:T(8,128)(2,1)S(1)}, u32[]{:S(2)}, u32[]{:S(2)}) collective-permute-start(bf16[2,32,256]{2,1,0:T(8,128)(2,1)S(1)} %get-tuple-element.92), channel_id=1, source_target_pairs={{0,16},{1,17},{2,18},{3,19},{4,20},{5,21},{6,22},{7,23},{8,24},{9,... | collective-permute-start | bytes 98312 | tf_op jit(solution)/shard_map/ppermute | solution.py:25
  67.4 5.2 %collective-permute-start.29 = (bf16[2,32,256]{2,1,0:T(8,128)(2,1)S(1)}, bf16[2,32,256]{2,1,0:T(8,128)(2,1)S(1)}, u32[]{:S(2)}, u32[]{:S(2)}) collective-permute-start(bf16[2,32,256]{2,1,0:T(8,128)(2,1)S(1)} %get-tuple-element.93), channel_id=1, source_target_pairs={{0,25},{1,24},{2,27},{3,26},{4,29},{5,28},{6,31},{7,30},{8,17},{9,... | collective-permute-start | bytes 98312 | tf_op jit(solution)/shard_map/ppermute | solution.py:25
  73.9 5.3 %collective-permute-start.30 = (bf16[4,2,32,256]{3,2,1,0:T(8,128)(2,1)S(1)}, bf16[4,2,32,256]{3,2,1,0:T(8,128)(2,1)S(1)}, u32[]{:S(2)}, u32[]{:S(2)}) collective-permute-start(bf16[4,2,32,256]{3,2,1,0:T(8,128)(2,1)S(1)} %get-tuple-element.95), channel_id=1, source_target_pairs={{0,7},{1,6},{2,5},{3,4},{4,3},{5,2},{6,1},{7,0},{8,15},{9,14},{10,... | collective-permute-start | bytes 393224 | tf_op jit(solution)/shard_map/ppermute | solution.py:25
  75.5 5.1 %collective-permute-start.31 = (bf16[4,2,32,256]{3,2,1,0:T(8,128)(2,1)S(1)}, bf16[4,2,32,256]{3,2,1,0:T(8,128)(2,1)S(1)}, u32[]{:S(2)}, u32[]{:S(2)}) collective-permute-start(bf16[4,2,32,256]{3,2,1,0:T(8,128)(2,1)S(1)} %get-tuple-element.96), channel_id=1, source_target_pairs={{0,2},{1,3},{2,0},{3,1},{4,6},{5,7},{6,4},{7,5},{8,10},{9,11},{10,... | collective-permute-start | bytes 393224 | tf_op jit(solution)/shard_map/ppermute | solution.py:25
  76.2 4.4 %collective-permute-start.32 = (bf16[4,2,32,256]{3,2,1,0:T(8,128)(2,1)S(1)}, bf16[4,2,32,256]{3,2,1,0:T(8,128)(2,1)S(1)}, u32[]{:S(2)}, u32[]{:S(2)}) collective-permute-start(bf16[4,2,32,256]{3,2,1,0:T(8,128)(2,1)S(1)} %get-tuple-element.97), channel_id=1, source_target_pairs={{0,5},{1,4},{2,7},{3,6},{4,1},{5,0},{6,3},{7,2},{8,13},{9,12},{10,... | collective-permute-start | bytes 393224 | tf_op jit(solution)/shard_map/ppermute | solution.py:25
  80.7 3.9 %collective-permute-start.33 = (bf16[2,32,256]{2,1,0:T(8,128)(2,1)S(1)}, bf16[2,32,256]{2,1,0:T(8,128)(2,1)S(1)}, u32[]{:S(2)}, u32[]{:S(2)}) collective-permute-start(bf16[2,32,256]{2,1,0:T(8,128)(2,1)S(1)} %get-tuple-element.99), channel_id=1, source_target_pairs={{0,9},{1,8},{2,11},{3,10},{4,13},{5,12},{6,15},{7,14},{8,1},{9,0},... | collective-permute-start | bytes 98312 | tf_op jit(solution)/shard_map/ppermute | solution.py:25
  80.8 4.9 %collective-permute-start.34 = (bf16[2,32,256]{2,1,0:T(8,128)(2,1)S(1)}, bf16[2,32,256]{2,1,0:T(8,128)(2,1)S(1)}, u32[]{:S(2)}, u32[]{:S(2)}) collective-permute-start(bf16[2,32,256]{2,1,0:T(8,128)(2,1)S(1)} %get-tuple-element.100), channel_id=1, source_target_pairs={{0,16},{1,17},{2,18},{3,19},{4,20},{5,21},{6,22},{7,23},{8,24},{9,... | collective-permute-start | bytes 98312 | tf_op jit(solution)/shard_map/ppermute | solution.py:25
  83.3 5.4 %collective-permute-start.35 = (bf16[2,32,256]{2,1,0:T(8,128)(2,1)S(1)}, bf16[2,32,256]{2,1,0:T(8,128)(2,1)S(1)}, u32[]{:S(2)}, u32[]{:S(2)}) collective-permute-start(bf16[2,32,256]{2,1,0:T(8,128)(2,1)S(1)} %get-tuple-element.101), channel_id=1, source_target_pairs={{0,25},{1,24},{2,27},{3,26},{4,29},{5,28},{6,31},{7,30},{8,17},{9,... | collective-permute-start | bytes 98312 | tf_op jit(solution)/shard_map/ppermute | solution.py:25
  90.1 7.0 %collective-permute-start.36 = (bf16[4,2,32,256]{3,2,1,0:T(8,128)(2,1)S(1)}, bf16[4,2,32,256]{3,2,1,0:T(8,128)(2,1)S(1)}, u32[]{:S(2)}, u32[]{:S(2)}) collective-permute-start(bf16[4,2,32,256]{3,2,1,0:T(8,128)(2,1)S(1)} %get-tuple-element.103), channel_id=1, source_target_pairs={{0,7},{1,6},{2,5},{3,4},{4,3},{5,2},{6,1},{7,0},{8,15},{9,14},{10,... | collective-permute-start | bytes 393224 | tf_op jit(solution)/shard_map/ppermute | solution.py:25
  91.5 5.6 %collective-permute-start.37 = (bf16[4,2,32,256]{3,2,1,0:T(8,128)(2,1)S(1)}, bf16[4,2,32,256]{3,2,1,0:T(8,128)(2,1)S(1)}, u32[]{:S(2)}, u32[]{:S(2)}) collective-permute-start(bf16[4,2,32,256]{3,2,1,0:T(8,128)(2,1)S(1)} %get-tuple-element.104), channel_id=1, source_target_pairs={{0,2},{1,3},{2,0},{3,1},{4,6},{5,7},{6,4},{7,5},{8,10},{9,11},{10,... | collective-permute-start | bytes 393224 | tf_op jit(solution)/shard_map/ppermute | solution.py:25
  92.1 5.0 %collective-permute-start.38 = (bf16[4,2,32,256]{3,2,1,0:T(8,128)(2,1)S(1)}, bf16[4,2,32,256]{3,2,1,0:T(8,128)(2,1)S(1)}, u32[]{:S(2)}, u32[]{:S(2)}) collective-permute-start(bf16[4,2,32,256]{3,2,1,0:T(8,128)(2,1)S(1)} %get-tuple-element.105), channel_id=1, source_target_pairs={{0,5},{1,4},{2,7},{3,6},{4,1},{5,0},{6,3},{7,2},{8,13},{9,12},{10,... | collective-permute-start | bytes 393224 | tf_op jit(solution)/shard_map/ppermute | solution.py:25
  93.1 14.9 %collective-permute-start.23 = (bf16[4,32,256]{2,1,0:T(8,128)(2,1)S(1)}, bf16[4,32,256]{2,1,0:T(8,128)(2,1)S(1)}, u32[]{:S(2)}, u32[]{:S(2)}) collective-permute-start(bf16[4,32,256]{2,1,0:T(8,128)(2,1)S(1)} %get-tuple-element.85), channel_id=1, source_target_pairs={{0,1},{1,0},{2,3},{3,2},{4,5},{5,4},{6,7},{7,6},{8,9},{9,8},{10,11... | collective-permute-start | bytes 196616 | tf_op jit(solution)/shard_map/ppermute | solution.py:25
  97.2 7.5 %collective-permute-start.39 = (bf16[2,32,256]{2,1,0:T(8,128)(2,1)S(1)}, bf16[2,32,256]{2,1,0:T(8,128)(2,1)S(1)}, u32[]{:S(2)}, u32[]{:S(2)}) collective-permute-start(bf16[2,32,256]{2,1,0:T(8,128)(2,1)S(1)} %get-tuple-element.107), channel_id=1, source_target_pairs={{0,9},{1,8},{2,11},{3,10},{4,13},{5,12},{6,15},{7,14},{8,1},{9,0},... | collective-permute-start | bytes 98312 | tf_op jit(solution)/shard_map/ppermute | solution.py:25
  97.2 7.5 %collective-permute-start.40 = (bf16[2,32,256]{2,1,0:T(8,128)(2,1)S(1)}, bf16[2,32,256]{2,1,0:T(8,128)(2,1)S(1)}, u32[]{:S(2)}, u32[]{:S(2)}) collective-permute-start(bf16[2,32,256]{2,1,0:T(8,128)(2,1)S(1)} %get-tuple-element.108), channel_id=1, source_target_pairs={{0,16},{1,17},{2,18},{3,19},{4,20},{5,21},{6,22},{7,23},{8,24},{9,... | collective-permute-start | bytes 98312 | tf_op jit(solution)/shard_map/ppermute | solution.py:25
  99.7 5.1 %collective-permute-start.41 = (bf16[2,32,256]{2,1,0:T(8,128)(2,1)S(1)}, bf16[2,32,256]{2,1,0:T(8,128)(2,1)S(1)}, u32[]{:S(2)}, u32[]{:S(2)}) collective-permute-start(bf16[2,32,256]{2,1,0:T(8,128)(2,1)S(1)} %get-tuple-element.109), channel_id=1, source_target_pairs={{0,25},{1,24},{2,27},{3,26},{4,29},{5,28},{6,31},{7,30},{8,17},{9,... | collective-permute-start | bytes 98312 | tf_op jit(solution)/shard_map/ppermute | solution.py:25
  101.1 7.6 %collective-permute-start.43 = (bf16[3,32,256]{2,1,0:T(8,128)(2,1)S(1)}, bf16[3,32,256]{2,1,0:T(8,128)(2,1)S(1)}, u32[]{:S(2)}, u32[]{:S(2)}) collective-permute-start(bf16[3,32,256]{2,1,0:T(8,128)(2,1)S(1)} %get-tuple-element.113), channel_id=1, source_target_pairs={{0,1},{1,0},{2,3},{3,2},{4,5},{5,4},{6,7},{7,6},{8,9},{9,8},{10,11... | collective-permute-start | bytes 147464 | tf_op jit(solution)/shard_map/ppermute | solution.py:25
  105.0 3.8 %collective-permute-start.42 = (bf16[32,256]{1,0:T(8,128)(2,1)S(1)}, bf16[32,256]{1,0:T(8,128)(2,1)S(1)}, u32[]{:S(2)}, u32[]{:S(2)}) collective-permute-start(bf16[32,256]{1,0:T(8,128)(2,1)S(1)} %get-tuple-element.111), channel_id=1, source_target_pairs={{0,1},{1,0},{2,3},{3,2},{4,5},{5,4},{6,7},{7,6},{8,9},{9,8},{10,11... | collective-permute-start | bytes 49160 | tf_op jit(solution)/shard_map/ppermute | solution.py:25
